TPU v7x, 32 devices: a whole 2x2x4 slice. The times are simulated.
32 devices in a mesh: row: 4 (over x, core), col: 8 (over z, y).
Axes of the slice: x: 2, y: 2, z: 4, core: 2. Of those that a mesh axis runs over, the one named last changes fastest.
Arguments:
- inputs: bfloat16 [256, 8192], P(None, 'row'), may hold values from -6 to 6
- gate_weight: bfloat16 [8192, 28672], P('row', 'col'), may hold values from -0.0625 to 0.0625
- up_weight: bfloat16 [8192, 28672], P('row', 'col'), may hold values from -0.0625 to 0.0625
- hidden_grad: bfloat16 [256, 28672], P('row', 'col'), may hold values from -6 to 6
Outputs:
- hidden: bfloat16 [256, 28672], P('row', 'col')
- input_grad: bfloat16 [256, 8192], P('col', 'row')
- gate_weight_grad: bfloat16 [8192, 28672], P('row', 'col')
- up_weight_grad: bfloat16 [8192, 28672], P('row', 'col')
All inputs are finite; a program needn't handle non-finite values.
Results may differ from a plain program's by a relative error of at most 0.005.
Values may be sent and summed in bfloat16 or wider, within the bound.
No kernel may reach another device: no remote copies, remote signals or barrier semaphores. Data moves between devices by JAX's collectives and lax.ppermute only.
A program may use at most 192 MiB of HBM per device.

v0:
```python
import jax
import jax.numpy as jnp
from jax import lax
from jax.sharding import PartitionSpec as P


def weight_term(token_rows, grad_piece):
    return lax.dot_general(
        token_rows, grad_piece, (((0,), (0,)), ((), ())), preferred_element_type=jnp.float32
    )


def input_term(grad_piece, weight_block):
    return lax.dot_general(
        grad_piece, weight_block, (((1,), (1,)), ((), ())), preferred_element_type=jnp.float32
    )


def local(inputs, gate_weight, up_weight, hidden_grad):
    token_rows = inputs
    gate_pre = lax.psum_scatter(
        jnp.dot(token_rows, gate_weight, preferred_element_type=jnp.float32),
        "row",
        scatter_dimension=0,
        tiled=True,
    )
    token_rows = inputs
    up_pre = lax.psum_scatter(
        jnp.dot(token_rows, up_weight, preferred_element_type=jnp.float32),
        "row",
        scatter_dimension=0,
        tiled=True,
    )
    sigma_gate = jax.nn.sigmoid(gate_pre)
    hidden = (gate_pre * sigma_gate * up_pre).astype(jnp.bfloat16)
    upstream = hidden_grad.astype(jnp.float32)
    gate_grad = (upstream * up_pre * sigma_gate * (1.0 + gate_pre * (1.0 - sigma_gate))).astype(
        jnp.bfloat16
    )
    up_grad = (upstream * gate_pre * sigma_gate).astype(jnp.bfloat16)
    grad_piece = lax.all_gather(gate_grad, "row", axis=0, tiled=True)
    token_rows = inputs
    gate_total = weight_term(token_rows, grad_piece)
    partial_value = input_term(grad_piece, gate_weight)
    input_total = partial_value
    gate_total, input_total = (gate_total, input_total)
    grad_piece = lax.all_gather(up_grad, "row", axis=0, tiled=True)
    token_rows = inputs
    up_total = weight_term(token_rows, grad_piece)
    earlier = input_total
    partial_value = earlier + input_term(grad_piece, up_weight)
    up_total, input_total = (up_total, partial_value)
    input_grad = lax.psum_scatter(input_total, "col", scatter_dimension=0, tiled=True).astype(
        jnp.bfloat16
    )
    return (hidden, input_grad, gate_total.astype(jnp.bfloat16), up_total.astype(jnp.bfloat16))


def solution(mesh):
    return jax.shard_map(
        local,
        mesh=mesh,
        in_specs=(P(None, "row"), P("row", "col"), P("row", "col"), P("row", "col")),
        out_specs=(P("row", "col"), P("col", "row"), P("row", "col"), P("row", "col")),
        check_vma=False,
    )
```

profile of v0, /device:TPU:0, one launch (start us, length us, event | category | flops | bytes accessed | tf_op | source)
XLA Modules:
  0.0 241.5 jit_solution(16381994101330893312)
XLA Ops:
  7.2 0.0 copy-start
  7.2 0.0 reduce-scatter.4.cloned.1.call-start
  7.2 1.2 copy-done
  8.4 9.1 %fusion.7 = f32[256,3584]{1,0:T(8,128)} fusion(bf16[256,2048]{1,0:T(8,128)(2,1)S(1)} %copy-done, bf16[2048,3584]{1,0:T(8,128)(2,1)} %param.5), kind=kOutput, calls=%fused_computation.14 | convolution fusion | flops 3758096384 | bytes 19398656 | tf_op jit(solution)/shard_map/dot_general | solution.py:22
  17.5 0.0 reduce-scatter.4.cloned.1.call-update
  17.5 0.0 reduce-scatter.6.cloned.1.call-start
  17.5 9.1 %fusion.8 = f32[256,3584]{1,0:T(8,128)} fusion(bf16[256,2048]{1,0:T(8,128)(2,1)S(1)} %copy-done, bf16[2048,3584]{1,0:T(8,128)(2,1)} %param.6), kind=kOutput, calls=%fused_computation.15 | convolution fusion | flops 3758096384 | bytes 19398656 | tf_op jit(solution)/shard_map/dot_general | solution.py:29
  26.6 0.0 copy-start.3
  26.6 0.0 reduce-scatter.6.cloned.1.call-update
  26.6 0.0 all-gather.3.cloned.1.call-start
  26.7 34.9 %reduce-scatter.4.cloned.1.call-done = f32[64,3584]{1,0:T(8,128)} async-done(((f32[256,3584]{1,0:T(8,128)}), f32[64,3584]{1,0:T(8,128)}) %reduce-scatter.4.cloned.1.call-update) | async-done | bytes 917520 | tf_op jit(solution)/shard_map/reduce_scatter | solution.py:21
  61.6 44.5 %reduce-scatter.6.cloned.1.call-done = f32[64,3584]{1,0:T(8,128)} async-done(((f32[256,3584]{1,0:T(8,128)}), f32[64,3584]{1,0:T(8,128)}) %reduce-scatter.6.cloned.1.call-update) | async-done | bytes 917520 | tf_op jit(solution)/shard_map/reduce_scatter | solution.py:28
  106.1 0.0 copy-done.3
  106.1 3.0 %fusion.4 = (bf16[64,3584]{1,0:T(8,128)(2,1)}, bf16[64,3584]{1,0:T(8,128)(2,1)}, bf16[64,3584]{1,0:T(8,128)(2,1)}) fusion(f32[64,3584]{1,0:T(8,128)} %reduce-scatter.6.cloned.1.call-done, bf16[64,3584]{1,0:T(8,128)(2,1)S(1)} %copy-done.3, f32[64,3584]{1,0:T(8,128)} %reduce-scatter.4.cloned.1.call-done), kind=kLoop, calls=%fused_computation.9 | loop fusion | flops 3899392 | bytes 3670016 | tf_op jit(solution)/shard_map/convert_element_type | solution.py:37
  109.1 0.0 all-gather.3.cloned.1.call-update
  109.1 0.0 all-gather.5.cloned.1.call-start
  109.2 0.5 all-gather.5.cloned.1.call-update
  109.7 0.2 reduce-scatter.8.cloned.1.call-start
  109.9 20.5 %all-gather.3.cloned.1.call-done = bf16[256,3584]{1,0:T(8,128)(2,1)} async-done(((bf16[64,3584]{1,0:T(8,128)(2,1)}), bf16[256,3584]{1,0:T(8,128)(2,1)}) %all-gather.3.cloned.1.call-update) | async-done | bytes 1835024 | tf_op jit(solution)/shard_map/all_gather | solution.py:41
  130.4 11.0 %fusion.9 = f32[256,2048]{1,0:T(8,128)} fusion(bf16[256,3584]{1,0:T(8,128)(2,1)} %all-gather.3.cloned.1.call-done, bf16[2048,3584]{1,0:T(8,128)(2,1)} %param.5), kind=kOutput, calls=%fused_computation.16 | convolution fusion | flops 3758096384 | bytes 18612224 | tf_op jit(solution)/shard_map/dot_general | solution.py:14
  141.4 12.1 %all-gather.5.cloned.1.call-done = bf16[256,3584]{1,0:T(8,128)(2,1)} async-done(((bf16[64,3584]{1,0:T(8,128)(2,1)}), bf16[256,3584]{1,0:T(8,128)(2,1)}) %all-gather.5.cloned.1.call-update) | async-done | bytes 1835024 | tf_op jit(solution)/shard_map/all_gather | solution.py:47
  153.5 0.0 copy-start.2
  153.6 11.7 %convolution_add_fusion = f32[256,2048]{1,0:T(8,128)} fusion(f32[256,2048]{1,0:T(8,128)} %fusion.9, bf16[256,3584]{1,0:T(8,128)(2,1)} %all-gather.5.cloned.1.call-done, bf16[2048,3584]{1,0:T(8,128)(2,1)} %param.6), kind=kOutput, calls=%fused_computation.4 | convolution fusion | flops 3758620672 | bytes 20709376 | tf_op jit(solution)/shard_map/dot_general | solution.py:14
  165.2 0.0 reduce-scatter.8.cloned.1.call-update
  165.3 0.0 copy-done.2
  165.3 7.6 %fusion.1 = bf16[2048,3584]{0,1:T(8,128)(2,1)} fusion(bf16[256,3584]{1,0:T(8,128)(2,1)S(1)} %copy-done.2, bf16[256,2048]{1,0:T(8,128)(2,1)S(1)} %copy-done), kind=kOutput, calls=%fused_computation.3 | convolution fusion | flops 3765436416 | bytes 17563648 | tf_op jit(solution)/shard_map/dot_general | solution.py:8
  172.9 18.9 %copy.9 = bf16[2048,3584]{1,0:T(8,128)(2,1)} copy(bf16[2048,3584]{0,1:T(8,128)(2,1)} %fusion.1) | data formatting | bytes 29360128
  191.7 0.0 copy-done.1
  191.7 7.4 %fusion = bf16[2048,3584]{0,1:T(8,128)(2,1)} fusion(bf16[256,3584]{1,0:T(8,128)(2,1)S(1)} %copy-done.1, bf16[256,2048]{1,0:T(8,128)(2,1)S(1)} %copy-done), kind=kOutput, calls=%fused_computation.2 | convolution fusion | flops 3765436416 | bytes 17563648 | tf_op jit(solution)/shard_map/dot_general | solution.py:8
  199.2 18.7 %copy.8 = bf16[2048,3584]{1,0:T(8,128)(2,1)} copy(bf16[2048,3584]{0,1:T(8,128)(2,1)} %fusion) | data formatting | bytes 29360128
  217.8 15.5 %reduce-scatter.8.cloned.1.call-done = f32[32,2048]{1,0:T(8,128)} async-done(((f32[256,2048]{1,0:T(8,128)}), f32[32,2048]{1,0:T(8,128)}) %reduce-scatter.8.cloned.1.call-update) | async-done | bytes 262160 | tf_op jit(solution)/shard_map/reduce_scatter | solution.py:53
  233.3 1.6 convert_element_type.31
  (1 shorter events, 0.0 us)
Async XLA Ops:
  7.2 1.2 copy-start
  7.2 54.4 %reduce-scatter.4.cloned.1.call-start = ((), (), s32[]{:S(2)}) async-start(), calls=%async_computation.3 | async-start | bytes 4587520 | tf_op jit(solution)/shard_map/reduce_scatter | solution.py:21
  17.5 88.6 %reduce-scatter.6.cloned.1.call-start = ((), (), s32[]{:S(2)}) async-start(), calls=%async_computation.4 | async-start | bytes 4587520 | tf_op jit(solution)/shard_map/reduce_scatter | solution.py:28
  26.6 79.5 %copy-start.3 = (bf16[64,3584]{1,0:T(8,128)(2,1)S(1)}, bf16[64,3584]{1,0:T(8,128)(2,1)}, u32[]{:S(2)}) copy-start(bf16[64,3584]{1,0:T(8,128)(2,1)} %param.7) | copy-start | bytes 1376260
  26.6 103.8 %all-gather.3.cloned.1.call-start = ((), (), s32[]{:S(2)}) async-start(), calls=%async_computation.5 | async-start | bytes 2293760 | tf_op jit(solution)/shard_map/all_gather | solution.py:41
  109.1 44.4 %all-gather.5.cloned.1.call-start = ((), (), s32[]{:S(2)}) async-start(), calls=%async_computation.6 | async-start | bytes 2293760 | tf_op jit(solution)/shard_map/all_gather | solution.py:47
  109.7 123.6 %reduce-scatter.8.cloned.1.call-start = ((), (), s32[]{:S(2)}) async-start(), calls=%async_computation.7 | async-start | bytes 2359296 | tf_op jit(solution)/shard_map/reduce_scatter | solution.py:53
  153.5 11.7 %copy-start.2 = (bf16[256,3584]{1,0:T(8,128)(2,1)S(1)}, bf16[256,3584]{1,0:T(8,128)(2,1)}, u32[]{:S(2)}) copy-start(bf16[256,3584]{1,0:T(8,128)(2,1)} %all-gather.5.cloned.1.call-done) | copy-start | bytes 5505028
  172.9 18.9 %copy-start.1 = (bf16[256,3584]{1,0:T(8,128)(2,1)S(1)}, bf16[256,3584]{1,0:T(8,128)(2,1)}, u32[]{:S(2)}) copy-start(bf16[256,3584]{1,0:T(8,128)(2,1)} %all-gather.3.cloned.1.call-done) | copy-start | bytes 5505028
Sparse Core Ops, SparseCore 0:
  17.6 43.9 reduce-scatter.3
  64.9 41.2 reduce-scatter.5
  109.2 21.1 all-gather.2
  132.4 21.1 all-gather.4
  165.4 67.8 reduce-scatter.7
where the time goes:
time: 243 us; the launch traced here: 241 us
  waiting for transfers between devices  128 us (53%)
  matrix products  55.9 us (23%)
  local copies, waits for them, and re-layouts  38.7 us (16%)
  between operations  13.8 us (6%)
  other arithmetic  4.57 us (2%)
    reduce_scatter x1, waiting for transfers between devices, local(): lax.psum_scatter(jnp.dot(token_rows, up_weight, preferred_element_type=jn...  44.5 us
    unnamed x10, local copies, waits for them, and re-layouts  38.7 us
    reduce_scatter x1, waiting for transfers between devices, local(): lax.psum_scatter(jnp.dot(token_rows, gate_weight, preferred_element_type=...  34.9 us
    dot_general x2, matrix products, input_term(): lax.dot_general(grad_piece, weight_block, (((1,), (1,)), ((), ())), prefe...  22.7 us
    all_gather x1, waiting for transfers between devices, local(): grad_piece = lax.all_gather(gate_grad, 'row', axis=0, tiled=True)  20.5 us
    reduce_scatter x1, waiting for transfers between devices, local(): lax.psum_scatter(input_total, 'col', scatter_dimension=0, tiled=True)  15.5 us
    dot_general x2, matrix products, weight_term(): lax.dot_general(token_rows, grad_piece, (((0,), (0,)), ((), ())), preferr...  15 us
    all_gather x1, waiting for transfers between devices, local(): grad_piece = lax.all_gather(up_grad, 'row', axis=0, tiled=True)  12.1 us
  transfers between devices with their start and end apart: 5, of which 5 were waited for; matrix products, arithmetic and copies ran while one was open for 30% of the time, Pallas kernels for 0%

commit v1 on v0

v1 whole, which is shorter than its diff:
```python
import functools

import jax
import jax.numpy as jnp
from jax import lax
from jax.experimental import pallas as pl
from jax.experimental.pallas import tpu as pltpu
from jax.sharding import PartitionSpec as P

BF16 = jnp.bfloat16
F32 = jnp.float32
VMEM_BYTES = 40 * 1024 * 1024
SHARES = (2, 4, 4, 4)


def chunk_list(width):
    block = 256 if width % 256 == 0 else 128
    units = width // block
    total = sum(SHARES)
    edges = [0]
    run = 0
    for share in SHARES:
        run += share
        edges.append(max(min(units, round(units * run / total)), edges[-1]))
    return block, [(a, b - a) for a, b in zip(edges, edges[1:]) if b > a]


def forward_kernel(quarters, rows, x_ref, gate_ref, up_ref, keep_ref, send_ref, total):
    me = lax.axis_index("row")
    x = x_ref[...]
    for k, w_ref in enumerate((gate_ref, up_ref)):
        total[k] = jnp.dot(x, w_ref[...], preferred_element_type=F32)
    outer, core = me // 2, me % 2
    for step in range(quarters // 2):
        there = (outer + step) % (quarters // 2) * 2
        mine = pl.multiple_of((there + core) * rows, rows)
        other = pl.multiple_of((there + 1 - core) * rows, rows)
        for k in range(2):
            keep_ref[k, step] = total[k, pl.ds(mine, rows), :]
            send_ref[k, step] = total[k, pl.ds(other, rows), :].astype(BF16)


def forward_part(quarters, block, start, count, x, gate_weight, up_weight):
    tokens, depth = x.shape
    rows = tokens // quarters
    outer = quarters // 2
    weight = pl.BlockSpec((depth, block), lambda j: (0, start + j))
    out = pl.BlockSpec((2, outer, rows, block), lambda j: (0, 0, 0, j))
    shape = (2, outer, rows, count * block)
    return pl.pallas_call(
        functools.partial(forward_kernel, quarters, rows),
        grid=(count,),
        in_specs=[pl.BlockSpec((tokens, depth), lambda j: (0, 0)), weight, weight],
        out_specs=[out, out],
        out_shape=[jax.ShapeDtypeStruct(shape, F32), jax.ShapeDtypeStruct(shape, BF16)],
        scratch_shapes=[pltpu.VMEM((2, tokens, block), F32)],
        compiler_params=pltpu.CompilerParams(vmem_limit_bytes=VMEM_BYTES),
        cost_estimate=pl.CostEstimate(
            flops=4 * tokens * depth * count * block,
            bytes_accessed=4 * depth * count * block,
            transcendentals=0,
        ),
        name="forward_part",
    )(x, gate_weight, up_weight)


def backward_kernel(quarters, rows, first, *refs):
    xt_ref, gate_ref, up_ref = refs[:3]
    pieces = refs[3 : 3 + quarters]
    rest = refs[3 + quarters :]
    acc_in = None
    if not first:
        acc_in, rest = rest[0], rest[3:]
    gate_out, up_out, acc_ref, grads = rest
    me = lax.axis_index("row")
    outer, core = me // 2, me % 2
    for j, piece in enumerate(pieces):
        step, swap = j // 2, j % 2
        there = (outer + quarters // 2 - step) % (quarters // 2) * 2
        at = pl.multiple_of((there + (core + swap) % 2) * rows, rows)
        for k in range(2):
            grads[k, pl.ds(at, rows), :] = piece[k]
    xt = xt_ref[...]
    gate_out[...] = jnp.dot(xt, grads[0], preferred_element_type=F32).astype(BF16)
    up_out[...] = jnp.dot(xt, grads[1], preferred_element_type=F32).astype(BF16)
    dims = (((1,), (1,)), ((), ()))
    term = lax.dot_general(grads[0], gate_ref[...], dims, preferred_element_type=F32)
    term += lax.dot_general(grads[1], up_ref[...], dims, preferred_element_type=F32)

    @pl.when(pl.program_id(0) == 0)
    def _():
        acc_ref[...] = term if first else acc_in[...] + term

    @pl.when(pl.program_id(0) > 0)
    def _():
        acc_ref[...] += term


def backward_part(quarters, block, start, count, xt, gate_weight, up_weight, pieces, state):
    depth, tokens = xt.shape
    width = gate_weight.shape[1]
    rows = tokens // quarters
    weight = pl.BlockSpec((depth, block), lambda j: (0, start + j))
    acc = pl.BlockSpec((tokens, depth), lambda j: (0, 0))
    piece = pl.BlockSpec((2, rows, block), lambda j: (0, 0, j))
    in_specs = [pl.BlockSpec((depth, tokens), lambda j: (0, 0)), weight, weight]
    in_specs += [piece] * quarters
    first = state is None
    args = [xt, gate_weight, up_weight, *pieces]
    aliases = {}
    if not first:
        aliases = {len(args): 2, len(args) + 1: 0, len(args) + 2: 1}
        args += [state[2], state[0], state[1]]
        in_specs += [acc, pl.BlockSpec(memory_space=pl.ANY), pl.BlockSpec(memory_space=pl.ANY)]
    grad = jax.ShapeDtypeStruct((depth, width), BF16)
    return pl.pallas_call(
        functools.partial(backward_kernel, quarters, rows, first),
        grid=(count,),
        in_specs=in_specs,
        out_specs=[weight, weight, acc],
        out_shape=[grad, grad, jax.ShapeDtypeStruct((tokens, depth), F32)],
        scratch_shapes=[pltpu.VMEM((2, tokens, block), BF16)],
        input_output_aliases=aliases,
        compiler_params=pltpu.CompilerParams(vmem_limit_bytes=VMEM_BYTES),
        cost_estimate=pl.CostEstimate(
            flops=8 * tokens * depth * count * block,
            bytes_accessed=8 * depth * count * block,
            transcendentals=0,
        ),
        name="backward_part",
    )(*args)


def local(quarters, columns, inputs, gate_weight, up_weight, hidden_grad):
    outer = quarters // 2
    block, chunks = chunk_list(gate_weight.shape[1])
    swap = [(r, r ^ 1) for r in range(quarters)]

    def sibling(value):
        return lax.ppermute(value, "row", swap)

    def across(value, step):
        moves = [(r, (r // 2 + step) % outer * 2 + r % 2) for r in range(quarters)]
        return lax.ppermute(value, "row", moves)

    parts = [
        forward_part(quarters, block, start, count, inputs, gate_weight, up_weight)
        for start, count in chunks
    ]
    xt = inputs.T
    hidden_parts = []
    grad_parts = []
    for (start, count), (keep, send) in zip(chunks, parts):
        both = keep + sibling(send).astype(F32)
        pre = both[:, 0]
        for step in range(1, outer):
            pre = pre + across(both[:, step].astype(BF16), step).astype(F32)
        gate_pre, up_pre = pre[0], pre[1]
        sigma_gate = jax.nn.sigmoid(gate_pre)
        hidden_parts.append((gate_pre * sigma_gate * up_pre).astype(BF16))
        upstream = hidden_grad[:, start * block : (start + count) * block].astype(F32)
        gate_grad = upstream * up_pre * sigma_gate * (1.0 + gate_pre * (1.0 - sigma_gate))
        up_grad = upstream * gate_pre * sigma_gate
        mine = jnp.stack([gate_grad.astype(BF16), up_grad.astype(BF16)])
        pieces = [mine, sibling(mine)]
        for step in range(1, outer):
            far = across(mine, step)
            pieces += [far, sibling(far)]
        grad_parts.append(pieces)

    state = None
    for (start, count), pieces in zip(chunks, grad_parts):
        state = backward_part(
            quarters, block, start, count, xt, gate_weight, up_weight, pieces, state
        )
    gate_total, up_total, total = state

    rows = total.shape[0] // columns
    total = total.reshape(columns, rows, total.shape[1])
    position = lax.axis_index("col")
    bit = 1
    while bit < columns:
        mine = (position // bit) % 2
        pairs = total.reshape(total.shape[0] // 2, 2, rows, total.shape[2])
        keep = lax.dynamic_index_in_dim(pairs, mine, 1, keepdims=False)
        send = lax.dynamic_index_in_dim(pairs, 1 - mine, 1, keepdims=False)
        moves = [(c, c ^ bit) for c in range(columns)]
        total = keep + lax.ppermute(send.astype(BF16), "col", moves).astype(F32)
        bit *= 2
    input_grad = total[0].astype(BF16)
    return jnp.concatenate(hidden_parts, axis=1), input_grad, gate_total, up_total


def solution(mesh):
    return jax.shard_map(
        functools.partial(local, mesh.shape["row"], mesh.shape["col"]),
        mesh=mesh,
        in_specs=(P(None, "row"), P("row", "col"), P("row", "col"), P("row", "col")),
        out_specs=(P("row", "col"), P("col", "row"), P("row", "col"), P("row", "col")),
        check_vma=False,
    )
```

time: 243 us -> 130 us (0.53)
  waiting for transfers between devices: 128 us -> 40.4 us
  Pallas kernels: 0 us -> 56 us
  matrix products: 55.9 us -> 0 us
  local copies, waits for them, and re-layouts: 38.7 us -> 6.13 us
  starting transfers between devices: 0.38 us -> 17.6 us
  between operations: 13.8 us -> 0.98 us
  other arithmetic: 4.57 us -> 8.24 us
    reduce_scatter x3 -> x0, waiting for transfers between devices: 94.9 us -> none  [the longest x1 44.5 us: local(): lax.psum_scatter(jnp.dot(token_rows, up_weight, preferred_element_type=jn...]
    pallas_call x0 -> x8, Pallas kernels: none -> 56 us  [the longest x4 36 us: backward_part(): pl.pallas_call(functools.partial(backward_kernel, quarters, rows, first),...]
    dot_general x6 -> x0, matrix products: 55.9 us -> none  [the longest x2 22.7 us: input_term(): lax.dot_general(grad_piece, weight_block, (((1,), (1,)), ((), ())), prefe...]
    ppermute x0 -> x23, waiting for transfers between devices: none -> 40.4 us  [the longest x3 22.8 us: local(): total = keep + lax.ppermute(send.astype(BF16), 'col', moves).astype(F32)]
    unnamed x10 -> x25, local copies, waits for them, and re-layouts: 38.7 us -> 5.77 us
    all_gather x2 -> x0, waiting for transfers between devices: 32.6 us -> none  [the longest x1 20.5 us: local(): grad_piece = lax.all_gather(gate_grad, 'row', axis=0, tiled=True)]
    ppermute x0 -> x23, starting transfers between devices: none -> 17.6 us  [the longest x8 9.17 us: across(): return lax.ppermute(value, 'row', moves)]
    another operation x0 -> x7, other arithmetic: none -> 4.03 us  [local(): mine = jnp.stack([gate_grad.astype(BF16), up_grad.astype(BF16)])]
  transfers between devices with their start and end apart: 5 -> 23, of which waited for: 5 -> 8; matrix products, arithmetic and copies ran while one was open for 30% -> 5% of each run, Pallas kernels for 0% -> 33%
where the time goes in v1:
time: 130 us; the launch traced here: 129 us
  Pallas kernels  56 us (43%)
  waiting for transfers between devices  40.4 us (31%)
  starting transfers between devices  17.6 us (14%)
  other arithmetic  8.24 us (6%)
  local copies, waits for them, and re-layouts  6.13 us (5%)
    pallas_call x4, Pallas kernels, backward_part(): pl.pallas_call(functools.partial(backward_kernel, quarters, rows, first),...  36 us
    ppermute x3, waiting for transfers between devices, local(): total = keep + lax.ppermute(send.astype(BF16), 'col', moves).astype(F32)  22.8 us
    pallas_call x4, Pallas kernels, forward_part(): pl.pallas_call(functools.partial(forward_kernel, quarters, rows), grid=(c...  20 us
    ppermute x8, waiting for transfers between devices, across(): return lax.ppermute(value, 'row', moves)  17.6 us
    ppermute x8, starting transfers between devices, across(): return lax.ppermute(value, 'row', moves)  9.17 us
    ppermute x3, starting transfers between devices, local(): total = keep + lax.ppermute(send.astype(BF16), 'col', moves).astype(F32)  5.89 us
    unnamed x25, local copies, waits for them, and re-layouts  5.77 us
    another operation x7, other arithmetic, local(): mine = jnp.stack([gate_grad.astype(BF16), up_grad.astype(BF16)])  4.03 us
  transfers between devices with their start and end apart: 23, of which 8 were waited for; matrix products, arithmetic and copies ran while one was open for 5% of the time, Pallas kernels for 33%

profile of v1, /device:TPU:0, one launch (start us, length us, event | category | flops | bytes accessed | tf_op | source)
XLA Modules:
  0.0 129.3 jit_solution(8662704085523771763)
XLA Ops:
  0.6 1.2 copy-done
  1.9 3.1 %forward_part.4 = (f32[2,2,64,512]{3,2,1,0:T(8,128)S(1)}, bf16[2,2,64,512]{3,2,1,0:T(8,128)(2,1)S(1)}) custom-call(bf16[256,2048]{1,0:T(8,128)(2,1)S(1)} %copy-done, bf16[2048,3584]{1,0:T(8,128)(2,1)} %refs_1_.7, bf16[2048,3584]{1,0:T(8,128)(2,1)} %refs_2_.7), custom_call_target="tpu_custom_call" | custom-call | flops 1073741824 | bytes 4194304 | tf_op jit(solution)/shard_map/forward_part/pallas_call | solution.py:50
  5.5 5.6 %forward_part.6 = (f32[2,2,64,1024]{3,2,1,0:T(8,128)S(1)}, bf16[2,2,64,1024]{3,2,1,0:T(8,128)(2,1)S(1)}) custom-call(bf16[256,2048]{1,0:T(8,128)(2,1)S(1)} %copy-done, bf16[2048,3584]{1,0:T(8,128)(2,1)} %refs_1_.7, bf16[2048,3584]{1,0:T(8,128)(2,1)} %refs_2_.7), custom_call_target="tpu_custom_call" | custom-call | flops 2147483648 | bytes 8388608 | tf_op jit(solution)/shard_map/forward_part/pallas_call | solution.py:50
  11.3 5.6 %forward_part.5 = (f32[2,2,64,1024]{3,2,1,0:T(8,128)S(1)}, bf16[2,2,64,1024]{3,2,1,0:T(8,128)(2,1)S(1)}) custom-call(bf16[256,2048]{1,0:T(8,128)(2,1)S(1)} %copy-done, bf16[2048,3584]{1,0:T(8,128)(2,1)} %refs_1_.7, bf16[2048,3584]{1,0:T(8,128)(2,1)} %refs_2_.7), custom_call_target="tpu_custom_call" | custom-call | flops 2147483648 | bytes 8388608 | tf_op jit(solution)/shard_map/forward_part/pallas_call | solution.py:50
  17.7 2.6 %collective-permute-start.1 = (bf16[2,64,512]{2,1,0:T(8,128)(2,1)S(1)}, bf16[2,64,512]{2,1,0:T(8,128)(2,1)S(1)}, u32[]{:S(2)}, u32[]{:S(2)}) collective-permute-start(bf16[2,64,512]{2,1,0:T(8,128)(2,1)S(1)} %fusion.30), channel_id=1, source_target_pairs={{0,16},{8,24},{16,0},{24,8},{1,17},{9,25},{17,1},{25,9},{2,18},{10... | collective-permute-start | bytes 393224 | tf_op jit(solution)/shard_map/ppermute | solution.py:144
  20.2 5.6 %forward_part.7 = (f32[2,2,64,1024]{3,2,1,0:T(8,128)S(1)}, bf16[2,2,64,1024]{3,2,1,0:T(8,128)(2,1)S(1)}) custom-call(bf16[256,2048]{1,0:T(8,128)(2,1)S(1)} %copy-done, bf16[2048,3584]{1,0:T(8,128)(2,1)} %refs_1_.7, bf16[2048,3584]{1,0:T(8,128)(2,1)} %refs_2_.7), custom_call_target="tpu_custom_call" | custom-call | flops 2147483648 | bytes 8388608 | tf_op jit(solution)/shard_map/forward_part/pallas_call | solution.py:50
  27.6 1.7 %collective-permute-start.5 = (bf16[2,64,1024]{2,1,0:T(8,128)(2,1)S(1)}, bf16[2,64,1024]{2,1,0:T(8,128)(2,1)S(1)}, u32[]{:S(2)}, u32[]{:S(2)}) collective-permute-start(bf16[2,64,1024]{2,1,0:T(8,128)(2,1)S(1)} %fusion.21), channel_id=1, source_target_pairs={{0,16},{8,24},{16,0},{24,8},{1,17},{9,25},{17,1},{25,9},{2,18},{10... | collective-permute-start | bytes 786440 | tf_op jit(solution)/shard_map/ppermute | solution.py:144
  30.2 1.7 %collective-permute-start.7 = (bf16[2,64,1024]{2,1,0:T(8,128)(2,1)S(1)}, bf16[2,64,1024]{2,1,0:T(8,128)(2,1)S(1)}, u32[]{:S(2)}, u32[]{:S(2)}) collective-permute-start(bf16[2,64,1024]{2,1,0:T(8,128)(2,1)S(1)} %fusion.22), channel_id=1, source_target_pairs={{0,16},{8,24},{16,0},{24,8},{1,17},{9,25},{17,1},{25,9},{2,18},{10... | collective-permute-start | bytes 786440 | tf_op jit(solution)/shard_map/ppermute | solution.py:144
  31.9 1.5 %collective-permute-done.18.refs_5_ = bf16[2,64,512]{2,1,0:T(8,128)(2,1)S(1)} collective-permute-done((bf16[2,64,512]{2,1,0:T(8,128)(2,1)S(1)}, bf16[2,64,512]{2,1,0:T(8,128)(2,1)S(1)}, u32[]{:S(2)}, u32[]{:S(2)}) %collective-permute-start.18) | collective-permute-done | bytes 131104 | tf_op jit(solution)/shard_map/ppermute | solution.py:144
  33.4 5.6 %collective-permute-done.5 = bf16[2,64,1024]{2,1,0:T(8,128)(2,1)S(1)} collective-permute-done((bf16[2,64,1024]{2,1,0:T(8,128)(2,1)S(1)}, bf16[2,64,1024]{2,1,0:T(8,128)(2,1)S(1)}, u32[]{:S(2)}, u32[]{:S(2)}) %collective-permute-start.5) | collective-permute-done | bytes 262176 | tf_op jit(solution)/shard_map/ppermute | solution.py:144
  39.0 5.6 %collective-permute-done.3 = bf16[2,64,1024]{2,1,0:T(8,128)(2,1)S(1)} collective-permute-done((bf16[2,64,1024]{2,1,0:T(8,128)(2,1)S(1)}, bf16[2,64,1024]{2,1,0:T(8,128)(2,1)S(1)}, u32[]{:S(2)}, u32[]{:S(2)}) %collective-permute-start.3) | collective-permute-done | bytes 262176 | tf_op jit(solution)/shard_map/ppermute | solution.py:144
  44.6 1.0 fusion.34
  45.7 0.7 pad_maximum_fusion.3.refs_3_
  46.7 3.5 %collective-permute-done.7 = bf16[2,64,1024]{2,1,0:T(8,128)(2,1)S(1)} collective-permute-done((bf16[2,64,1024]{2,1,0:T(8,128)(2,1)S(1)}, bf16[2,64,1024]{2,1,0:T(8,128)(2,1)S(1)}, u32[]{:S(2)}, u32[]{:S(2)}) %collective-permute-start.7) | collective-permute-done | bytes 262176 | tf_op jit(solution)/shard_map/ppermute | solution.py:144
  50.5 0.8 fusion.36
  52.7 1.8 %collective-permute-start.9 = (bf16[2,64,1024]{2,1,0:T(8,128)(2,1)}, bf16[2,64,1024]{2,1,0:T(8,128)(2,1)}, u32[]{:S(2)}, u32[]{:S(2)}) collective-permute-start(bf16[2,64,1024]{2,1,0:T(8,128)(2,1)} %pad_maximum_fusion.1.refs_3_), channel_id=1, source_target_pairs={{0,16},{8,24},{16,0},{24,8},{1,17},{9,25},{17,1},{25,9},{2,18},{10... | collective-permute-start | bytes 786440 | tf_op jit(solution)/shard_map/ppermute | solution.py:144
  54.5 1.4 %collective-permute-done.15.refs_5_ = bf16[2,64,1024]{2,1,0:T(8,128)(2,1)} collective-permute-done((bf16[2,64,1024]{2,1,0:T(8,128)(2,1)}, bf16[2,64,1024]{2,1,0:T(8,128)(2,1)}, u32[]{:S(2)}, u32[]{:S(2)}) %collective-permute-start.15) | collective-permute-done | bytes 262176 | tf_op jit(solution)/shard_map/ppermute | solution.py:144
  57.1 0.9 copy-done.3
  58.0 0.9 copy-done.5
  58.9 0.9 copy-done.7
  59.8 5.8 %backward_part.4 = (bf16[2048,3584]{1,0:T(8,128)(2,1)}, bf16[2048,3584]{1,0:T(8,128)(2,1)}, f32[256,2048]{1,0:T(8,128)S(1)}) custom-call(bf16[2048,256]{1,0:T(8,128)(2,1)S(1)} %bitcast.139, bf16[2048,3584]{1,0:T(8,128)(2,1)} %refs_1_.7, bf16[2048,3584]{1,0:T(8,128)(2,1)} %refs_2_.7, bf16[2,64,512]{2,1,0:T(8,128)(2,1)S(1)} %pad_maximum_fusion.4.refs_3_, ...), custom_call_target="tpu_custom_call" | custom-call | flops 2147483648 | bytes 8388608 | tf_op jit(solution)/shard_map/backward_part/pallas_call | solution.py:116
  66.7 10.0 %backward_part.5 = (bf16[2048,3584]{1,0:T(8,128)(2,1)}, bf16[2048,3584]{1,0:T(8,128)(2,1)}, f32[256,2048]{1,0:T(8,128)S(1)}) custom-call(bf16[2048,256]{1,0:T(8,128)(2,1)S(1)} %bitcast.140, bf16[2048,3584]{1,0:T(8,128)(2,1)} %refs_1_.7, bf16[2048,3584]{1,0:T(8,128)(2,1)} %refs_2_.7, ...), custom_call_target="tpu_custom_call", output_to_operand_aliasing={{2}: (7, {}), {0}: (8, {}), {1}: (9, {})} | custom-call | flops 4294967296 | bytes 16777216 | tf_op jit(solution)/shard_map/backward_part/pallas_call | solution.py:116
  76.8 10.0 %backward_part.6 = (bf16[2048,3584]{1,0:T(8,128)(2,1)}, bf16[2048,3584]{1,0:T(8,128)(2,1)}, f32[256,2048]{1,0:T(8,128)S(1)}) custom-call(bf16[2048,256]{1,0:T(8,128)(2,1)S(1)} %bitcast.141, bf16[2048,3584]{1,0:T(8,128)(2,1)} %refs_1_.7, bf16[2048,3584]{1,0:T(8,128)(2,1)} %refs_2_.7, ...), custom_call_target="tpu_custom_call", output_to_operand_aliasing={{2}: (7, {}), {0}: (8, {}), {1}: (9, {})} | custom-call | flops 4294967296 | bytes 16777216 | tf_op jit(solution)/shard_map/backward_part/pallas_call | solution.py:116
  86.8 10.2 %backward_part.7 = (bf16[2048,3584]{1,0:T(8,128)(2,1)}, bf16[2048,3584]{1,0:T(8,128)(2,1)}, f32[256,2048]{1,0:T(8,128)S(1)}) custom-call(bf16[2048,256]{1,0:T(8,128)(2,1)S(1)} %bitcast.142, bf16[2048,3584]{1,0:T(8,128)(2,1)} %refs_1_.7, bf16[2048,3584]{1,0:T(8,128)(2,1)} %refs_2_.7, ...), custom_call_target="tpu_custom_call", output_to_operand_aliasing={{2}: (7, {}), {0}: (8, {}), {1}: (9, {})} | custom-call | flops 4294967296 | bytes 16777216 | tf_op jit(solution)/shard_map/backward_part/pallas_call | solution.py:116
  97.1 1.6 %collective-permute-start.20 = (bf16[4,32,2048]{2,1,0:T(8,128)(2,1)S(1)}, bf16[4,32,2048]{2,1,0:T(8,128)(2,1)}, u32[]{:S(2)}, u32[]{:S(2)}) collective-permute-start(bf16[4,32,2048]{2,1,0:T(8,128)(2,1)S(1)} %fusion), channel_id=1, source_target_pairs={{0,1},{1,0},{2,3},{3,2},{4,5},{5,4},{6,7},{7,6},{8,9},{9,8},{10,11... | collective-permute-start | bytes 1572872 | tf_op jit(solution)/shard_map/ppermute | solution.py:188
  98.7 12.8 %collective-permute-done.20 = bf16[4,32,2048]{2,1,0:T(8,128)(2,1)} collective-permute-done((bf16[4,32,2048]{2,1,0:T(8,128)(2,1)S(1)}, bf16[4,32,2048]{2,1,0:T(8,128)(2,1)}, u32[]{:S(2)}, u32[]{:S(2)}) %collective-permute-start.20) | collective-permute-done | bytes 524320 | tf_op jit(solution)/shard_map/ppermute | solution.py:188
  111.5 1.1 bitcast_add_fusion
  112.7 1.6 %collective-permute-start.21 = (bf16[2,32,2048]{2,1,0:T(8,128)(2,1)S(1)}, bf16[2,32,2048]{2,1,0:T(8,128)(2,1)S(1)}, u32[]{:S(2)}, u32[]{:S(2)}) collective-permute-start(bf16[2,32,2048]{2,1,0:T(8,128)(2,1)S(1)} %fusion.19), channel_id=1, source_target_pairs={{0,2},{1,3},{2,0},{3,1},{4,6},{5,7},{6,4},{7,5},{8,10},{9,11},{10,... | collective-permute-start | bytes 786440 | tf_op jit(solution)/shard_map/ppermute | solution.py:188
  114.4 6.3 %collective-permute-done.21 = bf16[2,32,2048]{2,1,0:T(8,128)(2,1)S(1)} collective-permute-done((bf16[2,32,2048]{2,1,0:T(8,128)(2,1)S(1)}, bf16[2,32,2048]{2,1,0:T(8,128)(2,1)S(1)}, u32[]{:S(2)}, u32[]{:S(2)}) %collective-permute-start.21) | collective-permute-done | bytes 262176 | tf_op jit(solution)/shard_map/ppermute | solution.py:188
  120.7 2.7 %collective-permute-start.22 = (bf16[1,32,2048]{2,1,0:T(8,128)(2,1)S(1)}, bf16[1,32,2048]{2,1,0:T(8,128)(2,1)S(1)}, u32[]{:S(2)}, u32[]{:S(2)}) collective-permute-start(bf16[1,32,2048]{2,1,0:T(8,128)(2,1)S(1)} %dynamic-slice_convert_fusion.1), channel_id=1, source_target_pairs={{0,4},{1,5},{2,6},{3,7},{4,0},{5,1},{6,2},{7,3},{8,12},{9,13},{10,... | collective-permute-start | bytes 393224 | tf_op jit(solution)/shard_map/ppermute | solution.py:188
  123.4 1.6 %pad_maximum_fusion = bf16[64,3584]{1,0:T(8,128)(2,1)} fusion(bf16[64,1024]{1,0:T(8,128)(2,1)S(1)} %copy-done.10, bf16[64,1024]{1,0:T(8,128)(2,1)S(1)} %copy-done.9, bf16[64,1024]{1,0:T(8,128)(2,1)S(1)} %copy-done.8, bf16[64,512]{1,0:T(8,128)(2,1)} %get-tuple-element.58), kind=kLoop, calls=%fused_computation.18 | loop fusion | flops 1835008 | bytes 917504 | tf_op jit(solution)/shard_map/concatenate | solution.py:191
  125.0 3.6 %collective-permute-done.22 = bf16[1,32,2048]{2,1,0:T(8,128)(2,1)S(1)} collective-permute-done((bf16[1,32,2048]{2,1,0:T(8,128)(2,1)S(1)}, bf16[1,32,2048]{2,1,0:T(8,128)(2,1)S(1)}, u32[]{:S(2)}, u32[]{:S(2)}) %collective-permute-start.22) | collective-permute-done | bytes 131104 | tf_op jit(solution)/shard_map/ppermute | solution.py:188
  (77 shorter events, 9.0 us)
Async XLA Ops:
  0.6 1.2 copy-start
  5.0 12.5 %collective-permute-start = (bf16[2,2,64,512]{3,2,0,1:T(8,128)(2,1)S(1)}, bf16[2,2,64,512]{3,2,0,1:T(8,128)(2,1)S(1)}, u32[]{:S(2)}, u32[]{:S(2)}) collective-permute-start(bf16[2,2,64,512]{3,2,0,1:T(8,128)(2,1)S(1)} %copy.26), channel_id=1, source_target_pairs={{0,8},{8,0},{16,24},{24,16},{1,9},{9,1},{17,25},{25,17},{2,10},{10... | collective-permute-start | bytes 786440 | tf_op jit(solution)/shard_map/ppermute | solution.py:140
  11.2 16.2 %collective-permute-start.4 = (bf16[2,2,64,1024]{3,2,0,1:T(8,128)(2,1)S(1)}, bf16[2,2,64,1024]{3,2,0,1:T(8,128)(2,1)S(1)}, u32[]{:S(2)}, u32[]{:S(2)}) collective-permute-start(bf16[2,2,64,1024]{3,2,0,1:T(8,128)(2,1)S(1)} %copy.30), channel_id=1, source_target_pairs={{0,8},{8,0},{16,24},{24,16},{1,9},{9,1},{17,25},{25,17},{2,10},{10... | collective-permute-start | bytes 1572872 | tf_op jit(solution)/shard_map/ppermute | solution.py:140
  17.0 12.3 %collective-permute-start.2 = (bf16[2,2,64,1024]{3,2,0,1:T(8,128)(2,1)S(1)}, bf16[2,2,64,1024]{3,2,0,1:T(8,128)(2,1)S(1)}, u32[]{:S(2)}, u32[]{:S(2)}) collective-permute-start(bf16[2,2,64,1024]{3,2,0,1:T(8,128)(2,1)S(1)} %copy.28), channel_id=1, source_target_pairs={{0,8},{8,0},{16,24},{24,16},{1,9},{9,1},{17,25},{25,17},{2,10},{10... | collective-permute-start | bytes 1572872 | tf_op jit(solution)/shard_map/ppermute | solution.py:140
  17.6 8.6 %copy-start.11 = (bf16[64,3584]{1,0:T(8,128)(2,1)S(1)}, bf16[64,3584]{1,0:T(8,128)(2,1)}, u32[]{:S(2)}) copy-start(bf16[64,3584]{1,0:T(8,128)(2,1)} %param.7) | copy-start | bytes 1376260
  17.7 8.5 %collective-permute-start.1 = (bf16[2,64,512]{2,1,0:T(8,128)(2,1)S(1)}, bf16[2,64,512]{2,1,0:T(8,128)(2,1)S(1)}, u32[]{:S(2)}, u32[]{:S(2)}) collective-permute-start(bf16[2,64,512]{2,1,0:T(8,128)(2,1)S(1)} %fusion.30), channel_id=1, source_target_pairs={{0,16},{8,24},{16,0},{24,8},{1,17},{9,25},{17,1},{25,9},{2,18},{10... | collective-permute-start | bytes 393224 | tf_op jit(solution)/shard_map/ppermute | solution.py:144
  25.9 30.0 %copy-start.1 = (bf16[256,2048]{1,0:T(8,128)(2,1)S(1)}, bf16[256,2048]{1,0:T(8,128)(2,1)}, u32[]{:S(2)}) copy-start(bf16[256,2048]{1,0:T(8,128)(2,1)} %x_ref.7) | copy-start | bytes 3145732
  25.9 4.0 %collective-permute-start.6 = (bf16[2,2,64,1024]{3,2,0,1:T(8,128)(2,1)S(1)}, bf16[2,2,64,1024]{3,2,0,1:T(8,128)(2,1)S(1)}, u32[]{:S(2)}, u32[]{:S(2)}) collective-permute-start(bf16[2,2,64,1024]{3,2,0,1:T(8,128)(2,1)S(1)} %copy.32), channel_id=1, source_target_pairs={{0,8},{8,0},{16,24},{24,16},{1,9},{9,1},{17,25},{25,17},{2,10},{10... | collective-permute-start | bytes 1572872 | tf_op jit(solution)/shard_map/ppermute | solution.py:140
  27.0 6.4 %collective-permute-start.18 = (bf16[2,64,512]{2,1,0:T(8,128)(2,1)S(1)}, bf16[2,64,512]{2,1,0:T(8,128)(2,1)S(1)}, u32[]{:S(2)}, u32[]{:S(2)}) collective-permute-start(bf16[2,64,512]{2,1,0:T(8,128)(2,1)S(1)} %pad_maximum_fusion.4.refs_3_), channel_id=1, source_target_pairs={{0,16},{8,24},{16,0},{24,8},{1,17},{9,25},{17,1},{25,9},{2,18},{10... | collective-permute-start | bytes 393224 | tf_op jit(solution)/shard_map/ppermute | solution.py:144
  27.4 24.7 %collective-permute-start.17 = (bf16[2,64,512]{2,1,0:T(8,128)(2,1)S(1)}, bf16[2,64,512]{2,1,0:T(8,128)(2,1)S(1)}, u32[]{:S(2)}, u32[]{:S(2)}) collective-permute-start(bf16[2,64,512]{2,1,0:T(8,128)(2,1)S(1)} %pad_maximum_fusion.4.refs_3_), channel_id=1, source_target_pairs={{0,8},{8,0},{16,24},{24,16},{1,9},{9,1},{17,25},{25,17},{2,10},{10... | collective-permute-start | bytes 393224 | tf_op jit(solution)/shard_map/ppermute | solution.py:140
  27.6 11.4 %collective-permute-start.5 = (bf16[2,64,1024]{2,1,0:T(8,128)(2,1)S(1)}, bf16[2,64,1024]{2,1,0:T(8,128)(2,1)S(1)}, u32[]{:S(2)}, u32[]{:S(2)}) collective-permute-start(bf16[2,64,1024]{2,1,0:T(8,128)(2,1)S(1)} %fusion.21), channel_id=1, source_target_pairs={{0,16},{8,24},{16,0},{24,8},{1,17},{9,25},{17,1},{25,9},{2,18},{10... | collective-permute-start | bytes 786440 | tf_op jit(solution)/shard_map/ppermute | solution.py:144
  29.6 15.0 %collective-permute-start.3 = (bf16[2,64,1024]{2,1,0:T(8,128)(2,1)S(1)}, bf16[2,64,1024]{2,1,0:T(8,128)(2,1)S(1)}, u32[]{:S(2)}, u32[]{:S(2)}) collective-permute-start(bf16[2,64,1024]{2,1,0:T(8,128)(2,1)S(1)} %fusion.20), channel_id=1, source_target_pairs={{0,16},{8,24},{16,0},{24,8},{1,17},{9,25},{17,1},{25,9},{2,18},{10... | collective-permute-start | bytes 786440 | tf_op jit(solution)/shard_map/ppermute | solution.py:144
  30.2 20.0 %collective-permute-start.7 = (bf16[2,64,1024]{2,1,0:T(8,128)(2,1)S(1)}, bf16[2,64,1024]{2,1,0:T(8,128)(2,1)S(1)}, u32[]{:S(2)}, u32[]{:S(2)}) collective-permute-start(bf16[2,64,1024]{2,1,0:T(8,128)(2,1)S(1)} %fusion.22), channel_id=1, source_target_pairs={{0,16},{8,24},{16,0},{24,8},{1,17},{9,25},{17,1},{25,9},{2,18},{10... | collective-permute-start | bytes 786440 | tf_op jit(solution)/shard_map/ppermute | solution.py:144
  33.3 23.1 %copy-start.2 = (bf16[2,64,512]{2,1,0:T(8,128)(2,1)}, bf16[2,64,512]{2,1,0:T(8,128)(2,1)S(1)}, u32[]{:S(2)}) copy-start(bf16[2,64,512]{2,1,0:T(8,128)(2,1)S(1)} %collective-permute-done.18.refs_5_) | copy-start | bytes 393220
  33.3 23.1 %collective-permute-start.19 = (bf16[2,64,512]{2,1,0:T(8,128)(2,1)S(1)}, bf16[2,64,512]{2,1,0:T(8,128)(2,1)S(1)}, u32[]{:S(2)}, u32[]{:S(2)}) collective-permute-start(bf16[2,64,512]{2,1,0:T(8,128)(2,1)S(1)} %collective-permute-done.18.refs_5_), channel_id=1, source_target_pairs={{0,8},{8,0},{16,24},{24,16},{1,9},{9,1},{17,25},{25,17},{2,10},{10... | collective-permute-start | bytes 393224 | tf_op jit(solution)/shard_map/ppermute | solution.py:140
  46.4 9.5 %collective-permute-start.15 = (bf16[2,64,1024]{2,1,0:T(8,128)(2,1)}, bf16[2,64,1024]{2,1,0:T(8,128)(2,1)}, u32[]{:S(2)}, u32[]{:S(2)}) collective-permute-start(bf16[2,64,1024]{2,1,0:T(8,128)(2,1)} %pad_maximum_fusion.3.refs_3_), channel_id=1, source_target_pairs={{0,16},{8,24},{16,0},{24,8},{1,17},{9,25},{17,1},{25,9},{2,18},{10... | collective-permute-start | bytes 786440 | tf_op jit(solution)/shard_map/ppermute | solution.py:144
  46.7 19.5 %collective-permute-start.14 = (bf16[2,64,1024]{2,1,0:T(8,128)(2,1)}, bf16[2,64,1024]{2,1,0:T(8,128)(2,1)}, u32[]{:S(2)}, u32[]{:S(2)}) collective-permute-start(bf16[2,64,1024]{2,1,0:T(8,128)(2,1)} %pad_maximum_fusion.3.refs_3_), channel_id=1, source_target_pairs={{0,8},{8,0},{16,24},{24,16},{1,9},{9,1},{17,25},{25,17},{2,10},{10... | collective-permute-start | bytes 786440 | tf_op jit(solution)/shard_map/ppermute | solution.py:140
  50.2 16.0 %collective-permute-start.12 = (bf16[2,64,1024]{2,1,0:T(8,128)(2,1)S(1)}, bf16[2,64,1024]{2,1,0:T(8,128)(2,1)}, u32[]{:S(2)}, u32[]{:S(2)}) collective-permute-start(bf16[2,64,1024]{2,1,0:T(8,128)(2,1)S(1)} %pad_maximum_fusion.2.refs_3_), channel_id=1, source_target_pairs={{0,16},{8,24},{16,0},{24,8},{1,17},{9,25},{17,1},{25,9},{2,18},{10... | collective-permute-start | bytes 786440 | tf_op jit(solution)/shard_map/ppermute | solution.py:144
  52.7 13.9 %collective-permute-start.9 = (bf16[2,64,1024]{2,1,0:T(8,128)(2,1)}, bf16[2,64,1024]{2,1,0:T(8,128)(2,1)}, u32[]{:S(2)}, u32[]{:S(2)}) collective-permute-start(bf16[2,64,1024]{2,1,0:T(8,128)(2,1)} %pad_maximum_fusion.1.refs_3_), channel_id=1, source_target_pairs={{0,16},{8,24},{16,0},{24,8},{1,17},{9,25},{17,1},{25,9},{2,18},{10... | collective-permute-start | bytes 786440 | tf_op jit(solution)/shard_map/ppermute | solution.py:144
  55.9 10.8 %collective-permute-start.16 = (bf16[2,64,1024]{2,1,0:T(8,128)(2,1)}, bf16[2,64,1024]{2,1,0:T(8,128)(2,1)}, u32[]{:S(2)}, u32[]{:S(2)}) collective-permute-start(bf16[2,64,1024]{2,1,0:T(8,128)(2,1)} %collective-permute-done.15.refs_5_), channel_id=1, source_target_pairs={{0,8},{8,0},{16,24},{24,16},{1,9},{9,1},{17,25},{25,17},{2,10},{10... | collective-permute-start | bytes 786440 | tf_op jit(solution)/shard_map/ppermute | solution.py:140
  57.1 0.9 copy-start.3
  58.0 0.9 copy-start.5
  65.6 11.1 %collective-permute-start.11 = (bf16[2,64,1024]{2,1,0:T(8,128)(2,1)S(1)}, bf16[2,64,1024]{2,1,0:T(8,128)(2,1)S(1)}, u32[]{:S(2)}, u32[]{:S(2)}) collective-permute-start(bf16[2,64,1024]{2,1,0:T(8,128)(2,1)S(1)} %pad_maximum_fusion.2.refs_3_), channel_id=1, source_target_pairs={{0,8},{8,0},{16,24},{24,16},{1,9},{9,1},{17,25},{25,17},{2,10},{10... | collective-permute-start | bytes 786440 | tf_op jit(solution)/shard_map/ppermute | solution.py:140
  66.1 20.7 %collective-permute-start.8 = (bf16[2,64,1024]{2,1,0:T(8,128)(2,1)}, bf16[2,64,1024]{2,1,0:T(8,128)(2,1)S(1)}, u32[]{:S(2)}, u32[]{:S(2)}) collective-permute-start(bf16[2,64,1024]{2,1,0:T(8,128)(2,1)} %pad_maximum_fusion.1.refs_3_), channel_id=1, source_target_pairs={{0,8},{8,0},{16,24},{24,16},{1,9},{9,1},{17,25},{25,17},{2,10},{10... | collective-permute-start | bytes 786440 | tf_op jit(solution)/shard_map/ppermute | solution.py:140
  66.2 10.6 %collective-permute-start.13 = (bf16[2,64,1024]{2,1,0:T(8,128)(2,1)}, bf16[2,64,1024]{2,1,0:T(8,128)(2,1)S(1)}, u32[]{:S(2)}, u32[]{:S(2)}) collective-permute-start(bf16[2,64,1024]{2,1,0:T(8,128)(2,1)} %collective-permute-done.12.refs_5_), channel_id=1, source_target_pairs={{0,8},{8,0},{16,24},{24,16},{1,9},{9,1},{17,25},{25,17},{2,10},{10... | collective-permute-start | bytes 786440 | tf_op jit(solution)/shard_map/ppermute | solution.py:140
  66.7 20.2 %collective-permute-start.10 = (bf16[2,64,1024]{2,1,0:T(8,128)(2,1)}, bf16[2,64,1024]{2,1,0:T(8,128)(2,1)S(1)}, u32[]{:S(2)}, u32[]{:S(2)}) collective-permute-start(bf16[2,64,1024]{2,1,0:T(8,128)(2,1)} %collective-permute-done.9.refs_5_), channel_id=1, source_target_pairs={{0,8},{8,0},{16,24},{24,16},{1,9},{9,1},{17,25},{25,17},{2,10},{10... | collective-permute-start | bytes 786440 | tf_op jit(solution)/shard_map/ppermute | solution.py:140
  86.8 36.6 %copy-start.8 = (bf16[64,1024]{1,0:T(8,128)(2,1)S(1)}, bf16[64,1024]{1,0:T(8,128)(2,1)}, u32[]{:S(2)}) copy-start(bf16[64,1024]{1,0:T(8,128)(2,1)} %get-tuple-element.52) | copy-start | bytes 393220
  86.8 36.6 %copy-start.9 = (bf16[64,1024]{1,0:T(8,128)(2,1)S(1)}, bf16[64,1024]{1,0:T(8,128)(2,1)}, u32[]{:S(2)}) copy-start(bf16[64,1024]{1,0:T(8,128)(2,1)} %get-tuple-element.55) | copy-start | bytes 393220
  86.8 36.6 %copy-start.10 = (bf16[64,1024]{1,0:T(8,128)(2,1)S(1)}, bf16[64,1024]{1,0:T(8,128)(2,1)}, u32[]{:S(2)}) copy-start(bf16[64,1024]{1,0:T(8,128)(2,1)} %get-tuple-element.54) | copy-start | bytes 393220
  97.1 14.4 %collective-permute-start.20 = (bf16[4,32,2048]{2,1,0:T(8,128)(2,1)S(1)}, bf16[4,32,2048]{2,1,0:T(8,128)(2,1)}, u32[]{:S(2)}, u32[]{:S(2)}) collective-permute-start(bf16[4,32,2048]{2,1,0:T(8,128)(2,1)S(1)} %fusion), channel_id=1, source_target_pairs={{0,1},{1,0},{2,3},{3,2},{4,5},{5,4},{6,7},{7,6},{8,9},{9,8},{10,11... | collective-permute-start | bytes 1572872 | tf_op jit(solution)/shard_map/ppermute | solution.py:188
  112.7 7.9 %collective-permute-start.21 = (bf16[2,32,2048]{2,1,0:T(8,128)(2,1)S(1)}, bf16[2,32,2048]{2,1,0:T(8,128)(2,1)S(1)}, u32[]{:S(2)}, u32[]{:S(2)}) collective-permute-start(bf16[2,32,2048]{2,1,0:T(8,128)(2,1)S(1)} %fusion.19), channel_id=1, source_target_pairs={{0,2},{1,3},{2,0},{3,1},{4,6},{5,7},{6,4},{7,5},{8,10},{9,11},{10,... | collective-permute-start | bytes 786440 | tf_op jit(solution)/shard_map/ppermute | solution.py:188
  120.7 7.9 %collective-permute-start.22 = (bf16[1,32,2048]{2,1,0:T(8,128)(2,1)S(1)}, bf16[1,32,2048]{2,1,0:T(8,128)(2,1)S(1)}, u32[]{:S(2)}, u32[]{:S(2)}) collective-permute-start(bf16[1,32,2048]{2,1,0:T(8,128)(2,1)S(1)} %dynamic-slice_convert_fusion.1), channel_id=1, source_target_pairs={{0,4},{1,5},{2,6},{3,7},{4,0},{5,1},{6,2},{7,3},{8,12},{9,13},{10,... | collective-permute-start | bytes 393224 | tf_op jit(solution)/shard_map/ppermute | solution.py:188
  (3 other events, 2.2 us)

commit v2 on v0

v2 whole, which is shorter than its diff:
```python
import functools

import jax
import jax.numpy as jnp
from jax import lax
from jax.experimental import pallas as pl
from jax.experimental.pallas import tpu as pltpu
from jax.sharding import PartitionSpec as P

BF16 = jnp.bfloat16
F32 = jnp.float32
VMEM_BYTES = 44 * 1024 * 1024
SHARES = (2, 4, 4, 4)
WHOLE = pl.BlockSpec(memory_space=pltpu.VMEM)
REMOTE = pl.BlockSpec(memory_space=pl.ANY)


def chunk_list(width):
    block = 256 if width % 256 == 0 else 128
    units = width // block
    total = sum(SHARES)
    edges = [0]
    run = 0
    for share in SHARES:
        run += share
        edges.append(max(min(units, round(units * run / total)), edges[-1]))
    return block, [(a, b - a) for a, b in zip(edges, edges[1:]) if b > a]


def call(kernel, name, in_specs, out_specs, out_shape, scratch, flops, moved, args, aliases=None):
    return pl.pallas_call(
        kernel,
        in_specs=in_specs,
        out_specs=out_specs,
        out_shape=out_shape,
        scratch_shapes=scratch,
        input_output_aliases=aliases or {},
        compiler_params=pltpu.CompilerParams(vmem_limit_bytes=VMEM_BYTES),
        cost_estimate=pl.CostEstimate(flops=flops, bytes_accessed=moved, transcendentals=0),
        name=name,
    )(*args)


def forward_kernel(quarters, rows, block, start, count, waits_for, x_ref, gate_ref, up_ref, *refs):
    own_ref, far_ref, send_ref, weights, total, sems = refs[waits_for:]
    copies = []
    for j in range(count):
        columns = pl.ds((start + j) * block, block)
        pair = [
            pltpu.make_async_copy(ref.at[:, columns], weights.at[k, j], sems.at[k, j])
            for k, ref in enumerate((gate_ref, up_ref))
        ]
        for copy in pair:
            copy.start()
        copies.append(pair)
    outer = quarters // 2
    me = lax.axis_index("row")
    place, core = me // 2, me % 2
    x = x_ref[...]
    for j in range(count):
        at = slice(j * block, (j + 1) * block)
        for k in range(2):
            copies[j][k].wait()
            total[k] = jnp.dot(x, weights[k, j], preferred_element_type=F32)
        for step in range(outer):
            there = (place + step) % outer * 2
            mine = pl.multiple_of((there + core) * rows, rows)
            other = pl.multiple_of((there + 1 - core) * rows, rows)
            for k in range(2):
                kept = total[k, pl.ds(mine, rows), :]
                if step == 0:
                    own_ref[k, :, at] = kept
                else:
                    far_ref[step - 1, k, :, at] = kept
                send_ref[step, k, :, at] = total[k, pl.ds(other, rows), :].astype(BF16)


def forward_part(quarters, block, start, count, x, gate_weight, up_weight, after):
    tokens, depth = x.shape
    rows = tokens // quarters
    outer = quarters // 2
    width = count * block
    return call(
        functools.partial(forward_kernel, quarters, rows, block, start, count, len(after)),
        "forward_part",
        [WHOLE, REMOTE, REMOTE] + [REMOTE] * len(after),
        [WHOLE] * 3,
        [
            jax.ShapeDtypeStruct((2, rows, width), F32),
            jax.ShapeDtypeStruct((outer - 1, 2, rows, width), F32),
            jax.ShapeDtypeStruct((outer, 2, rows, width), BF16),
        ],
        [
            pltpu.VMEM((2, count, depth, block), BF16),
            pltpu.VMEM((2, tokens, block), F32),
            pltpu.SemaphoreType.DMA((2, count)),
        ],
        4 * tokens * depth * width,
        4 * depth * width,
        (x, gate_weight, up_weight, *after),
    )


def middle_kernel(outer, at, first, own_ref, got_ref, upstream_ref, *refs):
    far_refs, rest = refs[: outer - 1], refs[outer - 1 :]
    if not first:
        rest[1][...] = rest[0][...]
        rest = rest[1:]
    hidden_ref, grads_ref = rest
    gate_pre = own_ref[0] + got_ref[0, 0].astype(F32)
    up_pre = own_ref[1] + got_ref[0, 1].astype(F32)
    for far in far_refs:
        gate_pre += far[0].astype(F32)
        up_pre += far[1].astype(F32)
    sigma_gate = jax.nn.sigmoid(gate_pre)
    upstream = upstream_ref[:, at].astype(F32)
    gated = gate_pre * sigma_gate
    hidden_ref[:, at] = (gated * up_pre).astype(BF16)
    slope = sigma_gate * (1.0 + gate_pre * (1.0 - sigma_gate))
    grads_ref[0] = (upstream * up_pre * slope).astype(BF16)
    grads_ref[1] = (upstream * gated).astype(BF16)


def middle_part(outer, at, own, got, far, hidden_grad, hidden):
    rows, width = own.shape[1:]
    first = hidden is None
    args = [own, got, hidden_grad, *far] + ([] if first else [hidden])
    return call(
        functools.partial(middle_kernel, outer, at, first),
        "middle_part",
        [WHOLE] * len(args),
        [WHOLE] * 2,
        [
            jax.ShapeDtypeStruct(hidden_grad.shape, BF16),
            jax.ShapeDtypeStruct((2, rows, width), BF16),
        ],
        [],
        20 * rows * width,
        8 * rows * width,
        args,
    )


def input_kernel(quarters, rows, split, columns, first, gate_ref, up_ref, *refs):
    pieces, rest = refs[:quarters], refs[quarters:]
    if not first:
        earlier, rest = rest[:2], rest[2:]
    halves, (grads, weights, sems) = rest[:2], rest[2:]
    parts, deep = split
    copies = []
    for d in range(parts):
        pair = [
            pltpu.make_async_copy(
                ref.at[pl.ds(d * deep, deep), columns], weights.at[k, d], sems.at[k, d]
            )
            for k, ref in enumerate((gate_ref, up_ref))
        ]
        for copy in pair:
            copy.start()
        copies.append(pair)
    outer = quarters // 2
    me = lax.axis_index("row")
    place, core = me // 2, me % 2
    for j, piece in enumerate(pieces):
        step, swap = j // 2, j % 2
        there = (place + outer - step) % outer * 2
        at = pl.multiple_of((there + (core + swap) % 2) * rows, rows)
        for k in range(2):
            grads[k, pl.ds(at, rows), :] = piece[k]
    dims = (((1,), (1,)), ((), ()))
    for d in range(parts):
        half, at = d // (parts // 2), pl.ds(d % (parts // 2) * deep, deep)
        copies[d][0].wait()
        term = lax.dot_general(grads[0], weights[0, d], dims, preferred_element_type=F32)
        copies[d][1].wait()
        term += lax.dot_general(grads[1], weights[1, d], dims, preferred_element_type=F32)
        halves[half][:, at] = term if first else earlier[half][:, at] + term


def input_part(quarters, block, start, count, gate_weight, up_weight, pieces, acc):
    depth = gate_weight.shape[0]
    rows = pieces[0].shape[1]
    tokens = rows * quarters
    width = count * block
    deep = 256 if depth % 256 == 0 else 128
    split = (depth // deep, deep)
    first = acc is None
    args = [gate_weight, up_weight, *pieces] + ([] if first else acc)
    half = jax.ShapeDtypeStruct((tokens, depth // 2), F32)
    *acc, grads = call(
        functools.partial(
            input_kernel, quarters, rows, split, pl.ds(start * block, width), first
        ),
        "input_part",
        [REMOTE] * 2 + [WHOLE] * (len(args) - 2),
        [WHOLE] * 3,
        [half, half, jax.ShapeDtypeStruct((2, tokens, width), BF16)],
        [
            pltpu.VMEM((2, split[0], deep, width), BF16),
            pltpu.SemaphoreType.DMA((2, split[0])),
        ],
        4 * tokens * depth * width,
        4 * depth * width,
        args,
    )
    return acc, grads


def weight_kernel(block, start, count, skipped, xt_ref, grads_ref, *refs):
    gate_out, up_out, products, sems = refs[skipped:]
    xt = xt_ref[...]
    copies = []
    for j in range(count):
        for k, out in enumerate((gate_out, up_out)):
            piece = grads_ref[k, :, j * block : (j + 1) * block]
            products[k, j] = jnp.dot(xt, piece, preferred_element_type=F32).astype(BF16)
            copy = pltpu.make_async_copy(
                products.at[k, j], out.at[:, pl.ds((start + j) * block, block)], sems.at[k, j]
            )
            copy.start()
            copies.append(copy)
    for copy in copies:
        copy.wait()


def weight_part(block, start, count, full, xt, grads, state, after):
    depth, tokens = xt.shape
    width = count * block
    args = [xt, grads, *after, *state]
    first = 2 + len(after)
    aliases = {first + k: k for k in range(len(state))}
    grad = jax.ShapeDtypeStruct((depth, full), BF16)
    return call(
        functools.partial(weight_kernel, block, start, count, len(args) - 2),
        "weight_part",
        [WHOLE] * 2 + [REMOTE] * len(after) + [REMOTE] * len(state),
        [REMOTE] * 2,
        [grad, grad],
        [
            pltpu.VMEM((2, count, depth, block), BF16),
            pltpu.SemaphoreType.DMA((2, count)),
        ],
        4 * tokens * depth * width,
        4 * depth * width,
        args,
        aliases,
    )


def token_sums(halves, columns, orders):
    position = lax.axis_index("col")
    bits = len(orders[0])
    rows = halves[0].shape[0] // columns
    halves = [half.reshape((2,) * bits + (rows, half.shape[1])) for half in halves]
    lefts = [list(reversed(range(bits))) for _ in halves]
    stages = []
    for stage in range(bits):
        kept, got = [], []
        for half, left, order in zip(halves, lefts, orders):
            bit = order[stage]
            axis = left.index(bit)
            left.remove(bit)
            mine = (position // 2**bit) % 2
            send = lax.dynamic_index_in_dim(half, 1 - mine, axis, keepdims=False)
            moves = [(c, c ^ 2**bit) for c in range(columns)]
            got.append(lax.ppermute(send.astype(BF16), "col", moves))
            kept.append(lax.dynamic_index_in_dim(half, mine, axis, keepdims=False))
        halves = [keep + far.astype(F32) for keep, far in zip(kept, got)]
        stages.append(halves)
    return stages


def local(quarters, columns, inputs, gate_weight, up_weight, hidden_grad):
    outer = quarters // 2
    full = gate_weight.shape[1]
    block, chunks = chunk_list(full)
    swap = [(r, r ^ 1) for r in range(quarters)]

    def sibling(value):
        return lax.ppermute(value, "row", swap)

    def across(value, step):
        moves = [(r, (r // 2 + step) % outer * 2 + r % 2) for r in range(quarters)]
        return lax.ppermute(value, "row", moves)

    owns, gots, sums = [], [], []
    for i, (start, count) in enumerate(chunks):
        after = sums[i - 2][:1] if i >= 2 else []
        own, far, send = forward_part(
            quarters, block, start, count, inputs, gate_weight, up_weight, after
        )
        got = sibling(send)
        owns.append(own)
        gots.append(got)
        sums.append(
            [(far[step - 1] + got[step].astype(F32)).astype(BF16) for step in range(1, outer)]
        )

    xt = inputs.T
    hidden = None
    pieces = []
    for (start, count), own, got, near in zip(chunks, owns, gots, sums):
        far = [across(value, step + 1) for step, value in enumerate(near)]
        at = slice(start * block, (start + count) * block)
        hidden, mine = middle_part(outer, at, own, got, far, hidden_grad, hidden)
        group = [mine, sibling(mine)]
        for step in range(1, outer):
            there = across(mine, step)
            group += [there, sibling(there)]
        pieces.append(group)

    acc = None
    grads = []
    for (start, count), group in zip(chunks, pieces):
        acc, whole = input_part(
            quarters, block, start, count, gate_weight, up_weight, group, acc
        )
        grads.append(whole)
    bits = columns.bit_length() - 1
    order = list(range(bits))
    stages = [acc] + token_sums(acc, columns, [order, order[1::-1] + order[2:]])
    input_grad = jnp.concatenate([half.astype(BF16) for half in stages[-1]], axis=1)
    state = []
    for i, ((start, count), whole) in enumerate(zip(chunks, grads)):
        after = stages[min(i, bits) - 1] if i else []
        state = weight_part(block, start, count, full, xt, whole, state, after)
    return hidden, input_grad, state[0], state[1]


def solution(mesh):
    return jax.shard_map(
        functools.partial(local, mesh.shape["row"], mesh.shape["col"]),
        mesh=mesh,
        in_specs=(P(None, "row"), P("row", "col"), P("row", "col"), P("row", "col")),
        out_specs=(P("row", "col"), P("col", "row"), P("row", "col"), P("row", "col")),
        check_vma=False,
    )
```

time: 243 us -> 128 us (0.53)
  waiting for transfers between devices: 128 us -> 26.3 us
  Pallas kernels: 0 us -> 72.5 us
  matrix products: 55.9 us -> 0 us
  local copies, waits for them, and re-layouts: 38.7 us -> 3.73 us
  starting transfers between devices: 0.38 us -> 22.9 us
  between operations: 13.8 us -> 1.08 us
  other arithmetic: 4.57 us -> 1.05 us
    reduce_scatter x3 -> x0, waiting for transfers between devices: 94.9 us -> none  [the longest x1 44.5 us: local(): lax.psum_scatter(jnp.dot(token_rows, up_weight, preferred_element_type=jn...]
    pallas_call x0 -> x16, Pallas kernels: none -> 72.5 us  [call(): pl.pallas_call(kernel, in_specs=in_specs, out_specs=out_specs, out_shape=...]
    dot_general x6 -> x0, matrix products: 55.9 us -> none  [the longest x2 22.7 us: input_term(): lax.dot_general(grad_piece, weight_block, (((1,), (1,)), ((), ())), prefe...]
    unnamed x10 -> x11, local copies, waits for them, and re-layouts: 38.7 us -> 3.49 us
    all_gather x2 -> x0, waiting for transfers between devices: 32.6 us -> none  [the longest x1 20.5 us: local(): grad_piece = lax.all_gather(gate_grad, 'row', axis=0, tiled=True)]
    ppermute x0 -> x26, waiting for transfers between devices: none -> 26.3 us  [the longest x8 22.4 us: across(): return lax.ppermute(value, 'row', moves)]
    ppermute x0 -> x26, starting transfers between devices: none -> 22.9 us  [the longest x8 11.5 us: across(): return lax.ppermute(value, 'row', moves)]
    convert_element_type x2 -> x6, other arithmetic: 4.57 us -> 0.22 us  [the longest x4 0.19 us: local(): (far[step - 1] + got[step].astype(F32)).astype(BF16)]
  transfers between devices with their start and end apart: 5 -> 26, of which waited for: 5 -> 7; matrix products, arithmetic and copies ran while one was open for 30% -> 1% of each run, Pallas kernels for 0% -> 47%
where the time goes in v2:
time: 128 us
  Pallas kernels  72.5 us (57%)
  waiting for transfers between devices  26.3 us (21%)
  starting transfers between devices  22.9 us (18%)
  local copies, waits for them, and re-layouts  3.73 us (3%)
    pallas_call x16, Pallas kernels, call(): pl.pallas_call(kernel, in_specs=in_specs, out_specs=out_specs, out_shape=...  72.5 us
    ppermute x8, waiting for transfers between devices, across(): return lax.ppermute(value, 'row', moves)  22.4 us
    ppermute x8, starting transfers between devices, across(): return lax.ppermute(value, 'row', moves)  11.5 us
    ppermute x6, starting transfers between devices, token_sums(): got.append(lax.ppermute(send.astype(BF16), 'col', moves))  8.43 us
    ppermute x6, waiting for transfers between devices, token_sums(): got.append(lax.ppermute(send.astype(BF16), 'col', moves))  3.85 us
    unnamed x11, local copies, waits for them, and re-layouts  3.49 us
    ppermute x12, starting transfers between devices, sibling(): return lax.ppermute(value, 'row', swap)  2.95 us
  transfers between devices with their start and end apart: 26, of which 7 were waited for; matrix products, arithmetic and copies ran while one was open for 1% of the time, Pallas kernels for 47%

profile of v2, /device:TPU:0, one launch (start us, length us, event | category | flops | bytes accessed | tf_op | source)
XLA Modules:
  0.0 127.6 jit_solution(4515705556074912677)
XLA Ops:
  0.6 1.2 copy-done
  1.9 4.1 %forward_part.6 = (f32[2,64,512]{2,1,0:T(8,128)S(1)}, f32[1,2,64,512]{3,2,1,0:T(8,128)S(1)}, bf16[2,2,64,512]{3,2,1,0:T(8,128)(2,1)S(1)}) custom-call(bf16[256,2048]{1,0:T(8,128)(2,1)S(1)} %copy-done, bf16[2048,3584]{1,0:T(8,128)(2,1)} %gate_ref.15, bf16[2048,3584]{1,0:T(8,128)(2,1)} %up_ref.15), custom_call_target="tpu_custom_call" | custom-call | flops 1073741824 | bytes 4194304 | tf_op jit(solution)/shard_map/forward_part/pallas_call | solution.py:31
  6.5 7.0 %forward_part.4 = (f32[2,64,1024]{2,1,0:T(8,128)S(1)}, f32[1,2,64,1024]{3,2,1,0:T(8,128)S(1)}, bf16[2,2,64,1024]{3,2,1,0:T(8,128)(2,1)S(1)}) custom-call(bf16[256,2048]{1,0:T(8,128)(2,1)S(1)} %copy-done, bf16[2048,3584]{1,0:T(8,128)(2,1)} %gate_ref.15, bf16[2048,3584]{1,0:T(8,128)(2,1)} %up_ref.15), custom_call_target="tpu_custom_call" | custom-call | flops 2147483648 | bytes 8388608 | tf_op jit(solution)/shard_map/forward_part/pallas_call | solution.py:31
  13.6 7.0 %forward_part.7 = (f32[2,64,1024]{2,1,0:T(8,128)S(1)}, f32[1,2,64,1024]{3,2,1,0:T(8,128)S(1)}, bf16[2,2,64,1024]{3,2,1,0:T(8,128)(2,1)S(1)}) custom-call(bf16[256,2048]{1,0:T(8,128)(2,1)S(1)} %copy-done, bf16[2048,3584]{1,0:T(8,128)(2,1)} %gate_ref.15, bf16[2048,3584]{1,0:T(8,128)(2,1)} %up_ref.15, bf16[2,64,512]{2,1,0:T(8,128)(2,1)S(1)} %fusion.5.refs_0_), custom_call_target="tpu_custom_call" | custom-call | flops 2147483648 | bytes 8388608 | tf_op jit(solution)/shard_map/forward_part/pallas_call | solution.py:31
  21.2 7.1 %forward_part.5 = (f32[2,64,1024]{2,1,0:T(8,128)S(1)}, f32[1,2,64,1024]{3,2,1,0:T(8,128)S(1)}, bf16[2,2,64,1024]{3,2,1,0:T(8,128)(2,1)S(1)}) custom-call(bf16[256,2048]{1,0:T(8,128)(2,1)S(1)} %copy-done, bf16[2048,3584]{1,0:T(8,128)(2,1)} %gate_ref.15, bf16[2048,3584]{1,0:T(8,128)(2,1)} %up_ref.15, bf16[2,64,1024]{2,1,0:T(8,128)(2,1)S(1)} %fusion.refs_0_), custom_call_target="tpu_custom_call" | custom-call | flops 2147483648 | bytes 8388608 | tf_op jit(solution)/shard_map/forward_part/pallas_call | solution.py:31
  28.4 2.9 %collective-permute-start.7 = (bf16[2,64,512]{2,1,0:T(8,128)(2,1)S(1)}, bf16[2,64,512]{2,1,0:T(8,128)(2,1)S(1)}, u32[]{:S(2)}, u32[]{:S(2)}) collective-permute-start(bf16[2,64,512]{2,1,0:T(8,128)(2,1)S(1)} %fusion.5.refs_0_), channel_id=1, source_target_pairs={{0,16},{8,24},{16,0},{24,8},{1,17},{9,25},{17,1},{25,9},{2,18},{10... | collective-permute-start | bytes 393224 | tf_op jit(solution)/shard_map/ppermute | solution.py:284
  31.4 2.1 %collective-permute-start.5 = (bf16[2,64,1024]{2,1,0:T(8,128)(2,1)S(1)}, bf16[2,64,1024]{2,1,0:T(8,128)(2,1)S(1)}, u32[]{:S(2)}, u32[]{:S(2)}) collective-permute-start(bf16[2,64,1024]{2,1,0:T(8,128)(2,1)S(1)} %fusion.2), channel_id=1, source_target_pairs={{0,16},{8,24},{16,0},{24,8},{1,17},{9,25},{17,1},{25,9},{2,18},{10... | collective-permute-start | bytes 786440 | tf_op jit(solution)/shard_map/ppermute | solution.py:284
  33.6 2.0 %collective-permute-done.7.refs_0_ = bf16[2,64,512]{2,1,0:T(8,128)(2,1)S(1)} collective-permute-done((bf16[2,64,512]{2,1,0:T(8,128)(2,1)S(1)}, bf16[2,64,512]{2,1,0:T(8,128)(2,1)S(1)}, u32[]{:S(2)}, u32[]{:S(2)}) %collective-permute-start.7) | collective-permute-done | bytes 131104 | tf_op jit(solution)/shard_map/ppermute | solution.py:284
  35.7 5.5 %collective-permute-done.6.refs_0_ = bf16[2,64,1024]{2,1,0:T(8,128)(2,1)S(1)} collective-permute-done((bf16[2,64,1024]{2,1,0:T(8,128)(2,1)S(1)}, bf16[2,64,1024]{2,1,0:T(8,128)(2,1)S(1)}, u32[]{:S(2)}, u32[]{:S(2)}) %collective-permute-start.6) | collective-permute-done | bytes 262176 | tf_op jit(solution)/shard_map/ppermute | solution.py:284
  41.4 2.1 %collective-permute-start.15 = (bf16[2,64,1024]{2,1,0:T(8,128)(2,1)S(1)}, bf16[2,64,1024]{2,1,0:T(8,128)(2,1)S(1)}, u32[]{:S(2)}, u32[]{:S(2)}) collective-permute-start(bf16[2,64,1024]{2,1,0:T(8,128)(2,1)S(1)} %get-tuple-element.62.refs_0_), channel_id=1, source_target_pairs={{0,16},{8,24},{16,0},{24,8},{1,17},{9,25},{17,1},{25,9},{2,18},{10... | collective-permute-start | bytes 786440 | tf_op jit(solution)/shard_map/ppermute | solution.py:284
  43.6 3.2 %collective-permute-done.5.refs_0_ = bf16[2,64,1024]{2,1,0:T(8,128)(2,1)S(1)} collective-permute-done((bf16[2,64,1024]{2,1,0:T(8,128)(2,1)S(1)}, bf16[2,64,1024]{2,1,0:T(8,128)(2,1)S(1)}, u32[]{:S(2)}, u32[]{:S(2)}) %collective-permute-start.5) | collective-permute-done | bytes 262176 | tf_op jit(solution)/shard_map/ppermute | solution.py:284
  47.0 2.1 %collective-permute-start.12 = (bf16[2,64,1024]{2,1,0:T(8,128)(2,1)S(1)}, bf16[2,64,1024]{2,1,0:T(8,128)(2,1)S(1)}, u32[]{:S(2)}, u32[]{:S(2)}) collective-permute-start(bf16[2,64,1024]{2,1,0:T(8,128)(2,1)S(1)} %get-tuple-element.61.refs_0_), channel_id=1, source_target_pairs={{0,16},{8,24},{16,0},{24,8},{1,17},{9,25},{17,1},{25,9},{2,18},{10... | collective-permute-start | bytes 786440 | tf_op jit(solution)/shard_map/ppermute | solution.py:284
  49.2 11.8 %collective-permute-done.18.refs_2_ = bf16[2,64,512]{2,1,0:T(8,128)(2,1)} collective-permute-done((bf16[2,64,512]{2,1,0:T(8,128)(2,1)S(1)}, bf16[2,64,512]{2,1,0:T(8,128)(2,1)}, u32[]{:S(2)}, u32[]{:S(2)}) %collective-permute-start.18) | collective-permute-done | bytes 131104 | tf_op jit(solution)/shard_map/ppermute | solution.py:284
  61.5 0.9 middle_part.7
  63.0 2.1 %collective-permute-start.9 = (bf16[2,64,1024]{2,1,0:T(8,128)(2,1)S(1)}, bf16[2,64,1024]{2,1,0:T(8,128)(2,1)}, u32[]{:S(2)}, u32[]{:S(2)}) collective-permute-start(bf16[2,64,1024]{2,1,0:T(8,128)(2,1)S(1)} %get-tuple-element.60.refs_0_), channel_id=1, source_target_pairs={{0,16},{8,24},{16,0},{24,8},{1,17},{9,25},{17,1},{25,9},{2,18},{10... | collective-permute-start | bytes 786440 | tf_op jit(solution)/shard_map/ppermute | solution.py:284
  65.1 0.7 copy.21
  65.9 0.9 copy-done.4
  66.8 6.0 %input_part.4 = (f32[256,1024]{1,0:T(8,128)S(1)}, f32[256,1024]{1,0:T(8,128)S(1)}, bf16[2,256,512]{2,1,0:T(8,128)(2,1)S(1)}) custom-call(bf16[2048,3584]{1,0:T(8,128)(2,1)} %gate_ref.15, bf16[2048,3584]{1,0:T(8,128)(2,1)} %up_ref.15, bf16[2,64,512]{2,1,0:T(8,128)(2,1)S(1)} %get-tuple-element.63.refs_0_, bf16[2,64,512]{2,1,0:T(8,128)(2,1)S(1)} %copy-done.4, ...), custom_call_target="tpu_custom_call" | custom-call | flops 1073741824 | bytes 4194304 | tf_op jit(solution)/shard_map/input_part/pallas_call | solution.py:31
  73.4 2.7 %weight_part.4 = (bf16[2048,3584]{1,0:T(8,128)(2,1)}, bf16[2048,3584]{1,0:T(8,128)(2,1)}) custom-call(bf16[2048,256]{1,0:T(8,128)(2,1)S(1)} %bitcast.39, bf16[2,256,512]{2,1,0:T(8,128)(2,1)S(1)} %get-tuple-element.75.grads_ref), custom_call_target="tpu_custom_call" | custom-call | flops 1073741824 | bytes 4194304 | tf_op jit(solution)/shard_map/weight_part/pallas_call | solution.py:31
  76.7 8.6 %input_part.5 = (f32[256,1024]{1,0:T(8,128)S(1)}, f32[256,1024]{1,0:T(8,128)S(1)}, bf16[2,256,1024]{2,1,0:T(8,128)(2,1)S(1)}) custom-call(bf16[2048,3584]{1,0:T(8,128)(2,1)} %gate_ref.15, bf16[2048,3584]{1,0:T(8,128)(2,1)} %up_ref.15, bf16[2,64,1024]{2,1,0:T(8,128)(2,1)S(1)} %get-tuple-element.62.refs_0_, ...), custom_call_target="tpu_custom_call" | custom-call | flops 2147483648 | bytes 8388608 | tf_op jit(solution)/shard_map/input_part/pallas_call | solution.py:31
  85.4 7.6 %input_part.6 = (f32[256,1024]{1,0:T(8,128)S(1)}, f32[256,1024]{1,0:T(8,128)S(1)}, bf16[2,256,1024]{2,1,0:T(8,128)(2,1)S(1)}) custom-call(bf16[2048,3584]{1,0:T(8,128)(2,1)} %gate_ref.15, bf16[2048,3584]{1,0:T(8,128)(2,1)} %up_ref.15, bf16[2,64,1024]{2,1,0:T(8,128)(2,1)S(1)} %get-tuple-element.61.refs_0_, ...), custom_call_target="tpu_custom_call" | custom-call | flops 2147483648 | bytes 8388608 | tf_op jit(solution)/shard_map/input_part/pallas_call | solution.py:31
  93.1 8.8 %input_part.7 = (f32[256,1024]{1,0:T(8,128)S(1)}, f32[256,1024]{1,0:T(8,128)S(1)}, bf16[2,256,1024]{2,1,0:T(8,128)(2,1)S(1)}) custom-call(bf16[2048,3584]{1,0:T(8,128)(2,1)} %gate_ref.15, bf16[2048,3584]{1,0:T(8,128)(2,1)} %up_ref.15, bf16[2,64,1024]{2,1,0:T(8,128)(2,1)S(1)} %get-tuple-element.60.refs_0_, ...), custom_call_target="tpu_custom_call" | custom-call | flops 2147483648 | bytes 8388608 | tf_op jit(solution)/shard_map/input_part/pallas_call | solution.py:31
  101.9 1.6 %collective-permute-start.20 = (bf16[2,2,32,1024]{3,2,0,1:T(8,128)(2,1)S(1)}, bf16[2,2,32,1024]{3,2,0,1:T(8,128)(2,1)S(1)}, u32[]{:S(2)}, u32[]{:S(2)}) collective-permute-start(bf16[2,2,32,1024]{3,2,0,1:T(8,128)(2,1)S(1)} %fusion.3), channel_id=1, source_target_pairs={{0,1},{1,0},{2,3},{3,2},{4,5},{5,4},{6,7},{7,6},{8,9},{9,8},{10,11... | collective-permute-start | bytes 786440 | tf_op jit(solution)/shard_map/ppermute | solution.py:266
  103.5 1.6 %collective-permute-start.23 = (bf16[2,2,32,1024]{3,2,0,1:T(8,128)(2,1)S(1)}, bf16[2,2,32,1024]{3,2,0,1:T(8,128)(2,1)S(1)}, u32[]{:S(2)}, u32[]{:S(2)}) collective-permute-start(bf16[2,2,32,1024]{3,2,0,1:T(8,128)(2,1)S(1)} %fusion.4), channel_id=1, source_target_pairs={{0,2},{1,3},{2,0},{3,1},{4,6},{5,7},{6,4},{7,5},{8,10},{9,11},{10,... | collective-permute-start | bytes 786440 | tf_op jit(solution)/shard_map/ppermute | solution.py:266
  105.2 4.1 %weight_part.5 = (bf16[2048,3584]{1,0:T(8,128)(2,1)}, bf16[2048,3584]{1,0:T(8,128)(2,1)}) custom-call(bf16[2048,256]{1,0:T(8,128)(2,1)S(1)} %bitcast.40, bf16[2,256,1024]{2,1,0:T(8,128)(2,1)S(1)} %get-tuple-element.74.grads_ref, f32[256,1024]{1,0:T(8,128)S(1)} %get-tuple-element.70.refs_0_, ...), custom_call_target="tpu_custom_call", output_to_operand_aliasing={{0}: (4, {}), {1}: (5, {})} | custom-call | flops 2147483648 | bytes 8388608 | tf_op jit(solution)/shard_map/weight_part/pallas_call | solution.py:31
  109.3 1.2 collective-permute-done.20
  110.7 1.2 collective-permute-done.23
  112.0 1.6 %collective-permute-start.21 = (bf16[2,32,1024]{2,1,0:T(8,128)(2,1)S(1)}, bf16[2,32,1024]{2,1,0:T(8,128)(2,1)S(1)}, u32[]{:S(2)}, u32[]{:S(2)}) collective-permute-start(bf16[2,32,1024]{2,1,0:T(8,128)(2,1)S(1)} %fusion.6), channel_id=1, source_target_pairs={{0,2},{1,3},{2,0},{3,1},{4,6},{5,7},{6,4},{7,5},{8,10},{9,11},{10,... | collective-permute-start | bytes 393224 | tf_op jit(solution)/shard_map/ppermute | solution.py:266
  114.1 4.1 %weight_part.6 = (bf16[2048,3584]{1,0:T(8,128)(2,1)}, bf16[2048,3584]{1,0:T(8,128)(2,1)}) custom-call(bf16[2048,256]{1,0:T(8,128)(2,1)S(1)} %bitcast.41, bf16[2,256,1024]{2,1,0:T(8,128)(2,1)S(1)} %get-tuple-element.73.grads_ref, f32[2,2,32,1024]{3,2,1,0:T(8,128)S(1)} %copy.22.refs_0_, ...), custom_call_target="tpu_custom_call", output_to_operand_aliasing={{0}: (4, {}), {1}: (5, {})} | custom-call | flops 2147483648 | bytes 8388608 | tf_op jit(solution)/shard_map/weight_part/pallas_call | solution.py:31
  118.3 2.7 %collective-permute-start.22 = (bf16[32,1024]{1,0:T(8,128)(2,1)S(1)}, bf16[32,1024]{1,0:T(8,128)(2,1)S(1)}, u32[]{:S(2)}, u32[]{:S(2)}) collective-permute-start(bf16[32,1024]{1,0:T(8,128)(2,1)S(1)} %fusion.10), channel_id=1, source_target_pairs={{0,4},{1,5},{2,6},{3,7},{4,0},{5,1},{6,2},{7,3},{8,12},{9,13},{10,... | collective-permute-start | bytes 196616 | tf_op jit(solution)/shard_map/ppermute | solution.py:266
  121.4 4.1 %weight_part.7 = (bf16[2048,3584]{1,0:T(8,128)(2,1)}, bf16[2048,3584]{1,0:T(8,128)(2,1)}) custom-call(bf16[2048,256]{1,0:T(8,128)(2,1)S(1)} %bitcast.42, bf16[2,256,1024]{2,1,0:T(8,128)(2,1)S(1)} %get-tuple-element.72.grads_ref, f32[2,32,1024]{2,1,0:T(8,128)S(1)} %bitcast_add_fusion.3.refs_0_, ...), custom_call_target="tpu_custom_call", output_to_operand_aliasing={{0}: (4, {}), {1}: (5, {})} | custom-call | flops 2147483648 | bytes 8388608 | tf_op jit(solution)/shard_map/weight_part/pallas_call | solution.py:31
  125.5 1.4 %collective-permute-done.25 = bf16[32,1024]{1,0:T(8,128)(2,1)S(1)} collective-permute-done((bf16[32,1024]{1,0:T(8,128)(2,1)S(1)}, bf16[32,1024]{1,0:T(8,128)(2,1)S(1)}, u32[]{:S(2)}, u32[]{:S(2)}) %collective-permute-start.25) | collective-permute-done | bytes 65568 | tf_op jit(solution)/shard_map/ppermute | solution.py:266
  (66 shorter events, 6.7 us)
Async XLA Ops:
  0.6 1.2 copy-start
  5.9 7.6 %collective-permute-start.3 = (bf16[2,2,64,512]{3,2,1,0:T(8,128)(2,1)S(1)}, bf16[2,2,64,512]{3,2,1,0:T(8,128)(2,1)S(1)}, u32[]{:S(2)}, u32[]{:S(2)}) collective-permute-start(bf16[2,2,64,512]{3,2,1,0:T(8,128)(2,1)S(1)} %get-tuple-element.50), channel_id=1, source_target_pairs={{0,8},{8,0},{16,24},{24,16},{1,9},{9,1},{17,25},{25,17},{2,10},{10... | collective-permute-start | bytes 786440 | tf_op jit(solution)/shard_map/ppermute | solution.py:280
  13.4 7.6 %collective-permute-start = (bf16[2,2,64,1024]{3,2,1,0:T(8,128)(2,1)S(1)}, bf16[2,2,64,1024]{3,2,1,0:T(8,128)(2,1)S(1)}, u32[]{:S(2)}, u32[]{:S(2)}) collective-permute-start(bf16[2,2,64,1024]{3,2,1,0:T(8,128)(2,1)S(1)} %get-tuple-element.45), channel_id=1, source_target_pairs={{0,8},{8,0},{16,24},{24,16},{1,9},{9,1},{17,25},{25,17},{2,10},{10... | collective-permute-start | bytes 1572872 | tf_op jit(solution)/shard_map/ppermute | solution.py:280
  20.5 10.8 %collective-permute-start.4 = (bf16[2,2,64,1024]{3,2,1,0:T(8,128)(2,1)S(1)}, bf16[2,2,64,1024]{3,2,1,0:T(8,128)(2,1)S(1)}, u32[]{:S(2)}, u32[]{:S(2)}) collective-permute-start(bf16[2,2,64,1024]{3,2,1,0:T(8,128)(2,1)S(1)} %get-tuple-element.52), channel_id=1, source_target_pairs={{0,8},{8,0},{16,24},{24,16},{1,9},{9,1},{17,25},{25,17},{2,10},{10... | collective-permute-start | bytes 1572872 | tf_op jit(solution)/shard_map/ppermute | solution.py:280
  21.1 14.5 %copy-start.2 = (bf16[64,3584]{1,0:T(8,128)(2,1)S(1)}, bf16[64,3584]{1,0:T(8,128)(2,1)}, u32[]{:S(2)}) copy-start(bf16[64,3584]{1,0:T(8,128)(2,1)} %upstream_ref.7) | copy-start | bytes 1376260
  21.1 44.0 %copy-start.1 = (bf16[256,2048]{1,0:T(8,128)(2,1)S(1)}, bf16[256,2048]{1,0:T(8,128)(2,1)}, u32[]{:S(2)}) copy-start(bf16[256,2048]{1,0:T(8,128)(2,1)} %x_ref.7) | copy-start | bytes 3145732
  28.2 5.2 %collective-permute-start.1 = (bf16[2,2,64,1024]{3,2,1,0:T(8,128)(2,1)S(1)}, bf16[2,2,64,1024]{3,2,1,0:T(8,128)(2,1)S(1)}, u32[]{:S(2)}, u32[]{:S(2)}) collective-permute-start(bf16[2,2,64,1024]{3,2,1,0:T(8,128)(2,1)S(1)} %get-tuple-element.47), channel_id=1, source_target_pairs={{0,8},{8,0},{16,24},{24,16},{1,9},{9,1},{17,25},{25,17},{2,10},{10... | collective-permute-start | bytes 1572872 | tf_op jit(solution)/shard_map/ppermute | solution.py:280
  28.4 7.2 %collective-permute-start.7 = (bf16[2,64,512]{2,1,0:T(8,128)(2,1)S(1)}, bf16[2,64,512]{2,1,0:T(8,128)(2,1)S(1)}, u32[]{:S(2)}, u32[]{:S(2)}) collective-permute-start(bf16[2,64,512]{2,1,0:T(8,128)(2,1)S(1)} %fusion.5.refs_0_), channel_id=1, source_target_pairs={{0,16},{8,24},{16,0},{24,8},{1,17},{9,25},{17,1},{25,9},{2,18},{10... | collective-permute-start | bytes 393224 | tf_op jit(solution)/shard_map/ppermute | solution.py:284
  31.3 9.9 %collective-permute-start.6 = (bf16[2,64,1024]{2,1,0:T(8,128)(2,1)S(1)}, bf16[2,64,1024]{2,1,0:T(8,128)(2,1)S(1)}, u32[]{:S(2)}, u32[]{:S(2)}) collective-permute-start(bf16[2,64,1024]{2,1,0:T(8,128)(2,1)S(1)} %fusion.refs_0_), channel_id=1, source_target_pairs={{0,16},{8,24},{16,0},{24,8},{1,17},{9,25},{17,1},{25,9},{2,18},{10... | collective-permute-start | bytes 786440 | tf_op jit(solution)/shard_map/ppermute | solution.py:284
  31.4 15.4 %collective-permute-start.5 = (bf16[2,64,1024]{2,1,0:T(8,128)(2,1)S(1)}, bf16[2,64,1024]{2,1,0:T(8,128)(2,1)S(1)}, u32[]{:S(2)}, u32[]{:S(2)}) collective-permute-start(bf16[2,64,1024]{2,1,0:T(8,128)(2,1)S(1)} %fusion.2), channel_id=1, source_target_pairs={{0,16},{8,24},{16,0},{24,8},{1,17},{9,25},{17,1},{25,9},{2,18},{10... | collective-permute-start | bytes 786440 | tf_op jit(solution)/shard_map/ppermute | solution.py:284
  33.5 27.5 %collective-permute-start.2 = (bf16[2,64,1024]{2,1,0:T(8,128)(2,1)S(1)}, bf16[2,64,1024]{2,1,0:T(8,128)(2,1)S(1)}, u32[]{:S(2)}, u32[]{:S(2)}) collective-permute-start(bf16[2,64,1024]{2,1,0:T(8,128)(2,1)S(1)} %fusion.1), channel_id=1, source_target_pairs={{0,16},{8,24},{16,0},{24,8},{1,17},{9,25},{17,1},{25,9},{2,18},{10... | collective-permute-start | bytes 786440 | tf_op jit(solution)/shard_map/ppermute | solution.py:284
  41.4 23.7 %collective-permute-start.15 = (bf16[2,64,1024]{2,1,0:T(8,128)(2,1)S(1)}, bf16[2,64,1024]{2,1,0:T(8,128)(2,1)S(1)}, u32[]{:S(2)}, u32[]{:S(2)}) collective-permute-start(bf16[2,64,1024]{2,1,0:T(8,128)(2,1)S(1)} %get-tuple-element.62.refs_0_), channel_id=1, source_target_pairs={{0,16},{8,24},{16,0},{24,8},{1,17},{9,25},{17,1},{25,9},{2,18},{10... | collective-permute-start | bytes 786440 | tf_op jit(solution)/shard_map/ppermute | solution.py:284
  43.6 17.4 %collective-permute-start.18 = (bf16[2,64,512]{2,1,0:T(8,128)(2,1)S(1)}, bf16[2,64,512]{2,1,0:T(8,128)(2,1)}, u32[]{:S(2)}, u32[]{:S(2)}) collective-permute-start(bf16[2,64,512]{2,1,0:T(8,128)(2,1)S(1)} %get-tuple-element.63.refs_0_), channel_id=1, source_target_pairs={{0,16},{8,24},{16,0},{24,8},{1,17},{9,25},{17,1},{25,9},{2,18},{10... | collective-permute-start | bytes 393224 | tf_op jit(solution)/shard_map/ppermute | solution.py:284
  43.6 18.7 %collective-permute-start.17 = (bf16[2,64,512]{2,1,0:T(8,128)(2,1)S(1)}, bf16[2,64,512]{2,1,0:T(8,128)(2,1)S(1)}, u32[]{:S(2)}, u32[]{:S(2)}) collective-permute-start(bf16[2,64,512]{2,1,0:T(8,128)(2,1)S(1)} %get-tuple-element.63.refs_0_), channel_id=1, source_target_pairs={{0,8},{8,0},{16,24},{24,16},{1,9},{9,1},{17,25},{25,17},{2,10},{10... | collective-permute-start | bytes 393224 | tf_op jit(solution)/shard_map/ppermute | solution.py:280
  47.0 26.1 %collective-permute-start.12 = (bf16[2,64,1024]{2,1,0:T(8,128)(2,1)S(1)}, bf16[2,64,1024]{2,1,0:T(8,128)(2,1)S(1)}, u32[]{:S(2)}, u32[]{:S(2)}) collective-permute-start(bf16[2,64,1024]{2,1,0:T(8,128)(2,1)S(1)} %get-tuple-element.61.refs_0_), channel_id=1, source_target_pairs={{0,16},{8,24},{16,0},{24,8},{1,17},{9,25},{17,1},{25,9},{2,18},{10... | collective-permute-start | bytes 786440 | tf_op jit(solution)/shard_map/ppermute | solution.py:284
  61.0 5.0 %collective-permute-start.19 = (bf16[2,64,512]{2,1,0:T(8,128)(2,1)}, bf16[2,64,512]{2,1,0:T(8,128)(2,1)}, u32[]{:S(2)}, u32[]{:S(2)}) collective-permute-start(bf16[2,64,512]{2,1,0:T(8,128)(2,1)} %collective-permute-done.18.refs_2_), channel_id=1, source_target_pairs={{0,8},{8,0},{16,24},{24,16},{1,9},{9,1},{17,25},{25,17},{2,10},{10... | collective-permute-start | bytes 393224 | tf_op jit(solution)/shard_map/ppermute | solution.py:280
  61.0 15.2 %collective-permute-start.14 = (bf16[2,64,1024]{2,1,0:T(8,128)(2,1)S(1)}, bf16[2,64,1024]{2,1,0:T(8,128)(2,1)}, u32[]{:S(2)}, u32[]{:S(2)}) collective-permute-start(bf16[2,64,1024]{2,1,0:T(8,128)(2,1)S(1)} %get-tuple-element.62.refs_0_), channel_id=1, source_target_pairs={{0,8},{8,0},{16,24},{24,16},{1,9},{9,1},{17,25},{25,17},{2,10},{10... | collective-permute-start | bytes 786440 | tf_op jit(solution)/shard_map/ppermute | solution.py:280
  62.4 0.7 copy-start.3
  63.0 13.5 %collective-permute-start.9 = (bf16[2,64,1024]{2,1,0:T(8,128)(2,1)S(1)}, bf16[2,64,1024]{2,1,0:T(8,128)(2,1)}, u32[]{:S(2)}, u32[]{:S(2)}) collective-permute-start(bf16[2,64,1024]{2,1,0:T(8,128)(2,1)S(1)} %get-tuple-element.60.refs_0_), channel_id=1, source_target_pairs={{0,16},{8,24},{16,0},{24,8},{1,17},{9,25},{17,1},{25,9},{2,18},{10... | collective-permute-start | bytes 786440 | tf_op jit(solution)/shard_map/ppermute | solution.py:284
  65.1 11.6 %collective-permute-start.16 = (bf16[2,64,1024]{2,1,0:T(8,128)(2,1)S(1)}, bf16[2,64,1024]{2,1,0:T(8,128)(2,1)}, u32[]{:S(2)}, u32[]{:S(2)}) collective-permute-start(bf16[2,64,1024]{2,1,0:T(8,128)(2,1)S(1)} %collective-permute-done.15.refs_2_), channel_id=1, source_target_pairs={{0,8},{8,0},{16,24},{24,16},{1,9},{9,1},{17,25},{25,17},{2,10},{10... | collective-permute-start | bytes 786440 | tf_op jit(solution)/shard_map/ppermute | solution.py:280
  65.9 0.9 copy-start.4
  72.8 12.6 %collective-permute-start.11 = (bf16[2,64,1024]{2,1,0:T(8,128)(2,1)S(1)}, bf16[2,64,1024]{2,1,0:T(8,128)(2,1)S(1)}, u32[]{:S(2)}, u32[]{:S(2)}) collective-permute-start(bf16[2,64,1024]{2,1,0:T(8,128)(2,1)S(1)} %get-tuple-element.61.refs_0_), channel_id=1, source_target_pairs={{0,8},{8,0},{16,24},{24,16},{1,9},{9,1},{17,25},{25,17},{2,10},{10... | collective-permute-start | bytes 786440 | tf_op jit(solution)/shard_map/ppermute | solution.py:280
  73.2 12.2 %collective-permute-start.13 = (bf16[2,64,1024]{2,1,0:T(8,128)(2,1)S(1)}, bf16[2,64,1024]{2,1,0:T(8,128)(2,1)S(1)}, u32[]{:S(2)}, u32[]{:S(2)}) collective-permute-start(bf16[2,64,1024]{2,1,0:T(8,128)(2,1)S(1)} %collective-permute-done.12.refs_2_), channel_id=1, source_target_pairs={{0,8},{8,0},{16,24},{24,16},{1,9},{9,1},{17,25},{25,17},{2,10},{10... | collective-permute-start | bytes 786440 | tf_op jit(solution)/shard_map/ppermute | solution.py:280
  76.2 16.9 %collective-permute-start.8 = (bf16[2,64,1024]{2,1,0:T(8,128)(2,1)S(1)}, bf16[2,64,1024]{2,1,0:T(8,128)(2,1)S(1)}, u32[]{:S(2)}, u32[]{:S(2)}) collective-permute-start(bf16[2,64,1024]{2,1,0:T(8,128)(2,1)S(1)} %get-tuple-element.60.refs_0_), channel_id=1, source_target_pairs={{0,8},{8,0},{16,24},{24,16},{1,9},{9,1},{17,25},{25,17},{2,10},{10... | collective-permute-start | bytes 786440 | tf_op jit(solution)/shard_map/ppermute | solution.py:280
  76.5 16.5 %collective-permute-start.10 = (bf16[2,64,1024]{2,1,0:T(8,128)(2,1)}, bf16[2,64,1024]{2,1,0:T(8,128)(2,1)S(1)}, u32[]{:S(2)}, u32[]{:S(2)}) collective-permute-start(bf16[2,64,1024]{2,1,0:T(8,128)(2,1)} %collective-permute-done.9.refs_2_), channel_id=1, source_target_pairs={{0,8},{8,0},{16,24},{24,16},{1,9},{9,1},{17,25},{25,17},{2,10},{10... | collective-permute-start | bytes 786440 | tf_op jit(solution)/shard_map/ppermute | solution.py:280
  101.9 8.6 %collective-permute-start.20 = (bf16[2,2,32,1024]{3,2,0,1:T(8,128)(2,1)S(1)}, bf16[2,2,32,1024]{3,2,0,1:T(8,128)(2,1)S(1)}, u32[]{:S(2)}, u32[]{:S(2)}) collective-permute-start(bf16[2,2,32,1024]{3,2,0,1:T(8,128)(2,1)S(1)} %fusion.3), channel_id=1, source_target_pairs={{0,1},{1,0},{2,3},{3,2},{4,5},{5,4},{6,7},{7,6},{8,9},{9,8},{10,11... | collective-permute-start | bytes 786440 | tf_op jit(solution)/shard_map/ppermute | solution.py:266
  103.5 8.3 %collective-permute-start.23 = (bf16[2,2,32,1024]{3,2,0,1:T(8,128)(2,1)S(1)}, bf16[2,2,32,1024]{3,2,0,1:T(8,128)(2,1)S(1)}, u32[]{:S(2)}, u32[]{:S(2)}) collective-permute-start(bf16[2,2,32,1024]{3,2,0,1:T(8,128)(2,1)S(1)} %fusion.4), channel_id=1, source_target_pairs={{0,2},{1,3},{2,0},{3,1},{4,6},{5,7},{6,4},{7,5},{8,10},{9,11},{10,... | collective-permute-start | bytes 786440 | tf_op jit(solution)/shard_map/ppermute | solution.py:266
  112.0 6.2 %collective-permute-start.21 = (bf16[2,32,1024]{2,1,0:T(8,128)(2,1)S(1)}, bf16[2,32,1024]{2,1,0:T(8,128)(2,1)S(1)}, u32[]{:S(2)}, u32[]{:S(2)}) collective-permute-start(bf16[2,32,1024]{2,1,0:T(8,128)(2,1)S(1)} %fusion.6), channel_id=1, source_target_pairs={{0,2},{1,3},{2,0},{3,1},{4,6},{5,7},{6,4},{7,5},{8,10},{9,11},{10,... | collective-permute-start | bytes 393224 | tf_op jit(solution)/shard_map/ppermute | solution.py:266
  113.6 7.3 %collective-permute-start.24 = (bf16[2,32,1024]{2,1,0:T(8,128)(2,1)S(1)}, bf16[2,32,1024]{2,1,0:T(8,128)(2,1)S(1)}, u32[]{:S(2)}, u32[]{:S(2)}) collective-permute-start(bf16[2,32,1024]{2,1,0:T(8,128)(2,1)S(1)} %fusion.7), channel_id=1, source_target_pairs={{0,1},{1,0},{2,3},{3,2},{4,5},{5,4},{6,7},{7,6},{8,9},{9,8},{10,11... | collective-permute-start | bytes 393224 | tf_op jit(solution)/shard_map/ppermute | solution.py:266
  118.3 7.2 %collective-permute-start.22 = (bf16[32,1024]{1,0:T(8,128)(2,1)S(1)}, bf16[32,1024]{1,0:T(8,128)(2,1)S(1)}, u32[]{:S(2)}, u32[]{:S(2)}) collective-permute-start(bf16[32,1024]{1,0:T(8,128)(2,1)S(1)} %fusion.10), channel_id=1, source_target_pairs={{0,4},{1,5},{2,6},{3,7},{4,0},{5,1},{6,2},{7,3},{8,12},{9,13},{10,... | collective-permute-start | bytes 196616 | tf_op jit(solution)/shard_map/ppermute | solution.py:266
  121.0 5.9 %collective-permute-start.25 = (bf16[32,1024]{1,0:T(8,128)(2,1)S(1)}, bf16[32,1024]{1,0:T(8,128)(2,1)S(1)}, u32[]{:S(2)}, u32[]{:S(2)}) collective-permute-start(bf16[32,1024]{1,0:T(8,128)(2,1)S(1)} %fusion.11), channel_id=1, source_target_pairs={{0,4},{1,5},{2,6},{3,7},{4,0},{5,1},{6,2},{7,3},{8,12},{9,13},{10,... | collective-permute-start | bytes 196616 | tf_op jit(solution)/shard_map/ppermute | solution.py:266

commit v3 on v2

v3 whole, which is shorter than its diff:
```python
import functools

import jax
import jax.numpy as jnp
from jax import lax
from jax.experimental import pallas as pl
from jax.experimental.pallas import tpu as pltpu
from jax.sharding import PartitionSpec as P

BF16 = jnp.bfloat16
F32 = jnp.float32
VMEM_BYTES = 12 * 1024 * 1024
SHARES = (2, 4, 5, 3)
SLOTS = 4
WHOLE = pl.BlockSpec(memory_space=pltpu.VMEM)
REMOTE = pl.BlockSpec(memory_space=pl.ANY)


def chunk_list(width):
    block = 256 if width % 256 == 0 else 128
    units = width // block
    total = sum(SHARES)
    edges = [0]
    run = 0
    for share in SHARES:
        run += share
        edges.append(max(min(units, round(units * run / total)), edges[-1]))
    return block, [(a, b - a) for a, b in zip(edges, edges[1:]) if b > a]


def call(kernel, name, in_specs, out_specs, out_shape, scratch, args, aliases=None):
    return pl.pallas_call(
        kernel,
        in_specs=in_specs,
        out_specs=out_specs,
        out_shape=out_shape,
        scratch_shapes=scratch,
        input_output_aliases=aliases or {},
        compiler_params=pltpu.CompilerParams(vmem_limit_bytes=VMEM_BYTES),
        cost_estimate=pl.CostEstimate(flops=1000, bytes_accessed=1000, transcendentals=0),
        name=name,
    )(*args)


def in_hbm(value):
    return pltpu.with_memory_space_constraint(value, pltpu.HBM)


def fetches(sources, columns, targets, sems):
    depth = sources[0].shape[0]
    parts = sems.shape[1]
    deep = depth // parts
    return [
        pltpu.make_async_copy(
            source.at[pl.ds(p * deep, deep), columns],
            target.at[pl.ds(p * deep, deep)],
            sems.at[k, p],
        )
        for p in range(parts)
        for k, (source, target) in enumerate(zip(sources, targets))
    ]


def forward_kernel(layout, ins, outs, *refs):
    quarters, rows, block, own_at, next_at = layout
    given, made, (total, own_sems, next_sems) = refs[:ins], refs[ins : ins + outs], refs[ins + outs :]
    x_ref, gate_ref, up_ref = given[:3]
    own_ref, far_ref, send_ref, *made = made
    start = []
    if own_at is None:
        weights = given[3:5]
    else:
        start = fetches((gate_ref, up_ref), own_at, made[1:3], own_sems)
        start.append(pltpu.make_async_copy(x_ref, made[0], next_sems.at[2, 0]))
        for copy in start:
            copy.start()
        x_ref, weights, made = made[0], made[1:3], made[3:]
    later = []
    if next_at is not None:
        later = fetches((gate_ref, up_ref), next_at, made, next_sems.at[:2])
    for copy in start:
        copy.wait()
    for copy in later:
        copy.start()
    outer = quarters // 2
    me = lax.axis_index("row")
    place, core = me // 2, me % 2
    x = x_ref[...]
    for j in range(weights[0].shape[1] // block):
        at = slice(j * block, (j + 1) * block)
        for k in range(2):
            total[k] = jnp.dot(x, weights[k][:, at], preferred_element_type=F32)
        for step in range(outer):
            there = (place + step) % outer * 2
            mine = pl.multiple_of((there + core) * rows, rows)
            other = pl.multiple_of((there + 1 - core) * rows, rows)
            for k in range(2):
                kept = total[k, pl.ds(mine, rows), :]
                if step == 0:
                    own_ref[k, :, at] = kept
                else:
                    far_ref[step - 1, k, :, at] = kept
                send_ref[step, k, :, at] = total[k, pl.ds(other, rows), :].astype(BF16)
    for copy in later:
        copy.wait()


def forward_part(quarters, block, chunk, following, x, gate_weight, up_weight, held, after):
    tokens, depth = x.shape
    rows = tokens // quarters
    outer = quarters // 2
    width = chunk[1] * block
    own_at = None if held else pl.ds(chunk[0] * block, width)
    next_at = None
    out_shape = [
        jax.ShapeDtypeStruct((2, rows, width), F32),
        jax.ShapeDtypeStruct((outer - 1, 2, rows, width), F32),
        jax.ShapeDtypeStruct((outer, 2, rows, width), BF16),
    ]
    if not held:
        x = pltpu.with_memory_space_constraint(x, pltpu.HBM)
        out_shape += [pltpu.VMEM(x.shape, BF16)] + [pltpu.VMEM((depth, width), BF16)] * 2
    if following is not None:
        next_at = pl.ds(following[0] * block, following[1] * block)
        out_shape += [pltpu.VMEM((depth, following[1] * block), BF16)] * 2
    args = (x, in_hbm(gate_weight), in_hbm(up_weight), *held, *after)
    parts = 4 if depth % 512 == 0 else 2
    own, far, send, *loaded = call(
        functools.partial(
            forward_kernel,
            (quarters, rows, block, own_at, next_at),
            len(args),
            len(out_shape),
        ),
        "forward_part",
        [WHOLE if held else REMOTE, REMOTE, REMOTE] + [WHOLE] * len(held) + [REMOTE] * len(after),
        [WHOLE] * len(out_shape),
        out_shape,
        [
            pltpu.VMEM((2, tokens, block), F32),
            pltpu.SemaphoreType.DMA((2, parts)),
            pltpu.SemaphoreType.DMA((3, parts)),
        ],
        args,
    )
    return own, far, send, loaded


def middle_kernel(outer, at, first, own_ref, got_ref, upstream_ref, *refs):
    far_refs, rest = refs[: outer - 1], refs[outer - 1 :]
    if not first:
        rest[1][...] = rest[0][...]
        rest = rest[1:]
    hidden_ref, grads_ref = rest
    gate_pre = own_ref[0] + got_ref[0, 0].astype(F32)
    up_pre = own_ref[1] + got_ref[0, 1].astype(F32)
    for far in far_refs:
        gate_pre += far[0].astype(F32)
        up_pre += far[1].astype(F32)
    sigma_gate = jax.nn.sigmoid(gate_pre)
    upstream = upstream_ref[:, at].astype(F32)
    gated = gate_pre * sigma_gate
    hidden_ref[:, at] = (gated * up_pre).astype(BF16)
    slope = sigma_gate * (1.0 + gate_pre * (1.0 - sigma_gate))
    grads_ref[0] = (upstream * up_pre * slope).astype(BF16)
    grads_ref[1] = (upstream * gated).astype(BF16)


def middle_part(outer, at, own, got, far, hidden_grad, hidden):
    rows, width = own.shape[1:]
    first = hidden is None
    args = [own, got, hidden_grad, *far] + ([] if first else [hidden])
    return call(
        functools.partial(middle_kernel, outer, at, first),
        "middle_part",
        [WHOLE] * len(args),
        [WHOLE] * 2,
        [
            jax.ShapeDtypeStruct(hidden_grad.shape, BF16),
            jax.ShapeDtypeStruct((2, rows, width), BF16),
        ],
        [],
        args,
    )


def input_kernel(quarters, rows, first, last, gate_ref, up_ref, *refs):
    pieces, rest = refs[:quarters], refs[quarters:]
    earlier = []
    if not first:
        count = 2 if last else 1
        earlier, rest = rest[:count], rest[count:]
    *sums, grads = rest
    outer = quarters // 2
    me = lax.axis_index("row")
    place, core = me // 2, me % 2
    for j, piece in enumerate(pieces):
        step, swap = j // 2, j % 2
        there = (place + outer - step) % outer * 2
        at = pl.multiple_of((there + (core + swap) % 2) * rows, rows)
        for k in range(2):
            grads[k, pl.ds(at, rows), :] = piece[k]
    weights = (gate_ref, up_ref)
    deep = 256 if gate_ref.shape[0] % 512 == 0 else 128
    if last:
        dims = (((1,), (1,)), ((), ()))
        half = sums[0].shape[1]
        for d in range(gate_ref.shape[0] // deep):
            index, at = d * deep // half, slice(d * deep % half, d * deep % half + deep)
            term = None if first else earlier[index][:, at]
            for k in range(2):
                piece = weights[k][d * deep : (d + 1) * deep, :]
                product = lax.dot_general(grads[k], piece, dims, preferred_element_type=F32)
                term = product if term is None else term + product
            sums[index][:, at] = term
        return
    flipped = [grads[k].T for k in range(2)]
    for d in range(gate_ref.shape[0] // deep):
        at = slice(d * deep, (d + 1) * deep)
        term = None if first else earlier[0][at, :]
        for k in range(2):
            product = jnp.dot(weights[k][at, :], flipped[k], preferred_element_type=F32)
            term = product if term is None else term + product
        if len(sums) == 1:
            sums[0][at, :] = term
        else:
            half = sums[0].shape[1]
            sums[d * deep // half][:, d * deep % half : d * deep % half + deep] = term.T


def input_part(quarters, held, pieces, acc, final):
    depth, width = held[0].shape
    rows = pieces[0].shape[1]
    tokens = rows * quarters
    first, last = acc is None, final == 0
    args = [*held, *pieces] + ([] if first else acc)
    sums = [jax.ShapeDtypeStruct((depth, tokens), F32)]
    if final <= 1:
        sums = [jax.ShapeDtypeStruct((tokens, depth // 2), F32)] * 2
    *acc, grads = call(
        functools.partial(input_kernel, quarters, rows, first, last),
        "input_part",
        [WHOLE] * len(args),
        [WHOLE] * (len(sums) + 1),
        sums + [jax.ShapeDtypeStruct((2, tokens, width), BF16)],
        [],
        args,
    )
    return acc, grads


def weight_kernel(block, start, count, skipped, xt_ref, grads_ref, *refs):
    gate_out, up_out, products, sems = refs[skipped:]
    xt = xt_ref[...]
    slots = products.shape[0]
    copies = []
    for j in range(count):
        for k, out in enumerate((gate_out, up_out)):
            piece = grads_ref[k, :, j * block : (j + 1) * block]
            slot = len(copies) % slots
            if len(copies) >= slots:
                copies[-slots].wait()
            products[slot] = jnp.dot(xt, piece, preferred_element_type=F32).astype(BF16)
            copy = pltpu.make_async_copy(
                products.at[slot], out.at[:, pl.ds((start + j) * block, block)], sems.at[slot]
            )
            copy.start()
            copies.append(copy)
    for copy in copies[-slots:]:
        copy.wait()


def weight_part(block, start, count, full, xt, grads, state, after):
    depth, tokens = xt.shape
    args = [xt, grads, *after, *[in_hbm(value) for value in state]]
    first = 2 + len(after)
    aliases = {first + k: k for k in range(len(state))}
    return call(
        functools.partial(weight_kernel, block, start, count, len(args) - 2),
        "weight_part",
        [WHOLE] * 2 + [REMOTE] * (len(args) - 2),
        [REMOTE] * 2,
        [pltpu.HBM((depth, full), BF16)] * 2,
        [pltpu.VMEM((SLOTS, depth, block), BF16), pltpu.SemaphoreType.DMA((SLOTS,))],
        args,
        aliases,
    )


def token_sums(halves, columns, orders):
    position = lax.axis_index("col")
    bits = len(orders[0])
    rows = halves[0].shape[0] // columns
    halves = [half.reshape((2,) * bits + (rows, half.shape[1])) for half in halves]
    lefts = [list(reversed(range(bits))) for _ in halves]
    stages = []
    for stage in range(bits):
        kept, got = [], []
        for half, left, order in zip(halves, lefts, orders):
            bit = order[stage]
            axis = left.index(bit)
            left.remove(bit)
            mine = (position // 2**bit) % 2
            send = lax.dynamic_index_in_dim(half, 1 - mine, axis, keepdims=False)
            moves = [(c, c ^ 2**bit) for c in range(columns)]
            got.append(lax.ppermute(send.astype(BF16), "col", moves))
            kept.append(lax.dynamic_index_in_dim(half, mine, axis, keepdims=False))
        halves = [keep + far.astype(F32) for keep, far in zip(kept, got)]
        stages.append(halves)
    return stages


def local(quarters, columns, inputs, gate_weight, up_weight, hidden_grad):
    outer = quarters // 2
    full = gate_weight.shape[1]
    block, chunks = chunk_list(full)
    swap = [(r, r ^ 1) for r in range(quarters)]

    def sibling(value):
        return lax.ppermute(value, "row", swap)

    def across(value, step):
        moves = [(r, (r // 2 + step) % outer * 2 + r % 2) for r in range(quarters)]
        return lax.ppermute(value, "row", moves)

    owns, gots, sums, weights = [], [], [], []
    x = inputs
    for i, chunk in enumerate(chunks):
        after = sums[i - 2][:1] if i >= 2 else []
        following = chunks[i + 1] if i + 1 < len(chunks) else None
        held = weights[i] if i else []
        own, far, send, loaded = forward_part(
            quarters, block, chunk, following, x, gate_weight, up_weight, held, after
        )
        if i == 0:
            x, loaded = loaded[0], loaded[1:]
        while loaded:
            weights.append(loaded[:2])
            loaded = loaded[2:]
        got = sibling(send)
        owns.append(own)
        gots.append(got)
        sums.append(
            [(far[step - 1] + got[step].astype(F32)).astype(BF16) for step in range(1, outer)]
        )

    xt = x.T
    hidden = None
    pieces = []
    for (start, count), own, got, near in zip(chunks, owns, gots, sums):
        far = [across(value, step + 1) for step, value in enumerate(near)]
        at = slice(start * block, (start + count) * block)
        hidden, mine = middle_part(outer, at, own, got, far, hidden_grad, hidden)
        group = [mine, sibling(mine)]
        for step in range(1, outer):
            there = across(mine, step)
            group += [there, sibling(there)]
        pieces.append(group)

    acc = None
    grads = []
    for i, (held, group) in enumerate(zip(weights, pieces)):
        acc, whole = input_part(quarters, held, group, acc, len(chunks) - 1 - i)
        grads.append(whole)
    bits = columns.bit_length() - 1
    order = list(range(bits))
    stages = [acc] + token_sums(acc, columns, [order, order[1::-1] + order[2:]])
    input_grad = jnp.concatenate([half.astype(BF16) for half in stages[-1]], axis=1)
    state = []
    for i, ((start, count), whole) in enumerate(zip(chunks, grads)):
        after = stages[min(i, bits) - 1] if i else []
        state = weight_part(block, start, count, full, xt, whole, state, after)
    return hidden, input_grad, state[0], state[1]


def solution(mesh):
    return jax.shard_map(
        functools.partial(local, mesh.shape["row"], mesh.shape["col"]),
        mesh=mesh,
        in_specs=(P(None, "row"), P("row", "col"), P("row", "col"), P("row", "col")),
        out_specs=(P("row", "col"), P("col", "row"), P("row", "col"), P("row", "col")),
        check_vma=False,
    )
```

time: 128 us -> 129 us (level)
  Pallas kernels: 72.5 us -> 54.1 us
  local copies, waits for them, and re-layouts: 3.73 us -> 19.9 us
  waiting for transfers between devices: 26.3 us -> 30.5 us
  starting transfers between devices: 22.9 us -> 21.2 us
    pallas_call x16, Pallas kernels: 72.5 us -> 54.1 us  [call(): pl.pallas_call(kernel, in_specs=in_specs, out_specs=out_specs, out_shape=...]
    unnamed x11 -> x74, local copies, waits for them, and re-layouts: 3.49 us -> 18.5 us
    ppermute x8, waiting for transfers between devices: 22.4 us -> 29.2 us  [across(): return lax.ppermute(value, 'row', moves)]
    ppermute x6, waiting for transfers between devices: 3.85 us -> 1.23 us  [token_sums(): got.append(lax.ppermute(send.astype(BF16), 'col', moves))]
  transfers between devices with their start and end apart: 26 -> 26, of which waited for: 7 -> 5; matrix products, arithmetic and copies ran while one was open for 1% -> 1% of each run, Pallas kernels for 47% -> 34%
where the time goes in v3:
time: 129 us; the launch traced here: 128 us
  Pallas kernels  54.1 us (42%)
  waiting for transfers between devices  30.5 us (24%)
  starting transfers between devices  21.2 us (16%)
  local copies, waits for them, and re-layouts  19.9 us (15%)
  between operations  1.3 us (1%)
    pallas_call x16, Pallas kernels, call(): pl.pallas_call(kernel, in_specs=in_specs, out_specs=out_specs, out_shape=...  54.1 us
    ppermute x8, waiting for transfers between devices, across(): return lax.ppermute(value, 'row', moves)  29.2 us
    unnamed x74, local copies, waits for them, and re-layouts  18.5 us
    ppermute x8, starting transfers between devices, across(): return lax.ppermute(value, 'row', moves)  10.5 us
    ppermute x6, starting transfers between devices, token_sums(): got.append(lax.ppermute(send.astype(BF16), 'col', moves))  7.3 us
    ppermute x12, starting transfers between devices, sibling(): return lax.ppermute(value, 'row', swap)  3.44 us
  transfers between devices with their start and end apart: 26, of which 5 were waited for; matrix products, arithmetic and copies ran while one was open for 1% of the time, Pallas kernels for 34%

profile of v3, /device:TPU:0, one launch (start us, length us, event | category | flops | bytes accessed | tf_op | source)
XLA Modules:
  0.0 128.1 jit_solution(6866250547780209699)
XLA Ops:
  0.6 7.0 %forward_part.4 = (f32[2,64,512]{2,1,0:T(8,128)S(1)}, f32[1,2,64,512]{3,2,1,0:T(8,128)S(1)}, bf16[2,2,64,512]{3,2,1,0:T(8,128)(2,1)S(1)}, bf16[256,2048]{1,0:T(8...) custom-call(bf16[256,2048]{1,0:T(8,128)(2,1)} %refs_0_.1, ...), custom_call_target="tpu_custom_call" | custom-call | flops 1000 | bytes 1000 | tf_op jit(solution)/shard_map/forward_part/pallas_call | solution.py:32
  8.2 8.0 %forward_part.5 = (f32[2,64,1024]{2,1,0:T(8,128)S(1)}, f32[1,2,64,1024]{3,2,1,0:T(8,128)S(1)}, bf16[2,2,64,1024]{3,2,1,0:T(8,128)(2,1)S(1)}, bf16[2048,1280]{1,0:T(8,128)(2,1)S(1)}, bf16[2048,1280]{1,0:T(8,128)(2,1)S(1)}) custom-call(bf16[256,2048]{1,0:T(8,128)(2,1)S(1)} %get-tuple-element.51.refs_0_, bf16[2048,3584]{1,0:T(8,128)(2,1)} %refs_1_.7, ...), custom_call_target="tpu_custom_call" | custom-call | flops 1000 | bytes 1000 | tf_op jit(solution)/shard_map/forward_part/pallas_call | solution.py:32
  16.8 5.9 %forward_part.6 = (f32[2,64,1280]{2,1,0:T(8,128)S(1)}, f32[1,2,64,1280]{3,2,1,0:T(8,128)S(1)}, bf16[2,2,64,1280]{3,2,1,0:T(8,128)(2,1)S(1)}, bf16[2048,768]{1,0:T(8,128)(2,1)S(1)}, bf16[2048,768]{1,0:T(8,128)(2,1)S(1)}) custom-call(bf16[256,2048]{1,0:T(8,128)(2,1)S(1)} %get-tuple-element.51.refs_0_, bf16[2048,3584]{1,0:T(8,128)(2,1)} %refs_1_.7, ...), custom_call_target="tpu_custom_call" | custom-call | flops 1000 | bytes 1000 | tf_op jit(solution)/shard_map/forward_part/pallas_call | solution.py:32
  23.4 2.6 %collective-permute-start.7 = (bf16[2,64,512]{2,1,0:T(8,128)(2,1)S(1)}, bf16[2,64,512]{2,1,0:T(8,128)(2,1)S(1)}, u32[]{:S(2)}, u32[]{:S(2)}) collective-permute-start(bf16[2,64,512]{2,1,0:T(8,128)(2,1)S(1)} %fusion.5.refs_5_), channel_id=1, source_target_pairs={{0,16},{8,24},{16,0},{24,8},{1,17},{9,25},{17,1},{25,9},{2,18},{10... | collective-permute-start | bytes 393224 | tf_op jit(solution)/shard_map/ppermute | solution.py:324
  26.1 2.0 %forward_part.7 = (f32[2,64,768]{2,1,0:T(8,128)S(1)}, f32[1,2,64,768]{3,2,1,0:T(8,128)S(1)}, bf16[2,2,64,768]{3,2,1,0:T(8,128)(2,1)S(1)}) custom-call(bf16[256,2048]{1,0:T(8,128)(2,1)S(1)} %get-tuple-element.51.refs_0_, bf16[2048,3584]{1,0:T(8,128)(2,1)} %refs_1_.7, bf16[2048,3584]{1,0:T(8,128)(2,1)} %refs_2_.7, ...), custom_call_target="tpu_custom_call" | custom-call | flops 1000 | bytes 1000 | tf_op jit(solution)/shard_map/forward_part/pallas_call | solution.py:32
  28.4 1.9 %collective-permute-start.5 = (bf16[2,64,1280]{2,1,0:T(8,128)(2,1)S(1)}, bf16[2,64,1280]{2,1,0:T(8,128)(2,1)S(1)}, u32[]{:S(2)}, u32[]{:S(2)}) collective-permute-start(bf16[2,64,1280]{2,1,0:T(8,128)(2,1)S(1)} %fusion), channel_id=1, source_target_pairs={{0,16},{8,24},{16,0},{24,8},{1,17},{9,25},{17,1},{25,9},{2,18},{10... | collective-permute-start | bytes 983048 | tf_op jit(solution)/shard_map/ppermute | solution.py:324
  30.5 5.4 %collective-permute-done.6.refs_0_ = bf16[2,64,1024]{2,1,0:T(8,128)(2,1)S(1)} collective-permute-done((bf16[2,64,1024]{2,1,0:T(8,128)(2,1)S(1)}, bf16[2,64,1024]{2,1,0:T(8,128)(2,1)S(1)}, u32[]{:S(2)}, u32[]{:S(2)}) %collective-permute-start.6) | collective-permute-done | bytes 262176 | tf_op jit(solution)/shard_map/ppermute | solution.py:324
  36.2 6.5 %collective-permute-done.5.refs_0_ = bf16[2,64,1280]{2,1,0:T(8,128)(2,1)S(1)} collective-permute-done((bf16[2,64,1280]{2,1,0:T(8,128)(2,1)S(1)}, bf16[2,64,1280]{2,1,0:T(8,128)(2,1)S(1)}, u32[]{:S(2)}, u32[]{:S(2)}) %collective-permute-start.5) | collective-permute-done | bytes 327712 | tf_op jit(solution)/shard_map/ppermute | solution.py:324
  43.0 1.8 %collective-permute-start.12 = (bf16[2,64,1280]{2,1,0:T(8,128)(2,1)S(1)}, bf16[2,64,1280]{2,1,0:T(8,128)(2,1)S(1)}, u32[]{:S(2)}, u32[]{:S(2)}) collective-permute-start(bf16[2,64,1280]{2,1,0:T(8,128)(2,1)S(1)} %get-tuple-element.75.refs_0_), channel_id=1, source_target_pairs={{0,16},{8,24},{16,0},{24,8},{1,17},{9,25},{17,1},{25,9},{2,18},{10... | collective-permute-start | bytes 983048 | tf_op jit(solution)/shard_map/ppermute | solution.py:324
  45.1 1.8 %collective-permute-start.18 = (bf16[2,64,512]{2,1,0:T(8,128)(2,1)S(1)}, bf16[2,64,512]{2,1,0:T(8,128)(2,1)S(1)}, u32[]{:S(2)}, u32[]{:S(2)}) collective-permute-start(bf16[2,64,512]{2,1,0:T(8,128)(2,1)S(1)} %get-tuple-element.79.refs_0_), channel_id=1, source_target_pairs={{0,16},{8,24},{16,0},{24,8},{1,17},{9,25},{17,1},{25,9},{2,18},{10... | collective-permute-start | bytes 393224 | tf_op jit(solution)/shard_map/ppermute | solution.py:324
  47.1 13.6 %collective-permute-done.18.refs_2_ = bf16[2,64,512]{2,1,0:T(8,128)(2,1)S(1)} collective-permute-done((bf16[2,64,512]{2,1,0:T(8,128)(2,1)S(1)}, bf16[2,64,512]{2,1,0:T(8,128)(2,1)S(1)}, u32[]{:S(2)}, u32[]{:S(2)}) %collective-permute-start.18) | collective-permute-done | bytes 131104 | tf_op jit(solution)/shard_map/ppermute | solution.py:324
  62.7 1.8 %collective-permute-start.9 = (bf16[2,64,768]{2,1,0:T(8,128)(2,1)}, bf16[2,64,768]{2,1,0:T(8,128)(2,1)}, u32[]{:S(2)}, u32[]{:S(2)}) collective-permute-start(bf16[2,64,768]{2,1,0:T(8,128)(2,1)} %get-tuple-element.74.refs_0_), channel_id=1, source_target_pairs={{0,16},{8,24},{16,0},{24,8},{1,17},{9,25},{17,1},{25,9},{2,18},{10... | collective-permute-start | bytes 589832 | tf_op jit(solution)/shard_map/ppermute | solution.py:324
  66.2 3.7 %collective-permute-done.9.refs_2_ = bf16[2,64,768]{2,1,0:T(8,128)(2,1)} collective-permute-done((bf16[2,64,768]{2,1,0:T(8,128)(2,1)}, bf16[2,64,768]{2,1,0:T(8,128)(2,1)}, u32[]{:S(2)}, u32[]{:S(2)}) %collective-permute-start.9) | collective-permute-done | bytes 196640 | tf_op jit(solution)/shard_map/ppermute | solution.py:324
  70.0 1.7 %copy-done.14 = bf16[2048,512]{1,0:T(8,128)(2,1)S(1)} copy-done((bf16[2048,512]{1,0:T(8,128)(2,1)S(1)}, bf16[2048,512]{1,0:T(8,128)(2,1)}, u32[]{:S(2)}) %copy-start.14) | copy-done | bytes 2097176
  71.7 1.7 %copy-done.16 = bf16[2048,512]{1,0:T(8,128)(2,1)S(1)} copy-done((bf16[2048,512]{1,0:T(8,128)(2,1)S(1)}, bf16[2048,512]{1,0:T(8,128)(2,1)}, u32[]{:S(2)}) %copy-start.16) | copy-done | bytes 2097176
  77.1 1.3 %input_part.4 = (f32[2048,256]{1,0:T(8,128)S(1)}, bf16[2,256,512]{2,1,0:T(8,128)(2,1)S(1)}) custom-call(bf16[2048,512]{1,0:T(8,128)(2,1)S(1)} %copy-done.14, bf16[2048,512]{1,0:T(8,128)(2,1)S(1)} %copy-done.16, bf16[2,64,512]{2,1,0:T(8,128)(2,1)S(1)} %copy-done.26, bf16[2,64,512]{2,1,0:T(8,128)(2,1)S(1)} %copy-done.30, bf16[2,64,512]{2,1,0:T(8,128)(2,1)S(1)} %copy-done.28, ...), custom_call_target="tpu_custom_call" | custom-call | flops 1000 | bytes 1000 | tf_op jit(solution)/shard_map/input_part/pallas_call | solution.py:32
  79.3 2.6 %copy-done.5 = bf16[2048,1024]{1,0:T(8,128)(2,1)S(1)} copy-done((bf16[2048,1024]{1,0:T(8,128)(2,1)S(1)}, bf16[2048,1024]{1,0:T(8,128)(2,1)}, u32[]{:S(2)}) %copy-start.5) | copy-done | bytes 4194328
  81.9 2.4 %input_part.5 = (f32[2048,256]{1,0:T(8,128)S(1)}, bf16[2,256,1024]{2,1,0:T(8,128)(2,1)S(1)}) custom-call(bf16[2048,1024]{1,0:T(8,128)(2,1)S(1)} %copy-done.3, bf16[2048,1024]{1,0:T(8,128)(2,1)S(1)} %copy-done.5, bf16[2,64,1024]{2,1,0:T(8,128)(2,1)S(1)} %get-tuple-element.76.refs_0_, bf16[2,64,1024]{2,1,0:T(8,128)(2,1)S(1)} %collective-permute-done.14.refs_1_, ...), custom_call_target="tpu_custom_call" | custom-call | flops 1000 | bytes 1000 | tf_op jit(solution)/shard_map/input_part/pallas_call | solution.py:32
  84.4 1.0 copy-done.19
  85.4 3.3 %input_part.6 = (f32[256,1024]{1,0:T(8,128)S(1)}, f32[256,1024]{1,0:T(8,128)S(1)}, bf16[2,256,1280]{2,1,0:T(8,128)(2,1)S(1)}) custom-call(bf16[2048,1280]{1,0:T(8,128)(2,1)S(1)} %bitcast.44, bf16[2048,1280]{1,0:T(8,128)(2,1)S(1)} %bitcast.46, bf16[2,64,1280]{2,1,0:T(8,128)(2,1)S(1)} %get-tuple-element.75.refs_0_, ...), custom_call_target="tpu_custom_call" | custom-call | flops 1000 | bytes 1000 | tf_op jit(solution)/shard_map/input_part/pallas_call | solution.py:32
  88.8 3.5 %input_part.7 = (f32[256,1024]{1,0:T(8,128)S(1)}, f32[256,1024]{1,0:T(8,128)S(1)}, bf16[2,256,768]{2,1,0:T(8,128)(2,1)S(1)}) custom-call(bf16[2048,768]{1,0:T(8,128)(2,1)S(1)} %copy-done.7, bf16[2048,768]{1,0:T(8,128)(2,1)S(1)} %copy-done.9, bf16[2,64,768]{2,1,0:T(8,128)(2,1)} %get-tuple-element.74.refs_0_, ...), custom_call_target="tpu_custom_call" | custom-call | flops 1000 | bytes 1000 | tf_op jit(solution)/shard_map/input_part/pallas_call | solution.py:32
  95.0 1.8 %collective-permute-start.20 = (bf16[2,2,32,1024]{3,2,0,1:T(8,128)(2,1)}, bf16[2,2,32,1024]{3,2,0,1:T(8,128)(2,1)S(1)}, u32[]{:S(2)}, u32[]{:S(2)}) collective-permute-start(bf16[2,2,32,1024]{3,2,0,1:T(8,128)(2,1)} %fusion.2), channel_id=1, source_target_pairs={{0,1},{1,0},{2,3},{3,2},{4,5},{5,4},{6,7},{7,6},{8,9},{9,8},{10,11... | collective-permute-start | bytes 786440 | tf_op jit(solution)/shard_map/ppermute | solution.py:306
  97.4 1.0 copy-done.24
  98.4 2.7 %weight_part.4 = (bf16[2048,3584]{1,0:T(8,128)(2,1)}, bf16[2048,3584]{1,0:T(8,128)(2,1)}) custom-call(bf16[2048,256]{1,0:T(8,128)(2,1)S(1)} %bitcast.39, bf16[2,256,512]{2,1,0:T(8,128)(2,1)S(1)} %copy-done.24), custom_call_target="tpu_custom_call" | custom-call | flops 1000 | bytes 1000 | tf_op jit(solution)/shard_map/weight_part/pallas_call | solution.py:32
  101.2 1.6 %collective-permute-start.23 = (bf16[2,2,32,1024]{3,2,0,1:T(8,128)(2,1)S(1)}, bf16[2,2,32,1024]{3,2,0,1:T(8,128)(2,1)S(1)}, u32[]{:S(2)}, u32[]{:S(2)}) collective-permute-start(bf16[2,2,32,1024]{3,2,0,1:T(8,128)(2,1)S(1)} %fusion.3), channel_id=1, source_target_pairs={{0,2},{1,3},{2,0},{3,1},{4,6},{5,7},{6,4},{7,5},{8,10},{9,11},{10,... | collective-permute-start | bytes 786440 | tf_op jit(solution)/shard_map/ppermute | solution.py:306
  102.8 1.2 copy-done.12
  104.1 1.2 copy-done.20
  105.3 5.5 %weight_part.5 = (bf16[2048,3584]{1,0:T(8,128)(2,1)}, bf16[2048,3584]{1,0:T(8,128)(2,1)}) custom-call(bf16[2048,256]{1,0:T(8,128)(2,1)S(1)} %bitcast.40, bf16[2,256,1024]{2,1,0:T(8,128)(2,1)S(1)} %copy-done.20, f32[256,1024]{1,0:T(8,128)S(1)} %copy-done.12, f32[256,1024]{1,0:T(8,128)S(1)} %get-tuple-element.85.refs_1_, ...), custom_call_target="tpu_custom_call", output_to_operand_aliasing={{0}: (4, {}), {1}: (5, {})} | custom-call | flops 1000 | bytes 1000 | tf_op jit(solution)/shard_map/weight_part/pallas_call | solution.py:32
  112.1 6.8 %weight_part.6 = (bf16[2048,3584]{1,0:T(8,128)(2,1)}, bf16[2048,3584]{1,0:T(8,128)(2,1)}) custom-call(bf16[2048,256]{1,0:T(8,128)(2,1)S(1)} %bitcast.41, bf16[2,256,1280]{2,1,0:T(8,128)(2,1)S(1)} %copy-done.18, f32[2,2,32,1024]{3,2,1,0:T(8,128)S(1)} %copy.22.refs_0_, ...), custom_call_target="tpu_custom_call", output_to_operand_aliasing={{0}: (4, {}), {1}: (5, {})} | custom-call | flops 1000 | bytes 1000 | tf_op jit(solution)/shard_map/weight_part/pallas_call | solution.py:32
  119.0 2.7 %collective-permute-start.22 = (bf16[32,1024]{1,0:T(8,128)(2,1)S(1)}, bf16[32,1024]{1,0:T(8,128)(2,1)S(1)}, u32[]{:S(2)}, u32[]{:S(2)}) collective-permute-start(bf16[32,1024]{1,0:T(8,128)(2,1)S(1)} %fusion.10), channel_id=1, source_target_pairs={{0,4},{1,5},{2,6},{3,7},{4,0},{5,1},{6,2},{7,3},{8,12},{9,13},{10,... | collective-permute-start | bytes 196616 | tf_op jit(solution)/shard_map/ppermute | solution.py:306
  122.1 4.1 %weight_part.7 = (bf16[2048,3584]{1,0:T(8,128)(2,1)}, bf16[2048,3584]{1,0:T(8,128)(2,1)}) custom-call(bf16[2048,256]{1,0:T(8,128)(2,1)S(1)} %bitcast.42, bf16[2,256,768]{2,1,0:T(8,128)(2,1)S(1)} %copy-done.22, f32[2,32,1024]{2,1,0:T(8,128)S(1)} %bitcast_add_fusion.3.refs_0_, ...), custom_call_target="tpu_custom_call", output_to_operand_aliasing={{0}: (4, {}), {1}: (5, {})} | custom-call | flops 1000 | bytes 1000 | tf_op jit(solution)/shard_map/weight_part/pallas_call | solution.py:32
  126.2 1.2 collective-permute-done.25
  (132 shorter events, 17.2 us)
Async XLA Ops:
  7.6 8.5 %copy-start.2 = (bf16[2048,1024]{1,0:T(8,128)(2,1)}, bf16[2048,1024]{1,0:T(8,128)(2,1)S(1)}, u32[]{:S(2)}) copy-start(bf16[2048,1024]{1,0:T(8,128)(2,1)S(1)} %get-tuple-element.52.refs_3_.gate_ref) | copy-start | bytes 12582916
  7.6 8.5 %copy-start.4 = (bf16[2048,1024]{1,0:T(8,128)(2,1)}, bf16[2048,1024]{1,0:T(8,128)(2,1)S(1)}, u32[]{:S(2)}) copy-start(bf16[2048,1024]{1,0:T(8,128)(2,1)S(1)} %get-tuple-element.53.refs_4_.up_ref) | copy-start | bytes 12582916
  7.6 8.5 %copy-start.13 = (bf16[2048,512]{1,0:T(8,128)(2,1)}, bf16[2048,512]{1,0:T(8,128)(2,1)S(1)}, u32[]{:S(2)}) copy-start(bf16[2048,512]{1,0:T(8,128)(2,1)S(1)} %get-tuple-element.77.gate_ref) | copy-start | bytes 6291460
  7.6 9.1 %collective-permute-start = (bf16[2,2,64,512]{3,2,1,0:T(8,128)(2,1)S(1)}, bf16[2,2,64,512]{3,2,1,0:T(8,128)(2,1)S(1)}, u32[]{:S(2)}, u32[]{:S(2)}) collective-permute-start(bf16[2,2,64,512]{3,2,1,0:T(8,128)(2,1)S(1)} %get-tuple-element.57), channel_id=1, source_target_pairs={{0,8},{8,0},{16,24},{24,16},{1,9},{9,1},{17,25},{25,17},{2,10},{10... | collective-permute-start | bytes 786440 | tf_op jit(solution)/shard_map/ppermute | solution.py:320
  16.2 9.8 %collective-permute-start.1 = (bf16[2,2,64,1024]{3,2,1,0:T(8,128)(2,1)S(1)}, bf16[2,2,64,1024]{3,2,1,0:T(8,128)(2,1)S(1)}, u32[]{:S(2)}, u32[]{:S(2)}) collective-permute-start(bf16[2,2,64,1024]{3,2,1,0:T(8,128)(2,1)S(1)} %get-tuple-element.61), channel_id=1, source_target_pairs={{0,8},{8,0},{16,24},{24,16},{1,9},{9,1},{17,25},{25,17},{2,10},{10... | collective-permute-start | bytes 1572872 | tf_op jit(solution)/shard_map/ppermute | solution.py:320
  22.8 5.6 %collective-permute-start.4 = (bf16[2,2,64,1280]{3,2,1,0:T(8,128)(2,1)S(1)}, bf16[2,2,64,1280]{3,2,1,0:T(8,128)(2,1)S(1)}, u32[]{:S(2)}, u32[]{:S(2)}) collective-permute-start(bf16[2,2,64,1280]{3,2,1,0:T(8,128)(2,1)S(1)} %get-tuple-element.66), channel_id=1, source_target_pairs={{0,8},{8,0},{16,24},{24,16},{1,9},{9,1},{17,25},{25,17},{2,10},{10... | collective-permute-start | bytes 1966088 | tf_op jit(solution)/shard_map/ppermute | solution.py:320
  23.4 7.0 %collective-permute-start.7 = (bf16[2,64,512]{2,1,0:T(8,128)(2,1)S(1)}, bf16[2,64,512]{2,1,0:T(8,128)(2,1)S(1)}, u32[]{:S(2)}, u32[]{:S(2)}) collective-permute-start(bf16[2,64,512]{2,1,0:T(8,128)(2,1)S(1)} %fusion.5.refs_5_), channel_id=1, source_target_pairs={{0,16},{8,24},{16,0},{24,8},{1,17},{9,25},{17,1},{25,9},{2,18},{10... | collective-permute-start | bytes 393224 | tf_op jit(solution)/shard_map/ppermute | solution.py:324
  26.0 9.9 %collective-permute-start.6 = (bf16[2,64,1024]{2,1,0:T(8,128)(2,1)S(1)}, bf16[2,64,1024]{2,1,0:T(8,128)(2,1)S(1)}, u32[]{:S(2)}, u32[]{:S(2)}) collective-permute-start(bf16[2,64,1024]{2,1,0:T(8,128)(2,1)S(1)} %fusion.1.refs_5_), channel_id=1, source_target_pairs={{0,16},{8,24},{16,0},{24,8},{1,17},{9,25},{17,1},{25,9},{2,18},{10... | collective-permute-start | bytes 786440 | tf_op jit(solution)/shard_map/ppermute | solution.py:324
  28.1 8.0 %collective-permute-start.2 = (bf16[2,2,64,768]{3,2,1,0:T(8,128)(2,1)S(1)}, bf16[2,2,64,768]{3,2,1,0:T(8,128)(2,1)S(1)}, u32[]{:S(2)}, u32[]{:S(2)}) collective-permute-start(bf16[2,2,64,768]{3,2,1,0:T(8,128)(2,1)S(1)} %get-tuple-element.63), channel_id=1, source_target_pairs={{0,8},{8,0},{16,24},{24,16},{1,9},{9,1},{17,25},{25,17},{2,10},{10... | collective-permute-start | bytes 1179656 | tf_op jit(solution)/shard_map/ppermute | solution.py:320
  28.4 14.2 %collective-permute-start.5 = (bf16[2,64,1280]{2,1,0:T(8,128)(2,1)S(1)}, bf16[2,64,1280]{2,1,0:T(8,128)(2,1)S(1)}, u32[]{:S(2)}, u32[]{:S(2)}) collective-permute-start(bf16[2,64,1280]{2,1,0:T(8,128)(2,1)S(1)} %fusion), channel_id=1, source_target_pairs={{0,16},{8,24},{16,0},{24,8},{1,17},{9,25},{17,1},{25,9},{2,18},{10... | collective-permute-start | bytes 983048 | tf_op jit(solution)/shard_map/ppermute | solution.py:324
  30.5 35.3 %copy-start.25 = (bf16[2,64,512]{2,1,0:T(8,128)(2,1)}, bf16[2,64,512]{2,1,0:T(8,128)(2,1)S(1)}, u32[]{:S(2)}) copy-start(bf16[2,64,512]{2,1,0:T(8,128)(2,1)S(1)} %get-tuple-element.79.refs_0_) | copy-start | bytes 393220
  43.0 22.2 %collective-permute-start.12 = (bf16[2,64,1280]{2,1,0:T(8,128)(2,1)S(1)}, bf16[2,64,1280]{2,1,0:T(8,128)(2,1)S(1)}, u32[]{:S(2)}, u32[]{:S(2)}) collective-permute-start(bf16[2,64,1280]{2,1,0:T(8,128)(2,1)S(1)} %get-tuple-element.75.refs_0_), channel_id=1, source_target_pairs={{0,16},{8,24},{16,0},{24,8},{1,17},{9,25},{17,1},{25,9},{2,18},{10... | collective-permute-start | bytes 983048 | tf_op jit(solution)/shard_map/ppermute | solution.py:324
  44.8 15.9 %collective-permute-start.3 = (bf16[2,64,768]{2,1,0:T(8,128)(2,1)S(1)}, bf16[2,64,768]{2,1,0:T(8,128)(2,1)S(1)}, u32[]{:S(2)}, u32[]{:S(2)}) collective-permute-start(bf16[2,64,768]{2,1,0:T(8,128)(2,1)S(1)} %fusion.4), channel_id=1, source_target_pairs={{0,16},{8,24},{16,0},{24,8},{1,17},{9,25},{17,1},{25,9},{2,18},{10... | collective-permute-start | bytes 589832 | tf_op jit(solution)/shard_map/ppermute | solution.py:324
  45.1 15.6 %collective-permute-start.18 = (bf16[2,64,512]{2,1,0:T(8,128)(2,1)S(1)}, bf16[2,64,512]{2,1,0:T(8,128)(2,1)S(1)}, u32[]{:S(2)}, u32[]{:S(2)}) collective-permute-start(bf16[2,64,512]{2,1,0:T(8,128)(2,1)S(1)} %get-tuple-element.79.refs_0_), channel_id=1, source_target_pairs={{0,16},{8,24},{16,0},{24,8},{1,17},{9,25},{17,1},{25,9},{2,18},{10... | collective-permute-start | bytes 393224 | tf_op jit(solution)/shard_map/ppermute | solution.py:324
  46.8 18.9 %collective-permute-start.15 = (bf16[2,64,1024]{2,1,0:T(8,128)(2,1)S(1)}, bf16[2,64,1024]{2,1,0:T(8,128)(2,1)S(1)}, u32[]{:S(2)}, u32[]{:S(2)}) collective-permute-start(bf16[2,64,1024]{2,1,0:T(8,128)(2,1)S(1)} %get-tuple-element.76.refs_0_), channel_id=1, source_target_pairs={{0,16},{8,24},{16,0},{24,8},{1,17},{9,25},{17,1},{25,9},{2,18},{10... | collective-permute-start | bytes 786440 | tf_op jit(solution)/shard_map/ppermute | solution.py:324
  47.1 15.0 %collective-permute-start.17 = (bf16[2,64,512]{2,1,0:T(8,128)(2,1)S(1)}, bf16[2,64,512]{2,1,0:T(8,128)(2,1)S(1)}, u32[]{:S(2)}, u32[]{:S(2)}) collective-permute-start(bf16[2,64,512]{2,1,0:T(8,128)(2,1)S(1)} %get-tuple-element.79.refs_0_), channel_id=1, source_target_pairs={{0,8},{8,0},{16,24},{24,16},{1,9},{9,1},{17,25},{25,17},{2,10},{10... | collective-permute-start | bytes 393224 | tf_op jit(solution)/shard_map/ppermute | solution.py:320
  60.6 3.9 %collective-permute-start.19 = (bf16[2,64,512]{2,1,0:T(8,128)(2,1)S(1)}, bf16[2,64,512]{2,1,0:T(8,128)(2,1)S(1)}, u32[]{:S(2)}, u32[]{:S(2)}) collective-permute-start(bf16[2,64,512]{2,1,0:T(8,128)(2,1)S(1)} %collective-permute-done.18.refs_2_), channel_id=1, source_target_pairs={{0,8},{8,0},{16,24},{24,16},{1,9},{9,1},{17,25},{25,17},{2,10},{10... | collective-permute-start | bytes 393224 | tf_op jit(solution)/shard_map/ppermute | solution.py:320
  60.7 5.1 %collective-permute-start.14 = (bf16[2,64,1024]{2,1,0:T(8,128)(2,1)S(1)}, bf16[2,64,1024]{2,1,0:T(8,128)(2,1)S(1)}, u32[]{:S(2)}, u32[]{:S(2)}) collective-permute-start(bf16[2,64,1024]{2,1,0:T(8,128)(2,1)S(1)} %get-tuple-element.76.refs_0_), channel_id=1, source_target_pairs={{0,8},{8,0},{16,24},{24,16},{1,9},{9,1},{17,25},{25,17},{2,10},{10... | collective-permute-start | bytes 786440 | tf_op jit(solution)/shard_map/ppermute | solution.py:320
  62.7 7.2 %collective-permute-start.9 = (bf16[2,64,768]{2,1,0:T(8,128)(2,1)}, bf16[2,64,768]{2,1,0:T(8,128)(2,1)}, u32[]{:S(2)}, u32[]{:S(2)}) collective-permute-start(bf16[2,64,768]{2,1,0:T(8,128)(2,1)} %get-tuple-element.74.refs_0_), channel_id=1, source_target_pairs={{0,16},{8,24},{16,0},{24,8},{1,17},{9,25},{17,1},{25,9},{2,18},{10... | collective-permute-start | bytes 589832 | tf_op jit(solution)/shard_map/ppermute | solution.py:324
  65.2 20.2 %collective-permute-start.11 = (bf16[2,64,1280]{2,1,0:T(8,128)(2,1)S(1)}, bf16[2,64,1280]{2,1,0:T(8,128)(2,1)S(1)}, u32[]{:S(2)}, u32[]{:S(2)}) collective-permute-start(bf16[2,64,1280]{2,1,0:T(8,128)(2,1)S(1)} %get-tuple-element.75.refs_0_), channel_id=1, source_target_pairs={{0,8},{8,0},{16,24},{24,16},{1,9},{9,1},{17,25},{25,17},{2,10},{10... | collective-permute-start | bytes 983048 | tf_op jit(solution)/shard_map/ppermute | solution.py:320
  65.2 20.2 %collective-permute-start.13 = (bf16[2,64,1280]{2,1,0:T(8,128)(2,1)S(1)}, bf16[2,64,1280]{2,1,0:T(8,128)(2,1)S(1)}, u32[]{:S(2)}, u32[]{:S(2)}) collective-permute-start(bf16[2,64,1280]{2,1,0:T(8,128)(2,1)S(1)} %collective-permute-done.12.refs_2_), channel_id=1, source_target_pairs={{0,8},{8,0},{16,24},{24,16},{1,9},{9,1},{17,25},{25,17},{2,10},{10... | collective-permute-start | bytes 983048 | tf_op jit(solution)/shard_map/ppermute | solution.py:320
  65.7 13.6 %collective-permute-start.16 = (bf16[2,64,1024]{2,1,0:T(8,128)(2,1)S(1)}, bf16[2,64,1024]{2,1,0:T(8,128)(2,1)S(1)}, u32[]{:S(2)}, u32[]{:S(2)}) collective-permute-start(bf16[2,64,1024]{2,1,0:T(8,128)(2,1)S(1)} %collective-permute-done.15.refs_2_), channel_id=1, source_target_pairs={{0,8},{8,0},{16,24},{24,16},{1,9},{9,1},{17,25},{25,17},{2,10},{10... | collective-permute-start | bytes 786440 | tf_op jit(solution)/shard_map/ppermute | solution.py:320
  65.8 23.0 %collective-permute-start.8 = (bf16[2,64,768]{2,1,0:T(8,128)(2,1)}, bf16[2,64,768]{2,1,0:T(8,128)(2,1)}, u32[]{:S(2)}, u32[]{:S(2)}) collective-permute-start(bf16[2,64,768]{2,1,0:T(8,128)(2,1)} %get-tuple-element.74.refs_0_), channel_id=1, source_target_pairs={{0,8},{8,0},{16,24},{24,16},{1,9},{9,1},{17,25},{25,17},{2,10},{10... | collective-permute-start | bytes 589832 | tf_op jit(solution)/shard_map/ppermute | solution.py:320
  70.0 18.8 %collective-permute-start.10 = (bf16[2,64,768]{2,1,0:T(8,128)(2,1)}, bf16[2,64,768]{2,1,0:T(8,128)(2,1)}, u32[]{:S(2)}, u32[]{:S(2)}) collective-permute-start(bf16[2,64,768]{2,1,0:T(8,128)(2,1)} %collective-permute-done.9.refs_2_), channel_id=1, source_target_pairs={{0,8},{8,0},{16,24},{24,16},{1,9},{9,1},{17,25},{25,17},{2,10},{10... | collective-permute-start | bytes 589832 | tf_op jit(solution)/shard_map/ppermute | solution.py:320
  70.0 9.3 %copy-start.3 = (bf16[2048,1024]{1,0:T(8,128)(2,1)S(1)}, bf16[2048,1024]{1,0:T(8,128)(2,1)}, u32[]{:S(2)}) copy-start(bf16[2048,1024]{1,0:T(8,128)(2,1)} %copy-done.2) | copy-start | bytes 12582916
  95.0 15.8 %collective-permute-start.20 = (bf16[2,2,32,1024]{3,2,0,1:T(8,128)(2,1)}, bf16[2,2,32,1024]{3,2,0,1:T(8,128)(2,1)S(1)}, u32[]{:S(2)}, u32[]{:S(2)}) collective-permute-start(bf16[2,2,32,1024]{3,2,0,1:T(8,128)(2,1)} %fusion.2), channel_id=1, source_target_pairs={{0,1},{1,0},{2,3},{3,2},{4,5},{5,4},{6,7},{7,6},{8,9},{9,8},{10,11... | collective-permute-start | bytes 786440 | tf_op jit(solution)/shard_map/ppermute | solution.py:306
  101.2 10.2 %collective-permute-start.23 = (bf16[2,2,32,1024]{3,2,0,1:T(8,128)(2,1)S(1)}, bf16[2,2,32,1024]{3,2,0,1:T(8,128)(2,1)S(1)}, u32[]{:S(2)}, u32[]{:S(2)}) collective-permute-start(bf16[2,2,32,1024]{3,2,0,1:T(8,128)(2,1)S(1)} %fusion.3), channel_id=1, source_target_pairs={{0,2},{1,3},{2,0},{3,1},{4,6},{5,7},{6,4},{7,5},{8,10},{9,11},{10,... | collective-permute-start | bytes 786440 | tf_op jit(solution)/shard_map/ppermute | solution.py:306
  110.9 8.1 %collective-permute-start.21 = (bf16[2,32,1024]{2,1,0:T(8,128)(2,1)S(1)}, bf16[2,32,1024]{2,1,0:T(8,128)(2,1)S(1)}, u32[]{:S(2)}, u32[]{:S(2)}) collective-permute-start(bf16[2,32,1024]{2,1,0:T(8,128)(2,1)S(1)} %fusion.6), channel_id=1, source_target_pairs={{0,2},{1,3},{2,0},{3,1},{4,6},{5,7},{6,4},{7,5},{8,10},{9,11},{10,... | collective-permute-start | bytes 393224 | tf_op jit(solution)/shard_map/ppermute | solution.py:306
  111.6 10.2 %collective-permute-start.24 = (bf16[2,32,1024]{2,1,0:T(8,128)(2,1)S(1)}, bf16[2,32,1024]{2,1,0:T(8,128)(2,1)S(1)}, u32[]{:S(2)}, u32[]{:S(2)}) collective-permute-start(bf16[2,32,1024]{2,1,0:T(8,128)(2,1)S(1)} %fusion.7), channel_id=1, source_target_pairs={{0,1},{1,0},{2,3},{3,2},{4,5},{5,4},{6,7},{7,6},{8,9},{9,8},{10,11... | collective-permute-start | bytes 393224 | tf_op jit(solution)/shard_map/ppermute | solution.py:306
  112.1 10.0 %copy-start.22 = (bf16[2,256,768]{2,1,0:T(8,128)(2,1)S(1)}, bf16[2,256,768]{2,1,0:T(8,128)(2,1)}, u32[]{:S(2)}) copy-start(bf16[2,256,768]{2,1,0:T(8,128)(2,1)} %copy-done.21) | copy-start | bytes 2359300
  119.0 7.2 %collective-permute-start.22 = (bf16[32,1024]{1,0:T(8,128)(2,1)S(1)}, bf16[32,1024]{1,0:T(8,128)(2,1)S(1)}, u32[]{:S(2)}, u32[]{:S(2)}) collective-permute-start(bf16[32,1024]{1,0:T(8,128)(2,1)S(1)} %fusion.10), channel_id=1, source_target_pairs={{0,4},{1,5},{2,6},{3,7},{4,0},{5,1},{6,2},{7,3},{8,12},{9,13},{10,... | collective-permute-start | bytes 196616 | tf_op jit(solution)/shard_map/ppermute | solution.py:306
  121.8 5.6 %collective-permute-start.25 = (bf16[32,1024]{1,0:T(8,128)(2,1)S(1)}, bf16[32,1024]{1,0:T(8,128)(2,1)S(1)}, u32[]{:S(2)}, u32[]{:S(2)}) collective-permute-start(bf16[32,1024]{1,0:T(8,128)(2,1)S(1)} %fusion.11), channel_id=1, source_target_pairs={{0,4},{1,5},{2,6},{3,7},{4,0},{5,1},{6,2},{7,3},{8,12},{9,13},{10,... | collective-permute-start | bytes 196616 | tf_op jit(solution)/shard_map/ppermute | solution.py:306
  (31 other events, 97.4 us)

commit v4 on v3

--- a/solution.py
+++ b/solution.py
@@ -9,9 +9,10 @@
 
 BF16 = jnp.bfloat16
 F32 = jnp.float32
-VMEM_BYTES = 12 * 1024 * 1024
+VMEM_BYTES = 8 * 1024 * 1024
 SHARES = (2, 4, 5, 3)
 SLOTS = 4
+COST = 40
 WHOLE = pl.BlockSpec(memory_space=pltpu.VMEM)
 REMOTE = pl.BlockSpec(memory_space=pl.ANY)
 
@@ -28,7 +29,7 @@
     return block, [(a, b - a) for a, b in zip(edges, edges[1:]) if b > a]
 
 
-def call(kernel, name, in_specs, out_specs, out_shape, scratch, args, aliases=None):
+def call(kernel, name, in_specs, out_specs, out_shape, scratch, size, args, aliases=None):
     return pl.pallas_call(
         kernel,
         in_specs=in_specs,
@@ -37,7 +38,9 @@
         scratch_shapes=scratch,
         input_output_aliases=aliases or {},
         compiler_params=pltpu.CompilerParams(vmem_limit_bytes=VMEM_BYTES),
-        cost_estimate=pl.CostEstimate(flops=1000, bytes_accessed=1000, transcendentals=0),
+        cost_estimate=pl.CostEstimate(
+            flops=COST * size, bytes_accessed=size, transcendentals=0
+        ),
         name=name,
     )(*args)
 
@@ -46,50 +49,68 @@
     return pltpu.with_memory_space_constraint(value, pltpu.HBM)
 
 
-def fetches(sources, columns, targets, sems):
-    depth = sources[0].shape[0]
-    parts = sems.shape[1]
-    deep = depth // parts
-    return [
-        pltpu.make_async_copy(
-            source.at[pl.ds(p * deep, deep), columns],
-            target.at[pl.ds(p * deep, deep)],
-            sems.at[k, p],
+def forward_kernel(layout, ins, outs, *refs):
+    quarters, rows, block, start, count, following, first = layout
+    given, made, (total, sems, x_sem) = refs[:ins], refs[ins : ins + outs], refs[ins + outs :]
+    sources = given[1:3]
+    own_ref, far_ref, send_ref, *made = made
+    x_ref, early = given[0], given[3:5]
+    folds = []
+    if first:
+        x_copy = pltpu.make_async_copy(x_ref, made[0], x_sem)
+        x_copy.start()
+        x_ref, made = made[0], made[1:]
+    weights, ahead = made[:2], made[2:]
+    queue = [
+        [
+            pltpu.make_async_copy(
+                source.at[:, pl.ds((start + j) * block, block)],
+                target.at[:, pl.ds(j * block, block)],
+                sems.at[k, j],
+            )
+            for k, (source, target) in enumerate(zip(sources, weights))
+        ]
+        for j in range(0 if first else 1, count)
+    ]
+    if ahead:
+        queue.append(
+            [
+                pltpu.make_async_copy(
+                    source.at[:, pl.ds(following * block, block)], target, sems.at[k, count]
+                )
+                for k, (source, target) in enumerate(zip(sources, ahead))
+            ]
         )
-        for p in range(parts)
-        for k, (source, target) in enumerate(zip(sources, targets))
-    ]
-
-
-def forward_kernel(layout, ins, outs, *refs):
-    quarters, rows, block, own_at, next_at = layout
-    given, made, (total, own_sems, next_sems) = refs[:ins], refs[ins : ins + outs], refs[ins + outs :]
-    x_ref, gate_ref, up_ref = given[:3]
-    own_ref, far_ref, send_ref, *made = made
-    start = []
-    if own_at is None:
-        weights = given[3:5]
+    for pair in queue[:2]:
+        for copy in pair:
+            copy.start()
+    if first:
+        x_copy.wait()
     else:
-        start = fetches((gate_ref, up_ref), own_at, made[1:3], own_sems)
-        start.append(pltpu.make_async_copy(x_ref, made[0], next_sems.at[2, 0]))
-        for copy in start:
+        folds = [
+            pltpu.make_async_copy(early[k], weights[k].at[:, pl.ds(0, block)], sems.at[k, 0])
+            for k in range(2)
+        ]
+        for copy in folds:
             copy.start()
-        x_ref, weights, made = made[0], made[1:3], made[3:]
-    later = []
-    if next_at is not None:
-        later = fetches((gate_ref, up_ref), next_at, made, next_sems.at[:2])
-    for copy in start:
-        copy.wait()
-    for copy in later:
-        copy.start()
     outer = quarters // 2
     me = lax.axis_index("row")
     place, core = me // 2, me % 2
     x = x_ref[...]
-    for j in range(weights[0].shape[1] // block):
+    taken = 0
+    for j in range(count):
         at = slice(j * block, (j + 1) * block)
+        if first or j:
+            for copy in queue[taken]:
+                copy.wait()
+            taken += 1
+            for copy in queue[taken + 1] if taken + 1 < len(queue) else []:
+                copy.start()
+            blocks = [ref[:, at] for ref in weights]
+        else:
+            blocks = [ref[...] for ref in early]
         for k in range(2):
-            total[k] = jnp.dot(x, weights[k][:, at], preferred_element_type=F32)
+            total[k] = jnp.dot(x, blocks[k], preferred_element_type=F32)
         for step in range(outer):
             there = (place + step) % outer * 2
             mine = pl.multiple_of((there + core) * rows, rows)
@@ -101,53 +122,53 @@
                 else:
                     far_ref[step - 1, k, :, at] = kept
                 send_ref[step, k, :, at] = total[k, pl.ds(other, rows), :].astype(BF16)
-    for copy in later:
+    for copy in folds:
         copy.wait()
-
-
-def forward_part(quarters, block, chunk, following, x, gate_weight, up_weight, held, after):
+    for pair in queue[taken:]:
+        for copy in pair:
+            copy.wait()
+
+
+def forward_part(quarters, block, chunk, following, x, gate_weight, up_weight, early, after):
     tokens, depth = x.shape
     rows = tokens // quarters
     outer = quarters // 2
-    width = chunk[1] * block
-    own_at = None if held else pl.ds(chunk[0] * block, width)
-    next_at = None
+    start, count = chunk
+    width = count * block
+    first = not early
     out_shape = [
         jax.ShapeDtypeStruct((2, rows, width), F32),
         jax.ShapeDtypeStruct((outer - 1, 2, rows, width), F32),
         jax.ShapeDtypeStruct((outer, 2, rows, width), BF16),
     ]
-    if not held:
-        x = pltpu.with_memory_space_constraint(x, pltpu.HBM)
-        out_shape += [pltpu.VMEM(x.shape, BF16)] + [pltpu.VMEM((depth, width), BF16)] * 2
+    if first:
+        x = in_hbm(x)
+        out_shape.append(pltpu.VMEM(x.shape, BF16))
+    out_shape += [pltpu.VMEM((depth, width), BF16)] * 2
     if following is not None:
-        next_at = pl.ds(following[0] * block, following[1] * block)
-        out_shape += [pltpu.VMEM((depth, following[1] * block), BF16)] * 2
-    args = (x, in_hbm(gate_weight), in_hbm(up_weight), *held, *after)
-    parts = 4 if depth % 512 == 0 else 2
-    own, far, send, *loaded = call(
-        functools.partial(
-            forward_kernel,
-            (quarters, rows, block, own_at, next_at),
-            len(args),
-            len(out_shape),
-        ),
+        out_shape += [pltpu.VMEM((depth, block), BF16)] * 2
+    args = (x, in_hbm(gate_weight), in_hbm(up_weight), *early, *after)
+    layout = (quarters, rows, block, start, count, following, first)
+    return call(
+        functools.partial(forward_kernel, layout, len(args), len(out_shape)),
         "forward_part",
-        [WHOLE if held else REMOTE, REMOTE, REMOTE] + [WHOLE] * len(held) + [REMOTE] * len(after),
+        [REMOTE if first else WHOLE, REMOTE, REMOTE]
+        + [WHOLE] * len(early)
+        + [REMOTE] * len(after),
         [WHOLE] * len(out_shape),
         out_shape,
         [
             pltpu.VMEM((2, tokens, block), F32),
-            pltpu.SemaphoreType.DMA((2, parts)),
-            pltpu.SemaphoreType.DMA((3, parts)),
+            pltpu.SemaphoreType.DMA((2, count + 1)),
+            pltpu.SemaphoreType.DMA,
         ],
+        tokens * depth * width,
         args,
     )
-    return own, far, send, loaded
-
-
-def middle_kernel(outer, at, first, own_ref, got_ref, upstream_ref, *refs):
-    far_refs, rest = refs[: outer - 1], refs[outer - 1 :]
+
+
+def middle_kernel(outer, at, first, skipped, own_ref, got_ref, upstream_ref, *refs):
+    far_refs, rest = refs[: outer - 1], refs[outer - 1 + skipped :]
     if not first:
         rest[1][...] = rest[0][...]
         rest = rest[1:]
@@ -166,26 +187,27 @@
     grads_ref[1] = (upstream * gated).astype(BF16)
 
 
-def middle_part(outer, at, own, got, far, hidden_grad, hidden):
+def middle_part(outer, at, own, got, far, hidden_grad, hidden, after):
     rows, width = own.shape[1:]
     first = hidden is None
-    args = [own, got, hidden_grad, *far] + ([] if first else [hidden])
+    args = [own, got, hidden_grad, *far, *after] + ([] if first else [hidden])
     return call(
-        functools.partial(middle_kernel, outer, at, first),
+        functools.partial(middle_kernel, outer, at, first, len(after)),
         "middle_part",
-        [WHOLE] * len(args),
+        [WHOLE] * (2 + outer) + [REMOTE] * len(after) + [WHOLE] * (not first),
         [WHOLE] * 2,
         [
             jax.ShapeDtypeStruct(hidden_grad.shape, BF16),
             jax.ShapeDtypeStruct((2, rows, width), BF16),
         ],
         [],
+        rows * width,
         args,
     )
 
 
-def input_kernel(quarters, rows, first, last, gate_ref, up_ref, *refs):
-    pieces, rest = refs[:quarters], refs[quarters:]
+def input_kernel(quarters, rows, first, last, skipped, gate_ref, up_ref, *refs):
+    pieces, rest = refs[:quarters], refs[quarters + skipped :]
     earlier = []
     if not first:
         count = 2 if last else 1
@@ -228,22 +250,23 @@
             sums[d * deep // half][:, d * deep % half : d * deep % half + deep] = term.T
 
 
-def input_part(quarters, held, pieces, acc, final):
+def input_part(quarters, held, pieces, acc, final, after):
     depth, width = held[0].shape
     rows = pieces[0].shape[1]
     tokens = rows * quarters
     first, last = acc is None, final == 0
-    args = [*held, *pieces] + ([] if first else acc)
+    args = [*held, *pieces, *after] + ([] if first else acc)
     sums = [jax.ShapeDtypeStruct((depth, tokens), F32)]
     if final <= 1:
         sums = [jax.ShapeDtypeStruct((tokens, depth // 2), F32)] * 2
     *acc, grads = call(
-        functools.partial(input_kernel, quarters, rows, first, last),
+        functools.partial(input_kernel, quarters, rows, first, last, len(after)),
         "input_part",
-        [WHOLE] * len(args),
+        [WHOLE] * (2 + quarters) + [REMOTE] * len(after) + [WHOLE] * (0 if first else len(acc)),
         [WHOLE] * (len(sums) + 1),
         sums + [jax.ShapeDtypeStruct((2, tokens, width), BF16)],
         [],
+        tokens * depth * width,
         args,
     )
     return acc, grads
@@ -282,6 +305,7 @@
         [REMOTE] * 2,
         [pltpu.HBM((depth, full), BF16)] * 2,
         [pltpu.VMEM((SLOTS, depth, block), BF16), pltpu.SemaphoreType.DMA((SLOTS,))],
+        tokens * depth * count * block,
         args,
         aliases,
     )
@@ -323,53 +347,65 @@
         moves = [(r, (r // 2 + step) % outer * 2 + r % 2) for r in range(quarters)]
         return lax.ppermute(value, "row", moves)
 
-    owns, gots, sums, weights = [], [], [], []
-    x = inputs
-    for i, chunk in enumerate(chunks):
-        after = sums[i - 2][:1] if i >= 2 else []
-        following = chunks[i + 1] if i + 1 < len(chunks) else None
-        held = weights[i] if i else []
-        own, far, send, loaded = forward_part(
-            quarters, block, chunk, following, x, gate_weight, up_weight, held, after
+    def forward(i, x, early, after):
+        following = chunks[i + 1][0] if i + 1 < len(chunks) else None
+        own, far, send, *loaded = forward_part(
+            quarters, block, chunks[i], following, x, gate_weight, up_weight, early, after
         )
         if i == 0:
             x, loaded = loaded[0], loaded[1:]
-        while loaded:
-            weights.append(loaded[:2])
-            loaded = loaded[2:]
+        weights.append(loaded[:2])
         got = sibling(send)
+        near = [(far[step - 1] + got[step].astype(F32)).astype(BF16) for step in range(1, outer)]
         owns.append(own)
         gots.append(got)
-        sums.append(
-            [(far[step - 1] + got[step].astype(F32)).astype(BF16) for step in range(1, outer)]
+        sums.append(near)
+        crossed.append([across(value, step + 1) for step, value in enumerate(near)])
+        return x, loaded[2:]
+
+    def middle(i, hidden, after):
+        start, count = chunks[i]
+        at = slice(start * block, (start + count) * block)
+        hidden, mine = middle_part(
+            outer, at, owns[i], gots[i], crossed[i], hidden_grad, hidden, after
         )
-
-    xt = x.T
-    hidden = None
-    pieces = []
-    for (start, count), own, got, near in zip(chunks, owns, gots, sums):
-        far = [across(value, step + 1) for step, value in enumerate(near)]
-        at = slice(start * block, (start + count) * block)
-        hidden, mine = middle_part(outer, at, own, got, far, hidden_grad, hidden)
         group = [mine, sibling(mine)]
         for step in range(1, outer):
             there = across(mine, step)
             group += [there, sibling(there)]
         pieces.append(group)
-
-    acc = None
-    grads = []
-    for i, (held, group) in enumerate(zip(weights, pieces)):
-        acc, whole = input_part(quarters, held, group, acc, len(chunks) - 1 - i)
-        grads.append(whole)
+        return hidden
+
+    weights, owns, gots, sums, crossed, pieces = [], [], [], [], [], []
+    number = len(chunks)
+    x, early, hidden = inputs, [], None
+    for i in range(number):
+        after = []
+        if i >= 2:
+            after = sums[i - 2][:1]
+        if i >= 3:
+            hidden = middle(i - 3, hidden, [])
+            after = after + [pieces[i - 3][0]]
+        x, early = forward(i, x, early, after)
+    for i in range(max(number - 3, 0), number):
+        hidden = middle(i, hidden, pieces[i - 2][2:3] if i >= 2 else [])
+
+    xt = x.T
     bits = columns.bit_length() - 1
     order = list(range(bits))
+    acc, state = None, []
+    grads = []
+    for i in range(number):
+        after = state[:1] if i == number - 1 else []
+        acc, whole = input_part(quarters, weights[i], pieces[i], acc, number - 1 - i, after)
+        grads.append(whole)
+        if i < number - 2:
+            state = weight_part(block, *chunks[i], full, xt, whole, state, [])
     stages = [acc] + token_sums(acc, columns, [order, order[1::-1] + order[2:]])
     input_grad = jnp.concatenate([half.astype(BF16) for half in stages[-1]], axis=1)
-    state = []
-    for i, ((start, count), whole) in enumerate(zip(chunks, grads)):
-        after = stages[min(i, bits) - 1] if i else []
-        state = weight_part(block, start, count, full, xt, whole, state, after)
+    for i in range(max(number - 2, 0), number):
+        after = stages[min(i - max(number - 2, 0), bits)]
+        state = weight_part(block, *chunks[i], full, xt, grads[i], state, after)
     return hidden, input_grad, state[0], state[1]
 
 

time: 129 us -> 114 us (0.88)
  Pallas kernels: 54.1 us -> 48.2 us
  waiting for transfers between devices: 30.5 us -> 26.6 us
  starting transfers between devices: 21.2 us -> 17.8 us
  local copies, waits for them, and re-layouts: 19.9 us -> 18.2 us
    ppermute x8, waiting for transfers between devices: 29.2 us -> 21.6 us  [across(): return lax.ppermute(value, 'row', moves)]
    pallas_call x16, Pallas kernels: 54.1 us -> 48.2 us  [call(): pl.pallas_call(kernel, in_specs=in_specs, out_specs=out_specs, out_shape=...]
    ppermute x6, waiting for transfers between devices: 1.23 us -> 4.93 us  [token_sums(): got.append(lax.ppermute(send.astype(BF16), 'col', moves))]
    ppermute x8, starting transfers between devices: 10.5 us -> 7.89 us  [across(): return lax.ppermute(value, 'row', moves)]
    unnamed x74 -> x44, local copies, waits for them, and re-layouts: 18.5 us -> 17.5 us
  transfers between devices with their start and end apart: 26 -> 26, of which waited for: 5 -> 7; matrix products, arithmetic and copies ran while one was open for 1% -> 2% of each run, Pallas kernels for 34% -> 36%
where the time goes in v4:
time: 114 us
  Pallas kernels  48.2 us (42%)
  waiting for transfers between devices  26.6 us (23%)
  local copies, waits for them, and re-layouts  18.2 us (16%)
  starting transfers between devices  17.8 us (16%)
  other arithmetic  1.99 us (2%)
    pallas_call x16, Pallas kernels, call(): pl.pallas_call(kernel, in_specs=in_specs, out_specs=out_specs, out_shape=...  48.2 us
    ppermute x8, waiting for transfers between devices, across(): return lax.ppermute(value, 'row', moves)  21.6 us
    unnamed x44, local copies, waits for them, and re-layouts  17.5 us
    ppermute x8, starting transfers between devices, across(): return lax.ppermute(value, 'row', moves)  7.89 us
    ppermute x6, starting transfers between devices, token_sums(): got.append(lax.ppermute(send.astype(BF16), 'col', moves))  7.68 us
    ppermute x6, waiting for transfers between devices, token_sums(): got.append(lax.ppermute(send.astype(BF16), 'col', moves))  4.93 us
  transfers between devices with their start and end apart: 26, of which 7 were waited for; matrix products, arithmetic and copies ran while one was open for 2% of the time, Pallas kernels for 36%

profile of v4, /device:TPU:0, one launch (start us, length us, event | category | flops | bytes accessed | tf_op | source)
XLA Modules:
  0.0 113.9 jit_solution(10090828290099233250)
XLA Ops:
  0.6 4.8 %forward_part.4 = (f32[2,64,512]{2,1,0:T(8,128)S(1)}, f32[1,2,64,512]{3,2,1,0:T(8,128)S(1)}, bf16[2,2,64,512]{3,2,1,0:T(8,128)(2,1)}, bf16[256,2048]{1,0:T(8,128...) custom-call(bf16[256,2048]{1,0:T(8,128)(2,1)} %refs_0_.1, ...), custom_call_target="tpu_custom_call" | custom-call | flops 10737418240 | bytes 268435456 | tf_op jit(solution)/shard_map/forward_part/pallas_call | solution.py:33
  6.8 1.3 %copy-done.7 = bf16[2048,512]{1,0:T(8,128)(2,1)} copy-done((bf16[2048,512]{1,0:T(8,128)(2,1)}, bf16[2048,512]{1,0:T(8,128)(2,1)S(1)}, u32[]{:S(2)}) %copy-start.7) | copy-done | bytes 2097176
  8.1 1.3 %copy-done.9 = bf16[2048,512]{1,0:T(8,128)(2,1)} copy-done((bf16[2048,512]{1,0:T(8,128)(2,1)}, bf16[2048,512]{1,0:T(8,128)(2,1)S(1)}, u32[]{:S(2)}) %copy-start.9) | copy-done | bytes 2097176
  9.9 5.0 %forward_part.5 = (f32[2,64,1024]{2,1,0:T(8,128)S(1)}, f32[1,2,64,1024]{3,2,1,0:T(8,128)S(1)}, bf16[2,2,64,1024]{3,2,1,0:T(8,128)(2,1)}, bf16[2048,1024]{1,0:T(8...) custom-call(bf16[256,2048]{1,0:T(8,128)(2,1)S(1)} %get-tuple-element.57, ...), custom_call_target="tpu_custom_call" | custom-call | flops 21474836480 | bytes 536870912 | tf_op jit(solution)/shard_map/forward_part/pallas_call | solution.py:33
  15.8 2.0 %copy-done.11 = bf16[2048,1024]{1,0:T(8,128)(2,1)} copy-done((bf16[2048,1024]{1,0:T(8,128)(2,1)}, bf16[2048,1024]{1,0:T(8,128)(2,1)S(1)}, u32[]{:S(2)}) %copy-start.11) | copy-done | bytes 4194328
  17.8 2.1 %copy-done.13 = bf16[2048,1024]{1,0:T(8,128)(2,1)} copy-done((bf16[2048,1024]{1,0:T(8,128)(2,1)}, bf16[2048,1024]{1,0:T(8,128)(2,1)S(1)}, u32[]{:S(2)}) %copy-start.13) | copy-done | bytes 4194328
  23.5 3.0 %collective-permute-start.2 = (bf16[2,64,512]{2,1,0:T(8,128)(2,1)S(1)}, bf16[2,64,512]{2,1,0:T(8,128)(2,1)S(1)}, u32[]{:S(2)}, u32[]{:S(2)}) collective-permute-start(bf16[2,64,512]{2,1,0:T(8,128)(2,1)S(1)} %fusion.5.refs_5_), channel_id=1, source_target_pairs={{0,16},{8,24},{16,0},{24,8},{1,17},{9,25},{17,1},{25,9},{2,18},{10... | collective-permute-start | bytes 393224 | tf_op jit(solution)/shard_map/ppermute | solution.py:348
  26.5 1.2 %copy-done.17 = bf16[2048,256]{1,0:T(8,128)(2,1)S(1)} copy-done((bf16[2048,256]{1,0:T(8,128)(2,1)S(1)}, bf16[2048,256]{1,0:T(8,128)(2,1)}, u32[]{:S(2)}) %copy-start.17) | copy-done | bytes 1048600
  27.8 1.2 %copy-done.19 = bf16[2048,256]{1,0:T(8,128)(2,1)S(1)} copy-done((bf16[2048,256]{1,0:T(8,128)(2,1)S(1)}, bf16[2048,256]{1,0:T(8,128)(2,1)}, u32[]{:S(2)}) %copy-start.19) | copy-done | bytes 1048600
  29.0 5.2 %forward_part.6 = (f32[2,64,1280]{2,1,0:T(8,128)S(1)}, f32[1,2,64,1280]{3,2,1,0:T(8,128)S(1)}, bf16[2,2,64,1280]{3,2,1,0:T(8,128)(2,1)S(1)}, bf16[2048,1280]{1,0...) custom-call(bf16[256,2048]{1,0:T(8,128)(2,1)S(1)} %get-tuple-element, ...), custom_call_target="tpu_custom_call" | custom-call | flops 26843545600 | bytes 671088640 | tf_op jit(solution)/shard_map/forward_part/pallas_call | solution.py:33
  34.3 2.3 %copy-done.15 = bf16[2048,1280]{1,0:T(8,128)(2,1)} copy-done((bf16[2048,1280]{1,0:T(8,128)(2,1)}, bf16[2048,1280]{1,0:T(8,128)(2,1)S(1)}, u32[]{:S(2)}) %copy-start.15) | copy-done | bytes 5242904
  37.4 1.7 %collective-permute-start.5 = (bf16[2,64,1024]{2,1,0:T(8,128)(2,1)S(1)}, bf16[2,64,1024]{2,1,0:T(8,128)(2,1)S(1)}, u32[]{:S(2)}, u32[]{:S(2)}) collective-permute-start(bf16[2,64,1024]{2,1,0:T(8,128)(2,1)S(1)} %fusion.1.refs_5_), channel_id=1, source_target_pairs={{0,16},{8,24},{16,0},{24,8},{1,17},{9,25},{17,1},{25,9},{2,18},{10... | collective-permute-start | bytes 786440 | tf_op jit(solution)/shard_map/ppermute | solution.py:348
  39.2 3.9 %collective-permute-done.9.refs_1_.refs_2_ = bf16[2,64,512]{2,1,0:T(8,128)(2,1)S(1)} collective-permute-done((bf16[2,64,512]{2,1,0:T(8,128)(2,1)S(1)}, bf16[2,64,512]{2,1,0:T(8,128)(2,1)S(1)}, u32[]{:S(2)}, u32[]{:S(2)}) %collective-permute-start.9) | collective-permute-done | bytes 131104 | tf_op jit(solution)/shard_map/ppermute | solution.py:348
  43.1 3.3 %forward_part.7 = (f32[2,64,768]{2,1,0:T(8,128)S(1)}, f32[1,2,64,768]{3,2,1,0:T(8,128)S(1)}, bf16[2,2,64,768]{3,2,1,0:T(8,128)(2,1)S(1)}, bf16[2048,768]{1,0:T(8,128)(2,1)S(1)}, bf16[2048,768]{1,0:T(8,128)(2,1)S(1)}) custom-call(bf16[256,2048]{1,0:T(8,128)(2,1)S(1)} %get-tuple-element.57.refs_0_, bf16[2048,3584]{1,0:T(8,128)(2,1)} %refs_1_.7, ...), custom_call_target="tpu_custom_call" | custom-call | flops 16106127360 | bytes 402653184 | tf_op jit(solution)/shard_map/forward_part/pallas_call | solution.py:33
  47.0 1.3 %input_part.4 = (f32[2048,256]{1,0:T(8,128)S(1)}, bf16[2,256,512]{2,1,0:T(8,128)(2,1)S(1)}) custom-call(bf16[2048,512]{1,0:T(8,128)(2,1)S(1)} %copy-done.8, bf16[2048,512]{1,0:T(8,128)(2,1)S(1)} %copy-done.10, bf16[2,64,512]{2,1,0:T(8,128)(2,1)S(1)} %get-tuple-element.69.refs_6_.refs_0_, bf16[2,64,512]{2,1,0:T(8,128)(2,1)S(1)} %collective-permute-done.15.refs_1_, ...), custom_call_target="tpu_custom_call" | custom-call | flops 10737418240 | bytes 268435456 | tf_op jit(solution)/shard_map/input_part/pallas_call | solution.py:33
  49.0 1.8 %collective-permute-start.8 = (bf16[2,64,1280]{2,1,0:T(8,128)(2,1)S(1)}, bf16[2,64,1280]{2,1,0:T(8,128)(2,1)S(1)}, u32[]{:S(2)}, u32[]{:S(2)}) collective-permute-start(bf16[2,64,1280]{2,1,0:T(8,128)(2,1)S(1)} %fusion), channel_id=1, source_target_pairs={{0,16},{8,24},{16,0},{24,8},{1,17},{9,25},{17,1},{25,9},{2,18},{10... | collective-permute-start | bytes 983048 | tf_op jit(solution)/shard_map/ppermute | solution.py:348
  51.2 6.6 %collective-permute-done.6.refs_1_.refs_2_ = bf16[2,64,1024]{2,1,0:T(8,128)(2,1)S(1)} collective-permute-done((bf16[2,64,1024]{2,1,0:T(8,128)(2,1)S(1)}, bf16[2,64,1024]{2,1,0:T(8,128)(2,1)S(1)}, u32[]{:S(2)}, u32[]{:S(2)}) %collective-permute-start.6) | collective-permute-done | bytes 262176 | tf_op jit(solution)/shard_map/ppermute | solution.py:348
  57.8 2.9 %weight_part.4 = (bf16[2048,3584]{1,0:T(8,128)(2,1)}, bf16[2048,3584]{1,0:T(8,128)(2,1)}) custom-call(bf16[2048,256]{1,0:T(8,128)(2,1)S(1)} %bitcast.43, bf16[2,256,512]{2,1,0:T(8,128)(2,1)S(1)} %get-tuple-element.91.grads_ref), custom_call_target="tpu_custom_call" | custom-call | flops 10737418240 | bytes 268435456 | tf_op jit(solution)/shard_map/weight_part/pallas_call | solution.py:33
  60.7 4.1 %collective-permute-done.8.refs_0_ = bf16[2,64,1280]{2,1,0:T(8,128)(2,1)S(1)} collective-permute-done((bf16[2,64,1280]{2,1,0:T(8,128)(2,1)S(1)}, bf16[2,64,1280]{2,1,0:T(8,128)(2,1)S(1)}, u32[]{:S(2)}, u32[]{:S(2)}) %collective-permute-start.8) | collective-permute-done | bytes 327712 | tf_op jit(solution)/shard_map/ppermute | solution.py:348
  65.4 3.6 %collective-permute-done.4.refs_0_ = bf16[2,64,768]{2,1,0:T(8,128)(2,1)S(1)} collective-permute-done((bf16[2,64,768]{2,1,0:T(8,128)(2,1)S(1)}, bf16[2,64,768]{2,1,0:T(8,128)(2,1)S(1)}, u32[]{:S(2)}, u32[]{:S(2)}) %collective-permute-start.4) | collective-permute-done | bytes 196640 | tf_op jit(solution)/shard_map/ppermute | solution.py:348
  70.2 2.5 %input_part.5 = (f32[2048,256]{1,0:T(8,128)S(1)}, bf16[2,256,1024]{2,1,0:T(8,128)(2,1)S(1)}) custom-call(bf16[2048,1024]{1,0:T(8,128)(2,1)S(1)} %copy-done.12, bf16[2048,1024]{1,0:T(8,128)(2,1)S(1)} %copy-done.14, bf16[2,64,1024]{2,1,0:T(8,128)(2,1)S(1)} %get-tuple-element.75.refs_0_, bf16[2,64,1024]{2,1,0:T(8,128)(2,1)S(1)} %collective-permute-done.13.refs_1_, ...), custom_call_target="tpu_custom_call" | custom-call | flops 21474836480 | bytes 536870912 | tf_op jit(solution)/shard_map/input_part/pallas_call | solution.py:33
  72.7 3.4 %collective-permute-done.18.refs_2_ = bf16[2,64,1280]{2,1,0:T(8,128)(2,1)S(1)} collective-permute-done((bf16[2,64,1280]{2,1,0:T(8,128)(2,1)S(1)}, bf16[2,64,1280]{2,1,0:T(8,128)(2,1)S(1)}, u32[]{:S(2)}, u32[]{:S(2)}) %collective-permute-start.18) | collective-permute-done | bytes 327712 | tf_op jit(solution)/shard_map/ppermute | solution.py:348
  76.1 5.5 %weight_part.5 = (bf16[2048,3584]{1,0:T(8,128)(2,1)}, bf16[2048,3584]{1,0:T(8,128)(2,1)}) custom-call(bf16[2048,256]{1,0:T(8,128)(2,1)S(1)} %bitcast.44, bf16[2,256,1024]{2,1,0:T(8,128)(2,1)S(1)} %get-tuple-element.90.grads_ref, bf16[2048,3584]{1,0:T(8,128)(2,1)} %get-tuple-element.92.refs_0_, ...), custom_call_target="tpu_custom_call", output_to_operand_aliasing={{0}: (2, {}), {1}: (3, {})} | custom-call | flops 21474836480 | bytes 536870912 | tf_op jit(solution)/shard_map/weight_part/pallas_call | solution.py:33
  82.2 3.4 %input_part.6 = (f32[256,1024]{1,0:T(8,128)S(1)}, f32[256,1024]{1,0:T(8,128)S(1)}, bf16[2,256,1280]{2,1,0:T(8,128)(2,1)S(1)}) custom-call(bf16[2048,1280]{1,0:T(8,128)(2,1)S(1)} %get-tuple-element.95.gate_ref, bf16[2048,1280]{1,0:T(8,128)(2,1)S(1)} %bitcast.52, bf16[2,64,1280]{2,1,0:T(8,128)(2,1)S(1)} %get-tuple-element.97.refs_0_, ...), custom_call_target="tpu_custom_call" | custom-call | flops 26843545600 | bytes 671088640 | tf_op jit(solution)/shard_map/input_part/pallas_call | solution.py:33
  85.6 1.7 %copy-done.6 = bf16[2048,3584]{1,0:T(8,128)(2,1)S(1)} copy-done((bf16[2048,3584]{1,0:T(8,128)(2,1)S(1)}, bf16[2048,3584]{1,0:T(8,128)(2,1)}, u32[]{:S(2)}) %copy-start.6) | copy-done | bytes 14680088
  87.3 1.9 %input_part.7 = (f32[256,1024]{1,0:T(8,128)S(1)}, f32[256,1024]{1,0:T(8,128)S(1)}, bf16[2,256,768]{2,1,0:T(8,128)(2,1)S(1)}) custom-call(bf16[2048,768]{1,0:T(8,128)(2,1)S(1)} %get-tuple-element.82.gate_ref, bf16[2048,768]{1,0:T(8,128)(2,1)S(1)} %get-tuple-element.83.up_ref, bf16[2,64,768]{2,1,0:T(8,128)(2,1)S(1)} %get-tuple-element.84.refs_0_, ...), custom_call_target="tpu_custom_call" | custom-call | flops 16106127360 | bytes 402653184 | tf_op jit(solution)/shard_map/input_part/pallas_call | solution.py:33
  89.2 1.6 %collective-permute-start.20 = (bf16[2,2,32,1024]{3,2,0,1:T(8,128)(2,1)S(1)}, bf16[2,2,32,1024]{3,2,0,1:T(8,128)(2,1)S(1)}, u32[]{:S(2)}, u32[]{:S(2)}) collective-permute-start(bf16[2,2,32,1024]{3,2,0,1:T(8,128)(2,1)S(1)} %fusion.2), channel_id=1, source_target_pairs={{0,1},{1,0},{2,3},{3,2},{4,5},{5,4},{6,7},{7,6},{8,9},{9,8},{10,11... | collective-permute-start | bytes 786440 | tf_op jit(solution)/shard_map/ppermute | solution.py:330
  90.9 1.6 %collective-permute-start.23 = (bf16[2,2,32,1024]{3,2,1,0:T(8,128)(2,1)S(1)}, bf16[2,2,32,1024]{3,2,1,0:T(8,128)(2,1)S(1)}, u32[]{:S(2)}, u32[]{:S(2)}) collective-permute-start(bf16[2,2,32,1024]{3,2,1,0:T(8,128)(2,1)S(1)} %fusion.3), channel_id=1, source_target_pairs={{0,2},{1,3},{2,0},{3,1},{4,6},{5,7},{6,4},{7,5},{8,10},{9,11},{10,... | collective-permute-start | bytes 786440 | tf_op jit(solution)/shard_map/ppermute | solution.py:330
  92.5 6.8 %weight_part.6 = (bf16[2048,3584]{1,0:T(8,128)(2,1)}, bf16[2048,3584]{1,0:T(8,128)(2,1)}) custom-call(bf16[2048,256]{1,0:T(8,128)(2,1)S(1)} %bitcast.45, bf16[2,256,1280]{2,1,0:T(8,128)(2,1)S(1)} %get-tuple-element.104.grads_ref, f32[256,1024]{1,0:T(8,128)S(1)} %get-tuple-element.101.refs_0_, ...), custom_call_target="tpu_custom_call", output_to_operand_aliasing={{0}: (4, {}), {1}: (5, {})} | custom-call | flops 26843545600 | bytes 671088640 | tf_op jit(solution)/shard_map/weight_part/pallas_call | solution.py:33
  101.0 4.1 %weight_part.7 = (bf16[2048,3584]{1,0:T(8,128)(2,1)}, bf16[2048,3584]{1,0:T(8,128)(2,1)}) custom-call(bf16[2048,256]{1,0:T(8,128)(2,1)S(1)} %bitcast.46, bf16[2,256,768]{2,1,0:T(8,128)(2,1)S(1)} %get-tuple-element.103.grads_ref, f32[2,2,32,1024]{3,2,1,0:T(8,128)S(1)} %copy.20.refs_0_, ...), custom_call_target="tpu_custom_call", output_to_operand_aliasing={{0}: (4, {}), {1}: (5, {})} | custom-call | flops 16106127360 | bytes 402653184 | tf_op jit(solution)/shard_map/weight_part/pallas_call | solution.py:33
  105.2 2.6 %collective-permute-start.22 = (bf16[32,1024]{1,0:T(8,128)(2,1)S(1)}, bf16[32,1024]{1,0:T(8,128)(2,1)S(1)}, u32[]{:S(2)}, u32[]{:S(2)}) collective-permute-start(bf16[32,1024]{1,0:T(8,128)(2,1)S(1)} %fusion.10), channel_id=1, source_target_pairs={{0,4},{1,5},{2,6},{3,7},{4,0},{5,1},{6,2},{7,3},{8,12},{9,13},{10,... | collective-permute-start | bytes 196616 | tf_op jit(solution)/shard_map/ppermute | solution.py:330
  108.3 4.1 %collective-permute-done.22 = bf16[32,1024]{1,0:T(8,128)(2,1)S(1)} collective-permute-done((bf16[32,1024]{1,0:T(8,128)(2,1)S(1)}, bf16[32,1024]{1,0:T(8,128)(2,1)S(1)}, u32[]{:S(2)}, u32[]{:S(2)}) %collective-permute-start.22) | collective-permute-done | bytes 65568 | tf_op jit(solution)/shard_map/ppermute | solution.py:330
  (100 shorter events, 14.7 us)
Async XLA Ops:
  9.4 13.1 %collective-permute-start = (bf16[2,2,64,512]{3,2,1,0:T(8,128)(2,1)}, bf16[2,2,64,512]{3,2,1,0:T(8,128)(2,1)S(1)}, u32[]{:S(2)}, u32[]{:S(2)}) collective-permute-start(bf16[2,2,64,512]{3,2,1,0:T(8,128)(2,1)} %get-tuple-element.63), channel_id=1, source_target_pairs={{0,8},{8,0},{16,24},{24,16},{1,9},{9,1},{17,25},{25,17},{2,10},{10... | collective-permute-start | bytes 786440 | tf_op jit(solution)/shard_map/ppermute | solution.py:344
  21.9 15.5 %collective-permute-start.1 = (bf16[2,2,64,1024]{3,2,1,0:T(8,128)(2,1)}, bf16[2,2,64,1024]{3,2,1,0:T(8,128)(2,1)S(1)}, u32[]{:S(2)}, u32[]{:S(2)}) collective-permute-start(bf16[2,2,64,1024]{3,2,1,0:T(8,128)(2,1)} %get-tuple-element.67), channel_id=1, source_target_pairs={{0,8},{8,0},{16,24},{24,16},{1,9},{9,1},{17,25},{25,17},{2,10},{10... | collective-permute-start | bytes 1572872 | tf_op jit(solution)/shard_map/ppermute | solution.py:344
  23.5 13.1 %collective-permute-start.2 = (bf16[2,64,512]{2,1,0:T(8,128)(2,1)S(1)}, bf16[2,64,512]{2,1,0:T(8,128)(2,1)S(1)}, u32[]{:S(2)}, u32[]{:S(2)}) collective-permute-start(bf16[2,64,512]{2,1,0:T(8,128)(2,1)S(1)} %fusion.5.refs_5_), channel_id=1, source_target_pairs={{0,16},{8,24},{16,0},{24,8},{1,17},{9,25},{17,1},{25,9},{2,18},{10... | collective-permute-start | bytes 393224 | tf_op jit(solution)/shard_map/ppermute | solution.py:348
  29.0 7.6 %copy-start = (bf16[64,3584]{1,0:T(8,128)(2,1)S(1)}, bf16[64,3584]{1,0:T(8,128)(2,1)}, u32[]{:S(2)}) copy-start(bf16[64,3584]{1,0:T(8,128)(2,1)} %upstream_ref.7) | copy-start | bytes 1376260
  29.0 7.6 %copy-start.4 = (f32[2,64,512]{2,1,0:T(8,128)S(1)}, f32[2,64,512]{2,1,0:T(8,128)}, u32[]{:S(2)}) copy-start(f32[2,64,512]{2,1,0:T(8,128)} %copy-done.3) | copy-start | bytes 786436
  29.0 8.4 %copy-start.2 = (f32[1,2,64,1024]{3,2,1,0:T(8,128)S(1)}, f32[1,2,64,1024]{3,2,1,0:T(8,128)}, u32[]{:S(2)}) copy-start(f32[1,2,64,1024]{3,2,1,0:T(8,128)} %copy-done.1) | copy-start | bytes 1572868
  36.6 12.3 %collective-permute-start.7 = (bf16[2,2,64,1280]{3,2,1,0:T(8,128)(2,1)S(1)}, bf16[2,2,64,1280]{3,2,1,0:T(8,128)(2,1)S(1)}, u32[]{:S(2)}, u32[]{:S(2)}) collective-permute-start(bf16[2,2,64,1280]{3,2,1,0:T(8,128)(2,1)S(1)} %get-tuple-element.77), channel_id=1, source_target_pairs={{0,8},{8,0},{16,24},{24,16},{1,9},{9,1},{17,25},{25,17},{2,10},{10... | collective-permute-start | bytes 1966088 | tf_op jit(solution)/shard_map/ppermute | solution.py:344
  36.7 6.4 %collective-permute-start.9 = (bf16[2,64,512]{2,1,0:T(8,128)(2,1)S(1)}, bf16[2,64,512]{2,1,0:T(8,128)(2,1)S(1)}, u32[]{:S(2)}, u32[]{:S(2)}) collective-permute-start(bf16[2,64,512]{2,1,0:T(8,128)(2,1)S(1)} %get-tuple-element.69.refs_6_.refs_0_), channel_id=1, source_target_pairs={{0,16},{8,24},{16,0},{24,8},{1,17},{9,25},{17,1},{25,9},{2,18},{10... | collective-permute-start | bytes 393224 | tf_op jit(solution)/shard_map/ppermute | solution.py:348
  36.8 10.2 %collective-permute-start.15 = (bf16[2,64,512]{2,1,0:T(8,128)(2,1)S(1)}, bf16[2,64,512]{2,1,0:T(8,128)(2,1)S(1)}, u32[]{:S(2)}, u32[]{:S(2)}) collective-permute-start(bf16[2,64,512]{2,1,0:T(8,128)(2,1)S(1)} %get-tuple-element.69.refs_6_.refs_0_), channel_id=1, source_target_pairs={{0,8},{8,0},{16,24},{24,16},{1,9},{9,1},{17,25},{25,17},{2,10},{10... | collective-permute-start | bytes 393224 | tf_op jit(solution)/shard_map/ppermute | solution.py:344
  37.4 10.9 %collective-permute-start.5 = (bf16[2,64,1024]{2,1,0:T(8,128)(2,1)S(1)}, bf16[2,64,1024]{2,1,0:T(8,128)(2,1)S(1)}, u32[]{:S(2)}, u32[]{:S(2)}) collective-permute-start(bf16[2,64,1024]{2,1,0:T(8,128)(2,1)S(1)} %fusion.1.refs_5_), channel_id=1, source_target_pairs={{0,16},{8,24},{16,0},{24,8},{1,17},{9,25},{17,1},{25,9},{2,18},{10... | collective-permute-start | bytes 786440 | tf_op jit(solution)/shard_map/ppermute | solution.py:348
  43.1 3.9 %collective-permute-start.16 = (bf16[2,64,512]{2,1,0:T(8,128)(2,1)S(1)}, bf16[2,64,512]{2,1,0:T(8,128)(2,1)S(1)}, u32[]{:S(2)}, u32[]{:S(2)}) collective-permute-start(bf16[2,64,512]{2,1,0:T(8,128)(2,1)S(1)} %collective-permute-done.9.refs_1_.refs_2_), channel_id=1, source_target_pairs={{0,8},{8,0},{16,24},{24,16},{1,9},{9,1},{17,25},{25,17},{2,10},{10... | collective-permute-start | bytes 393224 | tf_op jit(solution)/shard_map/ppermute | solution.py:344
  46.4 4.4 %collective-permute-start.3 = (bf16[2,2,64,768]{3,2,1,0:T(8,128)(2,1)S(1)}, bf16[2,2,64,768]{3,2,1,0:T(8,128)(2,1)S(1)}, u32[]{:S(2)}, u32[]{:S(2)}) collective-permute-start(bf16[2,2,64,768]{3,2,1,0:T(8,128)(2,1)S(1)} %get-tuple-element.71), channel_id=1, source_target_pairs={{0,8},{8,0},{16,24},{24,16},{1,9},{9,1},{17,25},{25,17},{2,10},{10... | collective-permute-start | bytes 1179656 | tf_op jit(solution)/shard_map/ppermute | solution.py:344
  48.6 9.2 %collective-permute-start.6 = (bf16[2,64,1024]{2,1,0:T(8,128)(2,1)S(1)}, bf16[2,64,1024]{2,1,0:T(8,128)(2,1)S(1)}, u32[]{:S(2)}, u32[]{:S(2)}) collective-permute-start(bf16[2,64,1024]{2,1,0:T(8,128)(2,1)S(1)} %get-tuple-element.75.refs_0_), channel_id=1, source_target_pairs={{0,16},{8,24},{16,0},{24,8},{1,17},{9,25},{17,1},{25,9},{2,18},{10... | collective-permute-start | bytes 786440 | tf_op jit(solution)/shard_map/ppermute | solution.py:348
  48.9 21.3 %collective-permute-start.13 = (bf16[2,64,1024]{2,1,0:T(8,128)(2,1)S(1)}, bf16[2,64,1024]{2,1,0:T(8,128)(2,1)S(1)}, u32[]{:S(2)}, u32[]{:S(2)}) collective-permute-start(bf16[2,64,1024]{2,1,0:T(8,128)(2,1)S(1)} %get-tuple-element.75.refs_0_), channel_id=1, source_target_pairs={{0,8},{8,0},{16,24},{24,16},{1,9},{9,1},{17,25},{25,17},{2,10},{10... | collective-permute-start | bytes 786440 | tf_op jit(solution)/shard_map/ppermute | solution.py:344
  49.0 15.8 %collective-permute-start.8 = (bf16[2,64,1280]{2,1,0:T(8,128)(2,1)S(1)}, bf16[2,64,1280]{2,1,0:T(8,128)(2,1)S(1)}, u32[]{:S(2)}, u32[]{:S(2)}) collective-permute-start(bf16[2,64,1280]{2,1,0:T(8,128)(2,1)S(1)} %fusion), channel_id=1, source_target_pairs={{0,16},{8,24},{16,0},{24,8},{1,17},{9,25},{17,1},{25,9},{2,18},{10... | collective-permute-start | bytes 983048 | tf_op jit(solution)/shard_map/ppermute | solution.py:348
  50.9 18.2 %collective-permute-start.4 = (bf16[2,64,768]{2,1,0:T(8,128)(2,1)S(1)}, bf16[2,64,768]{2,1,0:T(8,128)(2,1)S(1)}, u32[]{:S(2)}, u32[]{:S(2)}) collective-permute-start(bf16[2,64,768]{2,1,0:T(8,128)(2,1)S(1)} %fusion.4), channel_id=1, source_target_pairs={{0,16},{8,24},{16,0},{24,8},{1,17},{9,25},{17,1},{25,9},{2,18},{10... | collective-permute-start | bytes 589832 | tf_op jit(solution)/shard_map/ppermute | solution.py:348
  57.8 12.4 %collective-permute-start.14 = (bf16[2,64,1024]{2,1,0:T(8,128)(2,1)S(1)}, bf16[2,64,1024]{2,1,0:T(8,128)(2,1)S(1)}, u32[]{:S(2)}, u32[]{:S(2)}) collective-permute-start(bf16[2,64,1024]{2,1,0:T(8,128)(2,1)S(1)} %collective-permute-done.6.refs_1_.refs_2_), channel_id=1, source_target_pairs={{0,8},{8,0},{16,24},{24,16},{1,9},{9,1},{17,25},{25,17},{2,10},{10... | collective-permute-start | bytes 786440 | tf_op jit(solution)/shard_map/ppermute | solution.py:344
  57.8 12.4 %copy-start.12 = (bf16[2048,1024]{1,0:T(8,128)(2,1)S(1)}, bf16[2048,1024]{1,0:T(8,128)(2,1)}, u32[]{:S(2)}) copy-start(bf16[2048,1024]{1,0:T(8,128)(2,1)} %copy-done.11) | copy-start | bytes 12582916
  57.8 12.4 %copy-start.14 = (bf16[2048,1024]{1,0:T(8,128)(2,1)S(1)}, bf16[2048,1024]{1,0:T(8,128)(2,1)}, u32[]{:S(2)}) copy-start(bf16[2048,1024]{1,0:T(8,128)(2,1)} %copy-done.13) | copy-start | bytes 12582916
  65.1 11.0 %collective-permute-start.18 = (bf16[2,64,1280]{2,1,0:T(8,128)(2,1)S(1)}, bf16[2,64,1280]{2,1,0:T(8,128)(2,1)S(1)}, u32[]{:S(2)}, u32[]{:S(2)}) collective-permute-start(bf16[2,64,1280]{2,1,0:T(8,128)(2,1)S(1)} %get-tuple-element.97.refs_0_), channel_id=1, source_target_pairs={{0,16},{8,24},{16,0},{24,8},{1,17},{9,25},{17,1},{25,9},{2,18},{10... | collective-permute-start | bytes 983048 | tf_op jit(solution)/shard_map/ppermute | solution.py:348
  65.4 16.7 %collective-permute-start.17 = (bf16[2,64,1280]{2,1,0:T(8,128)(2,1)S(1)}, bf16[2,64,1280]{2,1,0:T(8,128)(2,1)S(1)}, u32[]{:S(2)}, u32[]{:S(2)}) collective-permute-start(bf16[2,64,1280]{2,1,0:T(8,128)(2,1)S(1)} %get-tuple-element.97.refs_0_), channel_id=1, source_target_pairs={{0,8},{8,0},{16,24},{24,16},{1,9},{9,1},{17,25},{25,17},{2,10},{10... | collective-permute-start | bytes 983048 | tf_op jit(solution)/shard_map/ppermute | solution.py:344
  69.9 11.6 %collective-permute-start.11 = (bf16[2,64,768]{2,1,0:T(8,128)(2,1)S(1)}, bf16[2,64,768]{2,1,0:T(8,128)(2,1)S(1)}, u32[]{:S(2)}, u32[]{:S(2)}) collective-permute-start(bf16[2,64,768]{2,1,0:T(8,128)(2,1)S(1)} %get-tuple-element.84.refs_0_), channel_id=1, source_target_pairs={{0,16},{8,24},{16,0},{24,8},{1,17},{9,25},{17,1},{25,9},{2,18},{10... | collective-permute-start | bytes 589832 | tf_op jit(solution)/shard_map/ppermute | solution.py:348
  70.2 15.4 %collective-permute-start.10 = (bf16[2,64,768]{2,1,0:T(8,128)(2,1)S(1)}, bf16[2,64,768]{2,1,0:T(8,128)(2,1)S(1)}, u32[]{:S(2)}, u32[]{:S(2)}) collective-permute-start(bf16[2,64,768]{2,1,0:T(8,128)(2,1)S(1)} %get-tuple-element.84.refs_0_), channel_id=1, source_target_pairs={{0,8},{8,0},{16,24},{24,16},{1,9},{9,1},{17,25},{25,17},{2,10},{10... | collective-permute-start | bytes 589832 | tf_op jit(solution)/shard_map/ppermute | solution.py:344
  70.2 11.9 %slice-start = ((s8[5242880]{0:T(1024)(128)(4,1)}), s8[1048576]{0:T(1024)(128)(4,1)S(1)}, s32[]{:S(2)}) async-start(s8[5242880]{0:T(1024)(128)(4,1)} %bitcast.51), calls=%async_computation | async-start | bytes 2097152
  76.1 6.1 %collective-permute-start.19 = (bf16[2,64,1280]{2,1,0:T(8,128)(2,1)S(1)}, bf16[2,64,1280]{2,1,0:T(8,128)(2,1)S(1)}, u32[]{:S(2)}, u32[]{:S(2)}) collective-permute-start(bf16[2,64,1280]{2,1,0:T(8,128)(2,1)S(1)} %collective-permute-done.18.refs_2_), channel_id=1, source_target_pairs={{0,8},{8,0},{16,24},{24,16},{1,9},{9,1},{17,25},{25,17},{2,10},{10... | collective-permute-start | bytes 983048 | tf_op jit(solution)/shard_map/ppermute | solution.py:344
  81.6 4.0 %collective-permute-start.12 = (bf16[2,64,768]{2,1,0:T(8,128)(2,1)S(1)}, bf16[2,64,768]{2,1,0:T(8,128)(2,1)S(1)}, u32[]{:S(2)}, u32[]{:S(2)}) collective-permute-start(bf16[2,64,768]{2,1,0:T(8,128)(2,1)S(1)} %collective-permute-done.11.refs_2_), channel_id=1, source_target_pairs={{0,8},{8,0},{16,24},{24,16},{1,9},{9,1},{17,25},{25,17},{2,10},{10... | collective-permute-start | bytes 589832 | tf_op jit(solution)/shard_map/ppermute | solution.py:344
  89.2 10.1 %collective-permute-start.20 = (bf16[2,2,32,1024]{3,2,0,1:T(8,128)(2,1)S(1)}, bf16[2,2,32,1024]{3,2,0,1:T(8,128)(2,1)S(1)}, u32[]{:S(2)}, u32[]{:S(2)}) collective-permute-start(bf16[2,2,32,1024]{3,2,0,1:T(8,128)(2,1)S(1)} %fusion.2), channel_id=1, source_target_pairs={{0,1},{1,0},{2,3},{3,2},{4,5},{5,4},{6,7},{7,6},{8,9},{9,8},{10,11... | collective-permute-start | bytes 786440 | tf_op jit(solution)/shard_map/ppermute | solution.py:330
  90.9 9.2 %collective-permute-start.23 = (bf16[2,2,32,1024]{3,2,1,0:T(8,128)(2,1)S(1)}, bf16[2,2,32,1024]{3,2,1,0:T(8,128)(2,1)S(1)}, u32[]{:S(2)}, u32[]{:S(2)}) collective-permute-start(bf16[2,2,32,1024]{3,2,1,0:T(8,128)(2,1)S(1)} %fusion.3), channel_id=1, source_target_pairs={{0,2},{1,3},{2,0},{3,1},{4,6},{5,7},{6,4},{7,5},{8,10},{9,11},{10,... | collective-permute-start | bytes 786440 | tf_op jit(solution)/shard_map/ppermute | solution.py:330
  99.5 5.6 %collective-permute-start.21 = (bf16[2,32,1024]{2,1,0:T(8,128)(2,1)S(1)}, bf16[2,32,1024]{2,1,0:T(8,128)(2,1)S(1)}, u32[]{:S(2)}, u32[]{:S(2)}) collective-permute-start(bf16[2,32,1024]{2,1,0:T(8,128)(2,1)S(1)} %fusion.6), channel_id=1, source_target_pairs={{0,2},{1,3},{2,0},{3,1},{4,6},{5,7},{6,4},{7,5},{8,10},{9,11},{10,... | collective-permute-start | bytes 393224 | tf_op jit(solution)/shard_map/ppermute | solution.py:330
  100.1 7.7 %collective-permute-start.24 = (bf16[2,32,1024]{2,1,0:T(8,128)(2,1)S(1)}, bf16[2,32,1024]{2,1,0:T(8,128)(2,1)S(1)}, u32[]{:S(2)}, u32[]{:S(2)}) collective-permute-start(bf16[2,32,1024]{2,1,0:T(8,128)(2,1)S(1)} %fusion.7), channel_id=1, source_target_pairs={{0,1},{1,0},{2,3},{3,2},{4,5},{5,4},{6,7},{7,6},{8,9},{9,8},{10,11... | collective-permute-start | bytes 393224 | tf_op jit(solution)/shard_map/ppermute | solution.py:330
  105.2 7.3 %collective-permute-start.22 = (bf16[32,1024]{1,0:T(8,128)(2,1)S(1)}, bf16[32,1024]{1,0:T(8,128)(2,1)S(1)}, u32[]{:S(2)}, u32[]{:S(2)}) collective-permute-start(bf16[32,1024]{1,0:T(8,128)(2,1)S(1)} %fusion.10), channel_id=1, source_target_pairs={{0,4},{1,5},{2,6},{3,7},{4,0},{5,1},{6,2},{7,3},{8,12},{9,13},{10,... | collective-permute-start | bytes 196616 | tf_op jit(solution)/shard_map/ppermute | solution.py:330
  107.9 5.3 %collective-permute-start.25 = (bf16[32,1024]{1,0:T(8,128)(2,1)S(1)}, bf16[32,1024]{1,0:T(8,128)(2,1)S(1)}, u32[]{:S(2)}, u32[]{:S(2)}) collective-permute-start(bf16[32,1024]{1,0:T(8,128)(2,1)S(1)} %fusion.11), channel_id=1, source_target_pairs={{0,4},{1,5},{2,6},{3,7},{4,0},{5,1},{6,2},{7,3},{8,12},{9,13},{10,... | collective-permute-start | bytes 196616 | tf_op jit(solution)/shard_map/ppermute | solution.py:330
  (16 other events, 34.8 us)

commit v5 on v4

--- a/solution.py
+++ b/solution.py
@@ -9,9 +9,9 @@
 
 BF16 = jnp.bfloat16
 F32 = jnp.float32
-VMEM_BYTES = 8 * 1024 * 1024
+VMEM_BYTES = 16 * 1024 * 1024
 SHARES = (2, 4, 5, 3)
-SLOTS = 4
+SLOTS = 3
 COST = 40
 WHOLE = pl.BlockSpec(memory_space=pltpu.VMEM)
 REMOTE = pl.BlockSpec(memory_space=pl.ANY)
@@ -51,34 +51,34 @@
 
 def forward_kernel(layout, ins, outs, *refs):
     quarters, rows, block, start, count, following, first = layout
-    given, made, (total, sems, x_sem) = refs[:ins], refs[ins : ins + outs], refs[ins + outs :]
+    given, made = refs[:ins], refs[ins : ins + outs]
+    weights, total, sems, x_sem = refs[ins + outs :]
     sources = given[1:3]
     own_ref, far_ref, send_ref, *made = made
     x_ref, early = given[0], given[3:5]
-    folds = []
     if first:
         x_copy = pltpu.make_async_copy(x_ref, made[0], x_sem)
         x_copy.start()
         x_ref, made = made[0], made[1:]
-    weights, ahead = made[:2], made[2:]
+    slots = weights.shape[1]
     queue = [
         [
             pltpu.make_async_copy(
                 source.at[:, pl.ds((start + j) * block, block)],
-                target.at[:, pl.ds(j * block, block)],
-                sems.at[k, j],
+                weights.at[k, j % slots],
+                sems.at[k, j % slots],
             )
-            for k, (source, target) in enumerate(zip(sources, weights))
+            for k, source in enumerate(sources)
         ]
         for j in range(0 if first else 1, count)
     ]
-    if ahead:
+    if made:
         queue.append(
             [
                 pltpu.make_async_copy(
-                    source.at[:, pl.ds(following * block, block)], target, sems.at[k, count]
+                    source.at[:, pl.ds(following * block, block)], target, sems.at[k, slots]
                 )
-                for k, (source, target) in enumerate(zip(sources, ahead))
+                for k, (source, target) in enumerate(zip(sources, made))
             ]
         )
     for pair in queue[:2]:
@@ -86,13 +86,6 @@
             copy.start()
     if first:
         x_copy.wait()
-    else:
-        folds = [
-            pltpu.make_async_copy(early[k], weights[k].at[:, pl.ds(0, block)], sems.at[k, 0])
-            for k in range(2)
-        ]
-        for copy in folds:
-            copy.start()
     outer = quarters // 2
     me = lax.axis_index("row")
     place, core = me // 2, me % 2
@@ -106,7 +99,7 @@
             taken += 1
             for copy in queue[taken + 1] if taken + 1 < len(queue) else []:
                 copy.start()
-            blocks = [ref[:, at] for ref in weights]
+            blocks = [weights[k, j % slots] for k in range(2)]
         else:
             blocks = [ref[...] for ref in early]
         for k in range(2):
@@ -122,8 +115,6 @@
                 else:
                     far_ref[step - 1, k, :, at] = kept
                 send_ref[step, k, :, at] = total[k, pl.ds(other, rows), :].astype(BF16)
-    for copy in folds:
-        copy.wait()
     for pair in queue[taken:]:
         for copy in pair:
             copy.wait()
@@ -144,7 +135,6 @@
     if first:
         x = in_hbm(x)
         out_shape.append(pltpu.VMEM(x.shape, BF16))
-    out_shape += [pltpu.VMEM((depth, width), BF16)] * 2
     if following is not None:
         out_shape += [pltpu.VMEM((depth, block), BF16)] * 2
     args = (x, in_hbm(gate_weight), in_hbm(up_weight), *early, *after)
@@ -158,8 +148,9 @@
         [WHOLE] * len(out_shape),
         out_shape,
         [
+            pltpu.VMEM((2, SLOTS, depth, block), BF16),
             pltpu.VMEM((2, tokens, block), F32),
-            pltpu.SemaphoreType.DMA((2, count + 1)),
+            pltpu.SemaphoreType.DMA((2, SLOTS + 1)),
             pltpu.SemaphoreType.DMA,
         ],
         tokens * depth * width,
@@ -206,13 +197,29 @@
     )
 
 
-def input_kernel(quarters, rows, first, last, skipped, gate_ref, up_ref, *refs):
+def input_kernel(quarters, rows, columns, first, last, skipped, gate_ref, up_ref, *refs):
     pieces, rest = refs[:quarters], refs[quarters + skipped :]
     earlier = []
     if not first:
         count = 2 if last else 1
         earlier, rest = rest[:count], rest[count:]
-    *sums, grads = rest
+    *sums, grads, weights, sems = rest
+    depth, deep = gate_ref.shape[0], weights.shape[2]
+    slots = weights.shape[1]
+    queue = [
+        [
+            pltpu.make_async_copy(
+                source.at[pl.ds(d * deep, deep), columns],
+                weights.at[k, d % slots],
+                sems.at[k, d % slots],
+            )
+            for k, source in enumerate((gate_ref, up_ref))
+        ]
+        for d in range(depth // deep)
+    ]
+    for pair in queue[: slots - 1]:
+        for copy in pair:
+            copy.start()
     outer = quarters // 2
     me = lax.axis_index("row")
     place, core = me // 2, me % 2
@@ -222,50 +229,57 @@
         at = pl.multiple_of((there + (core + swap) % 2) * rows, rows)
         for k in range(2):
             grads[k, pl.ds(at, rows), :] = piece[k]
-    weights = (gate_ref, up_ref)
-    deep = 256 if gate_ref.shape[0] % 512 == 0 else 128
-    if last:
-        dims = (((1,), (1,)), ((), ()))
-        half = sums[0].shape[1]
-        for d in range(gate_ref.shape[0] // deep):
-            index, at = d * deep // half, slice(d * deep % half, d * deep % half + deep)
-            term = None if first else earlier[index][:, at]
-            for k in range(2):
-                piece = weights[k][d * deep : (d + 1) * deep, :]
+    dims = (((1,), (1,)), ((), ()))
+    flipped = [] if last else [grads[k].T for k in range(2)]
+    half = depth // 2
+    for d, pair in enumerate(queue):
+        for copy in pair:
+            copy.wait()
+        for copy in queue[d + slots - 1] if d + slots - 1 < len(queue) else []:
+            copy.start()
+        at = slice(d * deep, (d + 1) * deep)
+        index, across = d * deep // half, slice(d * deep % half, d * deep % half + deep)
+        term = None
+        if not first:
+            term = earlier[index][:, across] if last else earlier[0][at, :]
+        for k in range(2):
+            piece = weights[k, d % slots]
+            if last:
                 product = lax.dot_general(grads[k], piece, dims, preferred_element_type=F32)
-                term = product if term is None else term + product
-            sums[index][:, at] = term
-        return
-    flipped = [grads[k].T for k in range(2)]
-    for d in range(gate_ref.shape[0] // deep):
-        at = slice(d * deep, (d + 1) * deep)
-        term = None if first else earlier[0][at, :]
-        for k in range(2):
-            product = jnp.dot(weights[k][at, :], flipped[k], preferred_element_type=F32)
+            else:
+                product = jnp.dot(piece, flipped[k], preferred_element_type=F32)
             term = product if term is None else term + product
-        if len(sums) == 1:
+        if last:
+            sums[index][:, across] = term
+        elif len(sums) == 1:
             sums[0][at, :] = term
         else:
-            half = sums[0].shape[1]
-            sums[d * deep // half][:, d * deep % half : d * deep % half + deep] = term.T
-
-
-def input_part(quarters, held, pieces, acc, final, after):
-    depth, width = held[0].shape
+            sums[index][:, across] = term.T
+
+
+def input_part(quarters, block, chunk, gate_weight, up_weight, pieces, acc, final, after):
+    depth = gate_weight.shape[0]
     rows = pieces[0].shape[1]
     tokens = rows * quarters
+    start, count = chunk
+    width = count * block
+    deep = 256 if depth % 512 == 0 else 128
     first, last = acc is None, final == 0
-    args = [*held, *pieces, *after] + ([] if first else acc)
+    args = [in_hbm(gate_weight), in_hbm(up_weight), *pieces, *after] + ([] if first else acc)
     sums = [jax.ShapeDtypeStruct((depth, tokens), F32)]
     if final <= 1:
         sums = [jax.ShapeDtypeStruct((tokens, depth // 2), F32)] * 2
+    columns = pl.ds(start * block, width)
     *acc, grads = call(
-        functools.partial(input_kernel, quarters, rows, first, last, len(after)),
+        functools.partial(input_kernel, quarters, rows, columns, first, last, len(after)),
         "input_part",
-        [WHOLE] * (2 + quarters) + [REMOTE] * len(after) + [WHOLE] * (0 if first else len(acc)),
+        [REMOTE] * 2
+        + [WHOLE] * quarters
+        + [REMOTE] * len(after)
+        + [WHOLE] * (0 if first else len(acc)),
         [WHOLE] * (len(sums) + 1),
         sums + [jax.ShapeDtypeStruct((2, tokens, width), BF16)],
-        [],
+        [pltpu.VMEM((2, SLOTS, deep, width), BF16), pltpu.SemaphoreType.DMA((2, SLOTS))],
         tokens * depth * width,
         args,
     )
@@ -354,14 +368,13 @@
         )
         if i == 0:
             x, loaded = loaded[0], loaded[1:]
-        weights.append(loaded[:2])
         got = sibling(send)
         near = [(far[step - 1] + got[step].astype(F32)).astype(BF16) for step in range(1, outer)]
         owns.append(own)
         gots.append(got)
         sums.append(near)
         crossed.append([across(value, step + 1) for step, value in enumerate(near)])
-        return x, loaded[2:]
+        return x, loaded
 
     def middle(i, hidden, after):
         start, count = chunks[i]
@@ -376,7 +389,7 @@
         pieces.append(group)
         return hidden
 
-    weights, owns, gots, sums, crossed, pieces = [], [], [], [], [], []
+    owns, gots, sums, crossed, pieces = [], [], [], [], []
     number = len(chunks)
     x, early, hidden = inputs, [], None
     for i in range(number):
@@ -396,8 +409,10 @@
     acc, state = None, []
     grads = []
     for i in range(number):
-        after = state[:1] if i == number - 1 else []
-        acc, whole = input_part(quarters, weights[i], pieces[i], acc, number - 1 - i, after)
+        after = [in_hbm(value) for value in state[:1]] if i == number - 1 else []
+        acc, whole = input_part(
+            quarters, block, chunks[i], gate_weight, up_weight, pieces[i], acc, number - 1 - i, after
+        )
         grads.append(whole)
         if i < number - 2:
             state = weight_part(block, *chunks[i], full, xt, whole, state, [])

time: 114 us -> 127 us (1.11)
  Pallas kernels: 48.2 us -> 69.6 us
  local copies, waits for them, and re-layouts: 18.2 us -> 7.51 us
  starting transfers between devices: 17.8 us -> 19.2 us
    pallas_call x16, Pallas kernels: 48.2 us -> 69.6 us  [call(): pl.pallas_call(kernel, in_specs=in_specs, out_specs=out_specs, out_shape=...]
    unnamed x44 -> x20, local copies, waits for them, and re-layouts: 17.5 us -> 6.62 us
    ppermute x8, starting transfers between devices: 7.89 us -> 9.33 us  [across(): return lax.ppermute(value, 'row', moves)]
  transfers between devices with their start and end apart: 26 -> 26, of which waited for: 7 -> 6; matrix products, arithmetic and copies ran while one was open for 2% -> 2% of each run, Pallas kernels for 36% -> 47%
where the time goes in v5:
time: 127 us
  Pallas kernels  69.6 us (55%)
  waiting for transfers between devices  27.3 us (21%)
  starting transfers between devices  19.2 us (15%)
  local copies, waits for them, and re-layouts  7.51 us (6%)
  other arithmetic  2 us (2%)
    pallas_call x16, Pallas kernels, call(): pl.pallas_call(kernel, in_specs=in_specs, out_specs=out_specs, out_shape=...  69.6 us
    ppermute x8, waiting for transfers between devices, across(): return lax.ppermute(value, 'row', moves)  22.4 us
    ppermute x8, starting transfers between devices, across(): return lax.ppermute(value, 'row', moves)  9.33 us
    ppermute x6, starting transfers between devices, token_sums(): got.append(lax.ppermute(send.astype(BF16), 'col', moves))  7.3 us
    unnamed x20, local copies, waits for them, and re-layouts  6.62 us
    ppermute x6, waiting for transfers between devices, token_sums(): got.append(lax.ppermute(send.astype(BF16), 'col', moves))  4.92 us
    ppermute x12, starting transfers between devices, sibling(): return lax.ppermute(value, 'row', swap)  2.6 us
  transfers between devices with their start and end apart: 26, of which 6 were waited for; matrix products, arithmetic and copies ran while one was open for 2% of the time, Pallas kernels for 47%

profile of v5, /device:TPU:0, one launch (start us, length us, event | category | flops | bytes accessed | tf_op | source)
XLA Modules:
  0.0 126.8 jit_solution(7543384204488186317)
XLA Ops:
  0.6 4.7 %forward_part.4 = (f32[2,64,512]{2,1,0:T(8,128)S(1)}, f32[1,2,64,512]{3,2,1,0:T(8,128)S(1)}, bf16[2,2,64,512]{3,2,1,0:T(8,128)(2,1)}, bf16[256,2048]{1,0:T(8,128...) custom-call(bf16[256,2048]{1,0:T(8,128)(2,1)} %refs_0_.1, bf16[2048,3584]{1,0:T(8,128)(2,1)} %gate_ref.7, ...), custom_call_target="tpu_custom_call" | custom-call | flops 10737418240 | bytes 268435456 | tf_op jit(solution)/shard_map/forward_part/pallas_call | solution.py:33
  7.3 5.1 %forward_part.5 = (f32[2,64,1024]{2,1,0:T(8,128)S(1)}, f32[1,2,64,1024]{3,2,1,0:T(8,128)S(1)}, bf16[2,2,64,1024]{3,2,1,0:T(8,128)(2,1)}, bf16[2048,256]{1,0:T(8,128)(2,1)S(1)}, bf16[2048,256]{1,0:T(8,128)(2,1)S(1)}) custom-call(bf16[256,2048]{1,0:T(8,128)(2,1)S(1)} %get-tuple-element.49.refs_0_, bf16[2048,3584]{1,0:T(8,128)(2,1)} %gate_ref.7, ...), custom_call_target="tpu_custom_call" | custom-call | flops 21474836480 | bytes 536870912 | tf_op jit(solution)/shard_map/forward_part/pallas_call | solution.py:33
  12.4 0.8 copy-done.1
  13.2 1.0 copy-done.6
  14.2 1.0 copy-done.8
  16.0 1.0 fusion.5.refs_5_
  16.9 3.0 %collective-permute-start.2 = (bf16[2,64,512]{2,1,0:T(8,128)(2,1)S(1)}, bf16[2,64,512]{2,1,0:T(8,128)(2,1)S(1)}, u32[]{:S(2)}, u32[]{:S(2)}) collective-permute-start(bf16[2,64,512]{2,1,0:T(8,128)(2,1)S(1)} %fusion.5.refs_5_), channel_id=1, source_target_pairs={{0,16},{8,24},{16,0},{24,8},{1,17},{9,25},{17,1},{25,9},{2,18},{10... | collective-permute-start | bytes 393224 | tf_op jit(solution)/shard_map/ppermute | solution.py:362
  19.9 1.2 copy-done.7
  21.2 1.2 copy-done.9
  22.4 5.5 %forward_part.6 = (f32[2,64,1280]{2,1,0:T(8,128)S(1)}, f32[1,2,64,1280]{3,2,1,0:T(8,128)S(1)}, bf16[2,2,64,1280]{3,2,1,0:T(8,128)(2,1)S(1)}, bf16[2048,256]{1,0:T(8,128)(2,1)S(1)}, bf16[2048,256]{1,0:T(8,128)(2,1)S(1)}) custom-call(bf16[256,2048]{1,0:T(8,128)(2,1)S(1)} %get-tuple-element.49.refs_0_, bf16[2048,3584]{1,0:T(8,128)(2,1)} %gate_ref.7, ...), custom_call_target="tpu_custom_call" | custom-call | flops 26843545600 | bytes 671088640 | tf_op jit(solution)/shard_map/forward_part/pallas_call | solution.py:33
  28.8 2.1 %collective-permute-start.5 = (bf16[2,64,1024]{2,1,0:T(8,128)(2,1)S(1)}, bf16[2,64,1024]{2,1,0:T(8,128)(2,1)S(1)}, u32[]{:S(2)}, u32[]{:S(2)}) collective-permute-start(bf16[2,64,1024]{2,1,0:T(8,128)(2,1)S(1)} %fusion.1.refs_5_), channel_id=1, source_target_pairs={{0,16},{8,24},{16,0},{24,8},{1,17},{9,25},{17,1},{25,9},{2,18},{10... | collective-permute-start | bytes 786440 | tf_op jit(solution)/shard_map/ppermute | solution.py:362
  30.8 4.2 %collective-permute-done.9.refs_1_.refs_2_ = bf16[2,64,512]{2,1,0:T(8,128)(2,1)S(1)} collective-permute-done((bf16[2,64,512]{2,1,0:T(8,128)(2,1)S(1)}, bf16[2,64,512]{2,1,0:T(8,128)(2,1)S(1)}, u32[]{:S(2)}, u32[]{:S(2)}) %collective-permute-start.9) | collective-permute-done | bytes 131104 | tf_op jit(solution)/shard_map/ppermute | solution.py:362
  35.0 3.6 %forward_part.7 = (f32[2,64,768]{2,1,0:T(8,128)S(1)}, f32[1,2,64,768]{3,2,1,0:T(8,128)S(1)}, bf16[2,2,64,768]{3,2,1,0:T(8,128)(2,1)S(1)}) custom-call(bf16[256,2048]{1,0:T(8,128)(2,1)S(1)} %get-tuple-element.49.refs_0_, bf16[2048,3584]{1,0:T(8,128)(2,1)} %gate_ref.7, bf16[2048,3584]{1,0:T(8,128)(2,1)} %up_ref.7, ...), custom_call_target="tpu_custom_call" | custom-call | flops 16106127360 | bytes 402653184 | tf_op jit(solution)/shard_map/forward_part/pallas_call | solution.py:33
  39.3 5.2 %input_part.4 = (f32[2048,256]{1,0:T(8,128)S(1)}, bf16[2,256,512]{2,1,0:T(8,128)(2,1)S(1)}) custom-call(bf16[2048,3584]{1,0:T(8,128)(2,1)} %gate_ref.7, bf16[2048,3584]{1,0:T(8,128)(2,1)} %up_ref.7, bf16[2,64,512]{2,1,0:T(8,128)(2,1)S(1)} %get-tuple-element.61.refs_6_.refs_0_, bf16[2,64,512]{2,1,0:T(8,128)(2,1)S(1)} %collective-permute-done.15.refs_1_, ...), custom_call_target="tpu_custom_call" | custom-call | flops 10737418240 | bytes 268435456 | tf_op jit(solution)/shard_map/input_part/pallas_call | solution.py:33
  44.9 2.1 %collective-permute-start.4 = (bf16[2,64,768]{2,1,0:T(8,128)(2,1)S(1)}, bf16[2,64,768]{2,1,0:T(8,128)(2,1)S(1)}, u32[]{:S(2)}, u32[]{:S(2)}) collective-permute-start(bf16[2,64,768]{2,1,0:T(8,128)(2,1)S(1)} %fusion.4), channel_id=1, source_target_pairs={{0,16},{8,24},{16,0},{24,8},{1,17},{9,25},{17,1},{25,9},{2,18},{10... | collective-permute-start | bytes 589832 | tf_op jit(solution)/shard_map/ppermute | solution.py:362
  47.1 6.8 %collective-permute-done.6.refs_1_.refs_2_ = bf16[2,64,1024]{2,1,0:T(8,128)(2,1)S(1)} collective-permute-done((bf16[2,64,1024]{2,1,0:T(8,128)(2,1)S(1)}, bf16[2,64,1024]{2,1,0:T(8,128)(2,1)S(1)}, u32[]{:S(2)}, u32[]{:S(2)}) %collective-permute-start.6) | collective-permute-done | bytes 262176 | tf_op jit(solution)/shard_map/ppermute | solution.py:362
  54.0 3.4 %weight_part.4 = (bf16[2048,3584]{1,0:T(8,128)(2,1)}, bf16[2048,3584]{1,0:T(8,128)(2,1)}) custom-call(bf16[2048,256]{1,0:T(8,128)(2,1)S(1)} %bitcast.43, bf16[2,256,512]{2,1,0:T(8,128)(2,1)S(1)} %get-tuple-element.77.grads_ref), custom_call_target="tpu_custom_call" | custom-call | flops 10737418240 | bytes 268435456 | tf_op jit(solution)/shard_map/weight_part/pallas_call | solution.py:33
  57.3 7.4 %collective-permute-done.8.refs_0_ = bf16[2,64,1280]{2,1,0:T(8,128)(2,1)S(1)} collective-permute-done((bf16[2,64,1280]{2,1,0:T(8,128)(2,1)S(1)}, bf16[2,64,1280]{2,1,0:T(8,128)(2,1)S(1)}, u32[]{:S(2)}, u32[]{:S(2)}) %collective-permute-start.8) | collective-permute-done | bytes 327712 | tf_op jit(solution)/shard_map/ppermute | solution.py:362
  65.0 0.9 middle_part.7
  66.2 1.8 %collective-permute-start.18 = (bf16[2,64,1280]{2,1,0:T(8,128)(2,1)S(1)}, bf16[2,64,1280]{2,1,0:T(8,128)(2,1)S(1)}, u32[]{:S(2)}, u32[]{:S(2)}) collective-permute-start(bf16[2,64,1280]{2,1,0:T(8,128)(2,1)S(1)} %get-tuple-element.81.refs_0_), channel_id=1, source_target_pairs={{0,16},{8,24},{16,0},{24,8},{1,17},{9,25},{17,1},{25,9},{2,18},{10... | collective-permute-start | bytes 983048 | tf_op jit(solution)/shard_map/ppermute | solution.py:362
  68.2 7.2 %input_part.5 = (f32[2048,256]{1,0:T(8,128)S(1)}, bf16[2,256,1024]{2,1,0:T(8,128)(2,1)S(1)}) custom-call(bf16[2048,3584]{1,0:T(8,128)(2,1)} %gate_ref.7, bf16[2048,3584]{1,0:T(8,128)(2,1)} %up_ref.7, bf16[2,64,1024]{2,1,0:T(8,128)(2,1)S(1)} %get-tuple-element.67.refs_0_, bf16[2,64,1024]{2,1,0:T(8,128)(2,1)S(1)} %collective-permute-done.13.refs_1_, ...), custom_call_target="tpu_custom_call" | custom-call | flops 21474836480 | bytes 536870912 | tf_op jit(solution)/shard_map/input_part/pallas_call | solution.py:33
  75.4 4.0 %collective-permute-done.18.refs_2_ = bf16[2,64,1280]{2,1,0:T(8,128)(2,1)S(1)} collective-permute-done((bf16[2,64,1280]{2,1,0:T(8,128)(2,1)S(1)}, bf16[2,64,1280]{2,1,0:T(8,128)(2,1)S(1)}, u32[]{:S(2)}, u32[]{:S(2)}) %collective-permute-start.18) | collective-permute-done | bytes 327712 | tf_op jit(solution)/shard_map/ppermute | solution.py:362
  79.4 6.1 %weight_part.5 = (bf16[2048,3584]{1,0:T(8,128)(2,1)}, bf16[2048,3584]{1,0:T(8,128)(2,1)}) custom-call(bf16[2048,256]{1,0:T(8,128)(2,1)S(1)} %bitcast.44, bf16[2,256,1024]{2,1,0:T(8,128)(2,1)S(1)} %get-tuple-element.76.grads_ref, bf16[2048,3584]{1,0:T(8,128)(2,1)} %get-tuple-element.78.refs_0_, ...), custom_call_target="tpu_custom_call", output_to_operand_aliasing={{0}: (2, {}), {1}: (3, {})} | custom-call | flops 21474836480 | bytes 536870912 | tf_op jit(solution)/shard_map/weight_part/pallas_call | solution.py:33
  86.2 8.8 %input_part.6 = (f32[256,1024]{1,0:T(8,128)S(1)}, f32[256,1024]{1,0:T(8,128)S(1)}, bf16[2,256,1280]{2,1,0:T(8,128)(2,1)S(1)}) custom-call(bf16[2048,3584]{1,0:T(8,128)(2,1)} %gate_ref.7, bf16[2048,3584]{1,0:T(8,128)(2,1)} %up_ref.7, bf16[2,64,1280]{2,1,0:T(8,128)(2,1)S(1)} %get-tuple-element.81.refs_0_, ...), custom_call_target="tpu_custom_call" | custom-call | flops 26843545600 | bytes 671088640 | tf_op jit(solution)/shard_map/input_part/pallas_call | solution.py:33
  94.9 5.9 %input_part.7 = (f32[256,1024]{1,0:T(8,128)S(1)}, f32[256,1024]{1,0:T(8,128)S(1)}, bf16[2,256,768]{2,1,0:T(8,128)(2,1)S(1)}) custom-call(bf16[2048,3584]{1,0:T(8,128)(2,1)} %gate_ref.7, bf16[2048,3584]{1,0:T(8,128)(2,1)} %up_ref.7, bf16[2,64,768]{2,1,0:T(8,128)(2,1)S(1)} %get-tuple-element.74.refs_0_, ...), custom_call_target="tpu_custom_call" | custom-call | flops 16106127360 | bytes 402653184 | tf_op jit(solution)/shard_map/input_part/pallas_call | solution.py:33
  100.9 1.6 %collective-permute-start.23 = (bf16[2,2,32,1024]{3,2,1,0:T(8,128)(2,1)S(1)}, bf16[2,2,32,1024]{3,2,1,0:T(8,128)(2,1)S(1)}, u32[]{:S(2)}, u32[]{:S(2)}) collective-permute-start(bf16[2,2,32,1024]{3,2,1,0:T(8,128)(2,1)S(1)} %fusion.3), channel_id=1, source_target_pairs={{0,2},{1,3},{2,0},{3,1},{4,6},{5,7},{6,4},{7,5},{8,10},{9,11},{10,... | collective-permute-start | bytes 786440 | tf_op jit(solution)/shard_map/ppermute | solution.py:344
  102.6 1.6 %collective-permute-start.20 = (bf16[2,2,32,1024]{3,2,0,1:T(8,128)(2,1)S(1)}, bf16[2,2,32,1024]{3,2,0,1:T(8,128)(2,1)S(1)}, u32[]{:S(2)}, u32[]{:S(2)}) collective-permute-start(bf16[2,2,32,1024]{3,2,0,1:T(8,128)(2,1)S(1)} %fusion.2), channel_id=1, source_target_pairs={{0,1},{1,0},{2,3},{3,2},{4,5},{5,4},{6,7},{7,6},{8,9},{9,8},{10,11... | collective-permute-start | bytes 786440 | tf_op jit(solution)/shard_map/ppermute | solution.py:344
  104.2 7.8 %weight_part.6 = (bf16[2048,3584]{1,0:T(8,128)(2,1)}, bf16[2048,3584]{1,0:T(8,128)(2,1)}) custom-call(bf16[2048,256]{1,0:T(8,128)(2,1)S(1)} %bitcast.45, bf16[2,256,1280]{2,1,0:T(8,128)(2,1)S(1)} %get-tuple-element.88.grads_ref, f32[256,1024]{1,0:T(8,128)S(1)} %get-tuple-element.85.refs_0_, ...), custom_call_target="tpu_custom_call", output_to_operand_aliasing={{0}: (4, {}), {1}: (5, {})} | custom-call | flops 26843545600 | bytes 671088640 | tf_op jit(solution)/shard_map/weight_part/pallas_call | solution.py:33
  113.2 4.8 %weight_part.7 = (bf16[2048,3584]{1,0:T(8,128)(2,1)}, bf16[2048,3584]{1,0:T(8,128)(2,1)}) custom-call(bf16[2048,256]{1,0:T(8,128)(2,1)S(1)} %bitcast.46, bf16[2,256,768]{2,1,0:T(8,128)(2,1)S(1)} %get-tuple-element.87.grads_ref, f32[2,2,32,1024]{3,2,1,0:T(8,128)S(1)} %copy.20.refs_0_, ...), custom_call_target="tpu_custom_call", output_to_operand_aliasing={{0}: (4, {}), {1}: (5, {})} | custom-call | flops 16106127360 | bytes 402653184 | tf_op jit(solution)/shard_map/weight_part/pallas_call | solution.py:33
  118.1 2.6 %collective-permute-start.25 = (bf16[32,1024]{1,0:T(8,128)(2,1)S(1)}, bf16[32,1024]{1,0:T(8,128)(2,1)S(1)}, u32[]{:S(2)}, u32[]{:S(2)}) collective-permute-start(bf16[32,1024]{1,0:T(8,128)(2,1)S(1)} %fusion.11), channel_id=1, source_target_pairs={{0,4},{1,5},{2,6},{3,7},{4,0},{5,1},{6,2},{7,3},{8,12},{9,13},{10,... | collective-permute-start | bytes 196616 | tf_op jit(solution)/shard_map/ppermute | solution.py:344
  121.2 2.5 %collective-permute-done.25 = bf16[32,1024]{1,0:T(8,128)(2,1)S(1)} collective-permute-done((bf16[32,1024]{1,0:T(8,128)(2,1)S(1)}, bf16[32,1024]{1,0:T(8,128)(2,1)S(1)}, u32[]{:S(2)}, u32[]{:S(2)}) %collective-permute-start.25) | collective-permute-done | bytes 65568 | tf_op jit(solution)/shard_map/ppermute | solution.py:344
  123.7 2.4 %collective-permute-done.22 = bf16[32,1024]{1,0:T(8,128)(2,1)S(1)} collective-permute-done((bf16[32,1024]{1,0:T(8,128)(2,1)S(1)}, bf16[32,1024]{1,0:T(8,128)(2,1)S(1)}, u32[]{:S(2)}, u32[]{:S(2)}) %collective-permute-start.22) | collective-permute-done | bytes 65568 | tf_op jit(solution)/shard_map/ppermute | solution.py:344
  (75 shorter events, 8.5 us)
Async XLA Ops:
  6.8 9.1 %collective-permute-start = (bf16[2,2,64,512]{3,2,1,0:T(8,128)(2,1)}, bf16[2,2,64,512]{3,2,1,0:T(8,128)(2,1)S(1)}, u32[]{:S(2)}, u32[]{:S(2)}) collective-permute-start(bf16[2,2,64,512]{3,2,1,0:T(8,128)(2,1)} %get-tuple-element.55), channel_id=1, source_target_pairs={{0,8},{8,0},{16,24},{24,16},{1,9},{9,1},{17,25},{25,17},{2,10},{10... | collective-permute-start | bytes 786440 | tf_op jit(solution)/shard_map/ppermute | solution.py:358
  13.2 1.0 copy-start.6
  15.1 13.6 %collective-permute-start.1 = (bf16[2,2,64,1024]{3,2,1,0:T(8,128)(2,1)}, bf16[2,2,64,1024]{3,2,1,0:T(8,128)(2,1)S(1)}, u32[]{:S(2)}, u32[]{:S(2)}) collective-permute-start(bf16[2,2,64,1024]{3,2,1,0:T(8,128)(2,1)} %get-tuple-element.59), channel_id=1, source_target_pairs={{0,8},{8,0},{16,24},{24,16},{1,9},{9,1},{17,25},{25,17},{2,10},{10... | collective-permute-start | bytes 1572872 | tf_op jit(solution)/shard_map/ppermute | solution.py:358
  16.9 11.1 %collective-permute-start.2 = (bf16[2,64,512]{2,1,0:T(8,128)(2,1)S(1)}, bf16[2,64,512]{2,1,0:T(8,128)(2,1)S(1)}, u32[]{:S(2)}, u32[]{:S(2)}) collective-permute-start(bf16[2,64,512]{2,1,0:T(8,128)(2,1)S(1)} %fusion.5.refs_5_), channel_id=1, source_target_pairs={{0,16},{8,24},{16,0},{24,8},{1,17},{9,25},{17,1},{25,9},{2,18},{10... | collective-permute-start | bytes 393224 | tf_op jit(solution)/shard_map/ppermute | solution.py:362
  19.9 1.2 copy-start.7
  21.2 1.2 copy-start.9
  22.4 5.6 %copy-start = (bf16[64,3584]{1,0:T(8,128)(2,1)S(1)}, bf16[64,3584]{1,0:T(8,128)(2,1)}, u32[]{:S(2)}) copy-start(bf16[64,3584]{1,0:T(8,128)(2,1)} %upstream_ref.7) | copy-start | bytes 1376260
  22.4 5.6 %copy-start.4 = (f32[2,64,512]{2,1,0:T(8,128)S(1)}, f32[2,64,512]{2,1,0:T(8,128)}, u32[]{:S(2)}) copy-start(f32[2,64,512]{2,1,0:T(8,128)} %copy-done.3) | copy-start | bytes 786436
  22.4 6.3 %copy-start.2 = (f32[1,2,64,1024]{3,2,1,0:T(8,128)S(1)}, f32[1,2,64,1024]{3,2,1,0:T(8,128)}, u32[]{:S(2)}) copy-start(f32[1,2,64,1024]{3,2,1,0:T(8,128)} %copy-done.1) | copy-start | bytes 1572868
  27.9 19.1 %collective-permute-start.7 = (bf16[2,2,64,1280]{3,2,1,0:T(8,128)(2,1)S(1)}, bf16[2,2,64,1280]{3,2,1,0:T(8,128)(2,1)S(1)}, u32[]{:S(2)}, u32[]{:S(2)}) collective-permute-start(bf16[2,2,64,1280]{3,2,1,0:T(8,128)(2,1)S(1)} %get-tuple-element.69), channel_id=1, source_target_pairs={{0,8},{8,0},{16,24},{24,16},{1,9},{9,1},{17,25},{25,17},{2,10},{10... | collective-permute-start | bytes 1966088 | tf_op jit(solution)/shard_map/ppermute | solution.py:358
  28.1 11.1 %collective-permute-start.15 = (bf16[2,64,512]{2,1,0:T(8,128)(2,1)S(1)}, bf16[2,64,512]{2,1,0:T(8,128)(2,1)S(1)}, u32[]{:S(2)}, u32[]{:S(2)}) collective-permute-start(bf16[2,64,512]{2,1,0:T(8,128)(2,1)S(1)} %get-tuple-element.61.refs_6_.refs_0_), channel_id=1, source_target_pairs={{0,8},{8,0},{16,24},{24,16},{1,9},{9,1},{17,25},{25,17},{2,10},{10... | collective-permute-start | bytes 393224 | tf_op jit(solution)/shard_map/ppermute | solution.py:358
  28.7 6.4 %collective-permute-start.9 = (bf16[2,64,512]{2,1,0:T(8,128)(2,1)S(1)}, bf16[2,64,512]{2,1,0:T(8,128)(2,1)S(1)}, u32[]{:S(2)}, u32[]{:S(2)}) collective-permute-start(bf16[2,64,512]{2,1,0:T(8,128)(2,1)S(1)} %get-tuple-element.61.refs_6_.refs_0_), channel_id=1, source_target_pairs={{0,16},{8,24},{16,0},{24,8},{1,17},{9,25},{17,1},{25,9},{2,18},{10... | collective-permute-start | bytes 393224 | tf_op jit(solution)/shard_map/ppermute | solution.py:362
  28.8 15.7 %collective-permute-start.5 = (bf16[2,64,1024]{2,1,0:T(8,128)(2,1)S(1)}, bf16[2,64,1024]{2,1,0:T(8,128)(2,1)S(1)}, u32[]{:S(2)}, u32[]{:S(2)}) collective-permute-start(bf16[2,64,1024]{2,1,0:T(8,128)(2,1)S(1)} %fusion.1.refs_5_), channel_id=1, source_target_pairs={{0,16},{8,24},{16,0},{24,8},{1,17},{9,25},{17,1},{25,9},{2,18},{10... | collective-permute-start | bytes 786440 | tf_op jit(solution)/shard_map/ppermute | solution.py:362
  35.0 4.2 %collective-permute-start.16 = (bf16[2,64,512]{2,1,0:T(8,128)(2,1)S(1)}, bf16[2,64,512]{2,1,0:T(8,128)(2,1)S(1)}, u32[]{:S(2)}, u32[]{:S(2)}) collective-permute-start(bf16[2,64,512]{2,1,0:T(8,128)(2,1)S(1)} %collective-permute-done.9.refs_1_.refs_2_), channel_id=1, source_target_pairs={{0,8},{8,0},{16,24},{24,16},{1,9},{9,1},{17,25},{25,17},{2,10},{10... | collective-permute-start | bytes 393224 | tf_op jit(solution)/shard_map/ppermute | solution.py:358
  38.7 6.2 %collective-permute-start.3 = (bf16[2,2,64,768]{3,2,1,0:T(8,128)(2,1)S(1)}, bf16[2,2,64,768]{3,2,1,0:T(8,128)(2,1)S(1)}, u32[]{:S(2)}, u32[]{:S(2)}) collective-permute-start(bf16[2,2,64,768]{3,2,1,0:T(8,128)(2,1)S(1)} %get-tuple-element.63), channel_id=1, source_target_pairs={{0,8},{8,0},{16,24},{24,16},{1,9},{9,1},{17,25},{25,17},{2,10},{10... | collective-permute-start | bytes 1179656 | tf_op jit(solution)/shard_map/ppermute | solution.py:358
  44.7 23.2 %collective-permute-start.13 = (bf16[2,64,1024]{2,1,0:T(8,128)(2,1)S(1)}, bf16[2,64,1024]{2,1,0:T(8,128)(2,1)S(1)}, u32[]{:S(2)}, u32[]{:S(2)}) collective-permute-start(bf16[2,64,1024]{2,1,0:T(8,128)(2,1)S(1)} %get-tuple-element.67.refs_0_), channel_id=1, source_target_pairs={{0,8},{8,0},{16,24},{24,16},{1,9},{9,1},{17,25},{25,17},{2,10},{10... | collective-permute-start | bytes 786440 | tf_op jit(solution)/shard_map/ppermute | solution.py:358
  44.8 9.2 %collective-permute-start.6 = (bf16[2,64,1024]{2,1,0:T(8,128)(2,1)S(1)}, bf16[2,64,1024]{2,1,0:T(8,128)(2,1)S(1)}, u32[]{:S(2)}, u32[]{:S(2)}) collective-permute-start(bf16[2,64,1024]{2,1,0:T(8,128)(2,1)S(1)} %get-tuple-element.67.refs_0_), channel_id=1, source_target_pairs={{0,16},{8,24},{16,0},{24,8},{1,17},{9,25},{17,1},{25,9},{2,18},{10... | collective-permute-start | bytes 786440 | tf_op jit(solution)/shard_map/ppermute | solution.py:362
  44.9 20.1 %collective-permute-start.4 = (bf16[2,64,768]{2,1,0:T(8,128)(2,1)S(1)}, bf16[2,64,768]{2,1,0:T(8,128)(2,1)S(1)}, u32[]{:S(2)}, u32[]{:S(2)}) collective-permute-start(bf16[2,64,768]{2,1,0:T(8,128)(2,1)S(1)} %fusion.4), channel_id=1, source_target_pairs={{0,16},{8,24},{16,0},{24,8},{1,17},{9,25},{17,1},{25,9},{2,18},{10... | collective-permute-start | bytes 589832 | tf_op jit(solution)/shard_map/ppermute | solution.py:362
  47.0 17.7 %collective-permute-start.8 = (bf16[2,64,1280]{2,1,0:T(8,128)(2,1)S(1)}, bf16[2,64,1280]{2,1,0:T(8,128)(2,1)S(1)}, u32[]{:S(2)}, u32[]{:S(2)}) collective-permute-start(bf16[2,64,1280]{2,1,0:T(8,128)(2,1)S(1)} %fusion), channel_id=1, source_target_pairs={{0,16},{8,24},{16,0},{24,8},{1,17},{9,25},{17,1},{25,9},{2,18},{10... | collective-permute-start | bytes 983048 | tf_op jit(solution)/shard_map/ppermute | solution.py:362
  54.0 14.2 %collective-permute-start.14 = (bf16[2,64,1024]{2,1,0:T(8,128)(2,1)S(1)}, bf16[2,64,1024]{2,1,0:T(8,128)(2,1)S(1)}, u32[]{:S(2)}, u32[]{:S(2)}) collective-permute-start(bf16[2,64,1024]{2,1,0:T(8,128)(2,1)S(1)} %collective-permute-done.6.refs_1_.refs_2_), channel_id=1, source_target_pairs={{0,8},{8,0},{16,24},{24,16},{1,9},{9,1},{17,25},{25,17},{2,10},{10... | collective-permute-start | bytes 786440 | tf_op jit(solution)/shard_map/ppermute | solution.py:358
  65.9 19.6 %collective-permute-start.11 = (bf16[2,64,768]{2,1,0:T(8,128)(2,1)S(1)}, bf16[2,64,768]{2,1,0:T(8,128)(2,1)S(1)}, u32[]{:S(2)}, u32[]{:S(2)}) collective-permute-start(bf16[2,64,768]{2,1,0:T(8,128)(2,1)S(1)} %get-tuple-element.74.refs_0_), channel_id=1, source_target_pairs={{0,16},{8,24},{16,0},{24,8},{1,17},{9,25},{17,1},{25,9},{2,18},{10... | collective-permute-start | bytes 589832 | tf_op jit(solution)/shard_map/ppermute | solution.py:362
  66.2 28.7 %collective-permute-start.10 = (bf16[2,64,768]{2,1,0:T(8,128)(2,1)S(1)}, bf16[2,64,768]{2,1,0:T(8,128)(2,1)S(1)}, u32[]{:S(2)}, u32[]{:S(2)}) collective-permute-start(bf16[2,64,768]{2,1,0:T(8,128)(2,1)S(1)} %get-tuple-element.74.refs_0_), channel_id=1, source_target_pairs={{0,8},{8,0},{16,24},{24,16},{1,9},{9,1},{17,25},{25,17},{2,10},{10... | collective-permute-start | bytes 589832 | tf_op jit(solution)/shard_map/ppermute | solution.py:358
  66.2 13.2 %collective-permute-start.18 = (bf16[2,64,1280]{2,1,0:T(8,128)(2,1)S(1)}, bf16[2,64,1280]{2,1,0:T(8,128)(2,1)S(1)}, u32[]{:S(2)}, u32[]{:S(2)}) collective-permute-start(bf16[2,64,1280]{2,1,0:T(8,128)(2,1)S(1)} %get-tuple-element.81.refs_0_), channel_id=1, source_target_pairs={{0,16},{8,24},{16,0},{24,8},{1,17},{9,25},{17,1},{25,9},{2,18},{10... | collective-permute-start | bytes 983048 | tf_op jit(solution)/shard_map/ppermute | solution.py:362
  68.0 18.2 %collective-permute-start.17 = (bf16[2,64,1280]{2,1,0:T(8,128)(2,1)S(1)}, bf16[2,64,1280]{2,1,0:T(8,128)(2,1)S(1)}, u32[]{:S(2)}, u32[]{:S(2)}) collective-permute-start(bf16[2,64,1280]{2,1,0:T(8,128)(2,1)S(1)} %get-tuple-element.81.refs_0_), channel_id=1, source_target_pairs={{0,8},{8,0},{16,24},{24,16},{1,9},{9,1},{17,25},{25,17},{2,10},{10... | collective-permute-start | bytes 983048 | tf_op jit(solution)/shard_map/ppermute | solution.py:358
  79.4 6.7 %collective-permute-start.19 = (bf16[2,64,1280]{2,1,0:T(8,128)(2,1)S(1)}, bf16[2,64,1280]{2,1,0:T(8,128)(2,1)S(1)}, u32[]{:S(2)}, u32[]{:S(2)}) collective-permute-start(bf16[2,64,1280]{2,1,0:T(8,128)(2,1)S(1)} %collective-permute-done.18.refs_2_), channel_id=1, source_target_pairs={{0,8},{8,0},{16,24},{24,16},{1,9},{9,1},{17,25},{25,17},{2,10},{10... | collective-permute-start | bytes 983048 | tf_op jit(solution)/shard_map/ppermute | solution.py:358
  85.6 9.4 %collective-permute-start.12 = (bf16[2,64,768]{2,1,0:T(8,128)(2,1)S(1)}, bf16[2,64,768]{2,1,0:T(8,128)(2,1)S(1)}, u32[]{:S(2)}, u32[]{:S(2)}) collective-permute-start(bf16[2,64,768]{2,1,0:T(8,128)(2,1)S(1)} %collective-permute-done.11.refs_2_), channel_id=1, source_target_pairs={{0,8},{8,0},{16,24},{24,16},{1,9},{9,1},{17,25},{25,17},{2,10},{10... | collective-permute-start | bytes 589832 | tf_op jit(solution)/shard_map/ppermute | solution.py:358
  100.9 11.2 %collective-permute-start.23 = (bf16[2,2,32,1024]{3,2,1,0:T(8,128)(2,1)S(1)}, bf16[2,2,32,1024]{3,2,1,0:T(8,128)(2,1)S(1)}, u32[]{:S(2)}, u32[]{:S(2)}) collective-permute-start(bf16[2,2,32,1024]{3,2,1,0:T(8,128)(2,1)S(1)} %fusion.3), channel_id=1, source_target_pairs={{0,2},{1,3},{2,0},{3,1},{4,6},{5,7},{6,4},{7,5},{8,10},{9,11},{10,... | collective-permute-start | bytes 786440 | tf_op jit(solution)/shard_map/ppermute | solution.py:344
  102.6 9.4 %collective-permute-start.20 = (bf16[2,2,32,1024]{3,2,0,1:T(8,128)(2,1)S(1)}, bf16[2,2,32,1024]{3,2,0,1:T(8,128)(2,1)S(1)}, u32[]{:S(2)}, u32[]{:S(2)}) collective-permute-start(bf16[2,2,32,1024]{3,2,0,1:T(8,128)(2,1)S(1)} %fusion.2), channel_id=1, source_target_pairs={{0,1},{1,0},{2,3},{3,2},{4,5},{5,4},{6,7},{7,6},{8,9},{9,8},{10,11... | collective-permute-start | bytes 786440 | tf_op jit(solution)/shard_map/ppermute | solution.py:344
  112.2 5.8 %collective-permute-start.24 = (bf16[2,32,1024]{2,1,0:T(8,128)(2,1)S(1)}, bf16[2,32,1024]{2,1,0:T(8,128)(2,1)S(1)}, u32[]{:S(2)}, u32[]{:S(2)}) collective-permute-start(bf16[2,32,1024]{2,1,0:T(8,128)(2,1)S(1)} %fusion.7), channel_id=1, source_target_pairs={{0,1},{1,0},{2,3},{3,2},{4,5},{5,4},{6,7},{7,6},{8,9},{9,8},{10,11... | collective-permute-start | bytes 393224 | tf_op jit(solution)/shard_map/ppermute | solution.py:344
  112.8 7.9 %collective-permute-start.21 = (bf16[2,32,1024]{2,1,0:T(8,128)(2,1)S(1)}, bf16[2,32,1024]{2,1,0:T(8,128)(2,1)S(1)}, u32[]{:S(2)}, u32[]{:S(2)}) collective-permute-start(bf16[2,32,1024]{2,1,0:T(8,128)(2,1)S(1)} %fusion.6), channel_id=1, source_target_pairs={{0,2},{1,3},{2,0},{3,1},{4,6},{5,7},{6,4},{7,5},{8,10},{9,11},{10,... | collective-permute-start | bytes 393224 | tf_op jit(solution)/shard_map/ppermute | solution.py:344
  118.1 5.7 %collective-permute-start.25 = (bf16[32,1024]{1,0:T(8,128)(2,1)S(1)}, bf16[32,1024]{1,0:T(8,128)(2,1)S(1)}, u32[]{:S(2)}, u32[]{:S(2)}) collective-permute-start(bf16[32,1024]{1,0:T(8,128)(2,1)S(1)} %fusion.11), channel_id=1, source_target_pairs={{0,4},{1,5},{2,6},{3,7},{4,0},{5,1},{6,2},{7,3},{8,12},{9,13},{10,... | collective-permute-start | bytes 196616 | tf_op jit(solution)/shard_map/ppermute | solution.py:344
  120.8 5.3 %collective-permute-start.22 = (bf16[32,1024]{1,0:T(8,128)(2,1)S(1)}, bf16[32,1024]{1,0:T(8,128)(2,1)S(1)}, u32[]{:S(2)}, u32[]{:S(2)}) collective-permute-start(bf16[32,1024]{1,0:T(8,128)(2,1)S(1)} %fusion.10), channel_id=1, source_target_pairs={{0,4},{1,5},{2,6},{3,7},{4,0},{5,1},{6,2},{7,3},{8,12},{9,13},{10,... | collective-permute-start | bytes 196616 | tf_op jit(solution)/shard_map/ppermute | solution.py:344
  (4 other events, 3.2 us)

commit v6 on v5

--- a/solution.py
+++ b/solution.py
@@ -9,9 +9,9 @@
 
 BF16 = jnp.bfloat16
 F32 = jnp.float32
-VMEM_BYTES = 16 * 1024 * 1024
+VMEM_BYTES = 24 * 1024 * 1024
 SHARES = (2, 4, 5, 3)
-SLOTS = 3
+SLOTS = 4
 COST = 40
 WHOLE = pl.BlockSpec(memory_space=pltpu.VMEM)
 REMOTE = pl.BlockSpec(memory_space=pl.ANY)
@@ -47,6 +47,20 @@
 
 def in_hbm(value):
     return pltpu.with_memory_space_constraint(value, pltpu.HBM)
+
+
+def in_order(value, after):
+    return call(
+        lambda *refs: None,
+        "in_order",
+        [REMOTE] * (1 + len(after)),
+        REMOTE,
+        jax.ShapeDtypeStruct(value.shape, value.dtype),
+        [],
+        1,
+        [value, *after],
+        {0: 0},
+    )
 
 
 def forward_kernel(layout, ins, outs, *refs):
@@ -81,7 +95,7 @@
                 for k, (source, target) in enumerate(zip(sources, made))
             ]
         )
-    for pair in queue[:2]:
+    for pair in queue[: slots - 1]:
         for copy in pair:
             copy.start()
     if first:
@@ -97,7 +111,8 @@
             for copy in queue[taken]:
                 copy.wait()
             taken += 1
-            for copy in queue[taken + 1] if taken + 1 < len(queue) else []:
+            more = taken + slots - 2
+            for copy in queue[more] if more < len(queue) else []:
                 copy.start()
             blocks = [weights[k, j % slots] for k in range(2)]
         else:
@@ -134,9 +149,9 @@
     ]
     if first:
         x = in_hbm(x)
-        out_shape.append(pltpu.VMEM(x.shape, BF16))
+        out_shape.append(jax.ShapeDtypeStruct(x.shape, BF16))
     if following is not None:
-        out_shape += [pltpu.VMEM((depth, block), BF16)] * 2
+        out_shape += [jax.ShapeDtypeStruct((depth, block), BF16)] * 2
     args = (x, in_hbm(gate_weight), in_hbm(up_weight), *early, *after)
     layout = (quarters, rows, block, start, count, following, first)
     return call(
@@ -197,28 +212,31 @@
     )
 
 
-def input_kernel(quarters, rows, columns, first, last, skipped, gate_ref, up_ref, *refs):
-    pieces, rest = refs[:quarters], refs[quarters + skipped :]
-    earlier = []
-    if not first:
-        count = 2 if last else 1
-        earlier, rest = rest[:count], rest[count:]
-    *sums, grads, weights, sems = rest
-    depth, deep = gate_ref.shape[0], weights.shape[2]
-    slots = weights.shape[1]
-    queue = [
-        [
+def input_kernel(layout, gate_ref, up_ref, *refs):
+    quarters, rows, columns, held, first, last, skipped, extra = layout
+    refs = refs[skipped:]
+    pieces, rest = refs[:quarters], refs[quarters:]
+    earlier, rest = rest[:extra], rest[extra:]
+    if first:
+        x_ref, rest = rest[0], rest[1:]
+    depth = gate_ref.shape[0]
+    half = depth // 2
+    if held:
+        *sums, grads = rest
+        weights, copies = (gate_ref, up_ref), []
+    else:
+        *sums, grads, scratch, sems = rest
+        weights = (scratch.at[0], scratch.at[1])
+        copies = [
             pltpu.make_async_copy(
-                source.at[pl.ds(d * deep, deep), columns],
-                weights.at[k, d % slots],
-                sems.at[k, d % slots],
+                source.at[pl.ds(h * half, half), columns],
+                scratch.at[k, pl.ds(h * half, half)],
+                sems.at[k, h],
             )
+            for h in range(2)
             for k, source in enumerate((gate_ref, up_ref))
         ]
-        for d in range(depth // deep)
-    ]
-    for pair in queue[: slots - 1]:
-        for copy in pair:
+        for copy in copies:
             copy.start()
     outer = quarters // 2
     me = lax.axis_index("row")
@@ -229,21 +247,23 @@
         at = pl.multiple_of((there + (core + swap) % 2) * rows, rows)
         for k in range(2):
             grads[k, pl.ds(at, rows), :] = piece[k]
+    if first:
+        xt_ref, sums = sums[0], sums[1:]
+        xt_ref[...] = x_ref[...].T
     dims = (((1,), (1,)), ((), ()))
     flipped = [] if last else [grads[k].T for k in range(2)]
-    half = depth // 2
-    for d, pair in enumerate(queue):
-        for copy in pair:
-            copy.wait()
-        for copy in queue[d + slots - 1] if d + slots - 1 < len(queue) else []:
-            copy.start()
+    deep = 256 if depth % 512 == 0 else 128
+    for d in range(depth // deep):
         at = slice(d * deep, (d + 1) * deep)
         index, across = d * deep // half, slice(d * deep % half, d * deep % half + deep)
+        if copies and d * deep % half == 0:
+            copies[2 * index].wait()
+            copies[2 * index + 1].wait()
         term = None
-        if not first:
+        if earlier:
             term = earlier[index][:, across] if last else earlier[0][at, :]
         for k in range(2):
-            piece = weights[k, d % slots]
+            piece = weights[k][at, :]
             if last:
                 product = lax.dot_general(grads[k], piece, dims, preferred_element_type=F32)
             else:
@@ -257,72 +277,103 @@
             sums[index][:, across] = term.T
 
 
-def input_part(quarters, block, chunk, gate_weight, up_weight, pieces, acc, final, after):
-    depth = gate_weight.shape[0]
+def input_part(quarters, block, chunk, weights, held, pieces, acc, final, x, after):
+    depth = x.shape[1]
     rows = pieces[0].shape[1]
     tokens = rows * quarters
     start, count = chunk
     width = count * block
-    deep = 256 if depth % 512 == 0 else 128
     first, last = acc is None, final == 0
-    args = [in_hbm(gate_weight), in_hbm(up_weight), *pieces, *after] + ([] if first else acc)
+    args = [*weights, *after, *pieces, *([x] if first else acc)]
     sums = [jax.ShapeDtypeStruct((depth, tokens), F32)]
     if final <= 1:
         sums = [jax.ShapeDtypeStruct((tokens, depth // 2), F32)] * 2
+    out_shape = sums + [jax.ShapeDtypeStruct((2, tokens, width), BF16)]
+    if first:
+        out_shape = [jax.ShapeDtypeStruct((depth, tokens), BF16)] + out_shape
     columns = pl.ds(start * block, width)
-    *acc, grads = call(
-        functools.partial(input_kernel, quarters, rows, columns, first, last, len(after)),
+    layout = (quarters, rows, columns, held, first, last, len(after), 0 if first else len(acc))
+    scratch = []
+    if not held:
+        scratch = [pltpu.VMEM((2, depth, width), BF16), pltpu.SemaphoreType.DMA((2, 2))]
+    out = call(
+        functools.partial(input_kernel, layout),
         "input_part",
-        [REMOTE] * 2
-        + [WHOLE] * quarters
+        [WHOLE if held else REMOTE] * 2
         + [REMOTE] * len(after)
-        + [WHOLE] * (0 if first else len(acc)),
-        [WHOLE] * (len(sums) + 1),
-        sums + [jax.ShapeDtypeStruct((2, tokens, width), BF16)],
-        [pltpu.VMEM((2, SLOTS, deep, width), BF16), pltpu.SemaphoreType.DMA((2, SLOTS))],
-        tokens * depth * width,
+        + [WHOLE] * (len(args) - 2 - len(after)),
+        [WHOLE] * len(out_shape),
+        out_shape,
+        scratch,
+        tokens * depth,
         args,
     )
-    return acc, grads
-
-
-def weight_kernel(block, start, count, skipped, xt_ref, grads_ref, *refs):
-    gate_out, up_out, products, sems = refs[skipped:]
+    xt, out = (out[0], out[1:]) if first else (None, out)
+    return xt, out[:-1], out[-1]
+
+
+def weight_kernel(block, chunk, ahead, skipped, xt_ref, grads_ref, *refs):
+    start, count = chunk
+    refs = refs[skipped:]
+    sources, refs = (refs[:2], refs[2:]) if ahead else ((), refs)
+    refs = refs[2:] if len(refs) > (8 if ahead else 4) else refs
+    gate_out, up_out, *loaded, products, sems = refs
+    fetched = []
+    if ahead:
+        loaded, fetch_sems = loaded[:2], loaded[2]
+        half = loaded[0].shape[0] // 2
+        fetched = [
+            pltpu.make_async_copy(
+                source.at[pl.ds(h * half, half), ahead],
+                target.at[pl.ds(h * half, half)],
+                fetch_sems.at[k, h],
+            )
+            for h in range(2)
+            for k, (source, target) in enumerate(zip(sources, loaded))
+        ]
+        for copy in fetched:
+            copy.start()
     xt = xt_ref[...]
-    slots = products.shape[0]
     copies = []
     for j in range(count):
         for k, out in enumerate((gate_out, up_out)):
             piece = grads_ref[k, :, j * block : (j + 1) * block]
-            slot = len(copies) % slots
-            if len(copies) >= slots:
-                copies[-slots].wait()
-            products[slot] = jnp.dot(xt, piece, preferred_element_type=F32).astype(BF16)
+            products[k, j] = jnp.dot(xt, piece, preferred_element_type=F32).astype(BF16)
             copy = pltpu.make_async_copy(
-                products.at[slot], out.at[:, pl.ds((start + j) * block, block)], sems.at[slot]
+                products.at[k, j], out.at[:, pl.ds((start + j) * block, block)], sems.at[k, j]
             )
             copy.start()
             copies.append(copy)
-    for copy in copies[-slots:]:
+    for copy in fetched + copies:
         copy.wait()
 
 
-def weight_part(block, start, count, full, xt, grads, state, after):
+def weight_part(block, chunk, full, xt, grads, state, after, ahead, sources):
     depth, tokens = xt.shape
-    args = [xt, grads, *after, *[in_hbm(value) for value in state]]
-    first = 2 + len(after)
+    start, count = chunk
+    columns = pl.ds(ahead[0] * block, ahead[1] * block) if ahead else None
+    sources = [in_hbm(value) for value in sources] if ahead else []
+    args = [xt, grads, *after, *sources, *[in_hbm(value) for value in state]]
+    first = len(args) - len(state)
     aliases = {first + k: k for k in range(len(state))}
-    return call(
-        functools.partial(weight_kernel, block, start, count, len(args) - 2),
+    out_shape = [pltpu.HBM((depth, full), BF16)] * 2
+    scratch = []
+    if ahead:
+        out_shape += [jax.ShapeDtypeStruct((depth, ahead[1] * block), BF16)] * 2
+        scratch = [pltpu.SemaphoreType.DMA((2, 2))]
+    out = call(
+        functools.partial(weight_kernel, block, chunk, columns, len(after)),
         "weight_part",
         [WHOLE] * 2 + [REMOTE] * (len(args) - 2),
-        [REMOTE] * 2,
-        [pltpu.HBM((depth, full), BF16)] * 2,
-        [pltpu.VMEM((SLOTS, depth, block), BF16), pltpu.SemaphoreType.DMA((SLOTS,))],
+        [REMOTE] * 2 + [WHOLE] * (len(out_shape) - 2),
+        out_shape,
+        scratch
+        + [pltpu.VMEM((2, count, depth, block), BF16), pltpu.SemaphoreType.DMA((2, count))],
         tokens * depth * count * block,
         args,
         aliases,
     )
+    return out[:2], out[2:]
 
 
 def token_sums(halves, columns, orders):
@@ -361,66 +412,89 @@
         moves = [(r, (r // 2 + step) % outer * 2 + r % 2) for r in range(quarters)]
         return lax.ppermute(value, "row", moves)
 
-    def forward(i, x, early, after):
-        following = chunks[i + 1][0] if i + 1 < len(chunks) else None
+    number = len(chunks)
+    both = [gate_weight, up_weight]
+    owns, gots, sums, crossed, pieces, groups, grads = [], [], [], [], [], [], []
+    held, flipped = {}, []
+
+    def forward(i, x, early):
+        following = chunks[i + 1][0] if i + 1 < number else None
+        after = sums[i - 1][:1] if i else []
         own, far, send, *loaded = forward_part(
             quarters, block, chunks[i], following, x, gate_weight, up_weight, early, after
         )
+        owns.append(own)
         if i == 0:
             x, loaded = loaded[0], loaded[1:]
+        elif i < 3:
+            send = in_order(send, crossed[i - 1][:1] + pieces[i - 1][:1])
+        else:
+            if i == number - 1:
+                relay(0, sums[-1][:1])
+                take_input(0, x, None, [])
+            send = in_order(send, crossed[i - 1][:1] + pieces[i - 3][2:3] + grads)
         got = sibling(send)
         near = [(far[step - 1] + got[step].astype(F32)).astype(BF16) for step in range(1, outer)]
-        owns.append(own)
         gots.append(got)
         sums.append(near)
         crossed.append([across(value, step + 1) for step, value in enumerate(near)])
         return x, loaded
 
-    def middle(i, hidden, after):
+    def middle(i, hidden):
         start, count = chunks[i]
         at = slice(start * block, (start + count) * block)
+        after = pieces[i - 2][2:3] if i >= 2 else []
         hidden, mine = middle_part(
             outer, at, owns[i], gots[i], crossed[i], hidden_grad, hidden, after
         )
-        group = [mine, sibling(mine)]
-        for step in range(1, outer):
-            there = across(mine, step)
-            group += [there, sibling(there)]
-        pieces.append(group)
+        pieces.append([mine, sibling(mine)] + [across(mine, step) for step in range(1, outer)])
         return hidden
 
-    owns, gots, sums, crossed, pieces = [], [], [], [], []
-    number = len(chunks)
+    def relay(i, after):
+        mine, near, *far = pieces[i]
+        group = [mine, near]
+        for there in far:
+            group += [there, sibling(in_order(there, after) if after else there)]
+        groups.append(group)
+
+    def take_input(i, x, acc, after):
+        weights = held[i] if i in held else [in_hbm(value) for value in both]
+        xt, total, whole = input_part(
+            quarters, block, chunks[i], weights, i in held, groups[i], acc, number - 1 - i, x, after
+        )
+        if i == 0:
+            flipped.append(xt)
+            totals.append(total)
+        grads.append(whole)
+        return total
+
+    totals = []
     x, early, hidden = inputs, [], None
     for i in range(number):
-        after = []
-        if i >= 2:
-            after = sums[i - 2][:1]
-        if i >= 3:
-            hidden = middle(i - 3, hidden, [])
-            after = after + [pieces[i - 3][0]]
-        x, early = forward(i, x, early, after)
-    for i in range(max(number - 3, 0), number):
-        hidden = middle(i, hidden, pieces[i - 2][2:3] if i >= 2 else [])
-
-    xt = x.T
+        x, early = forward(i, x, early)
+        hidden = middle(i, hidden)
+    acc, state = None, []
+    for i in range(number):
+        if i == 0 and grads:
+            acc = totals[0]
+        else:
+            last = i == number - 1
+            relay(i, [] if last else grads[-1:] + pieces[-1][:1] if i == number - 2 else sums[-1][:1])
+            after = pieces[i + 1][:1] + sums[-1][:1] if i == 1 < number - 1 else []
+            acc = take_input(i, x, acc, after)
+        if i < number - 2:
+            state, held[i + 2] = weight_part(
+                block, chunks[i], full, flipped[0], grads[i], state, [], chunks[i + 2], both
+            )
     bits = columns.bit_length() - 1
     order = list(range(bits))
-    acc, state = None, []
-    grads = []
-    for i in range(number):
-        after = [in_hbm(value) for value in state[:1]] if i == number - 1 else []
-        acc, whole = input_part(
-            quarters, block, chunks[i], gate_weight, up_weight, pieces[i], acc, number - 1 - i, after
-        )
-        grads.append(whole)
-        if i < number - 2:
-            state = weight_part(block, *chunks[i], full, xt, whole, state, [])
     stages = [acc] + token_sums(acc, columns, [order, order[1::-1] + order[2:]])
     input_grad = jnp.concatenate([half.astype(BF16) for half in stages[-1]], axis=1)
     for i in range(max(number - 2, 0), number):
         after = stages[min(i - max(number - 2, 0), bits)]
-        state = weight_part(block, *chunks[i], full, xt, grads[i], state, after)
+        state, _ = weight_part(
+            block, chunks[i], full, flipped[0], grads[i], state, after, None, []
+        )
     return hidden, input_grad, state[0], state[1]
 
 

time: 127 us -> 113 us (0.89)
  Pallas kernels: 69.6 us -> 55 us
  waiting for transfers between devices: 27.3 us -> 21.7 us
  starting transfers between devices: 19.2 us -> 24.2 us
  local copies, waits for them, and re-layouts: 7.51 us -> 9.3 us
    pallas_call x16 -> x22, Pallas kernels: 69.6 us -> 55 us  [call(): pl.pallas_call(kernel, in_specs=in_specs, out_specs=out_specs, out_shape=...]
    ppermute x8, waiting for transfers between devices: 22.4 us -> 12.5 us  [across(): return lax.ppermute(value, 'row', moves)]
    ppermute x12, waiting for transfers between devices: 0.03 us -> 3.3 us  [sibling(): return lax.ppermute(value, 'row', swap)]
    ppermute x8, starting transfers between devices: 9.33 us -> 12.6 us  [across(): return lax.ppermute(value, 'row', moves)]
    unnamed x20 -> x35, local copies, waits for them, and re-layouts: 6.62 us -> 9.11 us
    ppermute x6, starting transfers between devices: 7.3 us -> 9.53 us  [token_sums(): got.append(lax.ppermute(send.astype(BF16), 'col', moves))]
  transfers between devices with their start and end apart: 26 -> 26, of which waited for: 6 -> 10; matrix products, arithmetic and copies ran while one was open for 2% -> 0% of each run, Pallas kernels for 47% -> 42%
where the time goes in v6:
time: 113 us; the launch traced here: 112 us
  Pallas kernels  55 us (49%)
  starting transfers between devices  24.2 us (21%)
  waiting for transfers between devices  21.7 us (19%)
  local copies, waits for them, and re-layouts  9.3 us (8%)
    pallas_call x22, Pallas kernels, call(): pl.pallas_call(kernel, in_specs=in_specs, out_specs=out_specs, out_shape=...  55 us
    ppermute x8, starting transfers between devices, across(): return lax.ppermute(value, 'row', moves)  12.6 us
    ppermute x8, waiting for transfers between devices, across(): return lax.ppermute(value, 'row', moves)  12.5 us
    ppermute x6, starting transfers between devices, token_sums(): got.append(lax.ppermute(send.astype(BF16), 'col', moves))  9.53 us
    unnamed x35, local copies, waits for them, and re-layouts  9.11 us
    ppermute x6, waiting for transfers between devices, token_sums(): got.append(lax.ppermute(send.astype(BF16), 'col', moves))  5.96 us
    ppermute x12, waiting for transfers between devices, sibling(): return lax.ppermute(value, 'row', swap)  3.3 us
  transfers between devices with their start and end apart: 26, of which 10 were waited for; matrix products, arithmetic and copies ran while one was open for 0% of the time, Pallas kernels for 42%

profile of v6, /device:TPU:0, one launch (start us, length us, event | category | flops | bytes accessed | tf_op | source)
XLA Modules:
  0.0 112.3 jit_solution(10823853123750187434)
XLA Ops:
  0.6 4.6 %forward_part.4 = (f32[2,64,512]{2,1,0:T(8,128)S(1)}, f32[1,2,64,512]{3,2,1,0:T(8,128)S(1)}, bf16[2,2,64,512]{3,2,1,0:T(8,128)(2,1)S(1)}, bf16[256,2048]{1,0:T(8...) custom-call(bf16[256,2048]{1,0:T(8,128)(2,1)} %refs_0_.3, bf16[2048,3584]{1,0:T(8,128)(2,1)} %refs_0_.5, ...), custom_call_target="tpu_custom_call" | custom-call | flops 10737418240 | bytes 268435456 | tf_op jit(solution)/shard_map/forward_part/pallas_call | solution.py:33
  7.0 2.9 %collective-permute-start.1 = (bf16[2,64,512]{2,1,0:T(8,128)(2,1)S(1)}, bf16[2,64,512]{2,1,0:T(8,128)(2,1)S(1)}, u32[]{:S(2)}, u32[]{:S(2)}) collective-permute-start(bf16[2,64,512]{2,1,0:T(8,128)(2,1)S(1)} %fusion.5.refs_5_), channel_id=1, source_target_pairs={{0,16},{8,24},{16,0},{24,8},{1,17},{9,25},{17,1},{25,9},{2,18},{10... | collective-permute-start | bytes 393224 | tf_op jit(solution)/shard_map/ppermute | solution.py:413
  9.9 4.0 %forward_part.5 = (f32[2,64,1024]{2,1,0:T(8,128)S(1)}, f32[1,2,64,1024]{3,2,1,0:T(8,128)S(1)}, bf16[2,2,64,1024]{3,2,1,0:T(8,128)(2,1)S(1)}, bf16[2048,256]{1,0:T(8,128)(2,1)S(1)}, bf16[2048,256]{1,0:T(8,128)(2,1)S(1)}) custom-call(bf16[256,2048]{1,0:T(8,128)(2,1)S(1)} %get-tuple-element.54.refs_0_.refs_4_, bf16[2048,3584]{1,0:T(8,128)(2,1)} %refs_0_.5, ...), custom_call_target="tpu_custom_call" | custom-call | flops 21474836480 | bytes 536870912 | tf_op jit(solution)/shard_map/forward_part/pallas_call | solution.py:33
  14.1 1.9 %collective-permute-done.2.got_ref = bf16[2,2,64,1024]{3,2,1,0:T(8,128)(2,1)S(1)} collective-permute-done((bf16[2,2,64,1024]{3,2,1,0:T(8,128)(2,1)S(1)}, bf16[2,2,64,1024]{3,2,1,0:T(8,128)(2,1)S(1)}, u32[]{:S(2)}, u32[]{:S(2)}) %collective-permute-start.2) | collective-permute-done | bytes 524320 | tf_op jit(solution)/shard_map/ppermute | solution.py:409
  16.1 1.6 %collective-permute-start.3 = (bf16[2,64,1024]{2,1,0:T(8,128)(2,1)S(1)}, bf16[2,64,1024]{2,1,0:T(8,128)(2,1)S(1)}, u32[]{:S(2)}, u32[]{:S(2)}) collective-permute-start(bf16[2,64,1024]{2,1,0:T(8,128)(2,1)S(1)} %fusion.1.refs_5_), channel_id=1, source_target_pairs={{0,16},{8,24},{16,0},{24,8},{1,17},{9,25},{17,1},{25,9},{2,18},{10... | collective-permute-start | bytes 786440 | tf_op jit(solution)/shard_map/ppermute | solution.py:413
  17.7 4.7 %forward_part.6 = (f32[2,64,1280]{2,1,0:T(8,128)S(1)}, f32[1,2,64,1280]{3,2,1,0:T(8,128)S(1)}, bf16[2,2,64,1280]{3,2,1,0:T(8,128)(2,1)S(1)}, bf16[2048,256]{1,0:T(8,128)(2,1)S(1)}, bf16[2048,256]{1,0:T(8,128)(2,1)S(1)}) custom-call(bf16[256,2048]{1,0:T(8,128)(2,1)S(1)} %get-tuple-element.54.refs_0_.refs_4_, bf16[2048,3584]{1,0:T(8,128)(2,1)} %refs_0_.5, ...), custom_call_target="tpu_custom_call" | custom-call | flops 26843545600 | bytes 671088640 | tf_op jit(solution)/shard_map/forward_part/pallas_call | solution.py:33
  22.4 2.1 %collective-permute-done.3.refs_0_.refs_1_ = bf16[2,64,1024]{2,1,0:T(8,128)(2,1)S(1)} collective-permute-done((bf16[2,64,1024]{2,1,0:T(8,128)(2,1)S(1)}, bf16[2,64,1024]{2,1,0:T(8,128)(2,1)S(1)}, u32[]{:S(2)}, u32[]{:S(2)}) %collective-permute-start.3) | collective-permute-done | bytes 262176 | tf_op jit(solution)/shard_map/ppermute | solution.py:413
  25.4 1.5 %collective-permute-start.6 = (bf16[2,64,512]{2,1,0:T(8,128)(2,1)S(1)}, bf16[2,64,512]{2,1,0:T(8,128)(2,1)S(1)}, u32[]{:S(2)}, u32[]{:S(2)}) collective-permute-start(bf16[2,64,512]{2,1,0:T(8,128)(2,1)S(1)} %get-tuple-element.64.refs_2_.refs_0_), channel_id=1, source_target_pairs={{0,16},{8,24},{16,0},{24,8},{1,17},{9,25},{17,1},{25,9},{2,18},{10... | collective-permute-start | bytes 393224 | tf_op jit(solution)/shard_map/ppermute | solution.py:413
  27.2 4.2 %collective-permute-done.6.refs_2_.refs_1_ = bf16[2,64,512]{2,1,0:T(8,128)(2,1)S(1)} collective-permute-done((bf16[2,64,512]{2,1,0:T(8,128)(2,1)S(1)}, bf16[2,64,512]{2,1,0:T(8,128)(2,1)S(1)}, u32[]{:S(2)}, u32[]{:S(2)}) %collective-permute-start.6) | collective-permute-done | bytes 131104 | tf_op jit(solution)/shard_map/ppermute | solution.py:413
  32.3 1.5 %collective-permute-start.5 = (bf16[2,64,1280]{2,1,0:T(8,128)(2,1)S(1)}, bf16[2,64,1280]{2,1,0:T(8,128)(2,1)S(1)}, u32[]{:S(2)}, u32[]{:S(2)}) collective-permute-start(bf16[2,64,1280]{2,1,0:T(8,128)(2,1)S(1)} %fusion.refs_5_.refs_1_), channel_id=1, source_target_pairs={{0,16},{8,24},{16,0},{24,8},{1,17},{9,25},{17,1},{25,9},{2,18},{10... | collective-permute-start | bytes 983048 | tf_op jit(solution)/shard_map/ppermute | solution.py:413
  33.8 3.6 %forward_part.7 = (f32[2,64,768]{2,1,0:T(8,128)S(1)}, f32[1,2,64,768]{3,2,1,0:T(8,128)S(1)}, bf16[2,2,64,768]{3,2,1,0:T(8,128)(2,1)S(1)}) custom-call(bf16[256,2048]{1,0:T(8,128)(2,1)S(1)} %get-tuple-element.54.refs_0_.refs_4_, bf16[2048,3584]{1,0:T(8,128)(2,1)} %refs_0_.5, bf16[2048,3584]{1,0:T(8,128)(2,1)} %refs_1_.11, ...), custom_call_target="tpu_custom_call" | custom-call | flops 16106127360 | bytes 402653184 | tf_op jit(solution)/shard_map/forward_part/pallas_call | solution.py:33
  37.5 3.2 %input_part.4 = (bf16[2048,256]{1,0:T(8,128)(2,1)S(1)}, f32[2048,256]{1,0:T(8,128)S(1)}, bf16[2,256,512]{2,1,0:T(8,128)(2,1)S(1)}) custom-call(bf16[2048,3584]{1,0:T(8,128)(2,1)} %refs_0_.5, bf16[2048,3584]{1,0:T(8,128)(2,1)} %refs_1_.11, bf16[2,64,512]{2,1,0:T(8,128)(2,1)S(1)} %get-tuple-element.64.refs_2_.refs_0_, ...), custom_call_target="tpu_custom_call" | custom-call | flops 20971520 | bytes 524288 | tf_op jit(solution)/shard_map/input_part/pallas_call | solution.py:33
  41.6 1.5 %collective-permute-start.11 = (bf16[2,64,1024]{2,1,0:T(8,128)(2,1)}, bf16[2,64,1024]{2,1,0:T(8,128)(2,1)S(1)}, u32[]{:S(2)}, u32[]{:S(2)}) collective-permute-start(bf16[2,64,1024]{2,1,0:T(8,128)(2,1)} %get-tuple-element.71.refs_2_), channel_id=1, source_target_pairs={{0,16},{8,24},{16,0},{24,8},{1,17},{9,25},{17,1},{25,9},{2,18},{10... | collective-permute-start | bytes 786440 | tf_op jit(solution)/shard_map/ppermute | solution.py:413
  44.2 1.5 %collective-permute-start.10 = (bf16[2,64,768]{2,1,0:T(8,128)(2,1)S(1)}, bf16[2,64,768]{2,1,0:T(8,128)(2,1)}, u32[]{:S(2)}, u32[]{:S(2)}) collective-permute-start(bf16[2,64,768]{2,1,0:T(8,128)(2,1)S(1)} %fusion.4.refs_1_), channel_id=1, source_target_pairs={{0,16},{8,24},{16,0},{24,8},{1,17},{9,25},{17,1},{25,9},{2,18},{10... | collective-permute-start | bytes 589832 | tf_op jit(solution)/shard_map/ppermute | solution.py:413
  45.7 5.3 %collective-permute-done.11.refs_1_.refs_4_ = bf16[2,64,1024]{2,1,0:T(8,128)(2,1)S(1)} collective-permute-done((bf16[2,64,1024]{2,1,0:T(8,128)(2,1)}, bf16[2,64,1024]{2,1,0:T(8,128)(2,1)S(1)}, u32[]{:S(2)}, u32[]{:S(2)}) %collective-permute-start.11) | collective-permute-done | bytes 262176 | tf_op jit(solution)/shard_map/ppermute | solution.py:413
  54.4 1.6 %collective-permute-start.18 = (bf16[2,64,1280]{2,1,0:T(8,128)(2,1)S(1)}, bf16[2,64,1280]{2,1,0:T(8,128)(2,1)S(1)}, u32[]{:S(2)}, u32[]{:S(2)}) collective-permute-start(bf16[2,64,1280]{2,1,0:T(8,128)(2,1)S(1)} %get-tuple-element.81.refs_0_), channel_id=1, source_target_pairs={{0,16},{8,24},{16,0},{24,8},{1,17},{9,25},{17,1},{25,9},{2,18},{10... | collective-permute-start | bytes 983048 | tf_op jit(solution)/shard_map/ppermute | solution.py:413
  58.0 1.8 %middle_part.7 = (bf16[64,3584]{1,0:T(8,128)(2,1)}, bf16[2,64,768]{2,1,0:T(8,128)(2,1)S(1)}) custom-call(f32[2,64,768]{2,1,0:T(8,128)S(1)} %copy-done.12, bf16[2,2,64,768]{3,2,1,0:T(8,128)(2,1)S(1)} %copy-done.4, bf16[64,3584]{1,0:T(8,128)(2,1)S(1)} %copy-done, bf16[2,64,768]{2,1,0:T(8,128)(2,1)} %collective-permute-done.10.refs_0_, ...), custom_call_target="tpu_custom_call" | custom-call | flops 1966080 | bytes 49152 | tf_op jit(solution)/shard_map/middle_part/pallas_call | solution.py:33
  61.4 1.2 %copy-done.14 = bf16[2048,256]{1,0:T(8,128)(2,1)S(1)} copy-done((bf16[2048,256]{1,0:T(8,128)(2,1)S(1)}, bf16[2048,256]{1,0:T(8,128)(2,1)}, u32[]{:S(2)}) %copy-start.14) | copy-done | bytes 1048600
  62.6 6.2 %weight_part.4 = (bf16[2048,3584]{1,0:T(8,128)(2,1)}, bf16[2048,3584]{1,0:T(8,128)(2,1)}, bf16[2048,1280]{1,0:T(8,128)(2,1)S(1)}, bf16[2048,1280]{1,0:T(8,128)(2,1)S(1)}) custom-call(bf16[2048,256]{1,0:T(8,128)(2,1)S(1)} %copy-done.14, bf16[2,256,512]{2,1,0:T(8,128)(2,1)S(1)} %copy-done.8, bf16[2048,3584]{1,0:T(8,128)(2,1)} %refs_0_.5, ...), custom_call_target="tpu_custom_call" | custom-call | flops 10737418240 | bytes 268435456 | tf_op jit(solution)/shard_map/weight_part/pallas_call | solution.py:33
  69.5 5.9 %input_part.5 = (f32[2048,256]{1,0:T(8,128)S(1)}, bf16[2,256,1024]{2,1,0:T(8,128)(2,1)S(1)}) custom-call(bf16[2048,3584]{1,0:T(8,128)(2,1)} %refs_0_.5, bf16[2048,3584]{1,0:T(8,128)(2,1)} %refs_1_.11, bf16[2,64,1280]{2,1,0:T(8,128)(2,1)S(1)} %get-tuple-element.81.refs_0_, bf16[2,64,768]{2,1,0:T(8,128)(2,1)S(1)} %fusion.4.refs_1_, ...), custom_call_target="tpu_custom_call" | custom-call | flops 20971520 | bytes 524288 | tf_op jit(solution)/shard_map/input_part/pallas_call | solution.py:33
  75.9 6.5 %weight_part.5 = (bf16[2048,3584]{1,0:T(8,128)(2,1)}, bf16[2048,3584]{1,0:T(8,128)(2,1)}, bf16[2048,768]{1,0:T(8,128)(2,1)S(1)}, bf16[2048,768]{1,0:T(8,128)(2,1)S(1)}) custom-call(bf16[2048,256]{1,0:T(8,128)(2,1)S(1)} %copy-done.15, bf16[2,256,1024]{2,1,0:T(8,128)(2,1)S(1)} %get-tuple-element.83.grads_ref.refs_1_, ...), custom_call_target="tpu_custom_call", output_to_operand_aliasing={{0}: (4, {}), {1}: (5, {})} | custom-call | flops 21474836480 | bytes 536870912 | tf_op jit(solution)/shard_map/weight_part/pallas_call | solution.py:33
  82.4 3.1 %input_part.6 = (f32[256,1024]{1,0:T(8,128)S(1)}, f32[256,1024]{1,0:T(8,128)S(1)}, bf16[2,256,1280]{2,1,0:T(8,128)(2,1)S(1)}) custom-call(bf16[2048,1280]{1,0:T(8,128)(2,1)S(1)} %get-tuple-element.89.gate_ref, bf16[2048,1280]{1,0:T(8,128)(2,1)S(1)} %get-tuple-element.90.up_ref, bf16[2,64,1280]{2,1,0:T(8,128)(2,1)S(1)} %get-tuple-element.81.refs_0_, ...), custom_call_target="tpu_custom_call" | custom-call | flops 20971520 | bytes 524288 | tf_op jit(solution)/shard_map/input_part/pallas_call | solution.py:33
  85.6 1.8 %input_part.7 = (f32[256,1024]{1,0:T(8,128)S(1)}, f32[256,1024]{1,0:T(8,128)S(1)}, bf16[2,256,768]{2,1,0:T(8,128)(2,1)S(1)}) custom-call(bf16[2048,768]{1,0:T(8,128)(2,1)S(1)} %get-tuple-element.86.gate_ref, bf16[2048,768]{1,0:T(8,128)(2,1)S(1)} %get-tuple-element.87.up_ref, bf16[2,64,768]{2,1,0:T(8,128)(2,1)S(1)} %get-tuple-element.88.refs_2_.refs_0_, ...), custom_call_target="tpu_custom_call" | custom-call | flops 20971520 | bytes 524288 | tf_op jit(solution)/shard_map/input_part/pallas_call | solution.py:33
  87.5 1.6 %collective-permute-start.20 = (bf16[2,2,32,1024]{3,2,0,1:T(8,128)(2,1)S(1)}, bf16[2,2,32,1024]{3,2,0,1:T(8,128)(2,1)S(1)}, u32[]{:S(2)}, u32[]{:S(2)}) collective-permute-start(bf16[2,2,32,1024]{3,2,0,1:T(8,128)(2,1)S(1)} %fusion.2), channel_id=1, source_target_pairs={{0,1},{1,0},{2,3},{3,2},{4,5},{5,4},{6,7},{7,6},{8,9},{9,8},{10,11... | collective-permute-start | bytes 786440 | tf_op jit(solution)/shard_map/ppermute | solution.py:395
  89.1 1.6 %collective-permute-start.23 = (bf16[2,2,32,1024]{3,2,1,0:T(8,128)(2,1)S(1)}, bf16[2,2,32,1024]{3,2,1,0:T(8,128)(2,1)S(1)}, u32[]{:S(2)}, u32[]{:S(2)}) collective-permute-start(bf16[2,2,32,1024]{3,2,1,0:T(8,128)(2,1)S(1)} %fusion.3), channel_id=1, source_target_pairs={{0,2},{1,3},{2,0},{3,1},{4,6},{5,7},{6,4},{7,5},{8,10},{9,11},{10,... | collective-permute-start | bytes 786440 | tf_op jit(solution)/shard_map/ppermute | solution.py:395
  90.8 4.8 %weight_part.6 = (bf16[2048,3584]{1,0:T(8,128)(2,1)}, bf16[2048,3584]{1,0:T(8,128)(2,1)}) custom-call(bf16[2048,256]{1,0:T(8,128)(2,1)S(1)} %copy-done.15, bf16[2,256,1280]{2,1,0:T(8,128)(2,1)S(1)} %get-tuple-element.97.grads_ref, f32[256,1024]{1,0:T(8,128)S(1)} %get-tuple-element.94.refs_0_, ...), custom_call_target="tpu_custom_call", output_to_operand_aliasing={{0}: (4, {}), {1}: (5, {})} | custom-call | flops 26843545600 | bytes 671088640 | tf_op jit(solution)/shard_map/weight_part/pallas_call | solution.py:33
  96.1 1.7 %collective-permute-start.21 = (bf16[2,32,1024]{2,1,0:T(8,128)(2,1)S(1)}, bf16[2,32,1024]{2,1,0:T(8,128)(2,1)S(1)}, u32[]{:S(2)}, u32[]{:S(2)}) collective-permute-start(bf16[2,32,1024]{2,1,0:T(8,128)(2,1)S(1)} %fusion.6), channel_id=1, source_target_pairs={{0,2},{1,3},{2,0},{3,1},{4,6},{5,7},{6,4},{7,5},{8,10},{9,11},{10,... | collective-permute-start | bytes 393224 | tf_op jit(solution)/shard_map/ppermute | solution.py:395
  97.9 1.6 %collective-permute-start.24 = (bf16[2,32,1024]{2,1,0:T(8,128)(2,1)S(1)}, bf16[2,32,1024]{2,1,0:T(8,128)(2,1)S(1)}, u32[]{:S(2)}, u32[]{:S(2)}) collective-permute-start(bf16[2,32,1024]{2,1,0:T(8,128)(2,1)S(1)} %fusion.7), channel_id=1, source_target_pairs={{0,1},{1,0},{2,3},{3,2},{4,5},{5,4},{6,7},{7,6},{8,9},{9,8},{10,11... | collective-permute-start | bytes 393224 | tf_op jit(solution)/shard_map/ppermute | solution.py:395
  99.5 3.4 %weight_part.7 = (bf16[2048,3584]{1,0:T(8,128)(2,1)}, bf16[2048,3584]{1,0:T(8,128)(2,1)}) custom-call(bf16[2048,256]{1,0:T(8,128)(2,1)S(1)} %copy-done.15, bf16[2,256,768]{2,1,0:T(8,128)(2,1)S(1)} %get-tuple-element.96.grads_ref, f32[2,2,32,1024]{3,2,1,0:T(8,128)S(1)} %copy.24.refs_0_, ...), custom_call_target="tpu_custom_call", output_to_operand_aliasing={{0}: (4, {}), {1}: (5, {})} | custom-call | flops 16106127360 | bytes 402653184 | tf_op jit(solution)/shard_map/weight_part/pallas_call | solution.py:33
  103.0 2.6 %collective-permute-start.22 = (bf16[32,1024]{1,0:T(8,128)(2,1)S(1)}, bf16[32,1024]{1,0:T(8,128)(2,1)S(1)}, u32[]{:S(2)}, u32[]{:S(2)}) collective-permute-start(bf16[32,1024]{1,0:T(8,128)(2,1)S(1)} %fusion.10), channel_id=1, source_target_pairs={{0,4},{1,5},{2,6},{3,7},{4,0},{5,1},{6,2},{7,3},{8,12},{9,13},{10,... | collective-permute-start | bytes 196616 | tf_op jit(solution)/shard_map/ppermute | solution.py:395
  106.1 4.1 %collective-permute-done.22 = bf16[32,1024]{1,0:T(8,128)(2,1)S(1)} collective-permute-done((bf16[32,1024]{1,0:T(8,128)(2,1)S(1)}, bf16[32,1024]{1,0:T(8,128)(2,1)S(1)}, u32[]{:S(2)}, u32[]{:S(2)}) %collective-permute-start.22) | collective-permute-done | bytes 65568 | tf_op jit(solution)/shard_map/ppermute | solution.py:395
  110.2 1.4 %collective-permute-done.25 = bf16[32,1024]{1,0:T(8,128)(2,1)S(1)} collective-permute-done((bf16[32,1024]{1,0:T(8,128)(2,1)S(1)}, bf16[32,1024]{1,0:T(8,128)(2,1)S(1)}, u32[]{:S(2)}, u32[]{:S(2)}) %collective-permute-start.25) | collective-permute-done | bytes 65568 | tf_op jit(solution)/shard_map/ppermute | solution.py:395
  (95 shorter events, 16.2 us)
Async XLA Ops:
  5.3 1.7 %collective-permute-start = (bf16[2,2,64,512]{3,2,1,0:T(8,128)(2,1)S(1)}, bf16[2,2,64,512]{3,2,1,0:T(8,128)(2,1)S(1)}, u32[]{:S(2)}, u32[]{:S(2)}) collective-permute-start(bf16[2,2,64,512]{3,2,1,0:T(8,128)(2,1)S(1)} %get-tuple-element.58), channel_id=1, source_target_pairs={{0,8},{8,0},{16,24},{24,16},{1,9},{9,1},{17,25},{25,17},{2,10},{10... | collective-permute-start | bytes 786440 | tf_op jit(solution)/shard_map/ppermute | solution.py:409
  7.0 6.9 %collective-permute-start.1 = (bf16[2,64,512]{2,1,0:T(8,128)(2,1)S(1)}, bf16[2,64,512]{2,1,0:T(8,128)(2,1)S(1)}, u32[]{:S(2)}, u32[]{:S(2)}) collective-permute-start(bf16[2,64,512]{2,1,0:T(8,128)(2,1)S(1)} %fusion.5.refs_5_), channel_id=1, source_target_pairs={{0,16},{8,24},{16,0},{24,8},{1,17},{9,25},{17,1},{25,9},{2,18},{10... | collective-permute-start | bytes 393224 | tf_op jit(solution)/shard_map/ppermute | solution.py:413
  9.9 4.0 %copy-start = (bf16[64,3584]{1,0:T(8,128)(2,1)S(1)}, bf16[64,3584]{1,0:T(8,128)(2,1)}, u32[]{:S(2)}) copy-start(bf16[64,3584]{1,0:T(8,128)(2,1)} %upstream_ref.7) | copy-start | bytes 1376260
  14.1 2.0 %collective-permute-start.2 = (bf16[2,2,64,1024]{3,2,1,0:T(8,128)(2,1)S(1)}, bf16[2,2,64,1024]{3,2,1,0:T(8,128)(2,1)S(1)}, u32[]{:S(2)}, u32[]{:S(2)}) collective-permute-start(bf16[2,2,64,1024]{3,2,1,0:T(8,128)(2,1)S(1)} %in_order.6), channel_id=1, source_target_pairs={{0,8},{8,0},{16,24},{24,16},{1,9},{9,1},{17,25},{25,17},{2,10},{10... | collective-permute-start | bytes 1572872 | tf_op jit(solution)/shard_map/ppermute | solution.py:409
  16.1 8.4 %collective-permute-start.3 = (bf16[2,64,1024]{2,1,0:T(8,128)(2,1)S(1)}, bf16[2,64,1024]{2,1,0:T(8,128)(2,1)S(1)}, u32[]{:S(2)}, u32[]{:S(2)}) collective-permute-start(bf16[2,64,1024]{2,1,0:T(8,128)(2,1)S(1)} %fusion.1.refs_5_), channel_id=1, source_target_pairs={{0,16},{8,24},{16,0},{24,8},{1,17},{9,25},{17,1},{25,9},{2,18},{10... | collective-permute-start | bytes 786440 | tf_op jit(solution)/shard_map/ppermute | solution.py:413
  22.4 9.1 %copy-start.5 = (f32[2,64,1280]{2,1,0:T(8,128)}, f32[2,64,1280]{2,1,0:T(8,128)S(1)}, u32[]{:S(2)}) copy-start(f32[2,64,1280]{2,1,0:T(8,128)S(1)} %get-tuple-element.76.own_ref) | copy-start | bytes 1966084
  25.4 8.4 %copy-start.9 = (bf16[64,3584]{1,0:T(8,128)(2,1)}, bf16[64,3584]{1,0:T(8,128)(2,1)S(1)}, u32[]{:S(2)}) copy-start(bf16[64,3584]{1,0:T(8,128)(2,1)S(1)} %get-tuple-element.77.refs_2_) | copy-start | bytes 1376260
  25.4 5.9 %collective-permute-start.4 = (bf16[2,2,64,1280]{3,2,1,0:T(8,128)(2,1)S(1)}, bf16[2,2,64,1280]{3,2,1,0:T(8,128)(2,1)S(1)}, u32[]{:S(2)}, u32[]{:S(2)}) collective-permute-start(bf16[2,2,64,1280]{3,2,1,0:T(8,128)(2,1)S(1)} %in_order.7), channel_id=1, source_target_pairs={{0,8},{8,0},{16,24},{24,16},{1,9},{9,1},{17,25},{25,17},{2,10},{10... | collective-permute-start | bytes 1966088 | tf_op jit(solution)/shard_map/ppermute | solution.py:409
  25.4 5.9 %collective-permute-start.6 = (bf16[2,64,512]{2,1,0:T(8,128)(2,1)S(1)}, bf16[2,64,512]{2,1,0:T(8,128)(2,1)S(1)}, u32[]{:S(2)}, u32[]{:S(2)}) collective-permute-start(bf16[2,64,512]{2,1,0:T(8,128)(2,1)S(1)} %get-tuple-element.64.refs_2_.refs_0_), channel_id=1, source_target_pairs={{0,16},{8,24},{16,0},{24,8},{1,17},{9,25},{17,1},{25,9},{2,18},{10... | collective-permute-start | bytes 393224 | tf_op jit(solution)/shard_map/ppermute | solution.py:413
  26.9 10.5 %collective-permute-start.7 = (bf16[2,64,512]{2,1,0:T(8,128)(2,1)S(1)}, bf16[2,64,512]{2,1,0:T(8,128)(2,1)S(1)}, u32[]{:S(2)}, u32[]{:S(2)}) collective-permute-start(bf16[2,64,512]{2,1,0:T(8,128)(2,1)S(1)} %get-tuple-element.64.refs_2_.refs_0_), channel_id=1, source_target_pairs={{0,8},{8,0},{16,24},{24,16},{1,9},{9,1},{17,25},{25,17},{2,10},{10... | collective-permute-start | bytes 393224 | tf_op jit(solution)/shard_map/ppermute | solution.py:409
  32.3 9.3 %collective-permute-start.5 = (bf16[2,64,1280]{2,1,0:T(8,128)(2,1)S(1)}, bf16[2,64,1280]{2,1,0:T(8,128)(2,1)S(1)}, u32[]{:S(2)}, u32[]{:S(2)}) collective-permute-start(bf16[2,64,1280]{2,1,0:T(8,128)(2,1)S(1)} %fusion.refs_5_.refs_1_), channel_id=1, source_target_pairs={{0,16},{8,24},{16,0},{24,8},{1,17},{9,25},{17,1},{25,9},{2,18},{10... | collective-permute-start | bytes 983048 | tf_op jit(solution)/shard_map/ppermute | solution.py:413
  33.8 3.7 %collective-permute-start.8 = (bf16[2,64,512]{2,1,0:T(8,128)(2,1)S(1)}, bf16[2,64,512]{2,1,0:T(8,128)(2,1)S(1)}, u32[]{:S(2)}, u32[]{:S(2)}) collective-permute-start(bf16[2,64,512]{2,1,0:T(8,128)(2,1)S(1)} %in_order.8), channel_id=1, source_target_pairs={{0,8},{8,0},{16,24},{24,16},{1,9},{9,1},{17,25},{25,17},{2,10},{10... | collective-permute-start | bytes 393224 | tf_op jit(solution)/shard_map/ppermute | solution.py:409
  37.4 3.3 %copy-start.11 = (f32[2,64,768]{2,1,0:T(8,128)}, f32[2,64,768]{2,1,0:T(8,128)S(1)}, u32[]{:S(2)}) copy-start(f32[2,64,768]{2,1,0:T(8,128)S(1)} %get-tuple-element.72.own_ref) | copy-start | bytes 1179652
  40.7 5.0 %copy-start.13 = (bf16[2048,256]{1,0:T(8,128)(2,1)}, bf16[2048,256]{1,0:T(8,128)(2,1)S(1)}, u32[]{:S(2)}) copy-start(bf16[2048,256]{1,0:T(8,128)(2,1)S(1)} %get-tuple-element.80.xt_ref) | copy-start | bytes 3145732
  41.6 1.7 %collective-permute-start.9 = (bf16[2,2,64,768]{3,2,1,0:T(8,128)(2,1)S(1)}, bf16[2,2,64,768]{3,2,1,0:T(8,128)(2,1)S(1)}, u32[]{:S(2)}, u32[]{:S(2)}) collective-permute-start(bf16[2,2,64,768]{3,2,1,0:T(8,128)(2,1)S(1)} %in_order.9), channel_id=1, source_target_pairs={{0,8},{8,0},{16,24},{24,16},{1,9},{9,1},{17,25},{25,17},{2,10},{10... | collective-permute-start | bytes 1179656 | tf_op jit(solution)/shard_map/ppermute | solution.py:409
  41.6 9.3 %collective-permute-start.11 = (bf16[2,64,1024]{2,1,0:T(8,128)(2,1)}, bf16[2,64,1024]{2,1,0:T(8,128)(2,1)S(1)}, u32[]{:S(2)}, u32[]{:S(2)}) collective-permute-start(bf16[2,64,1024]{2,1,0:T(8,128)(2,1)} %get-tuple-element.71.refs_2_), channel_id=1, source_target_pairs={{0,16},{8,24},{16,0},{24,8},{1,17},{9,25},{17,1},{25,9},{2,18},{10... | collective-permute-start | bytes 786440 | tf_op jit(solution)/shard_map/ppermute | solution.py:413
  44.2 11.9 %collective-permute-start.10 = (bf16[2,64,768]{2,1,0:T(8,128)(2,1)S(1)}, bf16[2,64,768]{2,1,0:T(8,128)(2,1)}, u32[]{:S(2)}, u32[]{:S(2)}) collective-permute-start(bf16[2,64,768]{2,1,0:T(8,128)(2,1)S(1)} %fusion.4.refs_1_), channel_id=1, source_target_pairs={{0,16},{8,24},{16,0},{24,8},{1,17},{9,25},{17,1},{25,9},{2,18},{10... | collective-permute-start | bytes 589832 | tf_op jit(solution)/shard_map/ppermute | solution.py:413
  45.7 23.8 %collective-permute-start.12 = (bf16[2,64,1024]{2,1,0:T(8,128)(2,1)}, bf16[2,64,1024]{2,1,0:T(8,128)(2,1)S(1)}, u32[]{:S(2)}, u32[]{:S(2)}) collective-permute-start(bf16[2,64,1024]{2,1,0:T(8,128)(2,1)} %get-tuple-element.71.refs_2_), channel_id=1, source_target_pairs={{0,8},{8,0},{16,24},{24,16},{1,9},{9,1},{17,25},{25,17},{2,10},{10... | collective-permute-start | bytes 786440 | tf_op jit(solution)/shard_map/ppermute | solution.py:409
  54.4 14.6 %collective-permute-start.18 = (bf16[2,64,1280]{2,1,0:T(8,128)(2,1)S(1)}, bf16[2,64,1280]{2,1,0:T(8,128)(2,1)S(1)}, u32[]{:S(2)}, u32[]{:S(2)}) collective-permute-start(bf16[2,64,1280]{2,1,0:T(8,128)(2,1)S(1)} %get-tuple-element.81.refs_0_), channel_id=1, source_target_pairs={{0,16},{8,24},{16,0},{24,8},{1,17},{9,25},{17,1},{25,9},{2,18},{10... | collective-permute-start | bytes 983048 | tf_op jit(solution)/shard_map/ppermute | solution.py:413
  56.0 13.4 %collective-permute-start.13 = (bf16[2,64,1024]{2,1,0:T(8,128)(2,1)S(1)}, bf16[2,64,1024]{2,1,0:T(8,128)(2,1)S(1)}, u32[]{:S(2)}, u32[]{:S(2)}) collective-permute-start(bf16[2,64,1024]{2,1,0:T(8,128)(2,1)S(1)} %in_order.10), channel_id=1, source_target_pairs={{0,8},{8,0},{16,24},{24,16},{1,9},{9,1},{17,25},{25,17},{2,10},{10... | collective-permute-start | bytes 786440 | tf_op jit(solution)/shard_map/ppermute | solution.py:409
  59.8 15.8 %collective-permute-start.15 = (bf16[2,64,768]{2,1,0:T(8,128)(2,1)S(1)}, bf16[2,64,768]{2,1,0:T(8,128)(2,1)S(1)}, u32[]{:S(2)}, u32[]{:S(2)}) collective-permute-start(bf16[2,64,768]{2,1,0:T(8,128)(2,1)S(1)} %get-tuple-element.88.refs_2_.refs_0_), channel_id=1, source_target_pairs={{0,16},{8,24},{16,0},{24,8},{1,17},{9,25},{17,1},{25,9},{2,18},{10... | collective-permute-start | bytes 589832 | tf_op jit(solution)/shard_map/ppermute | solution.py:413
  68.8 13.6 %collective-permute-start.17 = (bf16[2,64,1280]{2,1,0:T(8,128)(2,1)S(1)}, bf16[2,64,1280]{2,1,0:T(8,128)(2,1)S(1)}, u32[]{:S(2)}, u32[]{:S(2)}) collective-permute-start(bf16[2,64,1280]{2,1,0:T(8,128)(2,1)S(1)} %get-tuple-element.81.refs_0_), channel_id=1, source_target_pairs={{0,8},{8,0},{16,24},{24,16},{1,9},{9,1},{17,25},{25,17},{2,10},{10... | collective-permute-start | bytes 983048 | tf_op jit(solution)/shard_map/ppermute | solution.py:409
  69.1 16.5 %collective-permute-start.14 = (bf16[2,64,768]{2,1,0:T(8,128)(2,1)S(1)}, bf16[2,64,768]{2,1,0:T(8,128)(2,1)S(1)}, u32[]{:S(2)}, u32[]{:S(2)}) collective-permute-start(bf16[2,64,768]{2,1,0:T(8,128)(2,1)S(1)} %get-tuple-element.88.refs_2_.refs_0_), channel_id=1, source_target_pairs={{0,8},{8,0},{16,24},{24,16},{1,9},{9,1},{17,25},{25,17},{2,10},{10... | collective-permute-start | bytes 589832 | tf_op jit(solution)/shard_map/ppermute | solution.py:409
  69.5 6.5 %copy-start.15 = (bf16[2048,256]{1,0:T(8,128)(2,1)S(1)}, bf16[2048,256]{1,0:T(8,128)(2,1)}, u32[]{:S(2)}) copy-start(bf16[2048,256]{1,0:T(8,128)(2,1)} %copy-done.13) | copy-start | bytes 3145732
  75.4 7.1 %collective-permute-start.19 = (bf16[2,64,1280]{2,1,0:T(8,128)(2,1)S(1)}, bf16[2,64,1280]{2,1,0:T(8,128)(2,1)S(1)}, u32[]{:S(2)}, u32[]{:S(2)}) collective-permute-start(bf16[2,64,1280]{2,1,0:T(8,128)(2,1)S(1)} %in_order.11), channel_id=1, source_target_pairs={{0,8},{8,0},{16,24},{24,16},{1,9},{9,1},{17,25},{25,17},{2,10},{10... | collective-permute-start | bytes 983048 | tf_op jit(solution)/shard_map/ppermute | solution.py:409
  75.6 10.0 %collective-permute-start.16 = (bf16[2,64,768]{2,1,0:T(8,128)(2,1)S(1)}, bf16[2,64,768]{2,1,0:T(8,128)(2,1)S(1)}, u32[]{:S(2)}, u32[]{:S(2)}) collective-permute-start(bf16[2,64,768]{2,1,0:T(8,128)(2,1)S(1)} %collective-permute-done.15.refs_2_), channel_id=1, source_target_pairs={{0,8},{8,0},{16,24},{24,16},{1,9},{9,1},{17,25},{25,17},{2,10},{10... | collective-permute-start | bytes 589832 | tf_op jit(solution)/shard_map/ppermute | solution.py:409
  87.5 8.5 %collective-permute-start.20 = (bf16[2,2,32,1024]{3,2,0,1:T(8,128)(2,1)S(1)}, bf16[2,2,32,1024]{3,2,0,1:T(8,128)(2,1)S(1)}, u32[]{:S(2)}, u32[]{:S(2)}) collective-permute-start(bf16[2,2,32,1024]{3,2,0,1:T(8,128)(2,1)S(1)} %fusion.2), channel_id=1, source_target_pairs={{0,1},{1,0},{2,3},{3,2},{4,5},{5,4},{6,7},{7,6},{8,9},{9,8},{10,11... | collective-permute-start | bytes 786440 | tf_op jit(solution)/shard_map/ppermute | solution.py:395
  89.1 8.7 %collective-permute-start.23 = (bf16[2,2,32,1024]{3,2,1,0:T(8,128)(2,1)S(1)}, bf16[2,2,32,1024]{3,2,1,0:T(8,128)(2,1)S(1)}, u32[]{:S(2)}, u32[]{:S(2)}) collective-permute-start(bf16[2,2,32,1024]{3,2,1,0:T(8,128)(2,1)S(1)} %fusion.3), channel_id=1, source_target_pairs={{0,2},{1,3},{2,0},{3,1},{4,6},{5,7},{6,4},{7,5},{8,10},{9,11},{10,... | collective-permute-start | bytes 786440 | tf_op jit(solution)/shard_map/ppermute | solution.py:395
  96.1 6.8 %collective-permute-start.21 = (bf16[2,32,1024]{2,1,0:T(8,128)(2,1)S(1)}, bf16[2,32,1024]{2,1,0:T(8,128)(2,1)S(1)}, u32[]{:S(2)}, u32[]{:S(2)}) collective-permute-start(bf16[2,32,1024]{2,1,0:T(8,128)(2,1)S(1)} %fusion.6), channel_id=1, source_target_pairs={{0,2},{1,3},{2,0},{3,1},{4,6},{5,7},{6,4},{7,5},{8,10},{9,11},{10,... | collective-permute-start | bytes 393224 | tf_op jit(solution)/shard_map/ppermute | solution.py:395
  97.9 7.7 %collective-permute-start.24 = (bf16[2,32,1024]{2,1,0:T(8,128)(2,1)S(1)}, bf16[2,32,1024]{2,1,0:T(8,128)(2,1)S(1)}, u32[]{:S(2)}, u32[]{:S(2)}) collective-permute-start(bf16[2,32,1024]{2,1,0:T(8,128)(2,1)S(1)} %fusion.7), channel_id=1, source_target_pairs={{0,1},{1,0},{2,3},{3,2},{4,5},{5,4},{6,7},{7,6},{8,9},{9,8},{10,11... | collective-permute-start | bytes 393224 | tf_op jit(solution)/shard_map/ppermute | solution.py:395
  103.0 7.2 %collective-permute-start.22 = (bf16[32,1024]{1,0:T(8,128)(2,1)S(1)}, bf16[32,1024]{1,0:T(8,128)(2,1)S(1)}, u32[]{:S(2)}, u32[]{:S(2)}) collective-permute-start(bf16[32,1024]{1,0:T(8,128)(2,1)S(1)} %fusion.10), channel_id=1, source_target_pairs={{0,4},{1,5},{2,6},{3,7},{4,0},{5,1},{6,2},{7,3},{8,12},{9,13},{10,... | collective-permute-start | bytes 196616 | tf_op jit(solution)/shard_map/ppermute | solution.py:395
  105.7 5.9 %collective-permute-start.25 = (bf16[32,1024]{1,0:T(8,128)(2,1)S(1)}, bf16[32,1024]{1,0:T(8,128)(2,1)S(1)}, u32[]{:S(2)}, u32[]{:S(2)}) collective-permute-start(bf16[32,1024]{1,0:T(8,128)(2,1)S(1)} %fusion.11), channel_id=1, source_target_pairs={{0,4},{1,5},{2,6},{3,7},{4,0},{5,1},{6,2},{7,3},{8,12},{9,13},{10,... | collective-permute-start | bytes 196616 | tf_op jit(solution)/shard_map/ppermute | solution.py:395
  (10 other events, 11.7 us)

commit v7 on v6

--- a/solution.py
+++ b/solution.py
@@ -1,4 +1,5 @@
 import functools
+import math
 
 import jax
 import jax.numpy as jnp
@@ -9,9 +10,9 @@
 
 BF16 = jnp.bfloat16
 F32 = jnp.float32
-VMEM_BYTES = 24 * 1024 * 1024
+VMEM_BYTES = 6 * 1024 * 1024
 SHARES = (2, 4, 5, 3)
-SLOTS = 4
+SLOTS = 3
 COST = 40
 WHOLE = pl.BlockSpec(memory_space=pltpu.VMEM)
 REMOTE = pl.BlockSpec(memory_space=pl.ANY)
@@ -29,7 +30,9 @@
     return block, [(a, b - a) for a, b in zip(edges, edges[1:]) if b > a]
 
 
-def call(kernel, name, in_specs, out_specs, out_shape, scratch, size, args, aliases=None):
+def call(kernel, name, in_specs, out_specs, out_shape, scratch, size, args, aliases=None, room=0):
+    held = [item for item in scratch if len(getattr(item, 'shape', ())) > 2]
+    room += VMEM_BYTES + sum(math.prod(item.shape) * item.dtype.itemsize for item in held)
     return pl.pallas_call(
         kernel,
         in_specs=in_specs,
@@ -37,7 +40,7 @@
         out_shape=out_shape,
         scratch_shapes=scratch,
         input_output_aliases=aliases or {},
-        compiler_params=pltpu.CompilerParams(vmem_limit_bytes=VMEM_BYTES),
+        compiler_params=pltpu.CompilerParams(vmem_limit_bytes=room),
         cost_estimate=pl.CostEstimate(
             flops=COST * size, bytes_accessed=size, transcendentals=0
         ),
@@ -60,6 +63,24 @@
         1,
         [value, *after],
         {0: 0},
+    )
+
+
+def pack_kernel(count, *refs):
+    for step, ref in enumerate(refs[:count]):
+        refs[-1][step] = ref[...]
+
+
+def packed(values, after):
+    return call(
+        functools.partial(pack_kernel, len(values)),
+        "packed",
+        [WHOLE] * len(values) + [REMOTE] * len(after),
+        WHOLE,
+        jax.ShapeDtypeStruct((len(values), *values[0].shape), values[0].dtype),
+        [],
+        1,
+        [*values, *after],
     )
 
 
@@ -212,44 +233,67 @@
     )
 
 
-def input_kernel(layout, gate_ref, up_ref, *refs):
-    quarters, rows, columns, held, first, last, skipped, extra = layout
-    refs = refs[skipped:]
-    pieces, rest = refs[:quarters], refs[quarters:]
-    earlier, rest = rest[:extra], rest[extra:]
-    if first:
-        x_ref, rest = rest[0], rest[1:]
+def input_kernel(layout, ins, outs, *refs):
+    quarters, rows, block, chunk, held, first, last, skipped, write, old, ahead = layout
+    given, made, scratch = refs[:ins], list(refs[ins : ins + outs]), list(refs[ins + outs :])
+    (gate_ref, up_ref), given = given[:2], given[2 + skipped :]
+    outer = quarters // 2
+    pieces, given = given[: outer + 1], list(given[outer + 1 :])
+    sources = (gate_ref, up_ref)
     depth = gate_ref.shape[0]
     half = depth // 2
-    if held:
-        *sums, grads = rest
-        weights, copies = (gate_ref, up_ref), []
+    earlier = []
+    if first:
+        x_ref, xt_ref = given.pop(0), made.pop(0)
     else:
-        *sums, grads, scratch, sems = rest
-        weights = (scratch.at[0], scratch.at[1])
-        copies = [
+        earlier = [given.pop(0) for _ in range(old)]
+    if write and not first:
+        xt_ref = given.pop(0)
+    if ahead and held:
+        sources = (given.pop(0), given.pop(0))
+    loaded = [made.pop() for _ in range(2)][::-1] if ahead else []
+    grad_outs = [made.pop() for _ in range(2)][::-1] if write else []
+    grads = made.pop()
+    sums = made
+
+    def fetch(columns, targets, sems):
+        return [
             pltpu.make_async_copy(
                 source.at[pl.ds(h * half, half), columns],
-                scratch.at[k, pl.ds(h * half, half)],
+                target.at[pl.ds(h * half, half)],
                 sems.at[k, h],
             )
             for h in range(2)
-            for k, source in enumerate((gate_ref, up_ref))
+            for k, (source, target) in enumerate(zip(sources, targets))
         ]
+
+    weights, copies, later, writes = (gate_ref, up_ref), [], [], []
+    start, count = chunk
+    if not held:
+        store, sems = scratch.pop(0), scratch.pop(0)
+        weights = (store.at[0], store.at[1])
+        copies = fetch(pl.ds(start * block, count * block), weights, sems)
         for copy in copies:
             copy.start()
-    outer = quarters // 2
+    if ahead:
+        later = fetch(pl.ds(ahead[0] * block, ahead[1] * block), loaded, scratch.pop())
+    if held:
+        for copy in later:
+            copy.start()
     me = lax.axis_index("row")
     place, core = me // 2, me % 2
-    for j, piece in enumerate(pieces):
-        step, swap = j // 2, j % 2
+    for step in range(outer):
         there = (place + outer - step) % outer * 2
-        at = pl.multiple_of((there + (core + swap) % 2) * rows, rows)
+        mine = pl.multiple_of((there + core) * rows, rows)
+        other = pl.multiple_of((there + 1 - core) * rows, rows)
         for k in range(2):
-            grads[k, pl.ds(at, rows), :] = piece[k]
+            grads[k, pl.ds(mine, rows), :] = pieces[step][k]
+            grads[k, pl.ds(other, rows), :] = pieces[outer][step, k]
     if first:
-        xt_ref, sums = sums[0], sums[1:]
         xt_ref[...] = x_ref[...].T
+    if write:
+        products, sems = scratch
+        writes = weight_terms(block, chunk, xt_ref, grads, grad_outs, products, sems)
     dims = (((1,), (1,)), ((), ()))
     flipped = [] if last else [grads[k].T for k in range(2)]
     deep = 256 if depth % 512 == 0 else 128
@@ -259,6 +303,8 @@
         if copies and d * deep % half == 0:
             copies[2 * index].wait()
             copies[2 * index + 1].wait()
+            for copy in later[2 * index : 2 * index + 2]:
+                copy.start()
         term = None
         if earlier:
             term = earlier[index][:, across] if last else earlier[0][at, :]
@@ -275,68 +321,77 @@
             sums[0][at, :] = term
         else:
             sums[index][:, across] = term.T
-
-
-def input_part(quarters, block, chunk, weights, held, pieces, acc, final, x, after):
-    depth = x.shape[1]
-    rows = pieces[0].shape[1]
-    tokens = rows * quarters
+    for copy in writes + later:
+        copy.wait()
+
+
+def input_part(quarters, block, chunk, weights, held, pieces, acc, final, x, after, write, ahead):
+    depth, tokens = x.shape[1], x.shape[0]
+    rows = tokens // quarters
     start, count = chunk
     width = count * block
     first, last = acc is None, final == 0
     args = [*weights, *after, *pieces, *([x] if first else acc)]
-    sums = [jax.ShapeDtypeStruct((depth, tokens), F32)]
-    if final <= 1:
-        sums = [jax.ShapeDtypeStruct((tokens, depth // 2), F32)] * 2
-    out_shape = sums + [jax.ShapeDtypeStruct((2, tokens, width), BF16)]
-    if first:
-        out_shape = [jax.ShapeDtypeStruct((depth, tokens), BF16)] + out_shape
-    columns = pl.ds(start * block, width)
-    layout = (quarters, rows, columns, held, first, last, len(after), 0 if first else len(acc))
-    scratch = []
+    in_specs = [WHOLE if held else REMOTE] * 2 + [REMOTE] * len(after)
+    in_specs += [WHOLE] * (len(args) - len(in_specs))
+    out_shape = [jax.ShapeDtypeStruct((depth, tokens), BF16)] if first else []
+    out_shape += [jax.ShapeDtypeStruct((tokens, depth // 2), F32)] * 2 if final <= 1 else [
+        jax.ShapeDtypeStruct((depth, tokens), F32)
+    ]
+    out_shape.append(jax.ShapeDtypeStruct((2, tokens, width), BF16))
+    scratch, aliases, room = [], {}, 0
     if not held:
-        scratch = [pltpu.VMEM((2, depth, width), BF16), pltpu.SemaphoreType.DMA((2, 2))]
+        scratch += [pltpu.VMEM((2, depth, width), BF16), pltpu.SemaphoreType.DMA((2, 2))]
+    out_specs = [WHOLE] * len(out_shape)
+    if write:
+        xt, state, full = write
+        args += [] if first else [xt]
+        in_specs += [] if first else [WHOLE]
+    if ahead:
+        (chunk_ahead, sources), ahead = ahead, ahead[0]
+        if held:
+            args += [in_hbm(value) for value in sources]
+            in_specs += [REMOTE] * 2
+    if write:
+        aliases = {len(args) + k: len(out_shape) + k for k in range(len(state))}
+        args += [in_hbm(value) for value in state]
+        in_specs += [REMOTE] * len(state)
+        out_shape += [pltpu.HBM((depth, full), BF16)] * 2
+        out_specs += [REMOTE] * 2
+        scratch += [pltpu.VMEM((2, count, depth, block), BF16), pltpu.SemaphoreType.DMA((2, count))]
+    if ahead:
+        out_shape += [jax.ShapeDtypeStruct((depth, ahead[1] * block), BF16)] * 2
+        out_specs += [WHOLE] * 2
+        scratch.append(pltpu.SemaphoreType.DMA((2, 2)))
+    if held or ahead:
+        room = 4 * depth * max(width, ahead[1] * block if ahead else 0)
+    old = 0 if first else len(acc)
+    layout = (quarters, rows, block, chunk, held, first, last, len(after), bool(write), old, ahead)
     out = call(
-        functools.partial(input_kernel, layout),
+        functools.partial(input_kernel, layout, len(args), len(out_shape)),
         "input_part",
-        [WHOLE if held else REMOTE] * 2
-        + [REMOTE] * len(after)
-        + [WHOLE] * (len(args) - 2 - len(after)),
-        [WHOLE] * len(out_shape),
+        in_specs,
+        out_specs,
         out_shape,
         scratch,
-        tokens * depth,
+        tokens * depth * (1 if first else width),
         args,
-    )
-    xt, out = (out[0], out[1:]) if first else (None, out)
-    return xt, out[:-1], out[-1]
-
-
-def weight_kernel(block, chunk, ahead, skipped, xt_ref, grads_ref, *refs):
+        aliases,
+        room,
+    )
+    out = list(out)
+    xt = out.pop(0) if first else None
+    fetched = [out.pop() for _ in range(2)][::-1] if ahead else None
+    state = [out.pop() for _ in range(2)][::-1] if write else None
+    return xt, out[:-1], out[-1], state, fetched
+
+
+def weight_terms(block, chunk, xt_ref, grads_ref, outs, products, sems):
     start, count = chunk
-    refs = refs[skipped:]
-    sources, refs = (refs[:2], refs[2:]) if ahead else ((), refs)
-    refs = refs[2:] if len(refs) > (8 if ahead else 4) else refs
-    gate_out, up_out, *loaded, products, sems = refs
-    fetched = []
-    if ahead:
-        loaded, fetch_sems = loaded[:2], loaded[2]
-        half = loaded[0].shape[0] // 2
-        fetched = [
-            pltpu.make_async_copy(
-                source.at[pl.ds(h * half, half), ahead],
-                target.at[pl.ds(h * half, half)],
-                fetch_sems.at[k, h],
-            )
-            for h in range(2)
-            for k, (source, target) in enumerate(zip(sources, loaded))
-        ]
-        for copy in fetched:
-            copy.start()
     xt = xt_ref[...]
     copies = []
     for j in range(count):
-        for k, out in enumerate((gate_out, up_out)):
+        for k, out in enumerate(outs):
             piece = grads_ref[k, :, j * block : (j + 1) * block]
             products[k, j] = jnp.dot(xt, piece, preferred_element_type=F32).astype(BF16)
             copy = pltpu.make_async_copy(
@@ -344,36 +399,31 @@
             )
             copy.start()
             copies.append(copy)
-    for copy in fetched + copies:
+    return copies
+
+
+def weight_kernel(block, chunk, skipped, xt_ref, grads_ref, *refs):
+    *outs, products, sems = refs[skipped:]
+    for copy in weight_terms(block, chunk, xt_ref, grads_ref, outs, products, sems):
         copy.wait()
 
 
-def weight_part(block, chunk, full, xt, grads, state, after, ahead, sources):
+def weight_part(block, chunk, full, xt, grads, state, after):
     depth, tokens = xt.shape
-    start, count = chunk
-    columns = pl.ds(ahead[0] * block, ahead[1] * block) if ahead else None
-    sources = [in_hbm(value) for value in sources] if ahead else []
-    args = [xt, grads, *after, *sources, *[in_hbm(value) for value in state]]
+    count = chunk[1]
+    args = [xt, grads, *after, *[in_hbm(value) for value in state]]
     first = len(args) - len(state)
-    aliases = {first + k: k for k in range(len(state))}
-    out_shape = [pltpu.HBM((depth, full), BF16)] * 2
-    scratch = []
-    if ahead:
-        out_shape += [jax.ShapeDtypeStruct((depth, ahead[1] * block), BF16)] * 2
-        scratch = [pltpu.SemaphoreType.DMA((2, 2))]
-    out = call(
-        functools.partial(weight_kernel, block, chunk, columns, len(after)),
+    return call(
+        functools.partial(weight_kernel, block, chunk, len(args) - 2),
         "weight_part",
         [WHOLE] * 2 + [REMOTE] * (len(args) - 2),
-        [REMOTE] * 2 + [WHOLE] * (len(out_shape) - 2),
-        out_shape,
-        scratch
-        + [pltpu.VMEM((2, count, depth, block), BF16), pltpu.SemaphoreType.DMA((2, count))],
+        [REMOTE] * 2,
+        [pltpu.HBM((depth, full), BF16)] * 2,
+        [pltpu.VMEM((2, count, depth, block), BF16), pltpu.SemaphoreType.DMA((2, count))],
         tokens * depth * count * block,
         args,
-        aliases,
-    )
-    return out[:2], out[2:]
+        {first + k: k for k in range(len(state))},
+    )
 
 
 def token_sums(halves, columns, orders):
@@ -432,7 +482,7 @@
             if i == number - 1:
                 relay(0, sums[-1][:1])
                 take_input(0, x, None, [])
-            send = in_order(send, crossed[i - 1][:1] + pieces[i - 3][2:3] + grads)
+            send = in_order(send, crossed[i - 1][:1] + pieces[i - 1][:1] + pieces[i - 2][1:2] + grads)
         got = sibling(send)
         near = [(far[step - 1] + got[step].astype(F32)).astype(BF16) for step in range(1, outer)]
         gots.append(got)
@@ -440,61 +490,62 @@
         crossed.append([across(value, step + 1) for step, value in enumerate(near)])
         return x, loaded
 
-    def middle(i, hidden):
+    def middle(i, hidden, after):
         start, count = chunks[i]
         at = slice(start * block, (start + count) * block)
-        after = pieces[i - 2][2:3] if i >= 2 else []
         hidden, mine = middle_part(
             outer, at, owns[i], gots[i], crossed[i], hidden_grad, hidden, after
         )
-        pieces.append([mine, sibling(mine)] + [across(mine, step) for step in range(1, outer)])
+        pieces.append([mine] + [across(mine, step) for step in range(1, outer)])
         return hidden
 
     def relay(i, after):
-        mine, near, *far = pieces[i]
-        group = [mine, near]
-        for there in far:
-            group += [there, sibling(in_order(there, after) if after else there)]
-        groups.append(group)
+        groups.append(pieces[i] + [sibling(packed(pieces[i], after))])
 
     def take_input(i, x, acc, after):
         weights = held[i] if i in held else [in_hbm(value) for value in both]
-        xt, total, whole = input_part(
-            quarters, block, chunks[i], weights, i in held, groups[i], acc, number - 1 - i, x, after
+        write = (flipped[0] if i else None, state, full) if i < number - 2 else None
+        later = 2 if i == 0 else 1
+        ahead = None
+        if later < number - i and i + later not in held and i != 1:
+            ahead = (chunks[i + later], both)
+        xt, total, whole, written, fetched = input_part(
+            quarters, block, chunks[i], weights, i in held, groups[i], acc, number - 1 - i, x,
+            after, write, ahead,
         )
         if i == 0:
             flipped.append(xt)
             totals.append(total)
+        if written:
+            state[:] = written
+        if fetched:
+            held[i + later] = fetched
         grads.append(whole)
         return total
 
-    totals = []
+    totals, state = [], []
     x, early, hidden = inputs, [], None
     for i in range(number):
         x, early = forward(i, x, early)
-        hidden = middle(i, hidden)
-    acc, state = None, []
+        if i < 3:
+            hidden = middle(i, hidden, pieces[0][1:2] if i == 2 else [])
+    acc = None
     for i in range(number):
         if i == 0 and grads:
             acc = totals[0]
-        else:
-            last = i == number - 1
-            relay(i, [] if last else grads[-1:] + pieces[-1][:1] if i == number - 2 else sums[-1][:1])
-            after = pieces[i + 1][:1] + sums[-1][:1] if i == 1 < number - 1 else []
-            acc = take_input(i, x, acc, after)
-        if i < number - 2:
-            state, held[i + 2] = weight_part(
-                block, chunks[i], full, flipped[0], grads[i], state, [], chunks[i + 2], both
-            )
+            continue
+        after = sums[-1][:1] + pieces[i + 1][:1] if i == 1 and number > 3 else []
+        relay(i, grads[-1:] + pieces[-1][:1] if i > 1 else sums[-1][:1])
+        acc = take_input(i, x, acc, after)
+        for j in range(len(pieces), number if i else 0):
+            hidden = middle(j, hidden, grads[-1:])
     bits = columns.bit_length() - 1
     order = list(range(bits))
     stages = [acc] + token_sums(acc, columns, [order, order[1::-1] + order[2:]])
     input_grad = jnp.concatenate([half.astype(BF16) for half in stages[-1]], axis=1)
     for i in range(max(number - 2, 0), number):
         after = stages[min(i - max(number - 2, 0), bits)]
-        state, _ = weight_part(
-            block, chunks[i], full, flipped[0], grads[i], state, after, None, []
-        )
+        state = weight_part(block, chunks[i], full, flipped[0], grads[i], state, after)
     return hidden, input_grad, state[0], state[1]
 
 

time: 113 us -> 107 us (0.947)
  Pallas kernels: 55 us -> 50.3 us
  starting transfers between devices: 24.2 us -> 21.3 us
  local copies, waits for them, and re-layouts: 9.3 us -> 10.9 us
    pallas_call x22 -> x21, Pallas kernels: 55 us -> 50.3 us  [call(): pl.pallas_call(kernel, in_specs=in_specs, out_specs=out_specs, out_shape=...]
    ppermute x12 -> x8, waiting for transfers between devices: 3.3 us -> 6.15 us  [sibling(): return lax.ppermute(value, 'row', swap)]
    ppermute x8, waiting for transfers between devices: 12.5 us -> 9.69 us  [across(): return lax.ppermute(value, 'row', moves)]
    ppermute x8, starting transfers between devices: 12.6 us -> 10.5 us  [across(): return lax.ppermute(value, 'row', moves)]
    unnamed x35 -> x18, local copies, waits for them, and re-layouts: 9.11 us -> 10.7 us
  transfers between devices with their start and end apart: 26 -> 22, of which waited for: 10 -> 12; matrix products, arithmetic and copies ran while one was open for 0% -> 0% of each run, Pallas kernels for 42% -> 41%
where the time goes in v7:
time: 107 us; the launch traced here: 106 us
  Pallas kernels  50.3 us (47%)
  waiting for transfers between devices  21.7 us (20%)
  starting transfers between devices  21.3 us (20%)
  local copies, waits for them, and re-layouts  10.9 us (10%)
    pallas_call x21, Pallas kernels, call(): pl.pallas_call(kernel, in_specs=in_specs, out_specs=out_specs, out_shape=...  50.3 us
    unnamed x18, local copies, waits for them, and re-layouts  10.7 us
    ppermute x8, starting transfers between devices, across(): return lax.ppermute(value, 'row', moves)  10.5 us
    ppermute x8, waiting for transfers between devices, across(): return lax.ppermute(value, 'row', moves)  9.69 us
    ppermute x6, starting transfers between devices, token_sums(): got.append(lax.ppermute(send.astype(BF16), 'col', moves))  9.51 us
    ppermute x8, waiting for transfers between devices, sibling(): return lax.ppermute(value, 'row', swap)  6.15 us
    ppermute x6, waiting for transfers between devices, token_sums(): got.append(lax.ppermute(send.astype(BF16), 'col', moves))  5.9 us
  transfers between devices with their start and end apart: 22, of which 12 were waited for; matrix products, arithmetic and copies ran while one was open for 0% of the time, Pallas kernels for 41%

profile of v7, /device:TPU:0, one launch (start us, length us, event | category | flops | bytes accessed | tf_op | source)
XLA Modules:
  0.0 106.2 jit_solution(8348352196001228946)
XLA Ops:
  0.6 4.0 %forward_part.4 = (f32[2,64,512]{2,1,0:T(8,128)S(1)}, f32[1,2,64,512]{3,2,1,0:T(8,128)S(1)}, bf16[2,2,64,512]{3,2,1,0:T(8,128)(2,1)S(1)}, bf16[256,2048]{1,0:T(8...) custom-call(bf16[256,2048]{1,0:T(8,128)(2,1)} %refs_0_.3, bf16[2048,3584]{1,0:T(8,128)(2,1)} %refs_6_.1, ...), custom_call_target="tpu_custom_call" | custom-call | flops 10737418240 | bytes 268435456 | tf_op jit(solution)/shard_map/forward_part/pallas_call | solution.py:36
  5.2 1.2 %collective-permute-done.got_ref = bf16[2,2,64,512]{3,2,1,0:T(8,128)(2,1)S(1)} collective-permute-done((bf16[2,2,64,512]{3,2,1,0:T(8,128)(2,1)S(1)}, bf16[2,2,64,512]{3,2,1,0:T(8,128)(2,1)S(1)}, u32[]{:S(2)}, u32[]{:S(2)}) %collective-permute-start) | collective-permute-done | bytes 262176 | tf_op jit(solution)/shard_map/ppermute | solution.py:459
  6.4 2.9 %collective-permute-start.1 = (bf16[2,64,512]{2,1,0:T(8,128)(2,1)S(1)}, bf16[2,64,512]{2,1,0:T(8,128)(2,1)S(1)}, u32[]{:S(2)}, u32[]{:S(2)}) collective-permute-start(bf16[2,64,512]{2,1,0:T(8,128)(2,1)S(1)} %fusion.5.refs_5_), channel_id=1, source_target_pairs={{0,16},{8,24},{16,0},{24,8},{1,17},{9,25},{17,1},{25,9},{2,18},{10... | collective-permute-start | bytes 393224 | tf_op jit(solution)/shard_map/ppermute | solution.py:463
  9.3 4.4 %forward_part.5 = (f32[2,64,1024]{2,1,0:T(8,128)S(1)}, f32[1,2,64,1024]{3,2,1,0:T(8,128)S(1)}, bf16[2,2,64,1024]{3,2,1,0:T(8,128)(2,1)S(1)}, bf16[2048,256]{1,0:T(8,128)(2,1)S(1)}, bf16[2048,256]{1,0:T(8,128)(2,1)S(1)}) custom-call(bf16[256,2048]{1,0:T(8,128)(2,1)S(1)} %get-tuple-element.54.refs_0_.refs_5_, bf16[2048,3584]{1,0:T(8,128)(2,1)} %refs_6_.1, ...), custom_call_target="tpu_custom_call" | custom-call | flops 21474836480 | bytes 536870912 | tf_op jit(solution)/shard_map/forward_part/pallas_call | solution.py:36
  14.0 1.9 %collective-permute-done.2.got_ref = bf16[2,2,64,1024]{3,2,1,0:T(8,128)(2,1)S(1)} collective-permute-done((bf16[2,2,64,1024]{3,2,1,0:T(8,128)(2,1)S(1)}, bf16[2,2,64,1024]{3,2,1,0:T(8,128)(2,1)S(1)}, u32[]{:S(2)}, u32[]{:S(2)}) %collective-permute-start.2) | collective-permute-done | bytes 524320 | tf_op jit(solution)/shard_map/ppermute | solution.py:459
  15.9 1.1 %collective-permute-start.3 = (bf16[2,64,1024]{2,1,0:T(8,128)(2,1)S(1)}, bf16[2,64,1024]{2,1,0:T(8,128)(2,1)S(1)}, u32[]{:S(2)}, u32[]{:S(2)}) collective-permute-start(bf16[2,64,1024]{2,1,0:T(8,128)(2,1)S(1)} %fusion.1.refs_5_), channel_id=1, source_target_pairs={{0,16},{8,24},{16,0},{24,8},{1,17},{9,25},{17,1},{25,9},{2,18},{10... | collective-permute-start | bytes 786440 | tf_op jit(solution)/shard_map/ppermute | solution.py:463
  17.1 5.4 %forward_part.6 = (f32[2,64,1280]{2,1,0:T(8,128)S(1)}, f32[1,2,64,1280]{3,2,1,0:T(8,128)S(1)}, bf16[2,2,64,1280]{3,2,1,0:T(8,128)(2,1)S(1)}, bf16[2048,256]{1,0:T(8,128)(2,1)S(1)}, bf16[2048,256]{1,0:T(8,128)(2,1)S(1)}) custom-call(bf16[256,2048]{1,0:T(8,128)(2,1)S(1)} %get-tuple-element.54.refs_0_.refs_5_, bf16[2048,3584]{1,0:T(8,128)(2,1)} %refs_6_.1, ...), custom_call_target="tpu_custom_call" | custom-call | flops 26843545600 | bytes 671088640 | tf_op jit(solution)/shard_map/forward_part/pallas_call | solution.py:36
  22.5 1.9 %collective-permute-done.3.refs_0_.refs_1_ = bf16[2,64,1024]{2,1,0:T(8,128)(2,1)S(1)} collective-permute-done((bf16[2,64,1024]{2,1,0:T(8,128)(2,1)S(1)}, bf16[2,64,1024]{2,1,0:T(8,128)(2,1)S(1)}, u32[]{:S(2)}, u32[]{:S(2)}) %collective-permute-start.3) | collective-permute-done | bytes 262176 | tf_op jit(solution)/shard_map/ppermute | solution.py:463
  28.0 3.1 %collective-permute-done.6.refs_1_.refs_3_ = bf16[2,64,512]{2,1,0:T(8,128)(2,1)S(1)} collective-permute-done((bf16[2,64,512]{2,1,0:T(8,128)(2,1)S(1)}, bf16[2,64,512]{2,1,0:T(8,128)(2,1)S(1)}, u32[]{:S(2)}, u32[]{:S(2)}) %collective-permute-start.6) | collective-permute-done | bytes 131104 | tf_op jit(solution)/shard_map/ppermute | solution.py:463
  31.1 3.6 %forward_part.7 = (f32[2,64,768]{2,1,0:T(8,128)S(1)}, f32[1,2,64,768]{3,2,1,0:T(8,128)S(1)}, bf16[2,2,64,768]{3,2,1,0:T(8,128)(2,1)S(1)}) custom-call(bf16[256,2048]{1,0:T(8,128)(2,1)S(1)} %get-tuple-element.54.refs_0_.refs_5_, bf16[2048,3584]{1,0:T(8,128)(2,1)} %refs_6_.1, bf16[2048,3584]{1,0:T(8,128)(2,1)} %refs_7_.1, ...), custom_call_target="tpu_custom_call" | custom-call | flops 16106127360 | bytes 402653184 | tf_op jit(solution)/shard_map/forward_part/pallas_call | solution.py:36
  34.8 7.2 %input_part.4 = (bf16[2048,256]{1,0:T(8,128)(2,1)S(1)}, f32[2048,256]{1,0:T(8,128)S(1)}, bf16[2,256,512]{2,1,0:T(8,128)(2,1)S(1)}, bf16[2048,3584]{1,0:T(8,128)(...) custom-call(bf16[2048,3584]{1,0:T(8,128)(2,1)} %refs_6_.1, ...), custom_call_target="tpu_custom_call" | custom-call | flops 20971520 | bytes 524288 | tf_op jit(solution)/shard_map/input_part/pallas_call | solution.py:36
  42.0 1.2 %collective-permute-done.5.refs_0_.refs_1_ = bf16[2,64,1280]{2,1,0:T(8,128)(2,1)S(1)} collective-permute-done((bf16[2,64,1280]{2,1,0:T(8,128)(2,1)S(1)}, bf16[2,64,1280]{2,1,0:T(8,128)(2,1)S(1)}, u32[]{:S(2)}, u32[]{:S(2)}) %collective-permute-start.5) | collective-permute-done | bytes 327712 | tf_op jit(solution)/shard_map/ppermute | solution.py:463
  43.6 1.7 %collective-permute-done.9.got_ref = bf16[2,2,64,768]{3,2,1,0:T(8,128)(2,1)S(1)} collective-permute-done((bf16[2,2,64,768]{3,2,1,0:T(8,128)(2,1)S(1)}, bf16[2,2,64,768]{3,2,1,0:T(8,128)(2,1)S(1)}, u32[]{:S(2)}, u32[]{:S(2)}) %collective-permute-start.9) | collective-permute-done | bytes 393248 | tf_op jit(solution)/shard_map/ppermute | solution.py:459
  47.7 8.6 %input_part.5 = (f32[2048,256]{1,0:T(8,128)S(1)}, bf16[2,256,1024]{2,1,0:T(8,128)(2,1)S(1)}, bf16[2048,3584]{1,0:T(8,128)(2,1)}, bf16[2048,3584]{1,0:T(8,128)(2,1)}) custom-call(bf16[2048,3584]{1,0:T(8,128)(2,1)} %refs_6_.1, bf16[2048,3584]{1,0:T(8,128)(2,1)} %refs_7_.1, ...), custom_call_target="tpu_custom_call", output_to_operand_aliasing={{2}: (9, {}), {3}: (10, {})} | custom-call | flops 21474836480 | bytes 536870912 | tf_op jit(solution)/shard_map/input_part/pallas_call | solution.py:36
  56.3 3.5 %collective-permute-done.10.refs_0_ = bf16[2,64,768]{2,1,0:T(8,128)(2,1)S(1)} collective-permute-done((bf16[2,64,768]{2,1,0:T(8,128)(2,1)S(1)}, bf16[2,64,768]{2,1,0:T(8,128)(2,1)S(1)}, u32[]{:S(2)}, u32[]{:S(2)}) %collective-permute-start.10) | collective-permute-done | bytes 196640 | tf_op jit(solution)/shard_map/ppermute | solution.py:463
  62.9 5.3 %input_part.6 = (f32[256,1024]{1,0:T(8,128)S(1)}, f32[256,1024]{1,0:T(8,128)S(1)}, bf16[2,256,1280]{2,1,0:T(8,128)(2,1)S(1)}, bf16[2048,768]{1,0:T(8,128)(2,1)S(1)}, bf16[2048,768]{1,0:T(8,128)(2,1)S(1)}) custom-call(bf16[2048,1280]{1,0:T(8,128)(2,1)S(1)} %get-tuple-element.86.refs_0_, bf16[2048,1280]{1,0:T(8,128)(2,1)S(1)} %get-tuple-element.87.refs_1_, ...), custom_call_target="tpu_custom_call" | custom-call | flops 26843545600 | bytes 671088640 | tf_op jit(solution)/shard_map/input_part/pallas_call | solution.py:36
  68.2 1.6 %copy-done.1 = bf16[2048,768]{1,0:T(8,128)(2,1)} copy-done((bf16[2048,768]{1,0:T(8,128)(2,1)}, bf16[2048,768]{1,0:T(8,128)(2,1)S(1)}, u32[]{:S(2)}) %copy-start.1) | copy-done | bytes 3145752
  69.9 1.7 %copy-done.3 = bf16[2048,768]{1,0:T(8,128)(2,1)} copy-done((bf16[2048,768]{1,0:T(8,128)(2,1)}, bf16[2048,768]{1,0:T(8,128)(2,1)S(1)}, u32[]{:S(2)}) %copy-start.3) | copy-done | bytes 3145752
  73.4 1.9 %copy-done.2 = bf16[2048,768]{1,0:T(8,128)(2,1)S(1)} copy-done((bf16[2048,768]{1,0:T(8,128)(2,1)S(1)}, bf16[2048,768]{1,0:T(8,128)(2,1)}, u32[]{:S(2)}) %copy-start.2) | copy-done | bytes 3145752
  75.3 1.9 %copy-done.4 = bf16[2048,768]{1,0:T(8,128)(2,1)S(1)} copy-done((bf16[2048,768]{1,0:T(8,128)(2,1)S(1)}, bf16[2048,768]{1,0:T(8,128)(2,1)}, u32[]{:S(2)}) %copy-start.4) | copy-done | bytes 3145752
  77.2 1.2 %copy-done.6 = f32[256,1024]{1,0:T(8,128)S(1)} copy-done((f32[256,1024]{1,0:T(8,128)S(1)}, f32[256,1024]{1,0:T(8,128)}, u32[]{:S(2)}) %copy-start.6) | copy-done | bytes 1048600
  78.4 1.2 %copy-done.8 = f32[256,1024]{1,0:T(8,128)S(1)} copy-done((f32[256,1024]{1,0:T(8,128)S(1)}, f32[256,1024]{1,0:T(8,128)}, u32[]{:S(2)}) %copy-start.8) | copy-done | bytes 1048600
  79.6 1.8 %input_part.7 = (f32[256,1024]{1,0:T(8,128)S(1)}, f32[256,1024]{1,0:T(8,128)S(1)}, bf16[2,256,768]{2,1,0:T(8,128)(2,1)S(1)}) custom-call(bf16[2048,768]{1,0:T(8,128)(2,1)S(1)} %copy-done.2, bf16[2048,768]{1,0:T(8,128)(2,1)S(1)} %copy-done.4, bf16[2,64,768]{2,1,0:T(8,128)(2,1)S(1)} %get-tuple-element.88.refs_3_.refs_0_.refs_2_, ...), custom_call_target="tpu_custom_call" | custom-call | flops 16106127360 | bytes 402653184 | tf_op jit(solution)/shard_map/input_part/pallas_call | solution.py:36
  81.5 1.6 %collective-permute-start.16 = (bf16[2,2,32,1024]{3,2,0,1:T(8,128)(2,1)S(1)}, bf16[2,2,32,1024]{3,2,0,1:T(8,128)(2,1)S(1)}, u32[]{:S(2)}, u32[]{:S(2)}) collective-permute-start(bf16[2,2,32,1024]{3,2,0,1:T(8,128)(2,1)S(1)} %fusion.2), channel_id=1, source_target_pairs={{0,1},{1,0},{2,3},{3,2},{4,5},{5,4},{6,7},{7,6},{8,9},{9,8},{10,11... | collective-permute-start | bytes 786440 | tf_op jit(solution)/shard_map/ppermute | solution.py:445
  83.1 1.6 %collective-permute-start.19 = (bf16[2,2,32,1024]{3,2,1,0:T(8,128)(2,1)S(1)}, bf16[2,2,32,1024]{3,2,1,0:T(8,128)(2,1)S(1)}, u32[]{:S(2)}, u32[]{:S(2)}) collective-permute-start(bf16[2,2,32,1024]{3,2,1,0:T(8,128)(2,1)S(1)} %fusion.3), channel_id=1, source_target_pairs={{0,2},{1,3},{2,0},{3,1},{4,6},{5,7},{6,4},{7,5},{8,10},{9,11},{10,... | collective-permute-start | bytes 786440 | tf_op jit(solution)/shard_map/ppermute | solution.py:445
  84.8 4.8 %weight_part.2 = (bf16[2048,3584]{1,0:T(8,128)(2,1)}, bf16[2048,3584]{1,0:T(8,128)(2,1)}) custom-call(bf16[2048,256]{1,0:T(8,128)(2,1)S(1)} %get-tuple-element.80.refs_8_.xt_ref, bf16[2,256,1280]{2,1,0:T(8,128)(2,1)S(1)} %get-tuple-element.92.refs_2_.grads_ref, ...), custom_call_target="tpu_custom_call", output_to_operand_aliasing={{0}: (4, {}), {1}: (5, {})} | custom-call | flops 26843545600 | bytes 671088640 | tf_op jit(solution)/shard_map/weight_part/pallas_call | solution.py:36
  90.1 1.6 %collective-permute-start.17 = (bf16[2,32,1024]{2,1,0:T(8,128)(2,1)S(1)}, bf16[2,32,1024]{2,1,0:T(8,128)(2,1)S(1)}, u32[]{:S(2)}, u32[]{:S(2)}) collective-permute-start(bf16[2,32,1024]{2,1,0:T(8,128)(2,1)S(1)} %fusion.6), channel_id=1, source_target_pairs={{0,2},{1,3},{2,0},{3,1},{4,6},{5,7},{6,4},{7,5},{8,10},{9,11},{10,... | collective-permute-start | bytes 393224 | tf_op jit(solution)/shard_map/ppermute | solution.py:445
  91.8 1.6 %collective-permute-start.20 = (bf16[2,32,1024]{2,1,0:T(8,128)(2,1)S(1)}, bf16[2,32,1024]{2,1,0:T(8,128)(2,1)S(1)}, u32[]{:S(2)}, u32[]{:S(2)}) collective-permute-start(bf16[2,32,1024]{2,1,0:T(8,128)(2,1)S(1)} %fusion.7), channel_id=1, source_target_pairs={{0,1},{1,0},{2,3},{3,2},{4,5},{5,4},{6,7},{7,6},{8,9},{9,8},{10,11... | collective-permute-start | bytes 393224 | tf_op jit(solution)/shard_map/ppermute | solution.py:445
  93.4 3.4 %weight_part.3 = (bf16[2048,3584]{1,0:T(8,128)(2,1)}, bf16[2048,3584]{1,0:T(8,128)(2,1)}) custom-call(bf16[2048,256]{1,0:T(8,128)(2,1)S(1)} %get-tuple-element.80.refs_8_.xt_ref, bf16[2,256,768]{2,1,0:T(8,128)(2,1)S(1)} %get-tuple-element.97.grads_ref, f32[2,2,32,1024]{3,2,1,0:T(8,128)S(1)} %copy.21.refs_0_, ...), custom_call_target="tpu_custom_call", output_to_operand_aliasing={{0}: (4, {}), {1}: (5, {})} | custom-call | flops 16106127360 | bytes 402653184 | tf_op jit(solution)/shard_map/weight_part/pallas_call | solution.py:36
  96.9 2.7 %collective-permute-start.18 = (bf16[32,1024]{1,0:T(8,128)(2,1)S(1)}, bf16[32,1024]{1,0:T(8,128)(2,1)S(1)}, u32[]{:S(2)}, u32[]{:S(2)}) collective-permute-start(bf16[32,1024]{1,0:T(8,128)(2,1)S(1)} %fusion.10), channel_id=1, source_target_pairs={{0,4},{1,5},{2,6},{3,7},{4,0},{5,1},{6,2},{7,3},{8,12},{9,13},{10,... | collective-permute-start | bytes 196616 | tf_op jit(solution)/shard_map/ppermute | solution.py:445
  100.0 4.1 %collective-permute-done.18 = bf16[32,1024]{1,0:T(8,128)(2,1)S(1)} collective-permute-done((bf16[32,1024]{1,0:T(8,128)(2,1)S(1)}, bf16[32,1024]{1,0:T(8,128)(2,1)S(1)}, u32[]{:S(2)}, u32[]{:S(2)}) %collective-permute-start.18) | collective-permute-done | bytes 65568 | tf_op jit(solution)/shard_map/ppermute | solution.py:445
  104.1 1.4 %collective-permute-done.21 = bf16[32,1024]{1,0:T(8,128)(2,1)S(1)} collective-permute-done((bf16[32,1024]{1,0:T(8,128)(2,1)S(1)}, bf16[32,1024]{1,0:T(8,128)(2,1)S(1)}, u32[]{:S(2)}, u32[]{:S(2)}) %collective-permute-start.21) | collective-permute-done | bytes 65568 | tf_op jit(solution)/shard_map/ppermute | solution.py:445
  (69 shorter events, 13.9 us)
Async XLA Ops:
  4.7 1.7 %collective-permute-start = (bf16[2,2,64,512]{3,2,1,0:T(8,128)(2,1)S(1)}, bf16[2,2,64,512]{3,2,1,0:T(8,128)(2,1)S(1)}, u32[]{:S(2)}, u32[]{:S(2)}) collective-permute-start(bf16[2,2,64,512]{3,2,1,0:T(8,128)(2,1)S(1)} %get-tuple-element.58), channel_id=1, source_target_pairs={{0,8},{8,0},{16,24},{24,16},{1,9},{9,1},{17,25},{25,17},{2,10},{10... | collective-permute-start | bytes 786440 | tf_op jit(solution)/shard_map/ppermute | solution.py:459
  6.4 7.4 %collective-permute-start.1 = (bf16[2,64,512]{2,1,0:T(8,128)(2,1)S(1)}, bf16[2,64,512]{2,1,0:T(8,128)(2,1)S(1)}, u32[]{:S(2)}, u32[]{:S(2)}) collective-permute-start(bf16[2,64,512]{2,1,0:T(8,128)(2,1)S(1)} %fusion.5.refs_5_), channel_id=1, source_target_pairs={{0,16},{8,24},{16,0},{24,8},{1,17},{9,25},{17,1},{25,9},{2,18},{10... | collective-permute-start | bytes 393224 | tf_op jit(solution)/shard_map/ppermute | solution.py:463
  9.3 4.5 %copy-start = (bf16[64,3584]{1,0:T(8,128)(2,1)S(1)}, bf16[64,3584]{1,0:T(8,128)(2,1)}, u32[]{:S(2)}) copy-start(bf16[64,3584]{1,0:T(8,128)(2,1)} %upstream_ref.7) | copy-start | bytes 1376260
  13.9 2.0 %collective-permute-start.2 = (bf16[2,2,64,1024]{3,2,1,0:T(8,128)(2,1)S(1)}, bf16[2,2,64,1024]{3,2,1,0:T(8,128)(2,1)S(1)}, u32[]{:S(2)}, u32[]{:S(2)}) collective-permute-start(bf16[2,2,64,1024]{3,2,1,0:T(8,128)(2,1)S(1)} %in_order.3), channel_id=1, source_target_pairs={{0,8},{8,0},{16,24},{24,16},{1,9},{9,1},{17,25},{25,17},{2,10},{10... | collective-permute-start | bytes 1572872 | tf_op jit(solution)/shard_map/ppermute | solution.py:459
  15.9 8.4 %collective-permute-start.3 = (bf16[2,64,1024]{2,1,0:T(8,128)(2,1)S(1)}, bf16[2,64,1024]{2,1,0:T(8,128)(2,1)S(1)}, u32[]{:S(2)}, u32[]{:S(2)}) collective-permute-start(bf16[2,64,1024]{2,1,0:T(8,128)(2,1)S(1)} %fusion.1.refs_5_), channel_id=1, source_target_pairs={{0,16},{8,24},{16,0},{24,8},{1,17},{9,25},{17,1},{25,9},{2,18},{10... | collective-permute-start | bytes 786440 | tf_op jit(solution)/shard_map/ppermute | solution.py:463
  24.6 2.2 %collective-permute-start.4 = (bf16[2,2,64,1280]{3,2,1,0:T(8,128)(2,1)S(1)}, bf16[2,2,64,1280]{3,2,1,0:T(8,128)(2,1)S(1)}, u32[]{:S(2)}, u32[]{:S(2)}) collective-permute-start(bf16[2,2,64,1280]{3,2,1,0:T(8,128)(2,1)S(1)} %in_order.4), channel_id=1, source_target_pairs={{0,8},{8,0},{16,24},{24,16},{1,9},{9,1},{17,25},{25,17},{2,10},{10... | collective-permute-start | bytes 1966088 | tf_op jit(solution)/shard_map/ppermute | solution.py:459
  24.7 6.4 %collective-permute-start.6 = (bf16[2,64,512]{2,1,0:T(8,128)(2,1)S(1)}, bf16[2,64,512]{2,1,0:T(8,128)(2,1)S(1)}, u32[]{:S(2)}, u32[]{:S(2)}) collective-permute-start(bf16[2,64,512]{2,1,0:T(8,128)(2,1)S(1)} %get-tuple-element.64.refs_2_.refs_0_), channel_id=1, source_target_pairs={{0,16},{8,24},{16,0},{24,8},{1,17},{9,25},{17,1},{25,9},{2,18},{10... | collective-permute-start | bytes 393224 | tf_op jit(solution)/shard_map/ppermute | solution.py:463
  25.8 17.7 %collective-permute-start.7 = (bf16[2,64,1024]{2,1,0:T(8,128)(2,1)S(1)}, bf16[2,64,1024]{2,1,0:T(8,128)(2,1)S(1)}, u32[]{:S(2)}, u32[]{:S(2)}) collective-permute-start(bf16[2,64,1024]{2,1,0:T(8,128)(2,1)S(1)} %get-tuple-element.71.refs_2_.refs_0_.refs_4_), channel_id=1, source_target_pairs={{0,16},{8,24},{16,0},{24,8},{1,17},{9,25},{17,1},{25,9},{2,18},{10... | collective-permute-start | bytes 786440 | tf_op jit(solution)/shard_map/ppermute | solution.py:463
  26.8 16.4 %collective-permute-start.5 = (bf16[2,64,1280]{2,1,0:T(8,128)(2,1)S(1)}, bf16[2,64,1280]{2,1,0:T(8,128)(2,1)S(1)}, u32[]{:S(2)}, u32[]{:S(2)}) collective-permute-start(bf16[2,64,1280]{2,1,0:T(8,128)(2,1)S(1)} %fusion.refs_5_.refs_2_), channel_id=1, source_target_pairs={{0,16},{8,24},{16,0},{24,8},{1,17},{9,25},{17,1},{25,9},{2,18},{10... | collective-permute-start | bytes 983048 | tf_op jit(solution)/shard_map/ppermute | solution.py:463
  31.1 3.7 %collective-permute-start.8 = (bf16[2,2,64,512]{3,2,1,0:T(8,128)(2,1)S(1)}, bf16[2,2,64,512]{3,2,1,0:T(8,128)(2,1)S(1)}, u32[]{:S(2)}, u32[]{:S(2)}) collective-permute-start(bf16[2,2,64,512]{3,2,1,0:T(8,128)(2,1)S(1)} %packed.4), channel_id=1, source_target_pairs={{0,8},{8,0},{16,24},{24,16},{1,9},{9,1},{17,25},{25,17},{2,10},{10... | collective-permute-start | bytes 786440 | tf_op jit(solution)/shard_map/ppermute | solution.py:459
  43.5 1.8 %collective-permute-start.9 = (bf16[2,2,64,768]{3,2,1,0:T(8,128)(2,1)S(1)}, bf16[2,2,64,768]{3,2,1,0:T(8,128)(2,1)S(1)}, u32[]{:S(2)}, u32[]{:S(2)}) collective-permute-start(bf16[2,2,64,768]{3,2,1,0:T(8,128)(2,1)S(1)} %in_order.5), channel_id=1, source_target_pairs={{0,8},{8,0},{16,24},{24,16},{1,9},{9,1},{17,25},{25,17},{2,10},{10... | collective-permute-start | bytes 1179656 | tf_op jit(solution)/shard_map/ppermute | solution.py:459
  45.4 2.2 %collective-permute-start.11 = (bf16[2,2,64,1024]{3,2,1,0:T(8,128)(2,1)S(1)}, bf16[2,2,64,1024]{3,2,1,0:T(8,128)(2,1)S(1)}, u32[]{:S(2)}, u32[]{:S(2)}) collective-permute-start(bf16[2,2,64,1024]{3,2,1,0:T(8,128)(2,1)S(1)} %packed.5), channel_id=1, source_target_pairs={{0,8},{8,0},{16,24},{24,16},{1,9},{9,1},{17,25},{25,17},{2,10},{10... | collective-permute-start | bytes 1572872 | tf_op jit(solution)/shard_map/ppermute | solution.py:459
  45.6 15.1 %collective-permute-start.12 = (bf16[2,64,1280]{2,1,0:T(8,128)(2,1)S(1)}, bf16[2,64,1280]{2,1,0:T(8,128)(2,1)S(1)}, u32[]{:S(2)}, u32[]{:S(2)}) collective-permute-start(bf16[2,64,1280]{2,1,0:T(8,128)(2,1)S(1)} %get-tuple-element.76.refs_2_.refs_3_.refs_0_), channel_id=1, source_target_pairs={{0,16},{8,24},{16,0},{24,8},{1,17},{9,25},{17,1},{25,9},{2,18},{10... | collective-permute-start | bytes 983048 | tf_op jit(solution)/shard_map/ppermute | solution.py:463
  46.7 13.1 %collective-permute-start.10 = (bf16[2,64,768]{2,1,0:T(8,128)(2,1)S(1)}, bf16[2,64,768]{2,1,0:T(8,128)(2,1)S(1)}, u32[]{:S(2)}, u32[]{:S(2)}) collective-permute-start(bf16[2,64,768]{2,1,0:T(8,128)(2,1)S(1)} %fusion.4.refs_2_), channel_id=1, source_target_pairs={{0,16},{8,24},{16,0},{24,8},{1,17},{9,25},{17,1},{25,9},{2,18},{10... | collective-permute-start | bytes 589832 | tf_op jit(solution)/shard_map/ppermute | solution.py:463
  60.7 2.2 %collective-permute-start.13 = (bf16[2,2,64,1280]{3,2,1,0:T(8,128)(2,1)S(1)}, bf16[2,2,64,1280]{3,2,1,0:T(8,128)(2,1)S(1)}, u32[]{:S(2)}, u32[]{:S(2)}) collective-permute-start(bf16[2,2,64,1280]{3,2,1,0:T(8,128)(2,1)S(1)} %packed.6), channel_id=1, source_target_pairs={{0,8},{8,0},{16,24},{24,16},{1,9},{9,1},{17,25},{25,17},{2,10},{10... | collective-permute-start | bytes 1966088 | tf_op jit(solution)/shard_map/ppermute | solution.py:459
  60.8 10.7 %collective-permute-start.14 = (bf16[2,64,768]{2,1,0:T(8,128)(2,1)S(1)}, bf16[2,64,768]{2,1,0:T(8,128)(2,1)S(1)}, u32[]{:S(2)}, u32[]{:S(2)}) collective-permute-start(bf16[2,64,768]{2,1,0:T(8,128)(2,1)S(1)} %get-tuple-element.88.refs_3_.refs_0_.refs_2_), channel_id=1, source_target_pairs={{0,16},{8,24},{16,0},{24,8},{1,17},{9,25},{17,1},{25,9},{2,18},{10... | collective-permute-start | bytes 589832 | tf_op jit(solution)/shard_map/ppermute | solution.py:463
  68.2 1.6 %copy-start.1 = (bf16[2048,768]{1,0:T(8,128)(2,1)}, bf16[2048,768]{1,0:T(8,128)(2,1)S(1)}, u32[]{:S(2)}) copy-start(bf16[2048,768]{1,0:T(8,128)(2,1)S(1)} %get-tuple-element.90.refs_0_) | copy-start | bytes 9437188
  69.9 1.7 %copy-start.3 = (bf16[2048,768]{1,0:T(8,128)(2,1)}, bf16[2048,768]{1,0:T(8,128)(2,1)S(1)}, u32[]{:S(2)}) copy-start(bf16[2048,768]{1,0:T(8,128)(2,1)S(1)} %get-tuple-element.91.refs_1_) | copy-start | bytes 9437188
  71.6 1.0 copy-start.5
  71.6 1.4 %copy-start.7 = (f32[256,1024]{1,0:T(8,128)}, f32[256,1024]{1,0:T(8,128)S(1)}, u32[]{:S(2)}) copy-start(f32[256,1024]{1,0:T(8,128)S(1)} %get-tuple-element.94.refs_6_) | copy-start | bytes 3145732
  71.6 1.8 %collective-permute-start.15 = (bf16[2,2,64,768]{3,2,1,0:T(8,128)(2,1)S(1)}, bf16[2,2,64,768]{3,2,1,0:T(8,128)(2,1)S(1)}, u32[]{:S(2)}, u32[]{:S(2)}) collective-permute-start(bf16[2,2,64,768]{3,2,1,0:T(8,128)(2,1)S(1)} %packed.7), channel_id=1, source_target_pairs={{0,8},{8,0},{16,24},{24,16},{1,9},{9,1},{17,25},{25,17},{2,10},{10... | collective-permute-start | bytes 1179656 | tf_op jit(solution)/shard_map/ppermute | solution.py:459
  73.4 1.9 %copy-start.2 = (bf16[2048,768]{1,0:T(8,128)(2,1)S(1)}, bf16[2048,768]{1,0:T(8,128)(2,1)}, u32[]{:S(2)}) copy-start(bf16[2048,768]{1,0:T(8,128)(2,1)} %copy-done.1) | copy-start | bytes 9437188
  75.3 1.9 %copy-start.4 = (bf16[2048,768]{1,0:T(8,128)(2,1)S(1)}, bf16[2048,768]{1,0:T(8,128)(2,1)}, u32[]{:S(2)}) copy-start(bf16[2048,768]{1,0:T(8,128)(2,1)} %copy-done.3) | copy-start | bytes 9437188
  77.2 1.2 %copy-start.6 = (f32[256,1024]{1,0:T(8,128)S(1)}, f32[256,1024]{1,0:T(8,128)}, u32[]{:S(2)}) copy-start(f32[256,1024]{1,0:T(8,128)} %copy-done.5) | copy-start | bytes 3145732
  78.4 1.2 %copy-start.8 = (f32[256,1024]{1,0:T(8,128)S(1)}, f32[256,1024]{1,0:T(8,128)}, u32[]{:S(2)}) copy-start(f32[256,1024]{1,0:T(8,128)} %copy-done.7) | copy-start | bytes 3145732
  81.5 8.4 %collective-permute-start.16 = (bf16[2,2,32,1024]{3,2,0,1:T(8,128)(2,1)S(1)}, bf16[2,2,32,1024]{3,2,0,1:T(8,128)(2,1)S(1)}, u32[]{:S(2)}, u32[]{:S(2)}) collective-permute-start(bf16[2,2,32,1024]{3,2,0,1:T(8,128)(2,1)S(1)} %fusion.2), channel_id=1, source_target_pairs={{0,1},{1,0},{2,3},{3,2},{4,5},{5,4},{6,7},{7,6},{8,9},{9,8},{10,11... | collective-permute-start | bytes 786440 | tf_op jit(solution)/shard_map/ppermute | solution.py:445
  83.1 8.6 %collective-permute-start.19 = (bf16[2,2,32,1024]{3,2,1,0:T(8,128)(2,1)S(1)}, bf16[2,2,32,1024]{3,2,1,0:T(8,128)(2,1)S(1)}, u32[]{:S(2)}, u32[]{:S(2)}) collective-permute-start(bf16[2,2,32,1024]{3,2,1,0:T(8,128)(2,1)S(1)} %fusion.3), channel_id=1, source_target_pairs={{0,2},{1,3},{2,0},{3,1},{4,6},{5,7},{6,4},{7,5},{8,10},{9,11},{10,... | collective-permute-start | bytes 786440 | tf_op jit(solution)/shard_map/ppermute | solution.py:445
  90.1 6.8 %collective-permute-start.17 = (bf16[2,32,1024]{2,1,0:T(8,128)(2,1)S(1)}, bf16[2,32,1024]{2,1,0:T(8,128)(2,1)S(1)}, u32[]{:S(2)}, u32[]{:S(2)}) collective-permute-start(bf16[2,32,1024]{2,1,0:T(8,128)(2,1)S(1)} %fusion.6), channel_id=1, source_target_pairs={{0,2},{1,3},{2,0},{3,1},{4,6},{5,7},{6,4},{7,5},{8,10},{9,11},{10,... | collective-permute-start | bytes 393224 | tf_op jit(solution)/shard_map/ppermute | solution.py:445
  91.8 7.8 %collective-permute-start.20 = (bf16[2,32,1024]{2,1,0:T(8,128)(2,1)S(1)}, bf16[2,32,1024]{2,1,0:T(8,128)(2,1)S(1)}, u32[]{:S(2)}, u32[]{:S(2)}) collective-permute-start(bf16[2,32,1024]{2,1,0:T(8,128)(2,1)S(1)} %fusion.7), channel_id=1, source_target_pairs={{0,1},{1,0},{2,3},{3,2},{4,5},{5,4},{6,7},{7,6},{8,9},{9,8},{10,11... | collective-permute-start | bytes 393224 | tf_op jit(solution)/shard_map/ppermute | solution.py:445
  96.9 7.2 %collective-permute-start.18 = (bf16[32,1024]{1,0:T(8,128)(2,1)S(1)}, bf16[32,1024]{1,0:T(8,128)(2,1)S(1)}, u32[]{:S(2)}, u32[]{:S(2)}) collective-permute-start(bf16[32,1024]{1,0:T(8,128)(2,1)S(1)} %fusion.10), channel_id=1, source_target_pairs={{0,4},{1,5},{2,6},{3,7},{4,0},{5,1},{6,2},{7,3},{8,12},{9,13},{10,... | collective-permute-start | bytes 196616 | tf_op jit(solution)/shard_map/ppermute | solution.py:445
  99.6 5.9 %collective-permute-start.21 = (bf16[32,1024]{1,0:T(8,128)(2,1)S(1)}, bf16[32,1024]{1,0:T(8,128)(2,1)S(1)}, u32[]{:S(2)}, u32[]{:S(2)}) collective-permute-start(bf16[32,1024]{1,0:T(8,128)(2,1)S(1)} %fusion.11), channel_id=1, source_target_pairs={{0,4},{1,5},{2,6},{3,7},{4,0},{5,1},{6,2},{7,3},{8,12},{9,13},{10,... | collective-permute-start | bytes 196616 | tf_op jit(solution)/shard_map/ppermute | solution.py:445

commit v8 on v7

--- a/solution.py
+++ b/solution.py
@@ -11,7 +11,7 @@
 BF16 = jnp.bfloat16
 F32 = jnp.float32
 VMEM_BYTES = 6 * 1024 * 1024
-SHARES = (2, 4, 5, 3)
+SHARES = (3, 6, 5)
 SLOTS = 3
 COST = 40
 WHOLE = pl.BlockSpec(memory_space=pltpu.VMEM)
@@ -476,13 +476,13 @@
         owns.append(own)
         if i == 0:
             x, loaded = loaded[0], loaded[1:]
-        elif i < 3:
-            send = in_order(send, crossed[i - 1][:1] + pieces[i - 1][:1])
         else:
-            if i == number - 1:
+            after = crossed[i - 1][:1] + pieces[i - 1][:1]
+            if i == number - 1 and i > 1:
                 relay(0, sums[-1][:1])
                 take_input(0, x, None, [])
-            send = in_order(send, crossed[i - 1][:1] + pieces[i - 1][:1] + pieces[i - 2][1:2] + grads)
+                after += pieces[i - 2][1:2] + grads
+            send = in_order(send, after)
         got = sibling(send)
         near = [(far[step - 1] + got[step].astype(F32)).astype(BF16) for step in range(1, outer)]
         gots.append(got)
@@ -505,10 +505,7 @@
     def take_input(i, x, acc, after):
         weights = held[i] if i in held else [in_hbm(value) for value in both]
         write = (flipped[0] if i else None, state, full) if i < number - 2 else None
-        later = 2 if i == 0 else 1
-        ahead = None
-        if later < number - i and i + later not in held and i != 1:
-            ahead = (chunks[i + later], both)
+        ahead = (chunks[2], both) if i == 0 and number > 2 else None
         xt, total, whole, written, fetched = input_part(
             quarters, block, chunks[i], weights, i in held, groups[i], acc, number - 1 - i, x,
             after, write, ahead,
@@ -519,29 +516,25 @@
         if written:
             state[:] = written
         if fetched:
-            held[i + later] = fetched
+            held[2] = fetched
         grads.append(whole)
         return total
 
     totals, state = [], []
-    x, early, hidden = inputs, [], None
+    x, early, hidden, acc = inputs, [], None, None
     for i in range(number):
         x, early = forward(i, x, early)
-        if i < 3:
-            hidden = middle(i, hidden, pieces[0][1:2] if i == 2 else [])
-    acc = None
+        hidden = middle(i, hidden, [])
     for i in range(number):
         if i == 0 and grads:
             acc = totals[0]
             continue
-        after = sums[-1][:1] + pieces[i + 1][:1] if i == 1 and number > 3 else []
-        relay(i, grads[-1:] + pieces[-1][:1] if i > 1 else sums[-1][:1])
-        acc = take_input(i, x, acc, after)
-        for j in range(len(pieces), number if i else 0):
-            hidden = middle(j, hidden, grads[-1:])
+        relay(i, grads[1:2] if i > 1 else pieces[-1][:1])
+        acc = take_input(i, x, acc, pieces[-1][:1] if 0 < i < number - 1 else [])
     bits = columns.bit_length() - 1
     order = list(range(bits))
-    stages = [acc] + token_sums(acc, columns, [order, order[1::-1] + order[2:]])
+    orders = [order[:1] + order[2:] + order[1:2], order[1::-1] + order[2:]]
+    stages = [acc] + token_sums(acc, columns, orders)
     input_grad = jnp.concatenate([half.astype(BF16) for half in stages[-1]], axis=1)
     for i in range(max(number - 2, 0), number):
         after = stages[min(i - max(number - 2, 0), bits)]

time: 107 us -> 108 us (level)
  waiting for transfers between devices: 21.7 us -> 31.6 us
  Pallas kernels: 50.3 us -> 47.3 us
  local copies, waits for them, and re-layouts: 10.9 us -> 7.92 us
  starting transfers between devices: 21.3 us -> 19.4 us
    ppermute x8 -> x6, waiting for transfers between devices: 9.69 us -> 21 us  [across(): return lax.ppermute(value, 'row', moves)]
    ppermute x8 -> x6, starting transfers between devices: 10.5 us -> 7.23 us  [across(): return lax.ppermute(value, 'row', moves)]
    pallas_call x21 -> x16, Pallas kernels: 50.3 us -> 47.3 us  [call(): pl.pallas_call(kernel, in_specs=in_specs, out_specs=out_specs, out_shape=...]
    unnamed x18 -> x22, local copies, waits for them, and re-layouts: 10.7 us -> 7.77 us
    ppermute x6, waiting for transfers between devices: 5.9 us -> 3.82 us  [token_sums(): got.append(lax.ppermute(send.astype(BF16), 'col', moves))]
    ppermute x6, starting transfers between devices: 9.51 us -> 10.8 us  [token_sums(): got.append(lax.ppermute(send.astype(BF16), 'col', moves))]
    ppermute x8 -> x6, waiting for transfers between devices: 6.15 us -> 6.75 us  [sibling(): return lax.ppermute(value, 'row', swap)]
  transfers between devices with their start and end apart: 22 -> 18, of which waited for: 12 -> 10; matrix products, arithmetic and copies ran while one was open for 0% -> 0% of each run, Pallas kernels for 41% -> 36%
where the time goes in v8:
time: 108 us
  Pallas kernels  47.3 us (44%)
  waiting for transfers between devices  31.6 us (29%)
  starting transfers between devices  19.4 us (18%)
  local copies, waits for them, and re-layouts  7.92 us (7%)
    pallas_call x16, Pallas kernels, call(): pl.pallas_call(kernel, in_specs=in_specs, out_specs=out_specs, out_shape=...  47.3 us
    ppermute x6, waiting for transfers between devices, across(): return lax.ppermute(value, 'row', moves)  21 us
    ppermute x6, starting transfers between devices, token_sums(): got.append(lax.ppermute(send.astype(BF16), 'col', moves))  10.8 us
    unnamed x22, local copies, waits for them, and re-layouts  7.77 us
    ppermute x6, starting transfers between devices, across(): return lax.ppermute(value, 'row', moves)  7.23 us
    ppermute x6, waiting for transfers between devices, sibling(): return lax.ppermute(value, 'row', swap)  6.75 us
    ppermute x6, waiting for transfers between devices, token_sums(): got.append(lax.ppermute(send.astype(BF16), 'col', moves))  3.82 us
  transfers between devices with their start and end apart: 18, of which 10 were waited for; matrix products, arithmetic and copies ran while one was open for 0% of the time, Pallas kernels for 36%

profile of v8, /device:TPU:0, one launch (start us, length us, event | category | flops | bytes accessed | tf_op | source)
XLA Modules:
  0.0 108.1 jit_solution(11528660196123266581)
XLA Ops:
  0.6 4.9 %forward_part.3 = (f32[2,64,768]{2,1,0:T(8,128)S(1)}, f32[1,2,64,768]{3,2,1,0:T(8,128)S(1)}, bf16[2,2,64,768]{3,2,1,0:T(8,128)(2,1)S(1)}, bf16[256,2048]{1,0:T(8...) custom-call(bf16[256,2048]{1,0:T(8,128)(2,1)} %refs_0_.3, bf16[2048,3584]{1,0:T(8,128)(2,1)} %refs_0_.5, ...), custom_call_target="tpu_custom_call" | custom-call | flops 16106127360 | bytes 402653184 | tf_op jit(solution)/shard_map/forward_part/pallas_call | solution.py:36
  6.1 1.3 %collective-permute-done.got_ref = bf16[2,2,64,768]{3,2,1,0:T(8,128)(2,1)S(1)} collective-permute-done((bf16[2,2,64,768]{3,2,1,0:T(8,128)(2,1)S(1)}, bf16[2,2,64,768]{3,2,1,0:T(8,128)(2,1)S(1)}, u32[]{:S(2)}, u32[]{:S(2)}) %collective-permute-start) | collective-permute-done | bytes 393248 | tf_op jit(solution)/shard_map/ppermute | solution.py:459
  7.5 2.9 %collective-permute-start.1 = (bf16[2,64,768]{2,1,0:T(8,128)(2,1)S(1)}, bf16[2,64,768]{2,1,0:T(8,128)(2,1)S(1)}, u32[]{:S(2)}, u32[]{:S(2)}) collective-permute-start(bf16[2,64,768]{2,1,0:T(8,128)(2,1)S(1)} %fusion.4.refs_5_), channel_id=1, source_target_pairs={{0,16},{8,24},{16,0},{24,8},{1,17},{9,25},{17,1},{25,9},{2,18},{10... | collective-permute-start | bytes 589832 | tf_op jit(solution)/shard_map/ppermute | solution.py:463
  10.4 6.1 %forward_part.4 = (f32[2,64,1536]{2,1,0:T(8,128)S(1)}, f32[1,2,64,1536]{3,2,1,0:T(8,128)S(1)}, bf16[2,2,64,1536]{3,2,1,0:T(8,128)(2,1)S(1)}, bf16[2048,256]{1,0:T(8,128)(2,1)S(1)}, bf16[2048,256]{1,0:T(8,128)(2,1)S(1)}) custom-call(bf16[256,2048]{1,0:T(8,128)(2,1)S(1)} %get-tuple-element.41.refs_0_.refs_5_, bf16[2048,3584]{1,0:T(8,128)(2,1)} %refs_0_.5, ...), custom_call_target="tpu_custom_call" | custom-call | flops 32212254720 | bytes 805306368 | tf_op jit(solution)/shard_map/forward_part/pallas_call | solution.py:36
  17.6 1.4 %collective-permute-done.2.got_ref = bf16[2,2,64,1536]{3,2,1,0:T(8,128)(2,1)S(1)} collective-permute-done((bf16[2,2,64,1536]{3,2,1,0:T(8,128)(2,1)S(1)}, bf16[2,2,64,1536]{3,2,1,0:T(8,128)(2,1)S(1)}, u32[]{:S(2)}, u32[]{:S(2)}) %collective-permute-start.2) | collective-permute-done | bytes 786464 | tf_op jit(solution)/shard_map/ppermute | solution.py:459
  20.0 4.6 %collective-permute-done.4.refs_1_.refs_3_ = bf16[2,64,768]{2,1,0:T(8,128)(2,1)S(1)} collective-permute-done((bf16[2,64,768]{2,1,0:T(8,128)(2,1)S(1)}, bf16[2,64,768]{2,1,0:T(8,128)(2,1)S(1)}, u32[]{:S(2)}, u32[]{:S(2)}) %collective-permute-start.4) | collective-permute-done | bytes 196640 | tf_op jit(solution)/shard_map/ppermute | solution.py:463
  24.7 5.3 %forward_part.5 = (f32[2,64,1280]{2,1,0:T(8,128)S(1)}, f32[1,2,64,1280]{3,2,1,0:T(8,128)S(1)}, bf16[2,2,64,1280]{3,2,1,0:T(8,128)(2,1)S(1)}) custom-call(bf16[256,2048]{1,0:T(8,128)(2,1)S(1)} %get-tuple-element.41.refs_0_.refs_5_, bf16[2048,3584]{1,0:T(8,128)(2,1)} %refs_0_.5, bf16[2048,3584]{1,0:T(8,128)(2,1)} %refs_1_.9, ...), custom_call_target="tpu_custom_call" | custom-call | flops 26843545600 | bytes 671088640 | tf_op jit(solution)/shard_map/forward_part/pallas_call | solution.py:36
  30.0 9.3 %input_part.3 = (bf16[2048,256]{1,0:T(8,128)(2,1)S(1)}, f32[2048,256]{1,0:T(8,128)S(1)}, bf16[2,256,768]{2,1,0:T(8,128)(2,1)S(1)}, bf16[2048,3584]{1,0:T(8,128)(...) custom-call(bf16[2048,3584]{1,0:T(8,128)(2,1)} %refs_0_.5, ...), custom_call_target="tpu_custom_call" | custom-call | flops 20971520 | bytes 524288 | tf_op jit(solution)/shard_map/input_part/pallas_call | solution.py:36
  41.1 1.0 collective-permute-done.6.got_ref
  42.1 0.8 collective-permute-start.7
  42.9 15.5 %collective-permute-done.7.refs_0_ = bf16[2,64,1280]{2,1,0:T(8,128)(2,1)S(1)} collective-permute-done((bf16[2,64,1280]{2,1,0:T(8,128)(2,1)S(1)}, bf16[2,64,1280]{2,1,0:T(8,128)(2,1)S(1)}, u32[]{:S(2)}, u32[]{:S(2)}) %collective-permute-start.7) | collective-permute-done | bytes 327712 | tf_op jit(solution)/shard_map/ppermute | solution.py:463
  58.4 0.9 middle_part.5
  59.5 1.0 collective-permute-start.8
  60.5 1.3 %collective-permute-done.10.refs_5_ = bf16[2,2,64,1536]{3,2,1,0:T(8,128)(2,1)S(1)} collective-permute-done((bf16[2,2,64,1536]{3,2,1,0:T(8,128)(2,1)S(1)}, bf16[2,2,64,1536]{3,2,1,0:T(8,128)(2,1)S(1)}, u32[]{:S(2)}, u32[]{:S(2)}) %collective-permute-start.10) | collective-permute-done | bytes 786464 | tf_op jit(solution)/shard_map/ppermute | solution.py:459
  61.7 6.9 %input_part.4 = (f32[256,1024]{1,0:T(8,128)S(1)}, f32[256,1024]{1,0:T(8,128)S(1)}, bf16[2,256,1536]{2,1,0:T(8,128)(2,1)S(1)}) custom-call(bf16[2048,3584]{1,0:T(8,128)(2,1)} %refs_0_.5, bf16[2048,3584]{1,0:T(8,128)(2,1)} %refs_1_.9, bf16[2,64,1280]{2,1,0:T(8,128)(2,1)S(1)} %get-tuple-element.63.refs_2_.refs_0_, ...), custom_call_target="tpu_custom_call" | custom-call | flops 32212254720 | bytes 805306368 | tf_op jit(solution)/shard_map/input_part/pallas_call | solution.py:36
  68.7 0.9 collective-permute-done.8.refs_1_.refs_3_
  70.0 1.8 %collective-permute-done.11.refs_4_ = bf16[2,2,64,1280]{3,2,1,0:T(8,128)(2,1)S(1)} collective-permute-done((bf16[2,2,64,1280]{3,2,1,0:T(8,128)(2,1)S(1)}, bf16[2,2,64,1280]{3,2,1,0:T(8,128)(2,1)S(1)}, u32[]{:S(2)}, u32[]{:S(2)}) %collective-permute-start.11) | collective-permute-done | bytes 655392 | tf_op jit(solution)/shard_map/ppermute | solution.py:459
  71.8 2.5 %copy-done.2 = bf16[2048,1280]{1,0:T(8,128)(2,1)S(1)} copy-done((bf16[2048,1280]{1,0:T(8,128)(2,1)S(1)}, bf16[2048,1280]{1,0:T(8,128)(2,1)}, u32[]{:S(2)}) %copy-start.2) | copy-done | bytes 5242904
  74.3 2.5 %copy-done.4 = bf16[2048,1280]{1,0:T(8,128)(2,1)S(1)} copy-done((bf16[2048,1280]{1,0:T(8,128)(2,1)S(1)}, bf16[2048,1280]{1,0:T(8,128)(2,1)}, u32[]{:S(2)}) %copy-start.4) | copy-done | bytes 5242904
  76.8 1.2 %copy-done.8 = f32[256,1024]{1,0:T(8,128)S(1)} copy-done((f32[256,1024]{1,0:T(8,128)S(1)}, f32[256,1024]{1,0:T(8,128)}, u32[]{:S(2)}) %copy-start.8) | copy-done | bytes 1048600
  78.0 1.2 %copy-done.10 = f32[256,1024]{1,0:T(8,128)S(1)} copy-done((f32[256,1024]{1,0:T(8,128)S(1)}, f32[256,1024]{1,0:T(8,128)}, u32[]{:S(2)}) %copy-start.10) | copy-done | bytes 1048600
  79.2 2.9 %input_part.5 = (f32[256,1024]{1,0:T(8,128)S(1)}, f32[256,1024]{1,0:T(8,128)S(1)}, bf16[2,256,1280]{2,1,0:T(8,128)(2,1)S(1)}) custom-call(bf16[2048,1280]{1,0:T(8,128)(2,1)S(1)} %copy-done.2, bf16[2048,1280]{1,0:T(8,128)(2,1)S(1)} %copy-done.4, bf16[2,64,1280]{2,1,0:T(8,128)(2,1)S(1)} %get-tuple-element.63.refs_2_.refs_0_, ...), custom_call_target="tpu_custom_call" | custom-call | flops 26843545600 | bytes 671088640 | tf_op jit(solution)/shard_map/input_part/pallas_call | solution.py:36
  82.2 1.6 %collective-permute-start.12 = (bf16[2,2,32,1024]{3,2,1,0:T(8,128)(2,1)S(1)}, bf16[2,2,32,1024]{3,2,1,0:T(8,128)(2,1)S(1)}, u32[]{:S(2)}, u32[]{:S(2)}) collective-permute-start(bf16[2,2,32,1024]{3,2,1,0:T(8,128)(2,1)S(1)} %fusion.2), channel_id=1, source_target_pairs={{0,1},{1,0},{2,3},{3,2},{4,5},{5,4},{6,7},{7,6},{8,9},{9,8},{10,11... | collective-permute-start | bytes 786440 | tf_op jit(solution)/shard_map/ppermute | solution.py:445
  83.8 1.6 %collective-permute-start.15 = (bf16[2,2,32,1024]{3,2,1,0:T(8,128)(2,1)S(1)}, bf16[2,2,32,1024]{3,2,1,0:T(8,128)(2,1)S(1)}, u32[]{:S(2)}, u32[]{:S(2)}) collective-permute-start(bf16[2,2,32,1024]{3,2,1,0:T(8,128)(2,1)S(1)} %fusion.3), channel_id=1, source_target_pairs={{0,2},{1,3},{2,0},{3,1},{4,6},{5,7},{6,4},{7,5},{8,10},{9,11},{10,... | collective-permute-start | bytes 786440 | tf_op jit(solution)/shard_map/ppermute | solution.py:445
  85.5 5.4 %weight_part.2 = (bf16[2048,3584]{1,0:T(8,128)(2,1)}, bf16[2048,3584]{1,0:T(8,128)(2,1)}) custom-call(bf16[2048,256]{1,0:T(8,128)(2,1)S(1)} %copy-done.6, bf16[2,256,1536]{2,1,0:T(8,128)(2,1)S(1)} %get-tuple-element.65.refs_2_.grads_ref, f32[256,1024]{1,0:T(8,128)S(1)} %get-tuple-element.68.refs_0_, ...), custom_call_target="tpu_custom_call", output_to_operand_aliasing={{0}: (4, {}), {1}: (5, {})} | custom-call | flops 32212254720 | bytes 805306368 | tf_op jit(solution)/shard_map/weight_part/pallas_call | solution.py:36
  91.0 2.6 %collective-permute-start.13 = (bf16[2,32,1024]{2,1,0:T(8,128)(2,1)S(1)}, bf16[2,32,1024]{2,1,0:T(8,128)(2,1)S(1)}, u32[]{:S(2)}, u32[]{:S(2)}) collective-permute-start(bf16[2,32,1024]{2,1,0:T(8,128)(2,1)S(1)} %fusion.5), channel_id=1, source_target_pairs={{0,4},{1,5},{2,6},{3,7},{4,0},{5,1},{6,2},{7,3},{8,12},{9,13},{10,... | collective-permute-start | bytes 393224 | tf_op jit(solution)/shard_map/ppermute | solution.py:445
  93.8 1.3 %collective-permute-start.16 = (bf16[2,32,1024]{2,1,0:T(8,128)(2,1)S(1)}, bf16[2,32,1024]{2,1,0:T(8,128)(2,1)S(1)}, u32[]{:S(2)}, u32[]{:S(2)}) collective-permute-start(bf16[2,32,1024]{2,1,0:T(8,128)(2,1)S(1)} %fusion.6), channel_id=1, source_target_pairs={{0,1},{1,0},{2,3},{3,2},{4,5},{5,4},{6,7},{7,6},{8,9},{9,8},{10,11... | collective-permute-start | bytes 393224 | tf_op jit(solution)/shard_map/ppermute | solution.py:445
  95.1 4.8 %weight_part.3 = (bf16[2048,3584]{1,0:T(8,128)(2,1)}, bf16[2048,3584]{1,0:T(8,128)(2,1)}) custom-call(bf16[2048,256]{1,0:T(8,128)(2,1)S(1)} %copy-done.6, bf16[2,256,1280]{2,1,0:T(8,128)(2,1)S(1)} %get-tuple-element.71.grads_ref, f32[2,2,32,1024]{3,2,1,0:T(8,128)S(1)} %bitcast_add_fusion.1.refs_0_, ...), custom_call_target="tpu_custom_call", output_to_operand_aliasing={{0}: (4, {}), {1}: (5, {})} | custom-call | flops 26843545600 | bytes 671088640 | tf_op jit(solution)/shard_map/weight_part/pallas_call | solution.py:36
  99.9 1.6 %collective-permute-start.14 = (bf16[32,1024]{1,0:T(8,128)(2,1)S(1)}, bf16[32,1024]{1,0:T(8,128)(2,1)S(1)}, u32[]{:S(2)}, u32[]{:S(2)}) collective-permute-start(bf16[32,1024]{1,0:T(8,128)(2,1)S(1)} %fusion.9), channel_id=1, source_target_pairs={{0,2},{1,3},{2,0},{3,1},{4,6},{5,7},{6,4},{7,5},{8,10},{9,11},{10,... | collective-permute-start | bytes 196616 | tf_op jit(solution)/shard_map/ppermute | solution.py:445
  101.6 2.0 %collective-permute-start.17 = (bf16[32,1024]{1,0:T(8,128)(2,1)S(1)}, bf16[32,1024]{1,0:T(8,128)(2,1)S(1)}, u32[]{:S(2)}, u32[]{:S(2)}) collective-permute-start(bf16[32,1024]{1,0:T(8,128)(2,1)S(1)} %fusion.10), channel_id=1, source_target_pairs={{0,4},{1,5},{2,6},{3,7},{4,0},{5,1},{6,2},{7,3},{8,12},{9,13},{10,... | collective-permute-start | bytes 196616 | tf_op jit(solution)/shard_map/ppermute | solution.py:445
  103.6 1.3 %collective-permute-done.14 = bf16[32,1024]{1,0:T(8,128)(2,1)S(1)} collective-permute-done((bf16[32,1024]{1,0:T(8,128)(2,1)S(1)}, bf16[32,1024]{1,0:T(8,128)(2,1)S(1)}, u32[]{:S(2)}, u32[]{:S(2)}) %collective-permute-start.14) | collective-permute-done | bytes 65568 | tf_op jit(solution)/shard_map/ppermute | solution.py:445
  105.0 2.5 %collective-permute-done.17 = bf16[32,1024]{1,0:T(8,128)(2,1)S(1)} collective-permute-done((bf16[32,1024]{1,0:T(8,128)(2,1)S(1)}, bf16[32,1024]{1,0:T(8,128)(2,1)S(1)}, u32[]{:S(2)}, u32[]{:S(2)}) %collective-permute-start.17) | collective-permute-done | bytes 65568 | tf_op jit(solution)/shard_map/ppermute | solution.py:445
  (58 shorter events, 6.0 us)
Async XLA Ops:
  5.6 1.9 %collective-permute-start = (bf16[2,2,64,768]{3,2,1,0:T(8,128)(2,1)S(1)}, bf16[2,2,64,768]{3,2,1,0:T(8,128)(2,1)S(1)}, u32[]{:S(2)}, u32[]{:S(2)}) collective-permute-start(bf16[2,2,64,768]{3,2,1,0:T(8,128)(2,1)S(1)} %get-tuple-element.45), channel_id=1, source_target_pairs={{0,8},{8,0},{16,24},{24,16},{1,9},{9,1},{17,25},{25,17},{2,10},{10... | collective-permute-start | bytes 1179656 | tf_op jit(solution)/shard_map/ppermute | solution.py:459
  7.5 9.1 %collective-permute-start.1 = (bf16[2,64,768]{2,1,0:T(8,128)(2,1)S(1)}, bf16[2,64,768]{2,1,0:T(8,128)(2,1)S(1)}, u32[]{:S(2)}, u32[]{:S(2)}) collective-permute-start(bf16[2,64,768]{2,1,0:T(8,128)(2,1)S(1)} %fusion.4.refs_5_), channel_id=1, source_target_pairs={{0,16},{8,24},{16,0},{24,8},{1,17},{9,25},{17,1},{25,9},{2,18},{10... | collective-permute-start | bytes 589832 | tf_op jit(solution)/shard_map/ppermute | solution.py:463
  10.4 6.2 %copy-start = (bf16[64,3584]{1,0:T(8,128)(2,1)S(1)}, bf16[64,3584]{1,0:T(8,128)(2,1)}, u32[]{:S(2)}) copy-start(bf16[64,3584]{1,0:T(8,128)(2,1)} %upstream_ref.5) | copy-start | bytes 1376260
  16.7 2.4 %collective-permute-start.2 = (bf16[2,2,64,1536]{3,2,1,0:T(8,128)(2,1)S(1)}, bf16[2,2,64,1536]{3,2,1,0:T(8,128)(2,1)S(1)}, u32[]{:S(2)}, u32[]{:S(2)}) collective-permute-start(bf16[2,2,64,1536]{3,2,1,0:T(8,128)(2,1)S(1)} %in_order.2), channel_id=1, source_target_pairs={{0,8},{8,0},{16,24},{24,16},{1,9},{9,1},{17,25},{25,17},{2,10},{10... | collective-permute-start | bytes 2359304 | tf_op jit(solution)/shard_map/ppermute | solution.py:459
  16.8 7.8 %collective-permute-start.4 = (bf16[2,64,768]{2,1,0:T(8,128)(2,1)S(1)}, bf16[2,64,768]{2,1,0:T(8,128)(2,1)S(1)}, u32[]{:S(2)}, u32[]{:S(2)}) collective-permute-start(bf16[2,64,768]{2,1,0:T(8,128)(2,1)S(1)} %get-tuple-element.51.refs_2_.refs_0_), channel_id=1, source_target_pairs={{0,16},{8,24},{16,0},{24,8},{1,17},{9,25},{17,1},{25,9},{2,18},{10... | collective-permute-start | bytes 589832 | tf_op jit(solution)/shard_map/ppermute | solution.py:463
  19.2 20.2 %collective-permute-start.3 = (bf16[2,64,1536]{2,1,0:T(8,128)(2,1)S(1)}, bf16[2,64,1536]{2,1,0:T(8,128)(2,1)S(1)}, u32[]{:S(2)}, u32[]{:S(2)}) collective-permute-start(bf16[2,64,1536]{2,1,0:T(8,128)(2,1)S(1)} %fusion.refs_5_.refs_2_), channel_id=1, source_target_pairs={{0,16},{8,24},{16,0},{24,8},{1,17},{9,25},{17,1},{25,9},{2,18},{10... | collective-permute-start | bytes 1179656 | tf_op jit(solution)/shard_map/ppermute | solution.py:463
  24.6 5.4 %collective-permute-start.5 = (bf16[2,2,64,768]{3,2,1,0:T(8,128)(2,1)S(1)}, bf16[2,2,64,768]{3,2,1,0:T(8,128)(2,1)S(1)}, u32[]{:S(2)}, u32[]{:S(2)}) collective-permute-start(bf16[2,2,64,768]{3,2,1,0:T(8,128)(2,1)S(1)} %packed.3), channel_id=1, source_target_pairs={{0,8},{8,0},{16,24},{24,16},{1,9},{9,1},{17,25},{25,17},{2,10},{10... | collective-permute-start | bytes 1179656 | tf_op jit(solution)/shard_map/ppermute | solution.py:459
  39.3 29.3 %copy-start.1 = (bf16[2048,1280]{1,0:T(8,128)(2,1)}, bf16[2048,1280]{1,0:T(8,128)(2,1)S(1)}, u32[]{:S(2)}) copy-start(bf16[2048,1280]{1,0:T(8,128)(2,1)S(1)} %get-tuple-element.61.refs_0_) | copy-start | bytes 15728644
  39.3 29.3 %copy-start.3 = (bf16[2048,1280]{1,0:T(8,128)(2,1)}, bf16[2048,1280]{1,0:T(8,128)(2,1)S(1)}, u32[]{:S(2)}) copy-start(bf16[2048,1280]{1,0:T(8,128)(2,1)S(1)} %get-tuple-element.62.refs_1_) | copy-start | bytes 15728644
  39.4 29.3 %copy-start.5 = (bf16[2048,256]{1,0:T(8,128)(2,1)}, bf16[2048,256]{1,0:T(8,128)(2,1)S(1)}, u32[]{:S(2)}) copy-start(bf16[2048,256]{1,0:T(8,128)(2,1)S(1)} %get-tuple-element.70.xt_ref) | copy-start | bytes 3145732
  39.7 2.3 %collective-permute-start.6 = (bf16[2,2,64,1280]{3,2,1,0:T(8,128)(2,1)S(1)}, bf16[2,2,64,1280]{3,2,1,0:T(8,128)(2,1)S(1)}, u32[]{:S(2)}, u32[]{:S(2)}) collective-permute-start(bf16[2,2,64,1280]{3,2,1,0:T(8,128)(2,1)S(1)} %in_order.3), channel_id=1, source_target_pairs={{0,8},{8,0},{16,24},{24,16},{1,9},{9,1},{17,25},{25,17},{2,10},{10... | collective-permute-start | bytes 1966088 | tf_op jit(solution)/shard_map/ppermute | solution.py:459
  40.3 19.1 %collective-permute-start.9 = (bf16[2,64,1536]{2,1,0:T(8,128)(2,1)S(1)}, bf16[2,64,1536]{2,1,0:T(8,128)(2,1)S(1)}, u32[]{:S(2)}, u32[]{:S(2)}) collective-permute-start(bf16[2,64,1536]{2,1,0:T(8,128)(2,1)S(1)} %get-tuple-element.56.refs_2_.refs_0_.refs_3_), channel_id=1, source_target_pairs={{0,16},{8,24},{16,0},{24,8},{1,17},{9,25},{17,1},{25,9},{2,18},{10... | collective-permute-start | bytes 1179656 | tf_op jit(solution)/shard_map/ppermute | solution.py:463
  42.1 16.3 %collective-permute-start.7 = (bf16[2,64,1280]{2,1,0:T(8,128)(2,1)S(1)}, bf16[2,64,1280]{2,1,0:T(8,128)(2,1)S(1)}, u32[]{:S(2)}, u32[]{:S(2)}) collective-permute-start(bf16[2,64,1280]{2,1,0:T(8,128)(2,1)S(1)} %fusion.1), channel_id=1, source_target_pairs={{0,16},{8,24},{16,0},{24,8},{1,17},{9,25},{17,1},{25,9},{2,18},{10... | collective-permute-start | bytes 983048 | tf_op jit(solution)/shard_map/ppermute | solution.py:463
  59.4 2.4 %collective-permute-start.10 = (bf16[2,2,64,1536]{3,2,1,0:T(8,128)(2,1)S(1)}, bf16[2,2,64,1536]{3,2,1,0:T(8,128)(2,1)S(1)}, u32[]{:S(2)}, u32[]{:S(2)}) collective-permute-start(bf16[2,2,64,1536]{3,2,1,0:T(8,128)(2,1)S(1)} %packed.4), channel_id=1, source_target_pairs={{0,8},{8,0},{16,24},{24,16},{1,9},{9,1},{17,25},{25,17},{2,10},{10... | collective-permute-start | bytes 2359304 | tf_op jit(solution)/shard_map/ppermute | solution.py:459
  59.5 10.1 %collective-permute-start.8 = (bf16[2,64,1280]{2,1,0:T(8,128)(2,1)S(1)}, bf16[2,64,1280]{2,1,0:T(8,128)(2,1)S(1)}, u32[]{:S(2)}, u32[]{:S(2)}) collective-permute-start(bf16[2,64,1280]{2,1,0:T(8,128)(2,1)S(1)} %get-tuple-element.63.refs_2_.refs_0_), channel_id=1, source_target_pairs={{0,16},{8,24},{16,0},{24,8},{1,17},{9,25},{17,1},{25,9},{2,18},{10... | collective-permute-start | bytes 983048 | tf_op jit(solution)/shard_map/ppermute | solution.py:463
  68.7 1.0 copy-start.7
  68.7 1.4 %copy-start.9 = (f32[256,1024]{1,0:T(8,128)}, f32[256,1024]{1,0:T(8,128)S(1)}, u32[]{:S(2)}) copy-start(f32[256,1024]{1,0:T(8,128)S(1)} %get-tuple-element.67.refs_6_) | copy-start | bytes 3145732
  69.6 2.2 %collective-permute-start.11 = (bf16[2,2,64,1280]{3,2,1,0:T(8,128)(2,1)S(1)}, bf16[2,2,64,1280]{3,2,1,0:T(8,128)(2,1)S(1)}, u32[]{:S(2)}, u32[]{:S(2)}) collective-permute-start(bf16[2,2,64,1280]{3,2,1,0:T(8,128)(2,1)S(1)} %packed.5), channel_id=1, source_target_pairs={{0,8},{8,0},{16,24},{24,16},{1,9},{9,1},{17,25},{25,17},{2,10},{10... | collective-permute-start | bytes 1966088 | tf_op jit(solution)/shard_map/ppermute | solution.py:459
  71.8 2.5 %copy-start.2 = (bf16[2048,1280]{1,0:T(8,128)(2,1)S(1)}, bf16[2048,1280]{1,0:T(8,128)(2,1)}, u32[]{:S(2)}) copy-start(bf16[2048,1280]{1,0:T(8,128)(2,1)} %copy-done.1) | copy-start | bytes 15728644
  74.3 2.5 %copy-start.4 = (bf16[2048,1280]{1,0:T(8,128)(2,1)S(1)}, bf16[2048,1280]{1,0:T(8,128)(2,1)}, u32[]{:S(2)}) copy-start(bf16[2048,1280]{1,0:T(8,128)(2,1)} %copy-done.3) | copy-start | bytes 15728644
  76.8 1.2 %copy-start.8 = (f32[256,1024]{1,0:T(8,128)S(1)}, f32[256,1024]{1,0:T(8,128)}, u32[]{:S(2)}) copy-start(f32[256,1024]{1,0:T(8,128)} %copy-done.7) | copy-start | bytes 3145732
  78.0 1.2 %copy-start.10 = (f32[256,1024]{1,0:T(8,128)S(1)}, f32[256,1024]{1,0:T(8,128)}, u32[]{:S(2)}) copy-start(f32[256,1024]{1,0:T(8,128)} %copy-done.9) | copy-start | bytes 3145732
  79.2 6.3 %copy-start.6 = (bf16[2048,256]{1,0:T(8,128)(2,1)S(1)}, bf16[2048,256]{1,0:T(8,128)(2,1)}, u32[]{:S(2)}) copy-start(bf16[2048,256]{1,0:T(8,128)(2,1)} %copy-done.5) | copy-start | bytes 3145732
  82.2 8.7 %collective-permute-start.12 = (bf16[2,2,32,1024]{3,2,1,0:T(8,128)(2,1)S(1)}, bf16[2,2,32,1024]{3,2,1,0:T(8,128)(2,1)S(1)}, u32[]{:S(2)}, u32[]{:S(2)}) collective-permute-start(bf16[2,2,32,1024]{3,2,1,0:T(8,128)(2,1)S(1)} %fusion.2), channel_id=1, source_target_pairs={{0,1},{1,0},{2,3},{3,2},{4,5},{5,4},{6,7},{7,6},{8,9},{9,8},{10,11... | collective-permute-start | bytes 786440 | tf_op jit(solution)/shard_map/ppermute | solution.py:445
  83.8 9.9 %collective-permute-start.15 = (bf16[2,2,32,1024]{3,2,1,0:T(8,128)(2,1)S(1)}, bf16[2,2,32,1024]{3,2,1,0:T(8,128)(2,1)S(1)}, u32[]{:S(2)}, u32[]{:S(2)}) collective-permute-start(bf16[2,2,32,1024]{3,2,1,0:T(8,128)(2,1)S(1)} %fusion.3), channel_id=1, source_target_pairs={{0,2},{1,3},{2,0},{3,1},{4,6},{5,7},{6,4},{7,5},{8,10},{9,11},{10,... | collective-permute-start | bytes 786440 | tf_op jit(solution)/shard_map/ppermute | solution.py:445
  91.0 8.8 %collective-permute-start.13 = (bf16[2,32,1024]{2,1,0:T(8,128)(2,1)S(1)}, bf16[2,32,1024]{2,1,0:T(8,128)(2,1)S(1)}, u32[]{:S(2)}, u32[]{:S(2)}) collective-permute-start(bf16[2,32,1024]{2,1,0:T(8,128)(2,1)S(1)} %fusion.5), channel_id=1, source_target_pairs={{0,4},{1,5},{2,6},{3,7},{4,0},{5,1},{6,2},{7,3},{8,12},{9,13},{10,... | collective-permute-start | bytes 393224 | tf_op jit(solution)/shard_map/ppermute | solution.py:445
  93.8 7.8 %collective-permute-start.16 = (bf16[2,32,1024]{2,1,0:T(8,128)(2,1)S(1)}, bf16[2,32,1024]{2,1,0:T(8,128)(2,1)S(1)}, u32[]{:S(2)}, u32[]{:S(2)}) collective-permute-start(bf16[2,32,1024]{2,1,0:T(8,128)(2,1)S(1)} %fusion.6), channel_id=1, source_target_pairs={{0,1},{1,0},{2,3},{3,2},{4,5},{5,4},{6,7},{7,6},{8,9},{9,8},{10,11... | collective-permute-start | bytes 393224 | tf_op jit(solution)/shard_map/ppermute | solution.py:445
  99.9 5.0 %collective-permute-start.14 = (bf16[32,1024]{1,0:T(8,128)(2,1)S(1)}, bf16[32,1024]{1,0:T(8,128)(2,1)S(1)}, u32[]{:S(2)}, u32[]{:S(2)}) collective-permute-start(bf16[32,1024]{1,0:T(8,128)(2,1)S(1)} %fusion.9), channel_id=1, source_target_pairs={{0,2},{1,3},{2,0},{3,1},{4,6},{5,7},{6,4},{7,5},{8,10},{9,11},{10,... | collective-permute-start | bytes 196616 | tf_op jit(solution)/shard_map/ppermute | solution.py:445
  101.6 5.8 %collective-permute-start.17 = (bf16[32,1024]{1,0:T(8,128)(2,1)S(1)}, bf16[32,1024]{1,0:T(8,128)(2,1)S(1)}, u32[]{:S(2)}, u32[]{:S(2)}) collective-permute-start(bf16[32,1024]{1,0:T(8,128)(2,1)S(1)} %fusion.10), channel_id=1, source_target_pairs={{0,4},{1,5},{2,6},{3,7},{4,0},{5,1},{6,2},{7,3},{8,12},{9,13},{10,... | collective-permute-start | bytes 196616 | tf_op jit(solution)/shard_map/ppermute | solution.py:445

commit v9 on v7

--- a/solution.py
+++ b/solution.py
@@ -505,10 +505,7 @@
     def take_input(i, x, acc, after):
         weights = held[i] if i in held else [in_hbm(value) for value in both]
         write = (flipped[0] if i else None, state, full) if i < number - 2 else None
-        later = 2 if i == 0 else 1
-        ahead = None
-        if later < number - i and i + later not in held and i != 1:
-            ahead = (chunks[i + later], both)
+        ahead = (chunks[2], both) if i == 0 and number > 2 else None
         xt, total, whole, written, fetched = input_part(
             quarters, block, chunks[i], weights, i in held, groups[i], acc, number - 1 - i, x,
             after, write, ahead,
@@ -519,7 +516,7 @@
         if written:
             state[:] = written
         if fetched:
-            held[i + later] = fetched
+            held[2] = fetched
         grads.append(whole)
         return total
 
@@ -541,7 +538,8 @@
             hidden = middle(j, hidden, grads[-1:])
     bits = columns.bit_length() - 1
     order = list(range(bits))
-    stages = [acc] + token_sums(acc, columns, [order, order[1::-1] + order[2:]])
+    orders = [order[:1] + order[2:] + order[1:2], order[1::-1] + order[2:]]
+    stages = [acc] + token_sums(acc, columns, orders)
     input_grad = jnp.concatenate([half.astype(BF16) for half in stages[-1]], axis=1)
     for i in range(max(number - 2, 0), number):
         after = stages[min(i - max(number - 2, 0), bits)]

time: 107 us -> 102 us (0.953)
  local copies, waits for them, and re-layouts: 10.9 us -> 2.61 us
  starting transfers between devices: 21.3 us -> 23.3 us
  waiting for transfers between devices: 21.7 us -> 23.4 us
    unnamed x18 -> x10, local copies, waits for them, and re-layouts: 10.7 us -> 2.46 us
    ppermute x6, starting transfers between devices: 9.51 us -> 11.7 us  [token_sums(): got.append(lax.ppermute(send.astype(BF16), 'col', moves))]
    ppermute x8, waiting for transfers between devices: 9.69 us -> 11.7 us  [across(): return lax.ppermute(value, 'row', moves)]
    ppermute x6, waiting for transfers between devices: 5.9 us -> 4.31 us  [token_sums(): got.append(lax.ppermute(send.astype(BF16), 'col', moves))]
    ppermute x8, waiting for transfers between devices: 6.15 us -> 7.33 us  [sibling(): return lax.ppermute(value, 'row', swap)]
  transfers between devices with their start and end apart: 22 -> 22, of which waited for: 12 -> 14; matrix products, arithmetic and copies ran while one was open for 0% -> 0% of each run, Pallas kernels for 41% -> 41%
where the time goes in v9:
time: 102 us
  Pallas kernels  50.3 us (49%)
  waiting for transfers between devices  23.4 us (23%)
  starting transfers between devices  23.3 us (23%)
  local copies, waits for them, and re-layouts  2.61 us (3%)
  between operations  1.08 us (1%)
  other arithmetic  1.03 us (1%)
    pallas_call x21, Pallas kernels, call(): pl.pallas_call(kernel, in_specs=in_specs, out_specs=out_specs, out_shape=...  50.3 us
    ppermute x8, waiting for transfers between devices, across(): return lax.ppermute(value, 'row', moves)  11.7 us
    ppermute x6, starting transfers between devices, token_sums(): got.append(lax.ppermute(send.astype(BF16), 'col', moves))  11.7 us
    ppermute x8, starting transfers between devices, across(): return lax.ppermute(value, 'row', moves)  10.5 us
    ppermute x8, waiting for transfers between devices, sibling(): return lax.ppermute(value, 'row', swap)  7.33 us
    ppermute x6, waiting for transfers between devices, token_sums(): got.append(lax.ppermute(send.astype(BF16), 'col', moves))  4.31 us
    unnamed x10, local copies, waits for them, and re-layouts  2.46 us
  transfers between devices with their start and end apart: 22, of which 14 were waited for; matrix products, arithmetic and copies ran while one was open for 0% of the time, Pallas kernels for 41%

profile of v9, /device:TPU:0, one launch (start us, length us, event | category | flops | bytes accessed | tf_op | source)
XLA Modules:
  0.0 101.6 jit_solution(14246798673331923745)
XLA Ops:
  0.6 4.0 %forward_part.4 = (f32[2,64,512]{2,1,0:T(8,128)S(1)}, f32[1,2,64,512]{3,2,1,0:T(8,128)S(1)}, bf16[2,2,64,512]{3,2,1,0:T(8,128)(2,1)S(1)}, bf16[256,2048]{1,0:T(8...) custom-call(bf16[256,2048]{1,0:T(8,128)(2,1)} %refs_0_.4, bf16[2048,3584]{1,0:T(8,128)(2,1)} %refs_0_.7, ...), custom_call_target="tpu_custom_call" | custom-call | flops 10737418240 | bytes 268435456 | tf_op jit(solution)/shard_map/forward_part/pallas_call | solution.py:36
  5.2 1.2 %collective-permute-done.got_ref = bf16[2,2,64,512]{3,2,1,0:T(8,128)(2,1)S(1)} collective-permute-done((bf16[2,2,64,512]{3,2,1,0:T(8,128)(2,1)S(1)}, bf16[2,2,64,512]{3,2,1,0:T(8,128)(2,1)S(1)}, u32[]{:S(2)}, u32[]{:S(2)}) %collective-permute-start) | collective-permute-done | bytes 262176 | tf_op jit(solution)/shard_map/ppermute | solution.py:459
  6.4 2.9 %collective-permute-start.1 = (bf16[2,64,512]{2,1,0:T(8,128)(2,1)S(1)}, bf16[2,64,512]{2,1,0:T(8,128)(2,1)S(1)}, u32[]{:S(2)}, u32[]{:S(2)}) collective-permute-start(bf16[2,64,512]{2,1,0:T(8,128)(2,1)S(1)} %fusion.5.refs_5_), channel_id=1, source_target_pairs={{0,16},{8,24},{16,0},{24,8},{1,17},{9,25},{17,1},{25,9},{2,18},{10... | collective-permute-start | bytes 393224 | tf_op jit(solution)/shard_map/ppermute | solution.py:463
  9.3 4.4 %forward_part.5 = (f32[2,64,1024]{2,1,0:T(8,128)S(1)}, f32[1,2,64,1024]{3,2,1,0:T(8,128)S(1)}, bf16[2,2,64,1024]{3,2,1,0:T(8,128)(2,1)S(1)}, bf16[2048,256]{1,0:T(8,128)(2,1)S(1)}, bf16[2048,256]{1,0:T(8,128)(2,1)S(1)}) custom-call(bf16[256,2048]{1,0:T(8,128)(2,1)S(1)} %get-tuple-element.52.refs_0_.refs_5_, bf16[2048,3584]{1,0:T(8,128)(2,1)} %refs_0_.7, ...), custom_call_target="tpu_custom_call" | custom-call | flops 21474836480 | bytes 536870912 | tf_op jit(solution)/shard_map/forward_part/pallas_call | solution.py:36
  14.0 1.9 %collective-permute-done.2.got_ref = bf16[2,2,64,1024]{3,2,1,0:T(8,128)(2,1)S(1)} collective-permute-done((bf16[2,2,64,1024]{3,2,1,0:T(8,128)(2,1)S(1)}, bf16[2,2,64,1024]{3,2,1,0:T(8,128)(2,1)S(1)}, u32[]{:S(2)}, u32[]{:S(2)}) %collective-permute-start.2) | collective-permute-done | bytes 524320 | tf_op jit(solution)/shard_map/ppermute | solution.py:459
  15.9 1.1 %collective-permute-start.3 = (bf16[2,64,1024]{2,1,0:T(8,128)(2,1)S(1)}, bf16[2,64,1024]{2,1,0:T(8,128)(2,1)S(1)}, u32[]{:S(2)}, u32[]{:S(2)}) collective-permute-start(bf16[2,64,1024]{2,1,0:T(8,128)(2,1)S(1)} %fusion.1.refs_5_), channel_id=1, source_target_pairs={{0,16},{8,24},{16,0},{24,8},{1,17},{9,25},{17,1},{25,9},{2,18},{10... | collective-permute-start | bytes 786440 | tf_op jit(solution)/shard_map/ppermute | solution.py:463
  17.1 5.4 %forward_part.6 = (f32[2,64,1280]{2,1,0:T(8,128)S(1)}, f32[1,2,64,1280]{3,2,1,0:T(8,128)S(1)}, bf16[2,2,64,1280]{3,2,1,0:T(8,128)(2,1)S(1)}, bf16[2048,256]{1,0:T(8,128)(2,1)S(1)}, bf16[2048,256]{1,0:T(8,128)(2,1)S(1)}) custom-call(bf16[256,2048]{1,0:T(8,128)(2,1)S(1)} %get-tuple-element.52.refs_0_.refs_5_, bf16[2048,3584]{1,0:T(8,128)(2,1)} %refs_0_.7, ...), custom_call_target="tpu_custom_call" | custom-call | flops 26843545600 | bytes 671088640 | tf_op jit(solution)/shard_map/forward_part/pallas_call | solution.py:36
  22.5 1.9 %collective-permute-done.3.refs_0_.refs_1_ = bf16[2,64,1024]{2,1,0:T(8,128)(2,1)S(1)} collective-permute-done((bf16[2,64,1024]{2,1,0:T(8,128)(2,1)S(1)}, bf16[2,64,1024]{2,1,0:T(8,128)(2,1)S(1)}, u32[]{:S(2)}, u32[]{:S(2)}) %collective-permute-start.3) | collective-permute-done | bytes 262176 | tf_op jit(solution)/shard_map/ppermute | solution.py:463
  24.7 1.1 %collective-permute-start.6 = (bf16[2,64,512]{2,1,0:T(8,128)(2,1)S(1)}, bf16[2,64,512]{2,1,0:T(8,128)(2,1)S(1)}, u32[]{:S(2)}, u32[]{:S(2)}) collective-permute-start(bf16[2,64,512]{2,1,0:T(8,128)(2,1)S(1)} %get-tuple-element.62.refs_2_.refs_0_), channel_id=1, source_target_pairs={{0,16},{8,24},{16,0},{24,8},{1,17},{9,25},{17,1},{25,9},{2,18},{10... | collective-permute-start | bytes 393224 | tf_op jit(solution)/shard_map/ppermute | solution.py:463
  26.8 1.1 %collective-permute-start.5 = (bf16[2,64,1280]{2,1,0:T(8,128)(2,1)S(1)}, bf16[2,64,1280]{2,1,0:T(8,128)(2,1)S(1)}, u32[]{:S(2)}, u32[]{:S(2)}) collective-permute-start(bf16[2,64,1280]{2,1,0:T(8,128)(2,1)S(1)} %fusion.refs_5_.refs_2_), channel_id=1, source_target_pairs={{0,16},{8,24},{16,0},{24,8},{1,17},{9,25},{17,1},{25,9},{2,18},{10... | collective-permute-start | bytes 983048 | tf_op jit(solution)/shard_map/ppermute | solution.py:463
  28.0 3.1 %collective-permute-done.6.refs_1_.refs_3_ = bf16[2,64,512]{2,1,0:T(8,128)(2,1)S(1)} collective-permute-done((bf16[2,64,512]{2,1,0:T(8,128)(2,1)S(1)}, bf16[2,64,512]{2,1,0:T(8,128)(2,1)S(1)}, u32[]{:S(2)}, u32[]{:S(2)}) %collective-permute-start.6) | collective-permute-done | bytes 131104 | tf_op jit(solution)/shard_map/ppermute | solution.py:463
  31.1 3.6 %forward_part.7 = (f32[2,64,768]{2,1,0:T(8,128)S(1)}, f32[1,2,64,768]{3,2,1,0:T(8,128)S(1)}, bf16[2,2,64,768]{3,2,1,0:T(8,128)(2,1)S(1)}) custom-call(bf16[256,2048]{1,0:T(8,128)(2,1)S(1)} %get-tuple-element.52.refs_0_.refs_5_, bf16[2048,3584]{1,0:T(8,128)(2,1)} %refs_0_.7, bf16[2048,3584]{1,0:T(8,128)(2,1)} %refs_1_.13, ...), custom_call_target="tpu_custom_call" | custom-call | flops 16106127360 | bytes 402653184 | tf_op jit(solution)/shard_map/forward_part/pallas_call | solution.py:36
  34.8 7.2 %input_part.4 = (bf16[2048,256]{1,0:T(8,128)(2,1)S(1)}, f32[2048,256]{1,0:T(8,128)S(1)}, bf16[2,256,512]{2,1,0:T(8,128)(2,1)S(1)}, bf16[2048,3584]{1,0:T(8,128)(...) custom-call(bf16[2048,3584]{1,0:T(8,128)(2,1)} %refs_0_.7, ...), custom_call_target="tpu_custom_call" | custom-call | flops 20971520 | bytes 524288 | tf_op jit(solution)/shard_map/input_part/pallas_call | solution.py:36
  42.0 1.2 %collective-permute-done.5.refs_0_.refs_1_ = bf16[2,64,1280]{2,1,0:T(8,128)(2,1)S(1)} collective-permute-done((bf16[2,64,1280]{2,1,0:T(8,128)(2,1)S(1)}, bf16[2,64,1280]{2,1,0:T(8,128)(2,1)S(1)}, u32[]{:S(2)}, u32[]{:S(2)}) %collective-permute-start.5) | collective-permute-done | bytes 327712 | tf_op jit(solution)/shard_map/ppermute | solution.py:463
  43.6 1.7 %collective-permute-done.9.got_ref = bf16[2,2,64,768]{3,2,1,0:T(8,128)(2,1)S(1)} collective-permute-done((bf16[2,2,64,768]{3,2,1,0:T(8,128)(2,1)S(1)}, bf16[2,2,64,768]{3,2,1,0:T(8,128)(2,1)S(1)}, u32[]{:S(2)}, u32[]{:S(2)}) %collective-permute-start.9) | collective-permute-done | bytes 393248 | tf_op jit(solution)/shard_map/ppermute | solution.py:459
  47.7 8.6 %input_part.5 = (f32[2048,256]{1,0:T(8,128)S(1)}, bf16[2,256,1024]{2,1,0:T(8,128)(2,1)S(1)}, bf16[2048,3584]{1,0:T(8,128)(2,1)}, bf16[2048,3584]{1,0:T(8,128)(2,1)}) custom-call(bf16[2048,3584]{1,0:T(8,128)(2,1)} %refs_0_.7, bf16[2048,3584]{1,0:T(8,128)(2,1)} %refs_1_.13, ...), custom_call_target="tpu_custom_call", output_to_operand_aliasing={{2}: (9, {}), {3}: (10, {})} | custom-call | flops 21474836480 | bytes 536870912 | tf_op jit(solution)/shard_map/input_part/pallas_call | solution.py:36
  56.3 3.5 %collective-permute-done.10.refs_0_ = bf16[2,64,768]{2,1,0:T(8,128)(2,1)S(1)} collective-permute-done((bf16[2,64,768]{2,1,0:T(8,128)(2,1)S(1)}, bf16[2,64,768]{2,1,0:T(8,128)(2,1)S(1)}, u32[]{:S(2)}, u32[]{:S(2)}) %collective-permute-start.10) | collective-permute-done | bytes 196640 | tf_op jit(solution)/shard_map/ppermute | solution.py:463
  60.8 1.1 %collective-permute-start.12 = (bf16[2,64,768]{2,1,0:T(8,128)(2,1)S(1)}, bf16[2,64,768]{2,1,0:T(8,128)(2,1)S(1)}, u32[]{:S(2)}, u32[]{:S(2)}) collective-permute-start(bf16[2,64,768]{2,1,0:T(8,128)(2,1)S(1)} %get-tuple-element.84.refs_3_.refs_0_.refs_2_), channel_id=1, source_target_pairs={{0,16},{8,24},{16,0},{24,8},{1,17},{9,25},{17,1},{25,9},{2,18},{10... | collective-permute-start | bytes 589832 | tf_op jit(solution)/shard_map/ppermute | solution.py:463
  62.9 3.1 %input_part.6 = (f32[256,1024]{1,0:T(8,128)S(1)}, f32[256,1024]{1,0:T(8,128)S(1)}, bf16[2,256,1280]{2,1,0:T(8,128)(2,1)S(1)}) custom-call(bf16[2048,1280]{1,0:T(8,128)(2,1)S(1)} %get-tuple-element.85.refs_0_, bf16[2048,1280]{1,0:T(8,128)(2,1)S(1)} %get-tuple-element.86.refs_1_, bf16[2,64,1280]{2,1,0:T(8,128)(2,1)S(1)} %get-tuple-element.74.refs_2_.refs_3_.refs_0_, ...), custom_call_target="tpu_custom_call" | custom-call | flops 26843545600 | bytes 671088640 | tf_op jit(solution)/shard_map/input_part/pallas_call | solution.py:36
  66.1 2.1 %collective-permute-done.12.refs_1_.refs_3_ = bf16[2,64,768]{2,1,0:T(8,128)(2,1)S(1)} collective-permute-done((bf16[2,64,768]{2,1,0:T(8,128)(2,1)S(1)}, bf16[2,64,768]{2,1,0:T(8,128)(2,1)S(1)}, u32[]{:S(2)}, u32[]{:S(2)}) %collective-permute-start.12) | collective-permute-done | bytes 196640 | tf_op jit(solution)/shard_map/ppermute | solution.py:463
  68.4 1.6 %collective-permute-done.15.refs_4_ = bf16[2,2,64,768]{3,2,1,0:T(8,128)(2,1)S(1)} collective-permute-done((bf16[2,2,64,768]{3,2,1,0:T(8,128)(2,1)S(1)}, bf16[2,2,64,768]{3,2,1,0:T(8,128)(2,1)S(1)}, u32[]{:S(2)}, u32[]{:S(2)}) %collective-permute-start.15) | collective-permute-done | bytes 393248 | tf_op jit(solution)/shard_map/ppermute | solution.py:459
  70.0 1.2 %copy-done.2 = f32[256,1024]{1,0:T(8,128)S(1)} copy-done((f32[256,1024]{1,0:T(8,128)S(1)}, f32[256,1024]{1,0:T(8,128)}, u32[]{:S(2)}) %copy-start.2) | copy-done | bytes 1048600
  71.2 1.2 %copy-done.4 = f32[256,1024]{1,0:T(8,128)S(1)} copy-done((f32[256,1024]{1,0:T(8,128)S(1)}, f32[256,1024]{1,0:T(8,128)}, u32[]{:S(2)}) %copy-start.4) | copy-done | bytes 1048600
  72.4 4.0 %input_part.7 = (f32[256,1024]{1,0:T(8,128)S(1)}, f32[256,1024]{1,0:T(8,128)S(1)}, bf16[2,256,768]{2,1,0:T(8,128)(2,1)S(1)}) custom-call(bf16[2048,3584]{1,0:T(8,128)(2,1)} %refs_0_.7, bf16[2048,3584]{1,0:T(8,128)(2,1)} %refs_1_.13, bf16[2,64,768]{2,1,0:T(8,128)(2,1)S(1)} %get-tuple-element.84.refs_3_.refs_0_.refs_2_, ...), custom_call_target="tpu_custom_call" | custom-call | flops 16106127360 | bytes 402653184 | tf_op jit(solution)/shard_map/input_part/pallas_call | solution.py:36
  76.4 1.6 %collective-permute-start.16 = (bf16[2,2,32,1024]{3,2,1,0:T(8,128)(2,1)S(1)}, bf16[2,2,32,1024]{3,2,1,0:T(8,128)(2,1)S(1)}, u32[]{:S(2)}, u32[]{:S(2)}) collective-permute-start(bf16[2,2,32,1024]{3,2,1,0:T(8,128)(2,1)S(1)} %fusion.2), channel_id=1, source_target_pairs={{0,1},{1,0},{2,3},{3,2},{4,5},{5,4},{6,7},{7,6},{8,9},{9,8},{10,11... | collective-permute-start | bytes 786440 | tf_op jit(solution)/shard_map/ppermute | solution.py:445
  78.1 1.6 %collective-permute-start.19 = (bf16[2,2,32,1024]{3,2,1,0:T(8,128)(2,1)S(1)}, bf16[2,2,32,1024]{3,2,1,0:T(8,128)(2,1)S(1)}, u32[]{:S(2)}, u32[]{:S(2)}) collective-permute-start(bf16[2,2,32,1024]{3,2,1,0:T(8,128)(2,1)S(1)} %fusion.3), channel_id=1, source_target_pairs={{0,2},{1,3},{2,0},{3,1},{4,6},{5,7},{6,4},{7,5},{8,10},{9,11},{10,... | collective-permute-start | bytes 786440 | tf_op jit(solution)/shard_map/ppermute | solution.py:445
  79.7 4.8 %weight_part.2 = (bf16[2048,3584]{1,0:T(8,128)(2,1)}, bf16[2048,3584]{1,0:T(8,128)(2,1)}) custom-call(bf16[2048,256]{1,0:T(8,128)(2,1)S(1)} %get-tuple-element.78.refs_8_.xt_ref, bf16[2,256,1280]{2,1,0:T(8,128)(2,1)S(1)} %get-tuple-element.88.refs_2_.grads_ref, ...), custom_call_target="tpu_custom_call", output_to_operand_aliasing={{0}: (4, {}), {1}: (5, {})} | custom-call | flops 26843545600 | bytes 671088640 | tf_op jit(solution)/shard_map/weight_part/pallas_call | solution.py:36
  84.9 2.7 %collective-permute-start.17 = (bf16[2,32,1024]{2,1,0:T(8,128)(2,1)S(1)}, bf16[2,32,1024]{2,1,0:T(8,128)(2,1)S(1)}, u32[]{:S(2)}, u32[]{:S(2)}) collective-permute-start(bf16[2,32,1024]{2,1,0:T(8,128)(2,1)S(1)} %fusion.6), channel_id=1, source_target_pairs={{0,4},{1,5},{2,6},{3,7},{4,0},{5,1},{6,2},{7,3},{8,12},{9,13},{10,... | collective-permute-start | bytes 393224 | tf_op jit(solution)/shard_map/ppermute | solution.py:445
  87.7 1.6 %collective-permute-start.20 = (bf16[2,32,1024]{2,1,0:T(8,128)(2,1)S(1)}, bf16[2,32,1024]{2,1,0:T(8,128)(2,1)S(1)}, u32[]{:S(2)}, u32[]{:S(2)}) collective-permute-start(bf16[2,32,1024]{2,1,0:T(8,128)(2,1)S(1)} %fusion.7), channel_id=1, source_target_pairs={{0,1},{1,0},{2,3},{3,2},{4,5},{5,4},{6,7},{7,6},{8,9},{9,8},{10,11... | collective-permute-start | bytes 393224 | tf_op jit(solution)/shard_map/ppermute | solution.py:445
  89.3 3.4 %weight_part.3 = (bf16[2048,3584]{1,0:T(8,128)(2,1)}, bf16[2048,3584]{1,0:T(8,128)(2,1)}) custom-call(bf16[2048,256]{1,0:T(8,128)(2,1)S(1)} %get-tuple-element.78.refs_8_.xt_ref, bf16[2,256,768]{2,1,0:T(8,128)(2,1)S(1)} %get-tuple-element.93.grads_ref, ...), custom_call_target="tpu_custom_call", output_to_operand_aliasing={{0}: (4, {}), {1}: (5, {})} | custom-call | flops 16106127360 | bytes 402653184 | tf_op jit(solution)/shard_map/weight_part/pallas_call | solution.py:36
  94.5 3.2 %collective-permute-start.21 = (bf16[32,1024]{1,0:T(8,128)(2,1)S(1)}, bf16[32,1024]{1,0:T(8,128)(2,1)S(1)}, u32[]{:S(2)}, u32[]{:S(2)}) collective-permute-start(bf16[32,1024]{1,0:T(8,128)(2,1)S(1)} %fusion.11), channel_id=1, source_target_pairs={{0,4},{1,5},{2,6},{3,7},{4,0},{5,1},{6,2},{7,3},{8,12},{9,13},{10,... | collective-permute-start | bytes 196616 | tf_op jit(solution)/shard_map/ppermute | solution.py:445
  97.8 3.1 %collective-permute-done.21 = bf16[32,1024]{1,0:T(8,128)(2,1)S(1)} collective-permute-done((bf16[32,1024]{1,0:T(8,128)(2,1)S(1)}, bf16[32,1024]{1,0:T(8,128)(2,1)S(1)}, u32[]{:S(2)}, u32[]{:S(2)}) %collective-permute-start.21) | collective-permute-done | bytes 65568 | tf_op jit(solution)/shard_map/ppermute | solution.py:445
  (60 shorter events, 10.1 us)
Async XLA Ops:
  4.7 1.7 %collective-permute-start = (bf16[2,2,64,512]{3,2,1,0:T(8,128)(2,1)S(1)}, bf16[2,2,64,512]{3,2,1,0:T(8,128)(2,1)S(1)}, u32[]{:S(2)}, u32[]{:S(2)}) collective-permute-start(bf16[2,2,64,512]{3,2,1,0:T(8,128)(2,1)S(1)} %get-tuple-element.56), channel_id=1, source_target_pairs={{0,8},{8,0},{16,24},{24,16},{1,9},{9,1},{17,25},{25,17},{2,10},{10... | collective-permute-start | bytes 786440 | tf_op jit(solution)/shard_map/ppermute | solution.py:459
  6.4 7.4 %collective-permute-start.1 = (bf16[2,64,512]{2,1,0:T(8,128)(2,1)S(1)}, bf16[2,64,512]{2,1,0:T(8,128)(2,1)S(1)}, u32[]{:S(2)}, u32[]{:S(2)}) collective-permute-start(bf16[2,64,512]{2,1,0:T(8,128)(2,1)S(1)} %fusion.5.refs_5_), channel_id=1, source_target_pairs={{0,16},{8,24},{16,0},{24,8},{1,17},{9,25},{17,1},{25,9},{2,18},{10... | collective-permute-start | bytes 393224 | tf_op jit(solution)/shard_map/ppermute | solution.py:463
  9.3 4.5 %copy-start = (bf16[64,3584]{1,0:T(8,128)(2,1)S(1)}, bf16[64,3584]{1,0:T(8,128)(2,1)}, u32[]{:S(2)}) copy-start(bf16[64,3584]{1,0:T(8,128)(2,1)} %upstream_ref.7) | copy-start | bytes 1376260
  13.9 2.0 %collective-permute-start.2 = (bf16[2,2,64,1024]{3,2,1,0:T(8,128)(2,1)S(1)}, bf16[2,2,64,1024]{3,2,1,0:T(8,128)(2,1)S(1)}, u32[]{:S(2)}, u32[]{:S(2)}) collective-permute-start(bf16[2,2,64,1024]{3,2,1,0:T(8,128)(2,1)S(1)} %in_order.3), channel_id=1, source_target_pairs={{0,8},{8,0},{16,24},{24,16},{1,9},{9,1},{17,25},{25,17},{2,10},{10... | collective-permute-start | bytes 1572872 | tf_op jit(solution)/shard_map/ppermute | solution.py:459
  15.9 8.4 %collective-permute-start.3 = (bf16[2,64,1024]{2,1,0:T(8,128)(2,1)S(1)}, bf16[2,64,1024]{2,1,0:T(8,128)(2,1)S(1)}, u32[]{:S(2)}, u32[]{:S(2)}) collective-permute-start(bf16[2,64,1024]{2,1,0:T(8,128)(2,1)S(1)} %fusion.1.refs_5_), channel_id=1, source_target_pairs={{0,16},{8,24},{16,0},{24,8},{1,17},{9,25},{17,1},{25,9},{2,18},{10... | collective-permute-start | bytes 786440 | tf_op jit(solution)/shard_map/ppermute | solution.py:463
  24.6 2.2 %collective-permute-start.4 = (bf16[2,2,64,1280]{3,2,1,0:T(8,128)(2,1)S(1)}, bf16[2,2,64,1280]{3,2,1,0:T(8,128)(2,1)S(1)}, u32[]{:S(2)}, u32[]{:S(2)}) collective-permute-start(bf16[2,2,64,1280]{3,2,1,0:T(8,128)(2,1)S(1)} %in_order.4), channel_id=1, source_target_pairs={{0,8},{8,0},{16,24},{24,16},{1,9},{9,1},{17,25},{25,17},{2,10},{10... | collective-permute-start | bytes 1966088 | tf_op jit(solution)/shard_map/ppermute | solution.py:459
  24.7 6.4 %collective-permute-start.6 = (bf16[2,64,512]{2,1,0:T(8,128)(2,1)S(1)}, bf16[2,64,512]{2,1,0:T(8,128)(2,1)S(1)}, u32[]{:S(2)}, u32[]{:S(2)}) collective-permute-start(bf16[2,64,512]{2,1,0:T(8,128)(2,1)S(1)} %get-tuple-element.62.refs_2_.refs_0_), channel_id=1, source_target_pairs={{0,16},{8,24},{16,0},{24,8},{1,17},{9,25},{17,1},{25,9},{2,18},{10... | collective-permute-start | bytes 393224 | tf_op jit(solution)/shard_map/ppermute | solution.py:463
  25.8 17.7 %collective-permute-start.7 = (bf16[2,64,1024]{2,1,0:T(8,128)(2,1)S(1)}, bf16[2,64,1024]{2,1,0:T(8,128)(2,1)S(1)}, u32[]{:S(2)}, u32[]{:S(2)}) collective-permute-start(bf16[2,64,1024]{2,1,0:T(8,128)(2,1)S(1)} %get-tuple-element.69.refs_2_.refs_0_.refs_4_), channel_id=1, source_target_pairs={{0,16},{8,24},{16,0},{24,8},{1,17},{9,25},{17,1},{25,9},{2,18},{10... | collective-permute-start | bytes 786440 | tf_op jit(solution)/shard_map/ppermute | solution.py:463
  26.8 16.4 %collective-permute-start.5 = (bf16[2,64,1280]{2,1,0:T(8,128)(2,1)S(1)}, bf16[2,64,1280]{2,1,0:T(8,128)(2,1)S(1)}, u32[]{:S(2)}, u32[]{:S(2)}) collective-permute-start(bf16[2,64,1280]{2,1,0:T(8,128)(2,1)S(1)} %fusion.refs_5_.refs_2_), channel_id=1, source_target_pairs={{0,16},{8,24},{16,0},{24,8},{1,17},{9,25},{17,1},{25,9},{2,18},{10... | collective-permute-start | bytes 983048 | tf_op jit(solution)/shard_map/ppermute | solution.py:463
  31.1 3.7 %collective-permute-start.8 = (bf16[2,2,64,512]{3,2,1,0:T(8,128)(2,1)S(1)}, bf16[2,2,64,512]{3,2,1,0:T(8,128)(2,1)S(1)}, u32[]{:S(2)}, u32[]{:S(2)}) collective-permute-start(bf16[2,2,64,512]{3,2,1,0:T(8,128)(2,1)S(1)} %packed.4), channel_id=1, source_target_pairs={{0,8},{8,0},{16,24},{24,16},{1,9},{9,1},{17,25},{25,17},{2,10},{10... | collective-permute-start | bytes 786440 | tf_op jit(solution)/shard_map/ppermute | solution.py:459
  43.5 1.8 %collective-permute-start.9 = (bf16[2,2,64,768]{3,2,1,0:T(8,128)(2,1)S(1)}, bf16[2,2,64,768]{3,2,1,0:T(8,128)(2,1)S(1)}, u32[]{:S(2)}, u32[]{:S(2)}) collective-permute-start(bf16[2,2,64,768]{3,2,1,0:T(8,128)(2,1)S(1)} %in_order.5), channel_id=1, source_target_pairs={{0,8},{8,0},{16,24},{24,16},{1,9},{9,1},{17,25},{25,17},{2,10},{10... | collective-permute-start | bytes 1179656 | tf_op jit(solution)/shard_map/ppermute | solution.py:459
  45.4 2.2 %collective-permute-start.11 = (bf16[2,2,64,1024]{3,2,1,0:T(8,128)(2,1)S(1)}, bf16[2,2,64,1024]{3,2,1,0:T(8,128)(2,1)S(1)}, u32[]{:S(2)}, u32[]{:S(2)}) collective-permute-start(bf16[2,2,64,1024]{3,2,1,0:T(8,128)(2,1)S(1)} %packed.5), channel_id=1, source_target_pairs={{0,8},{8,0},{16,24},{24,16},{1,9},{9,1},{17,25},{25,17},{2,10},{10... | collective-permute-start | bytes 1572872 | tf_op jit(solution)/shard_map/ppermute | solution.py:459
  45.6 15.1 %collective-permute-start.13 = (bf16[2,64,1280]{2,1,0:T(8,128)(2,1)S(1)}, bf16[2,64,1280]{2,1,0:T(8,128)(2,1)S(1)}, u32[]{:S(2)}, u32[]{:S(2)}) collective-permute-start(bf16[2,64,1280]{2,1,0:T(8,128)(2,1)S(1)} %get-tuple-element.74.refs_2_.refs_3_.refs_0_), channel_id=1, source_target_pairs={{0,16},{8,24},{16,0},{24,8},{1,17},{9,25},{17,1},{25,9},{2,18},{10... | collective-permute-start | bytes 983048 | tf_op jit(solution)/shard_map/ppermute | solution.py:463
  46.7 13.1 %collective-permute-start.10 = (bf16[2,64,768]{2,1,0:T(8,128)(2,1)S(1)}, bf16[2,64,768]{2,1,0:T(8,128)(2,1)S(1)}, u32[]{:S(2)}, u32[]{:S(2)}) collective-permute-start(bf16[2,64,768]{2,1,0:T(8,128)(2,1)S(1)} %fusion.4.refs_2_), channel_id=1, source_target_pairs={{0,16},{8,24},{16,0},{24,8},{1,17},{9,25},{17,1},{25,9},{2,18},{10... | collective-permute-start | bytes 589832 | tf_op jit(solution)/shard_map/ppermute | solution.py:463
  60.7 2.2 %collective-permute-start.14 = (bf16[2,2,64,1280]{3,2,1,0:T(8,128)(2,1)S(1)}, bf16[2,2,64,1280]{3,2,1,0:T(8,128)(2,1)S(1)}, u32[]{:S(2)}, u32[]{:S(2)}) collective-permute-start(bf16[2,2,64,1280]{3,2,1,0:T(8,128)(2,1)S(1)} %packed.6), channel_id=1, source_target_pairs={{0,8},{8,0},{16,24},{24,16},{1,9},{9,1},{17,25},{25,17},{2,10},{10... | collective-permute-start | bytes 1966088 | tf_op jit(solution)/shard_map/ppermute | solution.py:459
  60.8 7.3 %collective-permute-start.12 = (bf16[2,64,768]{2,1,0:T(8,128)(2,1)S(1)}, bf16[2,64,768]{2,1,0:T(8,128)(2,1)S(1)}, u32[]{:S(2)}, u32[]{:S(2)}) collective-permute-start(bf16[2,64,768]{2,1,0:T(8,128)(2,1)S(1)} %get-tuple-element.84.refs_3_.refs_0_.refs_2_), channel_id=1, source_target_pairs={{0,16},{8,24},{16,0},{24,8},{1,17},{9,25},{17,1},{25,9},{2,18},{10... | collective-permute-start | bytes 589832 | tf_op jit(solution)/shard_map/ppermute | solution.py:463
  66.1 2.2 %copy-start.1 = (f32[256,1024]{1,0:T(8,128)}, f32[256,1024]{1,0:T(8,128)S(1)}, u32[]{:S(2)}) copy-start(f32[256,1024]{1,0:T(8,128)S(1)} %get-tuple-element.89.refs_5_) | copy-start | bytes 3145732
  66.1 2.2 %copy-start.3 = (f32[256,1024]{1,0:T(8,128)}, f32[256,1024]{1,0:T(8,128)S(1)}, u32[]{:S(2)}) copy-start(f32[256,1024]{1,0:T(8,128)S(1)} %get-tuple-element.90.refs_6_) | copy-start | bytes 3145732
  68.2 1.8 %collective-permute-start.15 = (bf16[2,2,64,768]{3,2,1,0:T(8,128)(2,1)S(1)}, bf16[2,2,64,768]{3,2,1,0:T(8,128)(2,1)S(1)}, u32[]{:S(2)}, u32[]{:S(2)}) collective-permute-start(bf16[2,2,64,768]{3,2,1,0:T(8,128)(2,1)S(1)} %packed.7), channel_id=1, source_target_pairs={{0,8},{8,0},{16,24},{24,16},{1,9},{9,1},{17,25},{25,17},{2,10},{10... | collective-permute-start | bytes 1179656 | tf_op jit(solution)/shard_map/ppermute | solution.py:459
  70.0 1.2 %copy-start.2 = (f32[256,1024]{1,0:T(8,128)S(1)}, f32[256,1024]{1,0:T(8,128)}, u32[]{:S(2)}) copy-start(f32[256,1024]{1,0:T(8,128)} %copy-done.1) | copy-start | bytes 3145732
  71.2 1.2 %copy-start.4 = (f32[256,1024]{1,0:T(8,128)S(1)}, f32[256,1024]{1,0:T(8,128)}, u32[]{:S(2)}) copy-start(f32[256,1024]{1,0:T(8,128)} %copy-done.3) | copy-start | bytes 3145732
  76.4 8.4 %collective-permute-start.16 = (bf16[2,2,32,1024]{3,2,1,0:T(8,128)(2,1)S(1)}, bf16[2,2,32,1024]{3,2,1,0:T(8,128)(2,1)S(1)}, u32[]{:S(2)}, u32[]{:S(2)}) collective-permute-start(bf16[2,2,32,1024]{3,2,1,0:T(8,128)(2,1)S(1)} %fusion.2), channel_id=1, source_target_pairs={{0,1},{1,0},{2,3},{3,2},{4,5},{5,4},{6,7},{7,6},{8,9},{9,8},{10,11... | collective-permute-start | bytes 786440 | tf_op jit(solution)/shard_map/ppermute | solution.py:445
  78.1 9.5 %collective-permute-start.19 = (bf16[2,2,32,1024]{3,2,1,0:T(8,128)(2,1)S(1)}, bf16[2,2,32,1024]{3,2,1,0:T(8,128)(2,1)S(1)}, u32[]{:S(2)}, u32[]{:S(2)}) collective-permute-start(bf16[2,2,32,1024]{3,2,1,0:T(8,128)(2,1)S(1)} %fusion.3), channel_id=1, source_target_pairs={{0,2},{1,3},{2,0},{3,1},{4,6},{5,7},{6,4},{7,5},{8,10},{9,11},{10,... | collective-permute-start | bytes 786440 | tf_op jit(solution)/shard_map/ppermute | solution.py:445
  84.9 8.5 %collective-permute-start.17 = (bf16[2,32,1024]{2,1,0:T(8,128)(2,1)S(1)}, bf16[2,32,1024]{2,1,0:T(8,128)(2,1)S(1)}, u32[]{:S(2)}, u32[]{:S(2)}) collective-permute-start(bf16[2,32,1024]{2,1,0:T(8,128)(2,1)S(1)} %fusion.6), channel_id=1, source_target_pairs={{0,4},{1,5},{2,6},{3,7},{4,0},{5,1},{6,2},{7,3},{8,12},{9,13},{10,... | collective-permute-start | bytes 393224 | tf_op jit(solution)/shard_map/ppermute | solution.py:445
  87.7 6.7 %collective-permute-start.20 = (bf16[2,32,1024]{2,1,0:T(8,128)(2,1)S(1)}, bf16[2,32,1024]{2,1,0:T(8,128)(2,1)S(1)}, u32[]{:S(2)}, u32[]{:S(2)}) collective-permute-start(bf16[2,32,1024]{2,1,0:T(8,128)(2,1)S(1)} %fusion.7), channel_id=1, source_target_pairs={{0,1},{1,0},{2,3},{3,2},{4,5},{5,4},{6,7},{7,6},{8,9},{9,8},{10,11... | collective-permute-start | bytes 393224 | tf_op jit(solution)/shard_map/ppermute | solution.py:445
  93.5 4.3 %collective-permute-start.18 = (bf16[32,1024]{1,0:T(8,128)(2,1)S(1)}, bf16[32,1024]{1,0:T(8,128)(2,1)S(1)}, u32[]{:S(2)}, u32[]{:S(2)}) collective-permute-start(bf16[32,1024]{1,0:T(8,128)(2,1)S(1)} %fusion.10), channel_id=1, source_target_pairs={{0,2},{1,3},{2,0},{3,1},{4,6},{5,7},{6,4},{7,5},{8,10},{9,11},{10,... | collective-permute-start | bytes 196616 | tf_op jit(solution)/shard_map/ppermute | solution.py:445
  94.5 6.5 %collective-permute-start.21 = (bf16[32,1024]{1,0:T(8,128)(2,1)S(1)}, bf16[32,1024]{1,0:T(8,128)(2,1)S(1)}, u32[]{:S(2)}, u32[]{:S(2)}) collective-permute-start(bf16[32,1024]{1,0:T(8,128)(2,1)S(1)} %fusion.11), channel_id=1, source_target_pairs={{0,4},{1,5},{2,6},{3,7},{4,0},{5,1},{6,2},{7,3},{8,12},{9,13},{10,... | collective-permute-start | bytes 196616 | tf_op jit(solution)/shard_map/ppermute | solution.py:445

commit v10 on v8

--- a/solution.py
+++ b/solution.py
@@ -11,7 +11,7 @@
 BF16 = jnp.bfloat16
 F32 = jnp.float32
 VMEM_BYTES = 6 * 1024 * 1024
-SHARES = (3, 6, 5)
+SHARES = (2, 4, 5, 3)
 SLOTS = 3
 COST = 40
 WHOLE = pl.BlockSpec(memory_space=pltpu.VMEM)
@@ -374,7 +374,7 @@
         out_specs,
         out_shape,
         scratch,
-        tokens * depth * (1 if first else width),
+        tokens * depth * width,
         args,
         aliases,
         room,
@@ -478,11 +478,9 @@
             x, loaded = loaded[0], loaded[1:]
         else:
             after = crossed[i - 1][:1] + pieces[i - 1][:1]
-            if i == number - 1 and i > 1:
-                relay(0, sums[-1][:1])
-                take_input(0, x, None, [])
-                after += pieces[i - 2][1:2] + grads
-            send = in_order(send, after)
+            send = in_order(send, after + (pieces[0][1:2] if i == 3 else []))
+        if i > 1 and len(pieces[i - 2]) < outer:
+            spread(i - 2, owns[-1:])
         got = sibling(send)
         near = [(far[step - 1] + got[step].astype(F32)).astype(BF16) for step in range(1, outer)]
         gots.append(got)
@@ -496,8 +494,14 @@
         hidden, mine = middle_part(
             outer, at, owns[i], gots[i], crossed[i], hidden_grad, hidden, after
         )
-        pieces.append([mine] + [across(mine, step) for step in range(1, outer)])
+        pieces.append([mine])
+        if i != 1 or number < 4:
+            spread(i, [])
         return hidden
+
+    def spread(i, after):
+        mine = in_order(pieces[i][0], after) if after else pieces[i][0]
+        pieces[i] += [across(mine, step) for step in range(1, outer)]
 
     def relay(i, after):
         groups.append(pieces[i] + [sibling(packed(pieces[i], after))])
@@ -524,13 +528,14 @@
     x, early, hidden, acc = inputs, [], None, None
     for i in range(number):
         x, early = forward(i, x, early)
-        hidden = middle(i, hidden, [])
+        if i < 3:
+            hidden = middle(i, hidden, [])
     for i in range(number):
-        if i == 0 and grads:
-            acc = totals[0]
-            continue
-        relay(i, grads[1:2] if i > 1 else pieces[-1][:1])
-        acc = take_input(i, x, acc, pieces[-1][:1] if 0 < i < number - 1 else [])
+        if i == 1:
+            for j in range(len(pieces), number):
+                hidden = middle(j, hidden, grads[-1:])
+        relay(i, grads[1:2] + pieces[-1][1:2] if i > 1 else grads[:1] + crossed[-1][:1] if i else owns[-1:])
+        acc = take_input(i, x, acc, sums[-1][:1] if i == 0 else pieces[-1][:1] if i == 1 else [])
     bits = columns.bit_length() - 1
     order = list(range(bits))
     orders = [order[:1] + order[2:] + order[1:2], order[1::-1] + order[2:]]

time: 108 us -> 107 us (level)
  waiting for transfers between devices: 31.6 us -> 23.3 us
  starting transfers between devices: 19.4 us -> 24.2 us
  Pallas kernels: 47.3 us -> 50.5 us
  local copies, waits for them, and re-layouts: 7.92 us -> 6.76 us
    ppermute x6 -> x8, waiting for transfers between devices: 21 us -> 13.5 us  [across(): return lax.ppermute(value, 'row', moves)]
    ppermute x6 -> x8, starting transfers between devices: 7.23 us -> 10.6 us  [across(): return lax.ppermute(value, 'row', moves)]
    pallas_call x16 -> x22, Pallas kernels: 47.3 us -> 50.5 us  [call(): pl.pallas_call(kernel, in_specs=in_specs, out_specs=out_specs, out_shape=...]
    ppermute x6 -> x8, waiting for transfers between devices: 6.75 us -> 5.51 us  [sibling(): return lax.ppermute(value, 'row', swap)]
    unnamed x22 -> x19, local copies, waits for them, and re-layouts: 7.77 us -> 6.61 us
  transfers between devices with their start and end apart: 18 -> 22, of which waited for: 10 -> 12; matrix products, arithmetic and copies ran while one was open for 0% -> 0% of each run, Pallas kernels for 36% -> 39%
where the time goes in v10:
time: 107 us
  Pallas kernels  50.5 us (47%)
  starting transfers between devices  24.2 us (23%)
  waiting for transfers between devices  23.3 us (22%)
  local copies, waits for them, and re-layouts  6.76 us (6%)
  between operations  1.15 us (1%)
    pallas_call x22, Pallas kernels, call(): pl.pallas_call(kernel, in_specs=in_specs, out_specs=out_specs, out_shape=...  50.5 us
    ppermute x8, waiting for transfers between devices, across(): return lax.ppermute(value, 'row', moves)  13.5 us
    ppermute x6, starting transfers between devices, token_sums(): got.append(lax.ppermute(send.astype(BF16), 'col', moves))  11.7 us
    ppermute x8, starting transfers between devices, across(): return lax.ppermute(value, 'row', moves)  10.6 us
    unnamed x19, local copies, waits for them, and re-layouts  6.61 us
    ppermute x8, waiting for transfers between devices, sibling(): return lax.ppermute(value, 'row', swap)  5.51 us
    ppermute x6, waiting for transfers between devices, token_sums(): got.append(lax.ppermute(send.astype(BF16), 'col', moves))  4.3 us
  transfers between devices with their start and end apart: 22, of which 12 were waited for; matrix products, arithmetic and copies ran while one was open for 0% of the time, Pallas kernels for 39%

profile of v10, /device:TPU:0, one launch (start us, length us, event | category | flops | bytes accessed | tf_op | source)
XLA Modules:
  0.0 106.9 jit_solution(12319477998180483412)
XLA Ops:
  0.6 4.1 %forward_part.4 = (f32[2,64,512]{2,1,0:T(8,128)S(1)}, f32[1,2,64,512]{3,2,1,0:T(8,128)S(1)}, bf16[2,2,64,512]{3,2,1,0:T(8,128)(2,1)S(1)}, bf16[256,2048]{1,0:T(8...) custom-call(bf16[256,2048]{1,0:T(8,128)(2,1)} %refs_0_.4, bf16[2048,3584]{1,0:T(8,128)(2,1)} %refs_0_.7, ...), custom_call_target="tpu_custom_call" | custom-call | flops 10737418240 | bytes 268435456 | tf_op jit(solution)/shard_map/forward_part/pallas_call | solution.py:36
  5.2 1.2 %collective-permute-done.got_ref = bf16[2,2,64,512]{3,2,1,0:T(8,128)(2,1)S(1)} collective-permute-done((bf16[2,2,64,512]{3,2,1,0:T(8,128)(2,1)S(1)}, bf16[2,2,64,512]{3,2,1,0:T(8,128)(2,1)S(1)}, u32[]{:S(2)}, u32[]{:S(2)}) %collective-permute-start) | collective-permute-done | bytes 262176 | tf_op jit(solution)/shard_map/ppermute | solution.py:459
  6.4 2.9 %collective-permute-start.1 = (bf16[2,64,512]{2,1,0:T(8,128)(2,1)S(1)}, bf16[2,64,512]{2,1,0:T(8,128)(2,1)S(1)}, u32[]{:S(2)}, u32[]{:S(2)}) collective-permute-start(bf16[2,64,512]{2,1,0:T(8,128)(2,1)S(1)} %fusion.5.refs_5_), channel_id=1, source_target_pairs={{0,16},{8,24},{16,0},{24,8},{1,17},{9,25},{17,1},{25,9},{2,18},{10... | collective-permute-start | bytes 393224 | tf_op jit(solution)/shard_map/ppermute | solution.py:463
  9.4 4.4 %forward_part.5 = (f32[2,64,1024]{2,1,0:T(8,128)S(1)}, f32[1,2,64,1024]{3,2,1,0:T(8,128)S(1)}, bf16[2,2,64,1024]{3,2,1,0:T(8,128)(2,1)S(1)}, bf16[2048,256]{1,0:T(8,128)(2,1)S(1)}, bf16[2048,256]{1,0:T(8,128)(2,1)S(1)}) custom-call(bf16[256,2048]{1,0:T(8,128)(2,1)S(1)} %get-tuple-element.52.refs_0_.refs_6_, bf16[2048,3584]{1,0:T(8,128)(2,1)} %refs_0_.7, ...), custom_call_target="tpu_custom_call" | custom-call | flops 21474836480 | bytes 536870912 | tf_op jit(solution)/shard_map/forward_part/pallas_call | solution.py:36
  14.0 1.9 %collective-permute-done.2.got_ref = bf16[2,2,64,1024]{3,2,1,0:T(8,128)(2,1)S(1)} collective-permute-done((bf16[2,2,64,1024]{3,2,1,0:T(8,128)(2,1)S(1)}, bf16[2,2,64,1024]{3,2,1,0:T(8,128)(2,1)S(1)}, u32[]{:S(2)}, u32[]{:S(2)}) %collective-permute-start.2) | collective-permute-done | bytes 524320 | tf_op jit(solution)/shard_map/ppermute | solution.py:459
  16.0 1.1 %collective-permute-start.3 = (bf16[2,64,1024]{2,1,0:T(8,128)(2,1)S(1)}, bf16[2,64,1024]{2,1,0:T(8,128)(2,1)S(1)}, u32[]{:S(2)}, u32[]{:S(2)}) collective-permute-start(bf16[2,64,1024]{2,1,0:T(8,128)(2,1)S(1)} %fusion.1.refs_5_), channel_id=1, source_target_pairs={{0,16},{8,24},{16,0},{24,8},{1,17},{9,25},{17,1},{25,9},{2,18},{10... | collective-permute-start | bytes 786440 | tf_op jit(solution)/shard_map/ppermute | solution.py:463
  17.1 5.4 %forward_part.6 = (f32[2,64,1280]{2,1,0:T(8,128)S(1)}, f32[1,2,64,1280]{3,2,1,0:T(8,128)S(1)}, bf16[2,2,64,1280]{3,2,1,0:T(8,128)(2,1)S(1)}, bf16[2048,256]{1,0:T(8,128)(2,1)S(1)}, bf16[2048,256]{1,0:T(8,128)(2,1)S(1)}) custom-call(bf16[256,2048]{1,0:T(8,128)(2,1)S(1)} %get-tuple-element.52.refs_0_.refs_6_, bf16[2048,3584]{1,0:T(8,128)(2,1)} %refs_0_.7, ...), custom_call_target="tpu_custom_call" | custom-call | flops 26843545600 | bytes 671088640 | tf_op jit(solution)/shard_map/forward_part/pallas_call | solution.py:36
  22.5 1.9 %collective-permute-done.3.refs_0_.refs_1_ = bf16[2,64,1024]{2,1,0:T(8,128)(2,1)S(1)} collective-permute-done((bf16[2,64,1024]{2,1,0:T(8,128)(2,1)S(1)}, bf16[2,64,1024]{2,1,0:T(8,128)(2,1)S(1)}, u32[]{:S(2)}, u32[]{:S(2)}) %collective-permute-start.3) | collective-permute-done | bytes 262176 | tf_op jit(solution)/shard_map/ppermute | solution.py:463
  24.7 1.1 %collective-permute-start.6 = (bf16[2,64,512]{2,1,0:T(8,128)(2,1)S(1)}, bf16[2,64,512]{2,1,0:T(8,128)(2,1)S(1)}, u32[]{:S(2)}, u32[]{:S(2)}) collective-permute-start(bf16[2,64,512]{2,1,0:T(8,128)(2,1)S(1)} %get-tuple-element.62.refs_2_.refs_0_.refs_3_), channel_id=1, source_target_pairs={{0,16},{8,24},{16,0},{24,8},{1,17},{9,25},{17,1},{25,9},{2,18},{10... | collective-permute-start | bytes 393224 | tf_op jit(solution)/shard_map/ppermute | solution.py:463
  26.9 1.1 %collective-permute-start.5 = (bf16[2,64,1280]{2,1,0:T(8,128)(2,1)S(1)}, bf16[2,64,1280]{2,1,0:T(8,128)(2,1)S(1)}, u32[]{:S(2)}, u32[]{:S(2)}) collective-permute-start(bf16[2,64,1280]{2,1,0:T(8,128)(2,1)S(1)} %fusion.refs_5_), channel_id=1, source_target_pairs={{0,16},{8,24},{16,0},{24,8},{1,17},{9,25},{17,1},{25,9},{2,18},{10... | collective-permute-start | bytes 983048 | tf_op jit(solution)/shard_map/ppermute | solution.py:463
  28.0 3.6 %forward_part.7 = (f32[2,64,768]{2,1,0:T(8,128)S(1)}, f32[1,2,64,768]{3,2,1,0:T(8,128)S(1)}, bf16[2,2,64,768]{3,2,1,0:T(8,128)(2,1)S(1)}) custom-call(bf16[256,2048]{1,0:T(8,128)(2,1)S(1)} %get-tuple-element.52.refs_0_.refs_6_, bf16[2048,3584]{1,0:T(8,128)(2,1)} %refs_0_.7, bf16[2048,3584]{1,0:T(8,128)(2,1)} %refs_1_.13, ...), custom_call_target="tpu_custom_call" | custom-call | flops 16106127360 | bytes 402653184 | tf_op jit(solution)/shard_map/forward_part/pallas_call | solution.py:36
  31.6 6.0 %collective-permute-done.5.refs_0_.refs_1_ = bf16[2,64,1280]{2,1,0:T(8,128)(2,1)S(1)} collective-permute-done((bf16[2,64,1280]{2,1,0:T(8,128)(2,1)S(1)}, bf16[2,64,1280]{2,1,0:T(8,128)(2,1)S(1)}, u32[]{:S(2)}, u32[]{:S(2)}) %collective-permute-start.5) | collective-permute-done | bytes 327712 | tf_op jit(solution)/shard_map/ppermute | solution.py:463
  38.7 1.1 %collective-permute-start.11 = (bf16[2,64,1024]{2,1,0:T(8,128)(2,1)S(1)}, bf16[2,64,1024]{2,1,0:T(8,128)(2,1)S(1)}, u32[]{:S(2)}, u32[]{:S(2)}) collective-permute-start(bf16[2,64,1024]{2,1,0:T(8,128)(2,1)S(1)} %in_order.7), channel_id=1, source_target_pairs={{0,16},{8,24},{16,0},{24,8},{1,17},{9,25},{17,1},{25,9},{2,18},{10... | collective-permute-start | bytes 786440 | tf_op jit(solution)/shard_map/ppermute | solution.py:463
  40.9 7.2 %input_part.4 = (bf16[2048,256]{1,0:T(8,128)(2,1)S(1)}, f32[2048,256]{1,0:T(8,128)S(1)}, bf16[2,256,512]{2,1,0:T(8,128)(2,1)S(1)}, bf16[2048,3584]{1,0:T(8,128)(...) custom-call(bf16[2048,3584]{1,0:T(8,128)(2,1)} %refs_0_.7, ...), custom_call_target="tpu_custom_call" | custom-call | flops 10737418240 | bytes 268435456 | tf_op jit(solution)/shard_map/input_part/pallas_call | solution.py:36
  48.2 2.9 %collective-permute-done.8.refs_0_.refs_3_ = bf16[2,64,768]{2,1,0:T(8,128)(2,1)S(1)} collective-permute-done((bf16[2,64,768]{2,1,0:T(8,128)(2,1)S(1)}, bf16[2,64,768]{2,1,0:T(8,128)(2,1)S(1)}, u32[]{:S(2)}, u32[]{:S(2)}) %collective-permute-start.8) | collective-permute-done | bytes 196640 | tf_op jit(solution)/shard_map/ppermute | solution.py:463
  51.3 1.1 %collective-permute-start.14 = (bf16[2,64,1280]{2,1,0:T(8,128)(2,1)S(1)}, bf16[2,64,1280]{2,1,0:T(8,128)(2,1)S(1)}, u32[]{:S(2)}, u32[]{:S(2)}) collective-permute-start(bf16[2,64,1280]{2,1,0:T(8,128)(2,1)S(1)} %get-tuple-element.74.refs_2_.refs_0_), channel_id=1, source_target_pairs={{0,16},{8,24},{16,0},{24,8},{1,17},{9,25},{17,1},{25,9},{2,18},{10... | collective-permute-start | bytes 983048 | tf_op jit(solution)/shard_map/ppermute | solution.py:463
  54.3 8.7 %input_part.5 = (f32[2048,256]{1,0:T(8,128)S(1)}, bf16[2,256,1024]{2,1,0:T(8,128)(2,1)S(1)}, bf16[2048,3584]{1,0:T(8,128)(2,1)}, bf16[2048,3584]{1,0:T(8,128)(2,1)}) custom-call(bf16[2048,3584]{1,0:T(8,128)(2,1)} %refs_0_.7, bf16[2048,3584]{1,0:T(8,128)(2,1)} %refs_1_.13, ...), custom_call_target="tpu_custom_call", output_to_operand_aliasing={{2}: (8, {}), {3}: (9, {})} | custom-call | flops 21474836480 | bytes 536870912 | tf_op jit(solution)/shard_map/input_part/pallas_call | solution.py:36
  63.0 2.6 %collective-permute-done.10.refs_1_.refs_3_ = bf16[2,64,768]{2,1,0:T(8,128)(2,1)S(1)} collective-permute-done((bf16[2,64,768]{2,1,0:T(8,128)(2,1)S(1)}, bf16[2,64,768]{2,1,0:T(8,128)(2,1)S(1)}, u32[]{:S(2)}, u32[]{:S(2)}) %collective-permute-start.10) | collective-permute-done | bytes 196640 | tf_op jit(solution)/shard_map/ppermute | solution.py:463
  66.3 1.5 %collective-permute-done.15.refs_4_ = bf16[2,2,64,1280]{3,2,1,0:T(8,128)(2,1)S(1)} collective-permute-done((bf16[2,2,64,1280]{3,2,1,0:T(8,128)(2,1)S(1)}, bf16[2,2,64,1280]{3,2,1,0:T(8,128)(2,1)S(1)}, u32[]{:S(2)}, u32[]{:S(2)}) %collective-permute-start.15) | collective-permute-done | bytes 655392 | tf_op jit(solution)/shard_map/ppermute | solution.py:459
  67.8 2.5 %copy-done.2 = bf16[2048,1280]{1,0:T(8,128)(2,1)S(1)} copy-done((bf16[2048,1280]{1,0:T(8,128)(2,1)S(1)}, bf16[2048,1280]{1,0:T(8,128)(2,1)}, u32[]{:S(2)}) %copy-start.2) | copy-done | bytes 5242904
  70.3 2.5 %copy-done.4 = bf16[2048,1280]{1,0:T(8,128)(2,1)S(1)} copy-done((bf16[2048,1280]{1,0:T(8,128)(2,1)S(1)}, bf16[2048,1280]{1,0:T(8,128)(2,1)}, u32[]{:S(2)}) %copy-start.4) | copy-done | bytes 5242904
  72.8 1.6 %copy-done.8 = f32[2048,256]{1,0:T(8,128)S(1)} copy-done((f32[2048,256]{1,0:T(8,128)S(1)}, f32[2048,256]{1,0:T(8,128)}, u32[]{:S(2)}) %copy-start.8) | copy-done | bytes 2097176
  74.4 3.1 %input_part.6 = (f32[256,1024]{1,0:T(8,128)S(1)}, f32[256,1024]{1,0:T(8,128)S(1)}, bf16[2,256,1280]{2,1,0:T(8,128)(2,1)S(1)}) custom-call(bf16[2048,1280]{1,0:T(8,128)(2,1)S(1)} %copy-done.2, bf16[2048,1280]{1,0:T(8,128)(2,1)S(1)} %copy-done.4, bf16[2,64,1280]{2,1,0:T(8,128)(2,1)S(1)} %get-tuple-element.74.refs_2_.refs_0_, ...), custom_call_target="tpu_custom_call" | custom-call | flops 26843545600 | bytes 671088640 | tf_op jit(solution)/shard_map/input_part/pallas_call | solution.py:36
  77.6 4.0 %input_part.7 = (f32[256,1024]{1,0:T(8,128)S(1)}, f32[256,1024]{1,0:T(8,128)S(1)}, bf16[2,256,768]{2,1,0:T(8,128)(2,1)S(1)}) custom-call(bf16[2048,3584]{1,0:T(8,128)(2,1)} %refs_0_.7, bf16[2048,3584]{1,0:T(8,128)(2,1)} %refs_1_.13, bf16[2,64,768]{2,1,0:T(8,128)(2,1)S(1)} %get-tuple-element.79.refs_2_.refs_0_, ...), custom_call_target="tpu_custom_call" | custom-call | flops 16106127360 | bytes 402653184 | tf_op jit(solution)/shard_map/input_part/pallas_call | solution.py:36
  81.7 1.6 %collective-permute-start.16 = (bf16[2,2,32,1024]{3,2,1,0:T(8,128)(2,1)S(1)}, bf16[2,2,32,1024]{3,2,1,0:T(8,128)(2,1)S(1)}, u32[]{:S(2)}, u32[]{:S(2)}) collective-permute-start(bf16[2,2,32,1024]{3,2,1,0:T(8,128)(2,1)S(1)} %fusion.2), channel_id=1, source_target_pairs={{0,1},{1,0},{2,3},{3,2},{4,5},{5,4},{6,7},{7,6},{8,9},{9,8},{10,11... | collective-permute-start | bytes 786440 | tf_op jit(solution)/shard_map/ppermute | solution.py:445
  83.3 1.6 %collective-permute-start.19 = (bf16[2,2,32,1024]{3,2,1,0:T(8,128)(2,1)S(1)}, bf16[2,2,32,1024]{3,2,1,0:T(8,128)(2,1)S(1)}, u32[]{:S(2)}, u32[]{:S(2)}) collective-permute-start(bf16[2,2,32,1024]{3,2,1,0:T(8,128)(2,1)S(1)} %fusion.3), channel_id=1, source_target_pairs={{0,2},{1,3},{2,0},{3,1},{4,6},{5,7},{6,4},{7,5},{8,10},{9,11},{10,... | collective-permute-start | bytes 786440 | tf_op jit(solution)/shard_map/ppermute | solution.py:445
  84.9 4.8 %weight_part.2 = (bf16[2048,3584]{1,0:T(8,128)(2,1)}, bf16[2048,3584]{1,0:T(8,128)(2,1)}) custom-call(bf16[2048,256]{1,0:T(8,128)(2,1)S(1)} %copy-done.6, bf16[2,256,1280]{2,1,0:T(8,128)(2,1)S(1)} %get-tuple-element.93.grads_ref, f32[256,1024]{1,0:T(8,128)S(1)} %get-tuple-element.90.refs_0_, ...), custom_call_target="tpu_custom_call", output_to_operand_aliasing={{0}: (4, {}), {1}: (5, {})} | custom-call | flops 26843545600 | bytes 671088640 | tf_op jit(solution)/shard_map/weight_part/pallas_call | solution.py:36
  90.2 2.7 %collective-permute-start.17 = (bf16[2,32,1024]{2,1,0:T(8,128)(2,1)S(1)}, bf16[2,32,1024]{2,1,0:T(8,128)(2,1)S(1)}, u32[]{:S(2)}, u32[]{:S(2)}) collective-permute-start(bf16[2,32,1024]{2,1,0:T(8,128)(2,1)S(1)} %fusion.6), channel_id=1, source_target_pairs={{0,4},{1,5},{2,6},{3,7},{4,0},{5,1},{6,2},{7,3},{8,12},{9,13},{10,... | collective-permute-start | bytes 393224 | tf_op jit(solution)/shard_map/ppermute | solution.py:445
  92.9 1.6 %collective-permute-start.20 = (bf16[2,32,1024]{2,1,0:T(8,128)(2,1)S(1)}, bf16[2,32,1024]{2,1,0:T(8,128)(2,1)S(1)}, u32[]{:S(2)}, u32[]{:S(2)}) collective-permute-start(bf16[2,32,1024]{2,1,0:T(8,128)(2,1)S(1)} %fusion.7), channel_id=1, source_target_pairs={{0,1},{1,0},{2,3},{3,2},{4,5},{5,4},{6,7},{7,6},{8,9},{9,8},{10,11... | collective-permute-start | bytes 393224 | tf_op jit(solution)/shard_map/ppermute | solution.py:445
  94.5 3.4 %weight_part.3 = (bf16[2048,3584]{1,0:T(8,128)(2,1)}, bf16[2048,3584]{1,0:T(8,128)(2,1)}) custom-call(bf16[2048,256]{1,0:T(8,128)(2,1)S(1)} %copy-done.6, bf16[2,256,768]{2,1,0:T(8,128)(2,1)S(1)} %get-tuple-element.92.grads_ref, f32[2,2,32,1024]{3,2,1,0:T(8,128)S(1)} %bitcast_add_fusion.1.refs_0_, ...), custom_call_target="tpu_custom_call", output_to_operand_aliasing={{0}: (4, {}), {1}: (5, {})} | custom-call | flops 16106127360 | bytes 402653184 | tf_op jit(solution)/shard_map/weight_part/pallas_call | solution.py:36
  99.7 3.2 %collective-permute-start.21 = (bf16[32,1024]{1,0:T(8,128)(2,1)S(1)}, bf16[32,1024]{1,0:T(8,128)(2,1)S(1)}, u32[]{:S(2)}, u32[]{:S(2)}) collective-permute-start(bf16[32,1024]{1,0:T(8,128)(2,1)S(1)} %fusion.11), channel_id=1, source_target_pairs={{0,4},{1,5},{2,6},{3,7},{4,0},{5,1},{6,2},{7,3},{8,12},{9,13},{10,... | collective-permute-start | bytes 196616 | tf_op jit(solution)/shard_map/ppermute | solution.py:445
  103.1 3.1 %collective-permute-done.21 = bf16[32,1024]{1,0:T(8,128)(2,1)S(1)} collective-permute-done((bf16[32,1024]{1,0:T(8,128)(2,1)S(1)}, bf16[32,1024]{1,0:T(8,128)(2,1)S(1)}, u32[]{:S(2)}, u32[]{:S(2)}) %collective-permute-start.21) | collective-permute-done | bytes 65568 | tf_op jit(solution)/shard_map/ppermute | solution.py:445
  (70 shorter events, 9.9 us)
Async XLA Ops:
  4.7 1.7 %collective-permute-start = (bf16[2,2,64,512]{3,2,1,0:T(8,128)(2,1)S(1)}, bf16[2,2,64,512]{3,2,1,0:T(8,128)(2,1)S(1)}, u32[]{:S(2)}, u32[]{:S(2)}) collective-permute-start(bf16[2,2,64,512]{3,2,1,0:T(8,128)(2,1)S(1)} %get-tuple-element.56), channel_id=1, source_target_pairs={{0,8},{8,0},{16,24},{24,16},{1,9},{9,1},{17,25},{25,17},{2,10},{10... | collective-permute-start | bytes 786440 | tf_op jit(solution)/shard_map/ppermute | solution.py:459
  6.4 7.4 %collective-permute-start.1 = (bf16[2,64,512]{2,1,0:T(8,128)(2,1)S(1)}, bf16[2,64,512]{2,1,0:T(8,128)(2,1)S(1)}, u32[]{:S(2)}, u32[]{:S(2)}) collective-permute-start(bf16[2,64,512]{2,1,0:T(8,128)(2,1)S(1)} %fusion.5.refs_5_), channel_id=1, source_target_pairs={{0,16},{8,24},{16,0},{24,8},{1,17},{9,25},{17,1},{25,9},{2,18},{10... | collective-permute-start | bytes 393224 | tf_op jit(solution)/shard_map/ppermute | solution.py:463
  9.4 4.5 %copy-start = (bf16[64,3584]{1,0:T(8,128)(2,1)S(1)}, bf16[64,3584]{1,0:T(8,128)(2,1)}, u32[]{:S(2)}) copy-start(bf16[64,3584]{1,0:T(8,128)(2,1)} %upstream_ref.7) | copy-start | bytes 1376260
  13.9 2.0 %collective-permute-start.2 = (bf16[2,2,64,1024]{3,2,1,0:T(8,128)(2,1)S(1)}, bf16[2,2,64,1024]{3,2,1,0:T(8,128)(2,1)S(1)}, u32[]{:S(2)}, u32[]{:S(2)}) collective-permute-start(bf16[2,2,64,1024]{3,2,1,0:T(8,128)(2,1)S(1)} %in_order.4), channel_id=1, source_target_pairs={{0,8},{8,0},{16,24},{24,16},{1,9},{9,1},{17,25},{25,17},{2,10},{10... | collective-permute-start | bytes 1572872 | tf_op jit(solution)/shard_map/ppermute | solution.py:459
  16.0 8.4 %collective-permute-start.3 = (bf16[2,64,1024]{2,1,0:T(8,128)(2,1)S(1)}, bf16[2,64,1024]{2,1,0:T(8,128)(2,1)S(1)}, u32[]{:S(2)}, u32[]{:S(2)}) collective-permute-start(bf16[2,64,1024]{2,1,0:T(8,128)(2,1)S(1)} %fusion.1.refs_5_), channel_id=1, source_target_pairs={{0,16},{8,24},{16,0},{24,8},{1,17},{9,25},{17,1},{25,9},{2,18},{10... | collective-permute-start | bytes 786440 | tf_op jit(solution)/shard_map/ppermute | solution.py:463
  24.6 2.2 %collective-permute-start.4 = (bf16[2,2,64,1280]{3,2,1,0:T(8,128)(2,1)S(1)}, bf16[2,2,64,1280]{3,2,1,0:T(8,128)(2,1)S(1)}, u32[]{:S(2)}, u32[]{:S(2)}) collective-permute-start(bf16[2,2,64,1280]{3,2,1,0:T(8,128)(2,1)S(1)} %in_order.5), channel_id=1, source_target_pairs={{0,8},{8,0},{16,24},{24,16},{1,9},{9,1},{17,25},{25,17},{2,10},{10... | collective-permute-start | bytes 1966088 | tf_op jit(solution)/shard_map/ppermute | solution.py:459
  24.7 13.2 %collective-permute-start.6 = (bf16[2,64,512]{2,1,0:T(8,128)(2,1)S(1)}, bf16[2,64,512]{2,1,0:T(8,128)(2,1)S(1)}, u32[]{:S(2)}, u32[]{:S(2)}) collective-permute-start(bf16[2,64,512]{2,1,0:T(8,128)(2,1)S(1)} %get-tuple-element.62.refs_2_.refs_0_.refs_3_), channel_id=1, source_target_pairs={{0,16},{8,24},{16,0},{24,8},{1,17},{9,25},{17,1},{25,9},{2,18},{10... | collective-permute-start | bytes 393224 | tf_op jit(solution)/shard_map/ppermute | solution.py:463
  26.9 10.8 %collective-permute-start.5 = (bf16[2,64,1280]{2,1,0:T(8,128)(2,1)S(1)}, bf16[2,64,1280]{2,1,0:T(8,128)(2,1)S(1)}, u32[]{:S(2)}, u32[]{:S(2)}) collective-permute-start(bf16[2,64,1280]{2,1,0:T(8,128)(2,1)S(1)} %fusion.refs_5_), channel_id=1, source_target_pairs={{0,16},{8,24},{16,0},{24,8},{1,17},{9,25},{17,1},{25,9},{2,18},{10... | collective-permute-start | bytes 983048 | tf_op jit(solution)/shard_map/ppermute | solution.py:463
  38.0 1.8 %collective-permute-start.7 = (bf16[2,2,64,768]{3,2,1,0:T(8,128)(2,1)S(1)}, bf16[2,2,64,768]{3,2,1,0:T(8,128)(2,1)S(1)}, u32[]{:S(2)}, u32[]{:S(2)}) collective-permute-start(bf16[2,2,64,768]{3,2,1,0:T(8,128)(2,1)S(1)} %in_order.6), channel_id=1, source_target_pairs={{0,8},{8,0},{16,24},{24,16},{1,9},{9,1},{17,25},{25,17},{2,10},{10... | collective-permute-start | bytes 1179656 | tf_op jit(solution)/shard_map/ppermute | solution.py:459
  38.1 2.9 %collective-permute-start.9 = (bf16[2,2,64,512]{3,2,1,0:T(8,128)(2,1)S(1)}, bf16[2,2,64,512]{3,2,1,0:T(8,128)(2,1)S(1)}, u32[]{:S(2)}, u32[]{:S(2)}) collective-permute-start(bf16[2,2,64,512]{3,2,1,0:T(8,128)(2,1)S(1)} %packed.4), channel_id=1, source_target_pairs={{0,8},{8,0},{16,24},{24,16},{1,9},{9,1},{17,25},{25,17},{2,10},{10... | collective-permute-start | bytes 786440 | tf_op jit(solution)/shard_map/ppermute | solution.py:459
  38.7 9.6 %collective-permute-start.11 = (bf16[2,64,1024]{2,1,0:T(8,128)(2,1)S(1)}, bf16[2,64,1024]{2,1,0:T(8,128)(2,1)S(1)}, u32[]{:S(2)}, u32[]{:S(2)}) collective-permute-start(bf16[2,64,1024]{2,1,0:T(8,128)(2,1)S(1)} %in_order.7), channel_id=1, source_target_pairs={{0,16},{8,24},{16,0},{24,8},{1,17},{9,25},{17,1},{25,9},{2,18},{10... | collective-permute-start | bytes 786440 | tf_op jit(solution)/shard_map/ppermute | solution.py:463
  39.8 11.3 %collective-permute-start.8 = (bf16[2,64,768]{2,1,0:T(8,128)(2,1)S(1)}, bf16[2,64,768]{2,1,0:T(8,128)(2,1)S(1)}, u32[]{:S(2)}, u32[]{:S(2)}) collective-permute-start(bf16[2,64,768]{2,1,0:T(8,128)(2,1)S(1)} %fusion.4.refs_2_), channel_id=1, source_target_pairs={{0,16},{8,24},{16,0},{24,8},{1,17},{9,25},{17,1},{25,9},{2,18},{10... | collective-permute-start | bytes 589832 | tf_op jit(solution)/shard_map/ppermute | solution.py:463
  48.2 14.8 %copy-start.1 = (bf16[2048,1280]{1,0:T(8,128)(2,1)}, bf16[2048,1280]{1,0:T(8,128)(2,1)S(1)}, u32[]{:S(2)}) copy-start(bf16[2048,1280]{1,0:T(8,128)(2,1)S(1)} %get-tuple-element.85.refs_0_) | copy-start | bytes 15728644
  48.2 14.8 %copy-start.3 = (bf16[2048,1280]{1,0:T(8,128)(2,1)}, bf16[2048,1280]{1,0:T(8,128)(2,1)S(1)}, u32[]{:S(2)}) copy-start(bf16[2048,1280]{1,0:T(8,128)(2,1)S(1)} %get-tuple-element.86.refs_1_) | copy-start | bytes 15728644
  48.2 14.8 %copy-start.5 = (bf16[2048,256]{1,0:T(8,128)(2,1)}, bf16[2048,256]{1,0:T(8,128)(2,1)S(1)}, u32[]{:S(2)}) copy-start(bf16[2048,256]{1,0:T(8,128)(2,1)S(1)} %get-tuple-element.81.refs_7_.xt_ref) | copy-start | bytes 3145732
  51.2 3.1 %collective-permute-start.12 = (bf16[2,2,64,1024]{3,2,1,0:T(8,128)(2,1)S(1)}, bf16[2,2,64,1024]{3,2,1,0:T(8,128)(2,1)S(1)}, u32[]{:S(2)}, u32[]{:S(2)}) collective-permute-start(bf16[2,2,64,1024]{3,2,1,0:T(8,128)(2,1)S(1)} %packed.5), channel_id=1, source_target_pairs={{0,8},{8,0},{16,24},{24,16},{1,9},{9,1},{17,25},{25,17},{2,10},{10... | collective-permute-start | bytes 1572872 | tf_op jit(solution)/shard_map/ppermute | solution.py:459
  51.3 11.7 %collective-permute-start.14 = (bf16[2,64,1280]{2,1,0:T(8,128)(2,1)S(1)}, bf16[2,64,1280]{2,1,0:T(8,128)(2,1)S(1)}, u32[]{:S(2)}, u32[]{:S(2)}) collective-permute-start(bf16[2,64,1280]{2,1,0:T(8,128)(2,1)S(1)} %get-tuple-element.74.refs_2_.refs_0_), channel_id=1, source_target_pairs={{0,16},{8,24},{16,0},{24,8},{1,17},{9,25},{17,1},{25,9},{2,18},{10... | collective-permute-start | bytes 983048 | tf_op jit(solution)/shard_map/ppermute | solution.py:463
  53.3 12.3 %collective-permute-start.10 = (bf16[2,64,768]{2,1,0:T(8,128)(2,1)S(1)}, bf16[2,64,768]{2,1,0:T(8,128)(2,1)S(1)}, u32[]{:S(2)}, u32[]{:S(2)}) collective-permute-start(bf16[2,64,768]{2,1,0:T(8,128)(2,1)S(1)} %get-tuple-element.79.refs_2_.refs_0_), channel_id=1, source_target_pairs={{0,16},{8,24},{16,0},{24,8},{1,17},{9,25},{17,1},{25,9},{2,18},{10... | collective-permute-start | bytes 589832 | tf_op jit(solution)/shard_map/ppermute | solution.py:463
  63.0 2.8 %copy-start.7 = (f32[2048,256]{1,0:T(8,128)}, f32[2048,256]{1,0:T(8,128)S(1)}, u32[]{:S(2)}) copy-start(f32[2048,256]{1,0:T(8,128)S(1)} %get-tuple-element.87.refs_5_) | copy-start | bytes 6291460
  65.7 2.2 %collective-permute-start.15 = (bf16[2,2,64,1280]{3,2,1,0:T(8,128)(2,1)S(1)}, bf16[2,2,64,1280]{3,2,1,0:T(8,128)(2,1)S(1)}, u32[]{:S(2)}, u32[]{:S(2)}) collective-permute-start(bf16[2,2,64,1280]{3,2,1,0:T(8,128)(2,1)S(1)} %packed.7), channel_id=1, source_target_pairs={{0,8},{8,0},{16,24},{24,16},{1,9},{9,1},{17,25},{25,17},{2,10},{10... | collective-permute-start | bytes 1966088 | tf_op jit(solution)/shard_map/ppermute | solution.py:459
  65.9 11.7 %collective-permute-start.13 = (bf16[2,2,64,768]{3,2,1,0:T(8,128)(2,1)S(1)}, bf16[2,2,64,768]{3,2,1,0:T(8,128)(2,1)S(1)}, u32[]{:S(2)}, u32[]{:S(2)}) collective-permute-start(bf16[2,2,64,768]{3,2,1,0:T(8,128)(2,1)S(1)} %packed.6), channel_id=1, source_target_pairs={{0,8},{8,0},{16,24},{24,16},{1,9},{9,1},{17,25},{25,17},{2,10},{10... | collective-permute-start | bytes 1179656 | tf_op jit(solution)/shard_map/ppermute | solution.py:459
  67.8 2.5 %copy-start.2 = (bf16[2048,1280]{1,0:T(8,128)(2,1)S(1)}, bf16[2048,1280]{1,0:T(8,128)(2,1)}, u32[]{:S(2)}) copy-start(bf16[2048,1280]{1,0:T(8,128)(2,1)} %copy-done.1) | copy-start | bytes 15728644
  70.3 2.5 %copy-start.4 = (bf16[2048,1280]{1,0:T(8,128)(2,1)S(1)}, bf16[2048,1280]{1,0:T(8,128)(2,1)}, u32[]{:S(2)}) copy-start(bf16[2048,1280]{1,0:T(8,128)(2,1)} %copy-done.3) | copy-start | bytes 15728644
  72.8 1.6 %copy-start.8 = (f32[2048,256]{1,0:T(8,128)S(1)}, f32[2048,256]{1,0:T(8,128)}, u32[]{:S(2)}) copy-start(f32[2048,256]{1,0:T(8,128)} %copy-done.7) | copy-start | bytes 6291460
  77.6 7.4 %copy-start.6 = (bf16[2048,256]{1,0:T(8,128)(2,1)S(1)}, bf16[2048,256]{1,0:T(8,128)(2,1)}, u32[]{:S(2)}) copy-start(bf16[2048,256]{1,0:T(8,128)(2,1)} %copy-done.5) | copy-start | bytes 3145732
  81.7 8.4 %collective-permute-start.16 = (bf16[2,2,32,1024]{3,2,1,0:T(8,128)(2,1)S(1)}, bf16[2,2,32,1024]{3,2,1,0:T(8,128)(2,1)S(1)}, u32[]{:S(2)}, u32[]{:S(2)}) collective-permute-start(bf16[2,2,32,1024]{3,2,1,0:T(8,128)(2,1)S(1)} %fusion.2), channel_id=1, source_target_pairs={{0,1},{1,0},{2,3},{3,2},{4,5},{5,4},{6,7},{7,6},{8,9},{9,8},{10,11... | collective-permute-start | bytes 786440 | tf_op jit(solution)/shard_map/ppermute | solution.py:445
  83.3 9.5 %collective-permute-start.19 = (bf16[2,2,32,1024]{3,2,1,0:T(8,128)(2,1)S(1)}, bf16[2,2,32,1024]{3,2,1,0:T(8,128)(2,1)S(1)}, u32[]{:S(2)}, u32[]{:S(2)}) collective-permute-start(bf16[2,2,32,1024]{3,2,1,0:T(8,128)(2,1)S(1)} %fusion.3), channel_id=1, source_target_pairs={{0,2},{1,3},{2,0},{3,1},{4,6},{5,7},{6,4},{7,5},{8,10},{9,11},{10,... | collective-permute-start | bytes 786440 | tf_op jit(solution)/shard_map/ppermute | solution.py:445
  90.2 8.5 %collective-permute-start.17 = (bf16[2,32,1024]{2,1,0:T(8,128)(2,1)S(1)}, bf16[2,32,1024]{2,1,0:T(8,128)(2,1)S(1)}, u32[]{:S(2)}, u32[]{:S(2)}) collective-permute-start(bf16[2,32,1024]{2,1,0:T(8,128)(2,1)S(1)} %fusion.6), channel_id=1, source_target_pairs={{0,4},{1,5},{2,6},{3,7},{4,0},{5,1},{6,2},{7,3},{8,12},{9,13},{10,... | collective-permute-start | bytes 393224 | tf_op jit(solution)/shard_map/ppermute | solution.py:445
  92.9 6.7 %collective-permute-start.20 = (bf16[2,32,1024]{2,1,0:T(8,128)(2,1)S(1)}, bf16[2,32,1024]{2,1,0:T(8,128)(2,1)S(1)}, u32[]{:S(2)}, u32[]{:S(2)}) collective-permute-start(bf16[2,32,1024]{2,1,0:T(8,128)(2,1)S(1)} %fusion.7), channel_id=1, source_target_pairs={{0,1},{1,0},{2,3},{3,2},{4,5},{5,4},{6,7},{7,6},{8,9},{9,8},{10,11... | collective-permute-start | bytes 393224 | tf_op jit(solution)/shard_map/ppermute | solution.py:445
  98.7 4.3 %collective-permute-start.18 = (bf16[32,1024]{1,0:T(8,128)(2,1)S(1)}, bf16[32,1024]{1,0:T(8,128)(2,1)S(1)}, u32[]{:S(2)}, u32[]{:S(2)}) collective-permute-start(bf16[32,1024]{1,0:T(8,128)(2,1)S(1)} %fusion.10), channel_id=1, source_target_pairs={{0,2},{1,3},{2,0},{3,1},{4,6},{5,7},{6,4},{7,5},{8,10},{9,11},{10,... | collective-permute-start | bytes 196616 | tf_op jit(solution)/shard_map/ppermute | solution.py:445
  99.7 6.5 %collective-permute-start.21 = (bf16[32,1024]{1,0:T(8,128)(2,1)S(1)}, bf16[32,1024]{1,0:T(8,128)(2,1)S(1)}, u32[]{:S(2)}, u32[]{:S(2)}) collective-permute-start(bf16[32,1024]{1,0:T(8,128)(2,1)S(1)} %fusion.11), channel_id=1, source_target_pairs={{0,4},{1,5},{2,6},{3,7},{4,0},{5,1},{6,2},{7,3},{8,12},{9,13},{10,... | collective-permute-start | bytes 196616 | tf_op jit(solution)/shard_map/ppermute | solution.py:445

commit v11 on v9

--- a/solution.py
+++ b/solution.py
@@ -532,7 +532,7 @@
             acc = totals[0]
             continue
         after = sums[-1][:1] + pieces[i + 1][:1] if i == 1 and number > 3 else []
-        relay(i, grads[-1:] + pieces[-1][:1] if i > 1 else sums[-1][:1])
+        relay(i, grads[1:2] + pieces[-1][:1] if i > 1 else sums[-1][:1])
         acc = take_input(i, x, acc, after)
         for j in range(len(pieces), number if i else 0):
             hidden = middle(j, hidden, grads[-1:])

time: 102 us -> 109 us (1.069)
  local copies, waits for them, and re-layouts: 2.61 us -> 6.73 us
  waiting for transfers between devices: 23.4 us -> 25.8 us
    unnamed x10 -> x18, local copies, waits for them, and re-layouts: 2.46 us -> 6.58 us
    ppermute x8, waiting for transfers between devices: 11.7 us -> 15.8 us  [across(): return lax.ppermute(value, 'row', moves)]
    ppermute x8, waiting for transfers between devices: 7.33 us -> 4.78 us  [sibling(): return lax.ppermute(value, 'row', swap)]
  transfers between devices with their start and end apart: 22 -> 22, of which waited for: 14 -> 12; matrix products, arithmetic and copies ran while one was open for 0% -> 0% of each run, Pallas kernels for 41% -> 39%
where the time goes in v11:
time: 109 us; the launch traced here: 108 us
  Pallas kernels  50.4 us (46%)
  waiting for transfers between devices  25.8 us (24%)
  starting transfers between devices  23.2 us (21%)
  local copies, waits for them, and re-layouts  6.73 us (6%)
    pallas_call x21, Pallas kernels, call(): pl.pallas_call(kernel, in_specs=in_specs, out_specs=out_specs, out_shape=...  50.4 us
    ppermute x8, waiting for transfers between devices, across(): return lax.ppermute(value, 'row', moves)  15.8 us
    ppermute x6, starting transfers between devices, token_sums(): got.append(lax.ppermute(send.astype(BF16), 'col', moves))  11.6 us
    ppermute x8, starting transfers between devices, across(): return lax.ppermute(value, 'row', moves)  10.5 us
    unnamed x18, local copies, waits for them, and re-layouts  6.58 us
    ppermute x6, waiting for transfers between devices, token_sums(): got.append(lax.ppermute(send.astype(BF16), 'col', moves))  5.21 us
    ppermute x8, waiting for transfers between devices, sibling(): return lax.ppermute(value, 'row', swap)  4.78 us
  transfers between devices with their start and end apart: 22, of which 12 were waited for; matrix products, arithmetic and copies ran while one was open for 0% of the time, Pallas kernels for 39%

profile of v11, /device:TPU:0, one launch (start us, length us, event | category | flops | bytes accessed | tf_op | source)
XLA Modules:
  0.0 108.3 jit_solution(5314664830240623369)
XLA Ops:
  0.6 4.1 %forward_part.4 = (f32[2,64,512]{2,1,0:T(8,128)S(1)}, f32[1,2,64,512]{3,2,1,0:T(8,128)S(1)}, bf16[2,2,64,512]{3,2,1,0:T(8,128)(2,1)S(1)}, bf16[256,2048]{1,0:T(8...) custom-call(bf16[256,2048]{1,0:T(8,128)(2,1)} %refs_0_.4, bf16[2048,3584]{1,0:T(8,128)(2,1)} %refs_0_.7, ...), custom_call_target="tpu_custom_call" | custom-call | flops 10737418240 | bytes 268435456 | tf_op jit(solution)/shard_map/forward_part/pallas_call | solution.py:36
  5.2 1.2 %collective-permute-done.got_ref = bf16[2,2,64,512]{3,2,1,0:T(8,128)(2,1)S(1)} collective-permute-done((bf16[2,2,64,512]{3,2,1,0:T(8,128)(2,1)S(1)}, bf16[2,2,64,512]{3,2,1,0:T(8,128)(2,1)S(1)}, u32[]{:S(2)}, u32[]{:S(2)}) %collective-permute-start) | collective-permute-done | bytes 262176 | tf_op jit(solution)/shard_map/ppermute | solution.py:459
  6.4 2.9 %collective-permute-start.1 = (bf16[2,64,512]{2,1,0:T(8,128)(2,1)S(1)}, bf16[2,64,512]{2,1,0:T(8,128)(2,1)S(1)}, u32[]{:S(2)}, u32[]{:S(2)}) collective-permute-start(bf16[2,64,512]{2,1,0:T(8,128)(2,1)S(1)} %fusion.5.refs_5_), channel_id=1, source_target_pairs={{0,16},{8,24},{16,0},{24,8},{1,17},{9,25},{17,1},{25,9},{2,18},{10... | collective-permute-start | bytes 393224 | tf_op jit(solution)/shard_map/ppermute | solution.py:463
  9.4 4.4 %forward_part.5 = (f32[2,64,1024]{2,1,0:T(8,128)S(1)}, f32[1,2,64,1024]{3,2,1,0:T(8,128)S(1)}, bf16[2,2,64,1024]{3,2,1,0:T(8,128)(2,1)S(1)}, bf16[2048,256]{1,0:T(8,128)(2,1)S(1)}, bf16[2048,256]{1,0:T(8,128)(2,1)S(1)}) custom-call(bf16[256,2048]{1,0:T(8,128)(2,1)S(1)} %get-tuple-element.52.refs_0_.refs_5_, bf16[2048,3584]{1,0:T(8,128)(2,1)} %refs_0_.7, ...), custom_call_target="tpu_custom_call" | custom-call | flops 21474836480 | bytes 536870912 | tf_op jit(solution)/shard_map/forward_part/pallas_call | solution.py:36
  14.0 1.9 %collective-permute-done.2.got_ref = bf16[2,2,64,1024]{3,2,1,0:T(8,128)(2,1)S(1)} collective-permute-done((bf16[2,2,64,1024]{3,2,1,0:T(8,128)(2,1)S(1)}, bf16[2,2,64,1024]{3,2,1,0:T(8,128)(2,1)S(1)}, u32[]{:S(2)}, u32[]{:S(2)}) %collective-permute-start.2) | collective-permute-done | bytes 524320 | tf_op jit(solution)/shard_map/ppermute | solution.py:459
  16.0 1.1 %collective-permute-start.3 = (bf16[2,64,1024]{2,1,0:T(8,128)(2,1)S(1)}, bf16[2,64,1024]{2,1,0:T(8,128)(2,1)S(1)}, u32[]{:S(2)}, u32[]{:S(2)}) collective-permute-start(bf16[2,64,1024]{2,1,0:T(8,128)(2,1)S(1)} %fusion.1.refs_5_), channel_id=1, source_target_pairs={{0,16},{8,24},{16,0},{24,8},{1,17},{9,25},{17,1},{25,9},{2,18},{10... | collective-permute-start | bytes 786440 | tf_op jit(solution)/shard_map/ppermute | solution.py:463
  17.1 5.4 %forward_part.6 = (f32[2,64,1280]{2,1,0:T(8,128)S(1)}, f32[1,2,64,1280]{3,2,1,0:T(8,128)S(1)}, bf16[2,2,64,1280]{3,2,1,0:T(8,128)(2,1)S(1)}, bf16[2048,256]{1,0:T(8,128)(2,1)S(1)}, bf16[2048,256]{1,0:T(8,128)(2,1)S(1)}) custom-call(bf16[256,2048]{1,0:T(8,128)(2,1)S(1)} %get-tuple-element.52.refs_0_.refs_5_, bf16[2048,3584]{1,0:T(8,128)(2,1)} %refs_0_.7, ...), custom_call_target="tpu_custom_call" | custom-call | flops 26843545600 | bytes 671088640 | tf_op jit(solution)/shard_map/forward_part/pallas_call | solution.py:36
  22.5 1.9 %collective-permute-done.3.refs_0_.refs_1_ = bf16[2,64,1024]{2,1,0:T(8,128)(2,1)S(1)} collective-permute-done((bf16[2,64,1024]{2,1,0:T(8,128)(2,1)S(1)}, bf16[2,64,1024]{2,1,0:T(8,128)(2,1)S(1)}, u32[]{:S(2)}, u32[]{:S(2)}) %collective-permute-start.3) | collective-permute-done | bytes 262176 | tf_op jit(solution)/shard_map/ppermute | solution.py:463
  24.7 1.1 %collective-permute-start.6 = (bf16[2,64,512]{2,1,0:T(8,128)(2,1)S(1)}, bf16[2,64,512]{2,1,0:T(8,128)(2,1)S(1)}, u32[]{:S(2)}, u32[]{:S(2)}) collective-permute-start(bf16[2,64,512]{2,1,0:T(8,128)(2,1)S(1)} %get-tuple-element.62.refs_2_.refs_0_), channel_id=1, source_target_pairs={{0,16},{8,24},{16,0},{24,8},{1,17},{9,25},{17,1},{25,9},{2,18},{10... | collective-permute-start | bytes 393224 | tf_op jit(solution)/shard_map/ppermute | solution.py:463
  26.9 1.1 %collective-permute-start.5 = (bf16[2,64,1280]{2,1,0:T(8,128)(2,1)S(1)}, bf16[2,64,1280]{2,1,0:T(8,128)(2,1)S(1)}, u32[]{:S(2)}, u32[]{:S(2)}) collective-permute-start(bf16[2,64,1280]{2,1,0:T(8,128)(2,1)S(1)} %fusion.refs_5_.refs_2_), channel_id=1, source_target_pairs={{0,16},{8,24},{16,0},{24,8},{1,17},{9,25},{17,1},{25,9},{2,18},{10... | collective-permute-start | bytes 983048 | tf_op jit(solution)/shard_map/ppermute | solution.py:463
  28.0 3.1 %collective-permute-done.6.refs_1_.refs_3_ = bf16[2,64,512]{2,1,0:T(8,128)(2,1)S(1)} collective-permute-done((bf16[2,64,512]{2,1,0:T(8,128)(2,1)S(1)}, bf16[2,64,512]{2,1,0:T(8,128)(2,1)S(1)}, u32[]{:S(2)}, u32[]{:S(2)}) %collective-permute-start.6) | collective-permute-done | bytes 131104 | tf_op jit(solution)/shard_map/ppermute | solution.py:463
  31.2 3.6 %forward_part.7 = (f32[2,64,768]{2,1,0:T(8,128)S(1)}, f32[1,2,64,768]{3,2,1,0:T(8,128)S(1)}, bf16[2,2,64,768]{3,2,1,0:T(8,128)(2,1)S(1)}) custom-call(bf16[256,2048]{1,0:T(8,128)(2,1)S(1)} %get-tuple-element.52.refs_0_.refs_5_, bf16[2048,3584]{1,0:T(8,128)(2,1)} %refs_0_.7, bf16[2048,3584]{1,0:T(8,128)(2,1)} %refs_1_.13, ...), custom_call_target="tpu_custom_call" | custom-call | flops 16106127360 | bytes 402653184 | tf_op jit(solution)/shard_map/forward_part/pallas_call | solution.py:36
  34.8 7.2 %input_part.4 = (bf16[2048,256]{1,0:T(8,128)(2,1)S(1)}, f32[2048,256]{1,0:T(8,128)S(1)}, bf16[2,256,512]{2,1,0:T(8,128)(2,1)S(1)}, bf16[2048,3584]{1,0:T(8,128)(...) custom-call(bf16[2048,3584]{1,0:T(8,128)(2,1)} %refs_0_.7, ...), custom_call_target="tpu_custom_call" | custom-call | flops 20971520 | bytes 524288 | tf_op jit(solution)/shard_map/input_part/pallas_call | solution.py:36
  42.1 1.2 %collective-permute-done.5.refs_0_.refs_1_ = bf16[2,64,1280]{2,1,0:T(8,128)(2,1)S(1)} collective-permute-done((bf16[2,64,1280]{2,1,0:T(8,128)(2,1)S(1)}, bf16[2,64,1280]{2,1,0:T(8,128)(2,1)S(1)}, u32[]{:S(2)}, u32[]{:S(2)}) %collective-permute-start.5) | collective-permute-done | bytes 327712 | tf_op jit(solution)/shard_map/ppermute | solution.py:463
  43.7 1.7 %collective-permute-done.9.got_ref = bf16[2,2,64,768]{3,2,1,0:T(8,128)(2,1)S(1)} collective-permute-done((bf16[2,2,64,768]{3,2,1,0:T(8,128)(2,1)S(1)}, bf16[2,2,64,768]{3,2,1,0:T(8,128)(2,1)S(1)}, u32[]{:S(2)}, u32[]{:S(2)}) %collective-permute-start.9) | collective-permute-done | bytes 393248 | tf_op jit(solution)/shard_map/ppermute | solution.py:459
  47.7 8.6 %input_part.5 = (f32[2048,256]{1,0:T(8,128)S(1)}, bf16[2,256,1024]{2,1,0:T(8,128)(2,1)S(1)}, bf16[2048,3584]{1,0:T(8,128)(2,1)}, bf16[2048,3584]{1,0:T(8,128)(2,1)}) custom-call(bf16[2048,3584]{1,0:T(8,128)(2,1)} %refs_0_.7, bf16[2048,3584]{1,0:T(8,128)(2,1)} %refs_1_.13, ...), custom_call_target="tpu_custom_call", output_to_operand_aliasing={{2}: (9, {}), {3}: (10, {})} | custom-call | flops 21474836480 | bytes 536870912 | tf_op jit(solution)/shard_map/input_part/pallas_call | solution.py:36
  56.3 3.5 %collective-permute-done.10.refs_0_ = bf16[2,64,768]{2,1,0:T(8,128)(2,1)S(1)} collective-permute-done((bf16[2,64,768]{2,1,0:T(8,128)(2,1)S(1)}, bf16[2,64,768]{2,1,0:T(8,128)(2,1)S(1)}, u32[]{:S(2)}, u32[]{:S(2)}) %collective-permute-start.10) | collective-permute-done | bytes 196640 | tf_op jit(solution)/shard_map/ppermute | solution.py:463
  60.9 1.1 %collective-permute-start.12 = (bf16[2,64,768]{2,1,0:T(8,128)(2,1)S(1)}, bf16[2,64,768]{2,1,0:T(8,128)(2,1)S(1)}, u32[]{:S(2)}, u32[]{:S(2)}) collective-permute-start(bf16[2,64,768]{2,1,0:T(8,128)(2,1)S(1)} %get-tuple-element.84.refs_0_.refs_3_.refs_2_), channel_id=1, source_target_pairs={{0,16},{8,24},{16,0},{24,8},{1,17},{9,25},{17,1},{25,9},{2,18},{10... | collective-permute-start | bytes 589832 | tf_op jit(solution)/shard_map/ppermute | solution.py:463
  62.0 6.2 %collective-permute-done.12.refs_1_.refs_3_ = bf16[2,64,768]{2,1,0:T(8,128)(2,1)S(1)} collective-permute-done((bf16[2,64,768]{2,1,0:T(8,128)(2,1)S(1)}, bf16[2,64,768]{2,1,0:T(8,128)(2,1)S(1)}, u32[]{:S(2)}, u32[]{:S(2)}) %collective-permute-start.12) | collective-permute-done | bytes 196640 | tf_op jit(solution)/shard_map/ppermute | solution.py:463
  68.3 2.5 %copy-done.2 = bf16[2048,1280]{1,0:T(8,128)(2,1)S(1)} copy-done((bf16[2048,1280]{1,0:T(8,128)(2,1)S(1)}, bf16[2048,1280]{1,0:T(8,128)(2,1)}, u32[]{:S(2)}) %copy-start.2) | copy-done | bytes 5242904
  70.8 2.5 %copy-done.4 = bf16[2048,1280]{1,0:T(8,128)(2,1)S(1)} copy-done((bf16[2048,1280]{1,0:T(8,128)(2,1)S(1)}, bf16[2048,1280]{1,0:T(8,128)(2,1)}, u32[]{:S(2)}) %copy-start.4) | copy-done | bytes 5242904
  73.3 1.6 %copy-done.8 = f32[2048,256]{1,0:T(8,128)S(1)} copy-done((f32[2048,256]{1,0:T(8,128)S(1)}, f32[2048,256]{1,0:T(8,128)}, u32[]{:S(2)}) %copy-start.8) | copy-done | bytes 2097176
  74.9 3.1 %input_part.6 = (f32[256,1024]{1,0:T(8,128)S(1)}, f32[256,1024]{1,0:T(8,128)S(1)}, bf16[2,256,1280]{2,1,0:T(8,128)(2,1)S(1)}) custom-call(bf16[2048,1280]{1,0:T(8,128)(2,1)S(1)} %copy-done.2, bf16[2048,1280]{1,0:T(8,128)(2,1)S(1)} %copy-done.4, bf16[2,64,1280]{2,1,0:T(8,128)(2,1)S(1)} %get-tuple-element.74.refs_2_.refs_3_.refs_0_, ...), custom_call_target="tpu_custom_call" | custom-call | flops 26843545600 | bytes 671088640 | tf_op jit(solution)/shard_map/input_part/pallas_call | solution.py:36
  78.0 4.0 %input_part.7 = (f32[256,1024]{1,0:T(8,128)S(1)}, f32[256,1024]{1,0:T(8,128)S(1)}, bf16[2,256,768]{2,1,0:T(8,128)(2,1)S(1)}) custom-call(bf16[2048,3584]{1,0:T(8,128)(2,1)} %refs_0_.7, bf16[2048,3584]{1,0:T(8,128)(2,1)} %refs_1_.13, bf16[2,64,768]{2,1,0:T(8,128)(2,1)S(1)} %get-tuple-element.84.refs_0_.refs_3_.refs_2_, ...), custom_call_target="tpu_custom_call" | custom-call | flops 16106127360 | bytes 402653184 | tf_op jit(solution)/shard_map/input_part/pallas_call | solution.py:36
  82.1 1.6 %collective-permute-start.16 = (bf16[2,2,32,1024]{3,2,1,0:T(8,128)(2,1)S(1)}, bf16[2,2,32,1024]{3,2,1,0:T(8,128)(2,1)S(1)}, u32[]{:S(2)}, u32[]{:S(2)}) collective-permute-start(bf16[2,2,32,1024]{3,2,1,0:T(8,128)(2,1)S(1)} %fusion.2), channel_id=1, source_target_pairs={{0,1},{1,0},{2,3},{3,2},{4,5},{5,4},{6,7},{7,6},{8,9},{9,8},{10,11... | collective-permute-start | bytes 786440 | tf_op jit(solution)/shard_map/ppermute | solution.py:445
  83.8 1.6 %collective-permute-start.19 = (bf16[2,2,32,1024]{3,2,1,0:T(8,128)(2,1)S(1)}, bf16[2,2,32,1024]{3,2,1,0:T(8,128)(2,1)S(1)}, u32[]{:S(2)}, u32[]{:S(2)}) collective-permute-start(bf16[2,2,32,1024]{3,2,1,0:T(8,128)(2,1)S(1)} %fusion.3), channel_id=1, source_target_pairs={{0,2},{1,3},{2,0},{3,1},{4,6},{5,7},{6,4},{7,5},{8,10},{9,11},{10,... | collective-permute-start | bytes 786440 | tf_op jit(solution)/shard_map/ppermute | solution.py:445
  85.4 4.8 %weight_part.2 = (bf16[2048,3584]{1,0:T(8,128)(2,1)}, bf16[2048,3584]{1,0:T(8,128)(2,1)}) custom-call(bf16[2048,256]{1,0:T(8,128)(2,1)S(1)} %copy-done.6, bf16[2,256,1280]{2,1,0:T(8,128)(2,1)S(1)} %get-tuple-element.93.grads_ref, f32[256,1024]{1,0:T(8,128)S(1)} %get-tuple-element.90.refs_0_, ...), custom_call_target="tpu_custom_call", output_to_operand_aliasing={{0}: (4, {}), {1}: (5, {})} | custom-call | flops 26843545600 | bytes 671088640 | tf_op jit(solution)/shard_map/weight_part/pallas_call | solution.py:36
  91.0 2.7 %collective-permute-start.17 = (bf16[2,32,1024]{2,1,0:T(8,128)(2,1)S(1)}, bf16[2,32,1024]{2,1,0:T(8,128)(2,1)S(1)}, u32[]{:S(2)}, u32[]{:S(2)}) collective-permute-start(bf16[2,32,1024]{2,1,0:T(8,128)(2,1)S(1)} %fusion.6), channel_id=1, source_target_pairs={{0,4},{1,5},{2,6},{3,7},{4,0},{5,1},{6,2},{7,3},{8,12},{9,13},{10,... | collective-permute-start | bytes 393224 | tf_op jit(solution)/shard_map/ppermute | solution.py:445
  93.8 1.6 %collective-permute-start.20 = (bf16[2,32,1024]{2,1,0:T(8,128)(2,1)S(1)}, bf16[2,32,1024]{2,1,0:T(8,128)(2,1)S(1)}, u32[]{:S(2)}, u32[]{:S(2)}) collective-permute-start(bf16[2,32,1024]{2,1,0:T(8,128)(2,1)S(1)} %fusion.7), channel_id=1, source_target_pairs={{0,1},{1,0},{2,3},{3,2},{4,5},{5,4},{6,7},{7,6},{8,9},{9,8},{10,11... | collective-permute-start | bytes 393224 | tf_op jit(solution)/shard_map/ppermute | solution.py:445
  95.3 3.4 %weight_part.3 = (bf16[2048,3584]{1,0:T(8,128)(2,1)}, bf16[2048,3584]{1,0:T(8,128)(2,1)}) custom-call(bf16[2048,256]{1,0:T(8,128)(2,1)S(1)} %copy-done.6, bf16[2,256,768]{2,1,0:T(8,128)(2,1)S(1)} %get-tuple-element.92.grads_ref, f32[2,2,32,1024]{3,2,1,0:T(8,128)S(1)} %bitcast_add_fusion.1.refs_0_, ...), custom_call_target="tpu_custom_call", output_to_operand_aliasing={{0}: (4, {}), {1}: (5, {})} | custom-call | flops 16106127360 | bytes 402653184 | tf_op jit(solution)/shard_map/weight_part/pallas_call | solution.py:36
  100.7 3.4 %collective-permute-start.21 = (bf16[32,1024]{1,0:T(8,128)(2,1)S(1)}, bf16[32,1024]{1,0:T(8,128)(2,1)S(1)}, u32[]{:S(2)}, u32[]{:S(2)}) collective-permute-start(bf16[32,1024]{1,0:T(8,128)(2,1)S(1)} %fusion.11), channel_id=1, source_target_pairs={{0,4},{1,5},{2,6},{3,7},{4,0},{5,1},{6,2},{7,3},{8,12},{9,13},{10,... | collective-permute-start | bytes 196616 | tf_op jit(solution)/shard_map/ppermute | solution.py:445
  104.3 3.3 %collective-permute-done.21 = bf16[32,1024]{1,0:T(8,128)(2,1)S(1)} collective-permute-done((bf16[32,1024]{1,0:T(8,128)(2,1)S(1)}, bf16[32,1024]{1,0:T(8,128)(2,1)S(1)}, u32[]{:S(2)}, u32[]{:S(2)}) %collective-permute-start.21) | collective-permute-done | bytes 65568 | tf_op jit(solution)/shard_map/ppermute | solution.py:445
  (68 shorter events, 9.7 us)
Async XLA Ops:
  4.7 1.7 %collective-permute-start = (bf16[2,2,64,512]{3,2,1,0:T(8,128)(2,1)S(1)}, bf16[2,2,64,512]{3,2,1,0:T(8,128)(2,1)S(1)}, u32[]{:S(2)}, u32[]{:S(2)}) collective-permute-start(bf16[2,2,64,512]{3,2,1,0:T(8,128)(2,1)S(1)} %get-tuple-element.56), channel_id=1, source_target_pairs={{0,8},{8,0},{16,24},{24,16},{1,9},{9,1},{17,25},{25,17},{2,10},{10... | collective-permute-start | bytes 786440 | tf_op jit(solution)/shard_map/ppermute | solution.py:459
  6.4 7.4 %collective-permute-start.1 = (bf16[2,64,512]{2,1,0:T(8,128)(2,1)S(1)}, bf16[2,64,512]{2,1,0:T(8,128)(2,1)S(1)}, u32[]{:S(2)}, u32[]{:S(2)}) collective-permute-start(bf16[2,64,512]{2,1,0:T(8,128)(2,1)S(1)} %fusion.5.refs_5_), channel_id=1, source_target_pairs={{0,16},{8,24},{16,0},{24,8},{1,17},{9,25},{17,1},{25,9},{2,18},{10... | collective-permute-start | bytes 393224 | tf_op jit(solution)/shard_map/ppermute | solution.py:463
  9.4 4.5 %copy-start = (bf16[64,3584]{1,0:T(8,128)(2,1)S(1)}, bf16[64,3584]{1,0:T(8,128)(2,1)}, u32[]{:S(2)}) copy-start(bf16[64,3584]{1,0:T(8,128)(2,1)} %upstream_ref.7) | copy-start | bytes 1376260
  13.9 2.0 %collective-permute-start.2 = (bf16[2,2,64,1024]{3,2,1,0:T(8,128)(2,1)S(1)}, bf16[2,2,64,1024]{3,2,1,0:T(8,128)(2,1)S(1)}, u32[]{:S(2)}, u32[]{:S(2)}) collective-permute-start(bf16[2,2,64,1024]{3,2,1,0:T(8,128)(2,1)S(1)} %in_order.3), channel_id=1, source_target_pairs={{0,8},{8,0},{16,24},{24,16},{1,9},{9,1},{17,25},{25,17},{2,10},{10... | collective-permute-start | bytes 1572872 | tf_op jit(solution)/shard_map/ppermute | solution.py:459
  16.0 8.4 %collective-permute-start.3 = (bf16[2,64,1024]{2,1,0:T(8,128)(2,1)S(1)}, bf16[2,64,1024]{2,1,0:T(8,128)(2,1)S(1)}, u32[]{:S(2)}, u32[]{:S(2)}) collective-permute-start(bf16[2,64,1024]{2,1,0:T(8,128)(2,1)S(1)} %fusion.1.refs_5_), channel_id=1, source_target_pairs={{0,16},{8,24},{16,0},{24,8},{1,17},{9,25},{17,1},{25,9},{2,18},{10... | collective-permute-start | bytes 786440 | tf_op jit(solution)/shard_map/ppermute | solution.py:463
  24.6 2.2 %collective-permute-start.4 = (bf16[2,2,64,1280]{3,2,1,0:T(8,128)(2,1)S(1)}, bf16[2,2,64,1280]{3,2,1,0:T(8,128)(2,1)S(1)}, u32[]{:S(2)}, u32[]{:S(2)}) collective-permute-start(bf16[2,2,64,1280]{3,2,1,0:T(8,128)(2,1)S(1)} %in_order.4), channel_id=1, source_target_pairs={{0,8},{8,0},{16,24},{24,16},{1,9},{9,1},{17,25},{25,17},{2,10},{10... | collective-permute-start | bytes 1966088 | tf_op jit(solution)/shard_map/ppermute | solution.py:459
  24.7 6.4 %collective-permute-start.6 = (bf16[2,64,512]{2,1,0:T(8,128)(2,1)S(1)}, bf16[2,64,512]{2,1,0:T(8,128)(2,1)S(1)}, u32[]{:S(2)}, u32[]{:S(2)}) collective-permute-start(bf16[2,64,512]{2,1,0:T(8,128)(2,1)S(1)} %get-tuple-element.62.refs_2_.refs_0_), channel_id=1, source_target_pairs={{0,16},{8,24},{16,0},{24,8},{1,17},{9,25},{17,1},{25,9},{2,18},{10... | collective-permute-start | bytes 393224 | tf_op jit(solution)/shard_map/ppermute | solution.py:463
  25.9 17.7 %collective-permute-start.7 = (bf16[2,64,1024]{2,1,0:T(8,128)(2,1)S(1)}, bf16[2,64,1024]{2,1,0:T(8,128)(2,1)S(1)}, u32[]{:S(2)}, u32[]{:S(2)}) collective-permute-start(bf16[2,64,1024]{2,1,0:T(8,128)(2,1)S(1)} %get-tuple-element.69.refs_2_.refs_0_.refs_4_), channel_id=1, source_target_pairs={{0,16},{8,24},{16,0},{24,8},{1,17},{9,25},{17,1},{25,9},{2,18},{10... | collective-permute-start | bytes 786440 | tf_op jit(solution)/shard_map/ppermute | solution.py:463
  26.9 16.4 %collective-permute-start.5 = (bf16[2,64,1280]{2,1,0:T(8,128)(2,1)S(1)}, bf16[2,64,1280]{2,1,0:T(8,128)(2,1)S(1)}, u32[]{:S(2)}, u32[]{:S(2)}) collective-permute-start(bf16[2,64,1280]{2,1,0:T(8,128)(2,1)S(1)} %fusion.refs_5_.refs_2_), channel_id=1, source_target_pairs={{0,16},{8,24},{16,0},{24,8},{1,17},{9,25},{17,1},{25,9},{2,18},{10... | collective-permute-start | bytes 983048 | tf_op jit(solution)/shard_map/ppermute | solution.py:463
  31.1 3.7 %collective-permute-start.8 = (bf16[2,2,64,512]{3,2,1,0:T(8,128)(2,1)S(1)}, bf16[2,2,64,512]{3,2,1,0:T(8,128)(2,1)S(1)}, u32[]{:S(2)}, u32[]{:S(2)}) collective-permute-start(bf16[2,2,64,512]{3,2,1,0:T(8,128)(2,1)S(1)} %packed.4), channel_id=1, source_target_pairs={{0,8},{8,0},{16,24},{24,16},{1,9},{9,1},{17,25},{25,17},{2,10},{10... | collective-permute-start | bytes 786440 | tf_op jit(solution)/shard_map/ppermute | solution.py:459
  42.1 14.2 %copy-start.1 = (bf16[2048,1280]{1,0:T(8,128)(2,1)}, bf16[2048,1280]{1,0:T(8,128)(2,1)S(1)}, u32[]{:S(2)}) copy-start(bf16[2048,1280]{1,0:T(8,128)(2,1)S(1)} %get-tuple-element.85.refs_0_) | copy-start | bytes 15728644
  42.1 14.2 %copy-start.3 = (bf16[2048,1280]{1,0:T(8,128)(2,1)}, bf16[2048,1280]{1,0:T(8,128)(2,1)S(1)}, u32[]{:S(2)}) copy-start(bf16[2048,1280]{1,0:T(8,128)(2,1)S(1)} %get-tuple-element.86.refs_1_) | copy-start | bytes 15728644
  42.1 14.2 %copy-start.5 = (bf16[2048,256]{1,0:T(8,128)(2,1)}, bf16[2048,256]{1,0:T(8,128)(2,1)S(1)}, u32[]{:S(2)}) copy-start(bf16[2048,256]{1,0:T(8,128)(2,1)S(1)} %get-tuple-element.78.refs_8_.xt_ref) | copy-start | bytes 3145732
  43.6 1.8 %collective-permute-start.9 = (bf16[2,2,64,768]{3,2,1,0:T(8,128)(2,1)S(1)}, bf16[2,2,64,768]{3,2,1,0:T(8,128)(2,1)S(1)}, u32[]{:S(2)}, u32[]{:S(2)}) collective-permute-start(bf16[2,2,64,768]{3,2,1,0:T(8,128)(2,1)S(1)} %in_order.5), channel_id=1, source_target_pairs={{0,8},{8,0},{16,24},{24,16},{1,9},{9,1},{17,25},{25,17},{2,10},{10... | collective-permute-start | bytes 1179656 | tf_op jit(solution)/shard_map/ppermute | solution.py:459
  45.4 2.2 %collective-permute-start.11 = (bf16[2,2,64,1024]{3,2,1,0:T(8,128)(2,1)S(1)}, bf16[2,2,64,1024]{3,2,1,0:T(8,128)(2,1)S(1)}, u32[]{:S(2)}, u32[]{:S(2)}) collective-permute-start(bf16[2,2,64,1024]{3,2,1,0:T(8,128)(2,1)S(1)} %packed.5), channel_id=1, source_target_pairs={{0,8},{8,0},{16,24},{24,16},{1,9},{9,1},{17,25},{25,17},{2,10},{10... | collective-permute-start | bytes 1572872 | tf_op jit(solution)/shard_map/ppermute | solution.py:459
  45.7 15.1 %collective-permute-start.14 = (bf16[2,64,1280]{2,1,0:T(8,128)(2,1)S(1)}, bf16[2,64,1280]{2,1,0:T(8,128)(2,1)S(1)}, u32[]{:S(2)}, u32[]{:S(2)}) collective-permute-start(bf16[2,64,1280]{2,1,0:T(8,128)(2,1)S(1)} %get-tuple-element.74.refs_2_.refs_3_.refs_0_), channel_id=1, source_target_pairs={{0,16},{8,24},{16,0},{24,8},{1,17},{9,25},{17,1},{25,9},{2,18},{10... | collective-permute-start | bytes 983048 | tf_op jit(solution)/shard_map/ppermute | solution.py:463
  46.7 13.1 %collective-permute-start.10 = (bf16[2,64,768]{2,1,0:T(8,128)(2,1)S(1)}, bf16[2,64,768]{2,1,0:T(8,128)(2,1)S(1)}, u32[]{:S(2)}, u32[]{:S(2)}) collective-permute-start(bf16[2,64,768]{2,1,0:T(8,128)(2,1)S(1)} %fusion.4.refs_2_), channel_id=1, source_target_pairs={{0,16},{8,24},{16,0},{24,8},{1,17},{9,25},{17,1},{25,9},{2,18},{10... | collective-permute-start | bytes 589832 | tf_op jit(solution)/shard_map/ppermute | solution.py:463
  56.3 4.5 %copy-start.7 = (f32[2048,256]{1,0:T(8,128)}, f32[2048,256]{1,0:T(8,128)S(1)}, u32[]{:S(2)}) copy-start(f32[2048,256]{1,0:T(8,128)S(1)} %get-tuple-element.87.refs_5_) | copy-start | bytes 6291460
  60.8 7.5 %collective-permute-start.15 = (bf16[2,2,64,1280]{3,2,1,0:T(8,128)(2,1)S(1)}, bf16[2,2,64,1280]{3,2,1,0:T(8,128)(2,1)S(1)}, u32[]{:S(2)}, u32[]{:S(2)}) collective-permute-start(bf16[2,2,64,1280]{3,2,1,0:T(8,128)(2,1)S(1)} %packed.7), channel_id=1, source_target_pairs={{0,8},{8,0},{16,24},{24,16},{1,9},{9,1},{17,25},{25,17},{2,10},{10... | collective-permute-start | bytes 1966088 | tf_op jit(solution)/shard_map/ppermute | solution.py:459
  60.9 7.3 %collective-permute-start.12 = (bf16[2,64,768]{2,1,0:T(8,128)(2,1)S(1)}, bf16[2,64,768]{2,1,0:T(8,128)(2,1)S(1)}, u32[]{:S(2)}, u32[]{:S(2)}) collective-permute-start(bf16[2,64,768]{2,1,0:T(8,128)(2,1)S(1)} %get-tuple-element.84.refs_0_.refs_3_.refs_2_), channel_id=1, source_target_pairs={{0,16},{8,24},{16,0},{24,8},{1,17},{9,25},{17,1},{25,9},{2,18},{10... | collective-permute-start | bytes 589832 | tf_op jit(solution)/shard_map/ppermute | solution.py:463
  68.2 9.8 %collective-permute-start.13 = (bf16[2,2,64,768]{3,2,1,0:T(8,128)(2,1)S(1)}, bf16[2,2,64,768]{3,2,1,0:T(8,128)(2,1)S(1)}, u32[]{:S(2)}, u32[]{:S(2)}) collective-permute-start(bf16[2,2,64,768]{3,2,1,0:T(8,128)(2,1)S(1)} %packed.6), channel_id=1, source_target_pairs={{0,8},{8,0},{16,24},{24,16},{1,9},{9,1},{17,25},{25,17},{2,10},{10... | collective-permute-start | bytes 1179656 | tf_op jit(solution)/shard_map/ppermute | solution.py:459
  68.3 2.5 %copy-start.2 = (bf16[2048,1280]{1,0:T(8,128)(2,1)S(1)}, bf16[2048,1280]{1,0:T(8,128)(2,1)}, u32[]{:S(2)}) copy-start(bf16[2048,1280]{1,0:T(8,128)(2,1)} %copy-done.1) | copy-start | bytes 15728644
  70.8 2.5 %copy-start.4 = (bf16[2048,1280]{1,0:T(8,128)(2,1)S(1)}, bf16[2048,1280]{1,0:T(8,128)(2,1)}, u32[]{:S(2)}) copy-start(bf16[2048,1280]{1,0:T(8,128)(2,1)} %copy-done.3) | copy-start | bytes 15728644
  73.3 1.6 %copy-start.8 = (f32[2048,256]{1,0:T(8,128)S(1)}, f32[2048,256]{1,0:T(8,128)}, u32[]{:S(2)}) copy-start(f32[2048,256]{1,0:T(8,128)} %copy-done.7) | copy-start | bytes 6291460
  78.0 7.4 %copy-start.6 = (bf16[2048,256]{1,0:T(8,128)(2,1)S(1)}, bf16[2048,256]{1,0:T(8,128)(2,1)}, u32[]{:S(2)}) copy-start(bf16[2048,256]{1,0:T(8,128)(2,1)} %copy-done.5) | copy-start | bytes 3145732
  82.1 8.8 %collective-permute-start.16 = (bf16[2,2,32,1024]{3,2,1,0:T(8,128)(2,1)S(1)}, bf16[2,2,32,1024]{3,2,1,0:T(8,128)(2,1)S(1)}, u32[]{:S(2)}, u32[]{:S(2)}) collective-permute-start(bf16[2,2,32,1024]{3,2,1,0:T(8,128)(2,1)S(1)} %fusion.2), channel_id=1, source_target_pairs={{0,1},{1,0},{2,3},{3,2},{4,5},{5,4},{6,7},{7,6},{8,9},{9,8},{10,11... | collective-permute-start | bytes 786440 | tf_op jit(solution)/shard_map/ppermute | solution.py:445
  83.8 9.9 %collective-permute-start.19 = (bf16[2,2,32,1024]{3,2,1,0:T(8,128)(2,1)S(1)}, bf16[2,2,32,1024]{3,2,1,0:T(8,128)(2,1)S(1)}, u32[]{:S(2)}, u32[]{:S(2)}) collective-permute-start(bf16[2,2,32,1024]{3,2,1,0:T(8,128)(2,1)S(1)} %fusion.3), channel_id=1, source_target_pairs={{0,2},{1,3},{2,0},{3,1},{4,6},{5,7},{6,4},{7,5},{8,10},{9,11},{10,... | collective-permute-start | bytes 786440 | tf_op jit(solution)/shard_map/ppermute | solution.py:445
  91.0 8.9 %collective-permute-start.17 = (bf16[2,32,1024]{2,1,0:T(8,128)(2,1)S(1)}, bf16[2,32,1024]{2,1,0:T(8,128)(2,1)S(1)}, u32[]{:S(2)}, u32[]{:S(2)}) collective-permute-start(bf16[2,32,1024]{2,1,0:T(8,128)(2,1)S(1)} %fusion.6), channel_id=1, source_target_pairs={{0,4},{1,5},{2,6},{3,7},{4,0},{5,1},{6,2},{7,3},{8,12},{9,13},{10,... | collective-permute-start | bytes 393224 | tf_op jit(solution)/shard_map/ppermute | solution.py:445
  93.8 6.9 %collective-permute-start.20 = (bf16[2,32,1024]{2,1,0:T(8,128)(2,1)S(1)}, bf16[2,32,1024]{2,1,0:T(8,128)(2,1)S(1)}, u32[]{:S(2)}, u32[]{:S(2)}) collective-permute-start(bf16[2,32,1024]{2,1,0:T(8,128)(2,1)S(1)} %fusion.7), channel_id=1, source_target_pairs={{0,1},{1,0},{2,3},{3,2},{4,5},{5,4},{6,7},{7,6},{8,9},{9,8},{10,11... | collective-permute-start | bytes 393224 | tf_op jit(solution)/shard_map/ppermute | solution.py:445
  99.9 4.3 %collective-permute-start.18 = (bf16[32,1024]{1,0:T(8,128)(2,1)S(1)}, bf16[32,1024]{1,0:T(8,128)(2,1)S(1)}, u32[]{:S(2)}, u32[]{:S(2)}) collective-permute-start(bf16[32,1024]{1,0:T(8,128)(2,1)S(1)} %fusion.10), channel_id=1, source_target_pairs={{0,2},{1,3},{2,0},{3,1},{4,6},{5,7},{6,4},{7,5},{8,10},{9,11},{10,... | collective-permute-start | bytes 196616 | tf_op jit(solution)/shard_map/ppermute | solution.py:445
  100.7 6.8 %collective-permute-start.21 = (bf16[32,1024]{1,0:T(8,128)(2,1)S(1)}, bf16[32,1024]{1,0:T(8,128)(2,1)S(1)}, u32[]{:S(2)}, u32[]{:S(2)}) collective-permute-start(bf16[32,1024]{1,0:T(8,128)(2,1)S(1)} %fusion.11), channel_id=1, source_target_pairs={{0,4},{1,5},{2,6},{3,7},{4,0},{5,1},{6,2},{7,3},{8,12},{9,13},{10,... | collective-permute-start | bytes 196616 | tf_op jit(solution)/shard_map/ppermute | solution.py:445
